TPU v7x, 32 devices: a whole 2x2x4 slice. The times are simulated.
32 devices in a mesh: clip: 2 (over x), frame: 8 (over z, y), head: 2 (over core).
Axes of the slice: x: 2, y: 2, z: 4, core: 2. Of those that a mesh axis runs over, the one named last changes fastest.
Arguments:
- queries: bfloat16 [8192, 1536], P(('clip', 'frame', 'head')), parts along dimension 0, may hold values from -12 to 12
- key_tokens: bfloat16 [8192, 1536], P(('clip', 'frame', 'head')), parts along dimension 0, may hold values from -6 to 6
- value_tokens: bfloat16 [8192, 1536], P(('clip', 'frame', 'head')), parts along dimension 0, may hold values from -6 to 6
- radial_table: int32 [8, 8], replicated, may hold values from 0 to 4, as said below
- out_weight: bfloat16 [1536, 3072], P('head'), may hold values from -1.5 to 1.5
Outputs:
- projected: bfloat16 [8192, 3072], P(('clip', 'frame', 'head')), parts along dimension 0
There are 2 independent parts, one for each index of `clip`. A program takes and returns all parts, laid end to end along the dimension named above; an argument that names none is the same for every part. Nothing has to cross between parts.
Inputs may be any that keep to these rules, and one draw needn't show every extreme that they name: radial_table[f, f] = 4; for 1 <= |f - g| <= 3 the entry lies from c - c // 2 to c, where c = 2 at distance 1 and 1 at distances 2 and 3; beyond distance 3 it is 0.
All inputs are finite; a program needn't handle non-finite values.
Results may differ from a plain program's by a relative error of at most 0.0055.
Values may be sent and summed in bfloat16 or wider, within the bound.
No kernel may reach another device: no remote copies, remote signals or barrier semaphores. Data moves between devices by JAX's collectives and lax.ppermute only.
A program may use at most 128 MiB of HBM per device.

v0:
```python
import functools
import math

import jax
import jax.numpy as jnp
from jax import lax
from jax.experimental import pallas as pl
from jax.experimental.pallas import tpu as pltpu
from jax.sharding import PartitionSpec as P

DH = 128
BS = 128
CROSS = 3
STAT_ROWS = 16
BATCH = 4
TILE = 768
NEG = -1e30
LOG2_SCALE = math.log2(math.e) / math.sqrt(DH)
MIB = 1024 * 1024


def frame_ids():
    frame = lax.axis_index("frame")
    odd = lax.rem(frame, 2)
    sign = 1 - 2 * odd
    return frame, sign


def entry(table_ref, query_frame, key_frame):
    frames = table_ref.shape[0]
    inside = (key_frame >= 0) & (key_frame < frames)
    count = table_ref[query_frame, jnp.clip(key_frame, 0, frames - 1)]
    return jnp.where(inside, count, 0)


def attend(problems):
    scores = []
    for query, parts in problems:
        row = []
        for keys, _, valid in parts:
            raw = lax.dot_general(
                query, keys, (((1,), (1,)), ((), ())), preferred_element_type=jnp.float32
            )
            row.append(raw if valid is None else jnp.where(valid, raw, NEG))
        scores.append(row)
    tops = []
    for row in scores:
        best = None
        for raw in row:
            for at in range(0, raw.shape[1], BS):
                piece = raw[:, at : at + BS]
                best = piece if best is None else jnp.maximum(best, piece)
        tops.append(best.max(axis=1, keepdims=True))
    weights = [
        [jnp.exp2((raw - top) * LOG2_SCALE) for raw in row] for row, top in zip(scores, tops)
    ]
    totals = []
    for row in weights:
        total = None
        for weight in row:
            for at in range(0, weight.shape[1], BS):
                piece = weight[:, at : at + BS]
                total = piece if total is None else total + piece
        totals.append(total.sum(axis=1, keepdims=True))
    results = []
    for (_, parts), row, top, total in zip(problems, weights, tops, totals):
        blended = 0.0
        for (_, values, _), weight in zip(parts, row):
            blended = blended + jnp.dot(
                weight.astype(jnp.bfloat16), values, preferred_element_type=jnp.float32
            )
        results.append((blended / total, top * LOG2_SCALE + jnp.log2(total)))
    return results


def attend_heads(heads, blocks, problem, out, dtype):
    rows = blocks * BS
    lanes = lax.broadcasted_iota(jnp.int32, (rows, DH), 1)
    stats = jnp.zeros((rows, DH), jnp.float32)
    items = [(place, head, block) for place, head in enumerate(heads) for block in range(blocks)]
    sums = {}
    for at in range(0, len(items), BATCH):
        chunk = items[at : at + BATCH]
        results = attend([problem(head, block) for _, head, block in chunk])
        for (place, head, block), (blended, logsum) in zip(chunk, results):
            out[block * BS : (block + 1) * BS, place * DH : (place + 1) * DH] = blended.astype(dtype)
            sums[head, block] = logsum
    for head in heads:
        column = jnp.concatenate([sums[head, block] for block in range(blocks)], axis=0)
        stats = jnp.where(lanes == head, column, stats)
    return stats


def head_cols(head):
    return slice(head * DH, (head + 1) * DH)


def pair(ref, col, block):
    rows = ref.shape[0] // 2
    cols = head_cols(col)
    return (
        ref[block * BS : (block + 1) * BS, cols],
        ref[rows + block * BS : rows + (block + 1) * BS, cols],
    )


def following(ref, first, col, first_col, block):
    if (block + 1) * BS < ref.shape[0] // 2:
        return pair(ref, col, block + 1)
    return pair(first, first_col, 0)


class Near:
    def __init__(self, refs):
        self.refs = refs

    def away(self, head):
        if head < 6:
            return self.refs["major1"], head
        if head < 9:
            return self.refs["major2"], head - 6
        return self.refs["major3"], head - 9

    def near(self, head):
        if head < 9:
            return self.refs["minor1"], head - 3
        return self.refs["minor2"], head - 9

    def near_first(self, head):
        if head < 9:
            return self.refs["first1"], head - 3
        return self.refs["first2"], head - 9

    def relay(self, head):
        if head < 6:
            return self.refs["minor2"], head
        return self.refs["minor3"], head - 6


def partner_kernel(heads, names, table_ref, query, keys, values, sib_keys, sib_values, *rest):
    refs = dict(zip(names, rest))
    out = rest[len(names)]
    buffers = Near(refs)
    rows = query.shape[0]
    blocks = rows // BS
    frame, sign = frame_ids()
    partner = frame + sign
    own_count = entry(table_ref, partner, frame)
    near_count = entry(table_ref, partner, frame + 2 * sign)
    away_valid = entry(table_ref, partner, frame - 2 * sign) > 0
    relay_valid = entry(table_ref, partner, frame + 4 * sign) > 0
    cross_valid = entry(table_ref, partner, frame - sign) > 0

    def problem(head, block):
        mine = slice(block * BS, (block + 1) * BS)
        cols = head_cols(head)
        parts = [(keys[mine, cols], values[mine, cols], None)]
        if block + 1 < blocks:
            after = slice((block + 1) * BS, (block + 2) * BS)
            parts.append((keys[after, cols], values[after, cols], own_count > 1))
        else:
            parts.append((sib_keys[:BS, cols], sib_values[:BS, cols], own_count > 1))
        away, col = buffers.away(head)
        parts.append((*pair(away, col, block), away_valid))
        if head < CROSS:
            parts.append((*pair(refs["major2"], CROSS + head, block), cross_valid))
        else:
            near, col = buffers.near(head)
            first, first_col = buffers.near_first(head)
            parts.append((*pair(near, col, block), near_count > 0))
            parts.append((*following(near, first, col, first_col, block), near_count > 1))
            relay, col = buffers.relay(head)
            parts.append((*pair(relay, col, block), relay_valid))
        return query[mine, cols], parts

    stats = attend_heads(heads, blocks, problem, out, out.dtype)
    out[rows:, :] = jnp.zeros((STAT_ROWS, out.shape[1]), out.dtype)
    rest_sum = stats.T[:STAT_ROWS]
    for part in range(3):
        piece = rest_sum.astype(jnp.bfloat16)
        out[rows:, part * rows : (part + 1) * rows] = piece
        rest_sum = rest_sum - piece.astype(jnp.float32)


def own_kernel(heads, names, table_ref, query, keys, values, sib_keys, sib_values, *rest):
    refs = dict(zip(names, rest))
    out, out_stats = rest[len(names) :]
    buffers = Near(refs)
    rows = query.shape[0]
    blocks = rows // BS
    frame, sign = frame_ids()
    near_valid = entry(table_ref, frame, frame + 2 * sign) > 0
    away_valid = entry(table_ref, frame, frame - 2 * sign) > 0
    cross_count = entry(table_ref, frame, frame - sign)
    far_valid = entry(table_ref, frame, frame - 3 * sign) > 0

    def problem(head, block):
        mine = slice(block * BS, (block + 1) * BS)
        cols = head_cols(head)
        parts = [
            (keys[:, cols], values[:, cols], None),
            (sib_keys[:, cols], sib_values[:, cols], None),
        ]
        away, col = buffers.away(head)
        parts.append((*pair(away, col, block), away_valid))
        if head < CROSS:
            cross = refs["major2"]
            parts.append((*pair(cross, CROSS + head, block), cross_count > 0))
            parts.append(
                (
                    *following(cross, refs["first2"], CROSS + head, CROSS + head, block),
                    cross_count > 1,
                )
            )
            parts.append((*pair(refs["major3"], CROSS + head, block), far_valid))
        else:
            near, col = buffers.near(head)
            parts.append((*pair(near, col, block), near_valid))
        return query[mine, cols], parts

    out_stats[...] = attend_heads(heads, blocks, problem, out, out.dtype)


def read_stats(ref):
    rows = ref.shape[0] - STAT_ROWS
    total = 0.0
    for part in range(3):
        total = total + ref[rows:, part * rows : (part + 1) * rows].astype(jnp.float32)
    padding = jnp.zeros((DH - STAT_ROWS, rows), jnp.float32)
    return jnp.concatenate([total, padding], axis=0).T


def final_kernel(own_heads, part_heads, *refs):
    count = len(own_heads)
    owns, stats = refs[0 : 2 * count : 2], refs[1 : 2 * count : 2]
    parts = refs[2 * count : 2 * count + len(part_heads)]
    weight, out, attended = refs[2 * count + len(part_heads) :]

    @pl.when(pl.program_id(0) == 0)
    def _():
        rows = out.shape[0]
        lanes = lax.broadcasted_iota(jnp.int32, (rows, DH), 1)
        own_sum = jnp.zeros((rows, DH), jnp.float32)
        own_at, part_at = {}, {}
        for ref, stat, heads in zip(owns, stats, own_heads):
            for place, head in enumerate(heads):
                own_at[head] = ref, place
                own_sum = jnp.where(lanes == head, stat[...], own_sum)
        part_sum = jnp.zeros((rows, DH), jnp.float32)
        for ref, heads in zip(parts, part_heads):
            received = read_stats(ref)
            for place, head in enumerate(heads):
                part_at[head] = ref, place
                part_sum = jnp.where(lanes == head, received, part_sum)
        top = jnp.maximum(own_sum, part_sum)
        own_weight = jnp.exp2(own_sum - top)
        part_weight = jnp.exp2(part_sum - top)
        total = own_weight + part_weight
        own_weight = own_weight / total
        part_weight = part_weight / total
        for head in sorted(own_at):
            own, own_place = own_at[head]
            part, part_place = part_at[head]
            mixed = (
                own_weight[:, head : head + 1] * own[:, head_cols(own_place)]
                + part_weight[:, head : head + 1]
                * part[:rows, head_cols(part_place)].astype(jnp.float32)
            )
            attended[:, head_cols(head)] = mixed.astype(attended.dtype)

    out[...] = jnp.dot(
        attended[...], weight[...], preferred_element_type=jnp.float32
    ).astype(out.dtype)


def whole(shape):
    return pl.BlockSpec(shape, lambda i: (0,) * len(shape))


def run(body, name, table, operands, out_shapes, flops):
    return pl.pallas_call(
        body,
        grid=(1,),
        in_specs=[pl.BlockSpec(memory_space=pltpu.SMEM)] + [whole(x.shape) for x in operands],
        out_specs=[whole(s.shape) for s in out_shapes],
        out_shape=out_shapes,
        compiler_params=pltpu.CompilerParams(vmem_limit_bytes=40 * MIB),
        cost_estimate=pl.CostEstimate(
            flops=flops, bytes_accessed=4 * MIB, transcendentals=flops // 512
        ),
        name=name,
    )(table, *operands)


def per_device(queries, key_tokens, value_tokens, radial_table, out_weight):
    frames = lax.axis_size("frame")
    cores = lax.axis_size("head")
    rows, features = queries.shape
    heads_all = features // DH

    def moves(target):
        return [(f, target(f)) for f in range(frames) if 0 <= target(f) < frames]

    partner_moves = moves(lambda f: f ^ 1)
    near_moves = moves(lambda f: f - 2 if f % 2 == 0 else f + 2)
    away_moves = moves(lambda f: f + 2 if f % 2 == 0 else f - 2)
    core_moves = [(c, cores - 1 - c) for c in range(cores)]

    def pack(first, last):
        cols = slice(first * DH, last * DH)
        return jnp.concatenate([key_tokens[:, cols], value_tokens[:, cols]], axis=0)

    def firsts(packed):
        return jnp.concatenate([packed[:BS], packed[rows : rows + BS]], axis=0)

    def beside(*packed):
        return jnp.concatenate(packed, axis=1)

    half = CROSS * DH
    major1 = lax.ppermute(pack(0, 6), "frame", away_moves)
    minor1 = lax.ppermute(pack(3, 9), "frame", near_moves)
    cross = lax.ppermute(pack(0, 3), "frame", partner_moves)
    partner_query = lax.ppermute(queries, "frame", partner_moves)
    sib_keys = lax.ppermute(key_tokens, "head", core_moves)
    sib_values = lax.ppermute(value_tokens, "head", core_moves)
    all_weight = lax.all_gather(out_weight, "head", axis=0, tiled=True)
    major2 = lax.ppermute(beside(pack(6, 9), cross), "frame", away_moves)
    minor2 = lax.ppermute(beside(pack(9, 12), minor1[:, :half]), "frame", near_moves)
    first1 = lax.ppermute(firsts(minor1), "head", core_moves)
    major3 = lax.ppermute(beside(pack(9, 12), major2[:, half:]), "frame", away_moves)
    minor3 = lax.ppermute(beside(minor1[:, half:], minor2[:, :half]), "frame", near_moves)
    first2 = lax.ppermute(
        firsts(beside(minor2[:, :half], major2[:, half:])), "head", core_moves
    )
    refs = {
        "major1": major1,
        "major2": major2,
        "major3": major3,
        "minor1": minor1,
        "minor2": minor2,
        "minor3": minor3,
        "first1": first1,
        "first2": first2,
    }
    local = (key_tokens, value_tokens, sib_keys, sib_values)

    def partner_part(heads, names):
        shape = jax.ShapeDtypeStruct((rows + STAT_ROWS, len(heads) * DH), jnp.bfloat16)
        (part,) = run(
            functools.partial(partner_kernel, heads, names),
            "partner_part",
            radial_table,
            (partner_query, *local, *(refs[n] for n in names)),
            [shape],
            len(heads) * rows * 6 * BS * DH * 4,
        )
        return lax.ppermute(part, "frame", partner_moves)

    def own_part(heads, names):
        return run(
            functools.partial(own_kernel, heads, names),
            "own_part",
            radial_table,
            (queries, *local, *(refs[n] for n in names)),
            [
                jax.ShapeDtypeStruct((rows, len(heads) * DH), jnp.float32),
                jax.ShapeDtypeStruct((rows, DH), jnp.float32),
            ],
            len(heads) * rows * 6 * BS * DH * 4,
        )

    part_heads = (tuple(range(0, 6)), tuple(range(6, 12)))
    own_heads = (tuple(range(3, 9)), (0, 1, 2, 9, 10, 11))
    part0 = partner_part(part_heads[0], ("major1", "major2", "minor1", "minor2", "first1"))
    own0 = own_part(own_heads[0], ("major1", "major2", "minor1"))
    part1 = partner_part(
        part_heads[1], ("major2", "major3", "minor1", "minor2", "minor3", "first1", "first2")
    )
    own1 = own_part(own_heads[1], ("major1", "major2", "major3", "minor2", "first2"))

    operands = (*own0, *own1, part0, part1)
    columns = out_weight.shape[1]
    projected = pl.pallas_call(
        functools.partial(final_kernel, own_heads, part_heads),
        grid=(columns // TILE,),
        in_specs=[whole(x.shape) for x in operands]
        + [pl.BlockSpec((features, TILE), lambda i: (0, i))],
        out_specs=pl.BlockSpec((rows, TILE), lambda i: (0, i)),
        out_shape=jax.ShapeDtypeStruct((rows, columns), jnp.bfloat16),
        scratch_shapes=[pltpu.VMEM((rows, features), jnp.bfloat16)],
        compiler_params=pltpu.CompilerParams(vmem_limit_bytes=40 * MIB),
        cost_estimate=pl.CostEstimate(
            flops=2 * rows * features * columns, bytes_accessed=12 * MIB, transcendentals=0
        ),
        name="merge_and_project",
    )(*operands, all_weight)
    return projected


def solution(mesh):
    in_specs = (
        P(("clip", "frame", "head"), None),
        P(("clip", "frame", "head"), None),
        P(("clip", "frame", "head"), None),
        P(),
        P("head", None),
    )
    out_specs = P(("clip", "frame", "head"), None)
    return jax.shard_map(
        per_device, mesh=mesh, in_specs=in_specs, out_specs=out_specs, check_vma=False
    )
```

profile of v0, /device:TPU:0, one launch (start us, length us, event | category | flops | bytes accessed | tf_op | source)
XLA Modules:
  0.0 115.1 jit_solution(9474205533518421246)
XLA Ops:
  6.5 0.7 all-gather.2.cloned.1.call-update
  7.3 0.4 copy-done
  7.7 1.1 copy-done.1
  8.9 3.1 %collective-permute-start.3 = (bf16[512,384]{1,0:T(8,128)(2,1)S(1)}, bf16[512,384]{1,0:T(8,128)(2,1)S(1)}, u32[]{:S(2)}, u32[]{:S(2)}) collective-permute-start(bf16[512,384]{1,0:T(8,128)(2,1)S(1)} %pad_maximum_fusion.7), channel_id=1, source_target_pairs={{0,2},{2,0},{4,6},{6,4},{8,10},{10,8},{12,14},{14,12},{1,3},{3,1},... | collective-permute-start | bytes 1179656 | tf_op jit(solution)/shard_map/ppermute | solution.py:322
  12.2 1.3 %collective-permute-start.5 = (bf16[512,768]{1,0:T(8,128)(2,1)S(1)}, bf16[512,768]{1,0:T(8,128)(2,1)S(1)}, u32[]{:S(2)}, u32[]{:S(2)}) collective-permute-start(bf16[512,768]{1,0:T(8,128)(2,1)S(1)} %pad_maximum_fusion.3), channel_id=1, source_target_pairs={{2,6},{4,0},{6,10},{8,4},{10,14},{12,8},{3,7},{5,1},{7,11},{9,5},{... | collective-permute-start | bytes 2359304 | tf_op jit(solution)/shard_map/ppermute | solution.py:321
  13.5 7.6 %collective-permute-done.3 = bf16[512,384]{1,0:T(8,128)(2,1)S(1)} collective-permute-done((bf16[512,384]{1,0:T(8,128)(2,1)S(1)}, bf16[512,384]{1,0:T(8,128)(2,1)S(1)}, u32[]{:S(2)}, u32[]{:S(2)}) %collective-permute-start.3) | collective-permute-done | bytes 393248 | tf_op jit(solution)/shard_map/ppermute | solution.py:322
  21.1 3.8 %collective-permute-start.4 = (bf16[512,768]{1,0:T(8,128)(2,1)S(1)}, bf16[512,768]{1,0:T(8,128)(2,1)S(1)}, u32[]{:S(2)}, u32[]{:S(2)}) collective-permute-start(bf16[512,768]{1,0:T(8,128)(2,1)S(1)} %pad_maximum_fusion.2), channel_id=1, source_target_pairs={{0,4},{4,8},{6,2},{8,12},{10,6},{14,10},{1,5},{5,9},{7,3},{9,13},{... | collective-permute-start | bytes 2359304 | tf_op jit(solution)/shard_map/ppermute | solution.py:327
  24.9 8.1 %collective-permute-done.5.rest_2_ = bf16[512,768]{1,0:T(8,128)(2,1)S(1)} collective-permute-done((bf16[512,768]{1,0:T(8,128)(2,1)S(1)}, bf16[512,768]{1,0:T(8,128)(2,1)S(1)}, u32[]{:S(2)}, u32[]{:S(2)}) %collective-permute-start.5) | collective-permute-done | bytes 786464 | tf_op jit(solution)/shard_map/ppermute | solution.py:321
  33.0 0.1 fusion.5
  33.1 7.6 %collective-permute-done.4.rest_1_.rest_0_ = bf16[512,768]{1,0:T(8,128)(2,1)S(1)} collective-permute-done((bf16[512,768]{1,0:T(8,128)(2,1)S(1)}, bf16[512,768]{1,0:T(8,128)(2,1)S(1)}, u32[]{:S(2)}, u32[]{:S(2)}) %collective-permute-start.4) | collective-permute-done | bytes 786464 | tf_op jit(solution)/shard_map/ppermute | solution.py:327
  40.8 0.1 pad_maximum_fusion.5
  40.9 1.4 %collective-permute-start.7 = (bf16[512,768]{1,0:T(8,128)(2,1)S(1)}, bf16[512,768]{1,0:T(8,128)(2,1)S(1)}, u32[]{:S(2)}, u32[]{:S(2)}) collective-permute-start(bf16[512,768]{1,0:T(8,128)(2,1)S(1)} %get-tuple-element.27), channel_id=1, source_target_pairs={{2,6},{4,0},{6,10},{8,4},{10,14},{12,8},{3,7},{5,1},{7,11},{9,5},{... | collective-permute-start | bytes 2359304 | tf_op jit(solution)/shard_map/ppermute | solution.py:328
  42.4 0.1 collective-permute-start
  42.4 0.5 collective-permute-start.1
  42.9 4.7 %collective-permute-start.9 = (bf16[256,1536]{1,0:T(8,128)(2,1)S(1)}, bf16[256,1536]{1,0:T(8,128)(2,1)S(1)}, u32[]{:S(2)}, u32[]{:S(2)}) collective-permute-start(bf16[256,1536]{1,0:T(8,128)(2,1)S(1)} %copy-done.3), channel_id=1, source_target_pairs={{0,2},{2,0},{4,6},{6,4},{8,10},{10,8},{12,14},{14,12},{1,3},{3,1},... | collective-permute-start | bytes 2359304 | tf_op jit(solution)/shard_map/ppermute | solution.py:323
  47.6 3.5 %collective-permute-start.2 = (bf16[512,768]{1,0:T(8,128)(2,1)S(1)}, bf16[512,768]{1,0:T(8,128)(2,1)S(1)}, u32[]{:S(2)}, u32[]{:S(2)}) collective-permute-start(bf16[512,768]{1,0:T(8,128)(2,1)S(1)} %pad_maximum_fusion.1), channel_id=1, source_target_pairs={{0,4},{4,8},{6,2},{8,12},{10,6},{14,10},{1,5},{5,9},{7,3},{9,13},{... | collective-permute-start | bytes 2359304 | tf_op jit(solution)/shard_map/ppermute | solution.py:320
  51.1 10.0 %collective-permute-done.7.rest_3_ = bf16[512,768]{1,0:T(8,128)(2,1)S(1)} collective-permute-done((bf16[512,768]{1,0:T(8,128)(2,1)S(1)}, bf16[512,768]{1,0:T(8,128)(2,1)S(1)}, u32[]{:S(2)}, u32[]{:S(2)}) %collective-permute-start.7) | collective-permute-done | bytes 786464 | tf_op jit(solution)/shard_map/ppermute | solution.py:328
  61.2 3.7 %collective-permute-start.6 = (bf16[512,768]{1,0:T(8,128)(2,1)S(1)}, bf16[512,768]{1,0:T(8,128)(2,1)S(1)}, u32[]{:S(2)}, u32[]{:S(2)}) collective-permute-start(bf16[512,768]{1,0:T(8,128)(2,1)S(1)} %get-tuple-element.28), channel_id=1, source_target_pairs={{0,4},{4,8},{6,2},{8,12},{10,6},{14,10},{1,5},{5,9},{7,3},{9,13},{... | collective-permute-start | bytes 2359304 | tf_op jit(solution)/shard_map/ppermute | solution.py:330
  65.0 1.5 %collective-permute-start.12 = (bf16[512,768]{1,0:T(8,128)(2,1)S(1)}, bf16[512,768]{1,0:T(8,128)(2,1)S(1)}, u32[]{:S(2)}, u32[]{:S(2)}) collective-permute-start(bf16[512,768]{1,0:T(8,128)(2,1)S(1)} %pad_maximum_fusion.6), channel_id=1, source_target_pairs={{2,6},{4,0},{6,10},{8,4},{10,14},{12,8},{3,7},{5,1},{7,11},{9,5},{... | collective-permute-start | bytes 2359304 | tf_op jit(solution)/shard_map/ppermute | solution.py:331
  66.6 0.1 collective-permute-start.10
  66.7 0.6 collective-permute-start.8
  67.3 1.7 %collective-permute-done.2.rest_0_ = bf16[512,768]{1,0:T(8,128)(2,1)S(1)} collective-permute-done((bf16[512,768]{1,0:T(8,128)(2,1)S(1)}, bf16[512,768]{1,0:T(8,128)(2,1)S(1)}, u32[]{:S(2)}, u32[]{:S(2)}) %collective-permute-start.2) | collective-permute-done | bytes 786464 | tf_op jit(solution)/shard_map/ppermute | solution.py:320
  69.0 3.2 %partner_part.2 = bf16[272,768]{1,0:T(8,128)(2,1)S(1)} custom-call(s32[8,8]{1,0:T(8,128)S(1)} %copy-done.4, bf16[256,1536]{1,0:T(8,128)(2,1)S(1)} %collective-permute-done.9.query, bf16[256,1536]{1,0:T(8,128)(2,1)S(1)} %copy-done, bf16[256,1536]{1,0:T(8,128)(2,1)S(1)} %copy-done.1, bf16[256,1536]{1,0:T(8,128)(2,1)S(1)} %collective-permute-done.sib_keys, ...), custom_call_target="tpu_custom_call" | custom-call | flops 603979776 | bytes 4194304 | tf_op jit(solution)/shard_map/partner_part/pallas_call | solution.py:281
  72.3 1.6 %collective-permute-start.11 = (bf16[272,768]{1,0:T(8,128)(2,1)S(1)}, bf16[272,768]{1,0:T(8,128)(2,1)S(1)}, u32[]{:S(2)}, u32[]{:S(2)}) collective-permute-start(bf16[272,768]{1,0:T(8,128)(2,1)S(1)} %partner_part.2), channel_id=1, source_target_pairs={{0,2},{2,0},{4,6},{6,4},{8,10},{10,8},{12,14},{14,12},{1,3},{3,1},... | collective-permute-start | bytes 1253384 | tf_op jit(solution)/shard_map/ppermute | solution.py:357
  73.8 10.9 %collective-permute-done.6.rest_2_.rest_1_ = bf16[512,768]{1,0:T(8,128)(2,1)S(1)} collective-permute-done((bf16[512,768]{1,0:T(8,128)(2,1)S(1)}, bf16[512,768]{1,0:T(8,128)(2,1)S(1)}, u32[]{:S(2)}, u32[]{:S(2)}) %collective-permute-start.6) | collective-permute-done | bytes 786464 | tf_op jit(solution)/shard_map/ppermute | solution.py:330
  84.7 3.7 %partner_part.3 = bf16[272,768]{1,0:T(8,128)(2,1)S(1)} custom-call(s32[8,8]{1,0:T(8,128)S(1)} %copy-done.4, bf16[256,1536]{1,0:T(8,128)(2,1)S(1)} %collective-permute-done.9.query, bf16[256,1536]{1,0:T(8,128)(2,1)S(1)} %copy-done, bf16[256,1536]{1,0:T(8,128)(2,1)S(1)} %copy-done.1, bf16[256,1536]{1,0:T(8,128)(2,1)S(1)} %collective-permute-done.sib_keys, ...), custom_call_target="tpu_custom_call" | custom-call | flops 603979776 | bytes 4194304 | tf_op jit(solution)/shard_map/partner_part/pallas_call | solution.py:281
  88.3 1.3 %collective-permute-start.13 = (bf16[272,768]{1,0:T(8,128)(2,1)S(1)}, bf16[272,768]{1,0:T(8,128)(2,1)S(1)}, u32[]{:S(2)}, u32[]{:S(2)}) collective-permute-start(bf16[272,768]{1,0:T(8,128)(2,1)S(1)} %partner_part.3), channel_id=1, source_target_pairs={{0,2},{2,0},{4,6},{6,4},{8,10},{10,8},{12,14},{14,12},{1,3},{3,1},... | collective-permute-start | bytes 1253384 | tf_op jit(solution)/shard_map/ppermute | solution.py:357
  89.6 3.0 %own_part.2 = (f32[256,768]{1,0:T(8,128)S(1)}, f32[256,128]{1,0:T(8,128)S(1)}) custom-call(s32[8,8]{1,0:T(8,128)S(1)} %copy-done.4, bf16[256,1536]{1,0:T(8,128)(2,1)S(1)} %copy-done.3, bf16[256,1536]{1,0:T(8,128)(2,1)S(1)} %copy-done, bf16[256,1536]{1,0:T(8,128)(2,1)S(1)} %copy-done.1, bf16[256,1536]{1,0:T(8,128)(2,1)S(1)} %collective-permute-done.sib_keys, ...), custom_call_target="tpu_custom_call" | custom-call | flops 603979776 | bytes 4194304 | tf_op jit(solution)/shard_map/own_part/pallas_call | solution.py:281
  92.6 3.4 %own_part.3 = (f32[256,768]{1,0:T(8,128)S(1)}, f32[256,128]{1,0:T(8,128)S(1)}) custom-call(s32[8,8]{1,0:T(8,128)S(1)} %copy-done.4, bf16[256,1536]{1,0:T(8,128)(2,1)S(1)} %copy-done.3, bf16[256,1536]{1,0:T(8,128)(2,1)S(1)} %copy-done, bf16[256,1536]{1,0:T(8,128)(2,1)S(1)} %copy-done.1, bf16[256,1536]{1,0:T(8,128)(2,1)S(1)} %collective-permute-done.sib_keys, ...), custom_call_target="tpu_custom_call" | custom-call | flops 603979776 | bytes 4194304 | tf_op jit(solution)/shard_map/own_part/pallas_call | solution.py:281
  96.0 2.9 %collective-permute-done.13.refs_5_ = bf16[272,768]{1,0:T(8,128)(2,1)S(1)} collective-permute-done((bf16[272,768]{1,0:T(8,128)(2,1)S(1)}, bf16[272,768]{1,0:T(8,128)(2,1)S(1)}, u32[]{:S(2)}, u32[]{:S(2)}) %collective-permute-start.13) | collective-permute-done | bytes 417824 | tf_op jit(solution)/shard_map/ppermute | solution.py:357
  98.9 3.7 %copy-done.2 = bf16[1536,3072]{1,0:T(8,128)(2,1)S(1)} copy-done((bf16[1536,3072]{1,0:T(8,128)(2,1)S(1)}, bf16[1536,3072]{1,0:T(8,128)(2,1)}, u32[]{:S(2)}) %copy-start.2) | copy-done | bytes 9437208
  102.6 5.6 %merge_and_project.1 = bf16[256,3072]{1,0:T(8,128)(2,1)} custom-call(f32[256,768]{1,0:T(8,128)S(1)} %get-tuple-element.9.refs_0_, f32[256,128]{1,0:T(8,128)S(1)} %get-tuple-element.10.refs_1_, f32[256,768]{1,0:T(8,128)S(1)} %get-tuple-element.11.refs_2_, f32[256,128]{1,0:T(8,128)S(1)} %get-tuple-element.12.refs_3_, ...), custom_call_target="tpu_custom_call" | custom-call | flops 2415919104 | bytes 12582912 | tf_op jit(solution)/shard_map/merge_and_project/pallas_call | solution.py:383
  (31 shorter events, 0.7 us)
Async XLA Ops:
  6.5 1.1 copy-start
  6.5 92.3 %all-gather.2.cloned.1.call-start = ((), (), s32[]{:S(2)}) async-start(), calls=%async_computation | async-start | bytes 14155776 | tf_op jit(solution)/shard_map/all_gather | solution.py:326
  7.7 1.1 copy-start.1
  8.9 12.1 %collective-permute-start.3 = (bf16[512,384]{1,0:T(8,128)(2,1)S(1)}, bf16[512,384]{1,0:T(8,128)(2,1)S(1)}, u32[]{:S(2)}, u32[]{:S(2)}) collective-permute-start(bf16[512,384]{1,0:T(8,128)(2,1)S(1)} %pad_maximum_fusion.7), channel_id=1, source_target_pairs={{0,2},{2,0},{4,6},{6,4},{8,10},{10,8},{12,14},{14,12},{1,3},{3,1},... | collective-permute-start | bytes 1179656 | tf_op jit(solution)/shard_map/ppermute | solution.py:322
  12.2 20.9 %collective-permute-start.5 = (bf16[512,768]{1,0:T(8,128)(2,1)S(1)}, bf16[512,768]{1,0:T(8,128)(2,1)S(1)}, u32[]{:S(2)}, u32[]{:S(2)}) collective-permute-start(bf16[512,768]{1,0:T(8,128)(2,1)S(1)} %pad_maximum_fusion.3), channel_id=1, source_target_pairs={{2,6},{4,0},{6,10},{8,4},{10,14},{12,8},{3,7},{5,1},{7,11},{9,5},{... | collective-permute-start | bytes 2359304 | tf_op jit(solution)/shard_map/ppermute | solution.py:321
  21.1 19.6 %collective-permute-start.4 = (bf16[512,768]{1,0:T(8,128)(2,1)S(1)}, bf16[512,768]{1,0:T(8,128)(2,1)S(1)}, u32[]{:S(2)}, u32[]{:S(2)}) collective-permute-start(bf16[512,768]{1,0:T(8,128)(2,1)S(1)} %pad_maximum_fusion.2), channel_id=1, source_target_pairs={{0,4},{4,8},{6,2},{8,12},{10,6},{14,10},{1,5},{5,9},{7,3},{9,13},{... | collective-permute-start | bytes 2359304 | tf_op jit(solution)/shard_map/ppermute | solution.py:327
  40.8 2.1 %copy-start.3 = (bf16[256,1536]{1,0:T(8,128)(2,1)S(1)}, bf16[256,1536]{1,0:T(8,128)(2,1)}, u32[]{:S(2)}) copy-start(bf16[256,1536]{1,0:T(8,128)(2,1)} %query.3) | copy-start | bytes 2359300
  40.9 20.3 %collective-permute-start.7 = (bf16[512,768]{1,0:T(8,128)(2,1)S(1)}, bf16[512,768]{1,0:T(8,128)(2,1)S(1)}, u32[]{:S(2)}, u32[]{:S(2)}) collective-permute-start(bf16[512,768]{1,0:T(8,128)(2,1)S(1)} %get-tuple-element.27), channel_id=1, source_target_pairs={{2,6},{4,0},{6,10},{8,4},{10,14},{12,8},{3,7},{5,1},{7,11},{9,5},{... | collective-permute-start | bytes 2359304 | tf_op jit(solution)/shard_map/ppermute | solution.py:328
  42.4 22.6 %collective-permute-start = (bf16[256,1536]{1,0:T(8,128)(2,1)S(1)}, bf16[256,1536]{1,0:T(8,128)(2,1)S(1)}, u32[]{:S(2)}, u32[]{:S(2)}) collective-permute-start(bf16[256,1536]{1,0:T(8,128)(2,1)S(1)} %copy-done), channel_id=1, source_target_pairs={{0,1},{1,0},{2,3},{3,2},{4,5},{5,4},{6,7},{7,6},{8,9},{9,8},{10,11... | collective-permute-start | bytes 2359304 | tf_op jit(solution)/shard_map/ppermute | solution.py:324
  42.4 24.2 %collective-permute-start.1 = (bf16[256,1536]{1,0:T(8,128)(2,1)S(1)}, bf16[256,1536]{1,0:T(8,128)(2,1)S(1)}, u32[]{:S(2)}, u32[]{:S(2)}) collective-permute-start(bf16[256,1536]{1,0:T(8,128)(2,1)S(1)} %copy-done.1), channel_id=1, source_target_pairs={{0,1},{1,0},{2,3},{3,2},{4,5},{5,4},{6,7},{7,6},{8,9},{9,8},{10,11... | collective-permute-start | bytes 2359304 | tf_op jit(solution)/shard_map/ppermute | solution.py:325
  42.9 23.8 %collective-permute-start.9 = (bf16[256,1536]{1,0:T(8,128)(2,1)S(1)}, bf16[256,1536]{1,0:T(8,128)(2,1)S(1)}, u32[]{:S(2)}, u32[]{:S(2)}) collective-permute-start(bf16[256,1536]{1,0:T(8,128)(2,1)S(1)} %copy-done.3), channel_id=1, source_target_pairs={{0,2},{2,0},{4,6},{6,4},{8,10},{10,8},{12,14},{14,12},{1,3},{3,1},... | collective-permute-start | bytes 2359304 | tf_op jit(solution)/shard_map/ppermute | solution.py:323
  47.6 21.4 %collective-permute-start.2 = (bf16[512,768]{1,0:T(8,128)(2,1)S(1)}, bf16[512,768]{1,0:T(8,128)(2,1)S(1)}, u32[]{:S(2)}, u32[]{:S(2)}) collective-permute-start(bf16[512,768]{1,0:T(8,128)(2,1)S(1)} %pad_maximum_fusion.1), channel_id=1, source_target_pairs={{0,4},{4,8},{6,2},{8,12},{10,6},{14,10},{1,5},{5,9},{7,3},{9,13},{... | collective-permute-start | bytes 2359304 | tf_op jit(solution)/shard_map/ppermute | solution.py:320
  61.2 23.5 %collective-permute-start.6 = (bf16[512,768]{1,0:T(8,128)(2,1)S(1)}, bf16[512,768]{1,0:T(8,128)(2,1)S(1)}, u32[]{:S(2)}, u32[]{:S(2)}) collective-permute-start(bf16[512,768]{1,0:T(8,128)(2,1)S(1)} %get-tuple-element.28), channel_id=1, source_target_pairs={{0,4},{4,8},{6,2},{8,12},{10,6},{14,10},{1,5},{5,9},{7,3},{9,13},{... | collective-permute-start | bytes 2359304 | tf_op jit(solution)/shard_map/ppermute | solution.py:330
  65.0 19.7 %collective-permute-start.12 = (bf16[512,768]{1,0:T(8,128)(2,1)S(1)}, bf16[512,768]{1,0:T(8,128)(2,1)S(1)}, u32[]{:S(2)}, u32[]{:S(2)}) collective-permute-start(bf16[512,768]{1,0:T(8,128)(2,1)S(1)} %pad_maximum_fusion.6), channel_id=1, source_target_pairs={{2,6},{4,0},{6,10},{8,4},{10,14},{12,8},{3,7},{5,1},{7,11},{9,5},{... | collective-permute-start | bytes 2359304 | tf_op jit(solution)/shard_map/ppermute | solution.py:331
  66.5 2.5 %copy-start.4 = (s32[8,8]{1,0:T(8,128)S(1)}, s32[8,8]{1,0:T(8,128)}, u32[]{:S(2)}) copy-start(s32[8,8]{1,0:T(8,128)} %table_ref.7) | copy-start | bytes 772
  66.6 2.4 %collective-permute-start.10 = (bf16[256,768]{1,0:T(8,128)(2,1)S(1)}, bf16[256,768]{1,0:T(8,128)(2,1)S(1)}, u32[]{:S(2)}, u32[]{:S(2)}) collective-permute-start(bf16[256,768]{1,0:T(8,128)(2,1)S(1)} %pad_maximum_fusion.8), channel_id=1, source_target_pairs={{0,1},{1,0},{2,3},{3,2},{4,5},{5,4},{6,7},{7,6},{8,9},{9,8},{10,11... | collective-permute-start | bytes 1179656 | tf_op jit(solution)/shard_map/ppermute | solution.py:329
  66.7 18.0 %collective-permute-start.8 = (bf16[256,768]{1,0:T(8,128)(2,1)S(1)}, bf16[256,768]{1,0:T(8,128)(2,1)S(1)}, u32[]{:S(2)}, u32[]{:S(2)}) collective-permute-start(bf16[256,768]{1,0:T(8,128)(2,1)S(1)} %fusion.3), channel_id=1, source_target_pairs={{0,1},{1,0},{2,3},{3,2},{4,5},{5,4},{6,7},{7,6},{8,9},{9,8},{10,11... | collective-permute-start | bytes 1179656 | tf_op jit(solution)/shard_map/ppermute | solution.py:332
  72.3 23.7 %collective-permute-start.11 = (bf16[272,768]{1,0:T(8,128)(2,1)S(1)}, bf16[272,768]{1,0:T(8,128)(2,1)S(1)}, u32[]{:S(2)}, u32[]{:S(2)}) collective-permute-start(bf16[272,768]{1,0:T(8,128)(2,1)S(1)} %partner_part.2), channel_id=1, source_target_pairs={{0,2},{2,0},{4,6},{6,4},{8,10},{10,8},{12,14},{14,12},{1,3},{3,1},... | collective-permute-start | bytes 1253384 | tf_op jit(solution)/shard_map/ppermute | solution.py:357
  88.3 10.5 %collective-permute-start.13 = (bf16[272,768]{1,0:T(8,128)(2,1)S(1)}, bf16[272,768]{1,0:T(8,128)(2,1)S(1)}, u32[]{:S(2)}, u32[]{:S(2)}) collective-permute-start(bf16[272,768]{1,0:T(8,128)(2,1)S(1)} %partner_part.3), channel_id=1, source_target_pairs={{0,2},{2,0},{4,6},{6,4},{8,10},{10,8},{12,14},{14,12},{1,3},{3,1},... | collective-permute-start | bytes 1253384 | tf_op jit(solution)/shard_map/ppermute | solution.py:357
  98.9 3.7 %copy-start.2 = (bf16[1536,3072]{1,0:T(8,128)(2,1)S(1)}, bf16[1536,3072]{1,0:T(8,128)(2,1)}, u32[]{:S(2)}) copy-start(bf16[1536,3072]{1,0:T(8,128)(2,1)} %all-gather.2.cloned.1.call-done.refs_6_) | copy-start | bytes 28311556
Sparse Core Ops, SparseCore 0:
  8.9 24.5 all-gather.1
where the time goes:
time: 115 us
  waiting for transfers between devices  49.6 us (43%)
  starting transfers between devices  26.9 us (23%)
  Pallas kernels  18.9 us (16%)
  between operations  13.6 us (12%)
  local copies, waits for them, and re-layouts  5.6 us (5%)
    pallas_call x4, Pallas kernels, run(): pl.pallas_call(body, grid=(1,), in_specs=[pl.BlockSpec(memory_space=pltpu...  13.2 us
    ppermute x1, waiting for transfers between devices, per_device(): lax.ppermute(beside(pack(9, 12), major2[:, half:]), 'frame', away_moves)  10.9 us
    ppermute x1, waiting for transfers between devices, per_device(): lax.ppermute(beside(pack(9, 12), minor1[:, :half]), 'frame', near_moves)  10 us
    ppermute x1, waiting for transfers between devices, per_device(): minor1 = lax.ppermute(pack(3, 9), 'frame', near_moves)  8.15 us
    ppermute x1, waiting for transfers between devices, per_device(): major2 = lax.ppermute(beside(pack(6, 9), cross), 'frame', away_moves)  7.63 us
    ppermute x1, waiting for transfers between devices, per_device(): cross = lax.ppermute(pack(0, 3), 'frame', partner_moves)  7.6 us
    pallas_call x1, Pallas kernels, per_device(): pl.pallas_call(functools.partial(final_kernel, own_heads, part_heads), gr...  5.65 us
    unnamed x10, local copies, waits for them, and re-layouts  5.17 us
  transfers between devices with their start and end apart: 15, of which 7 were waited for; matrix products, arithmetic and copies ran while one was open for 1% of the time, Pallas kernels for 11%

commit v1 on v0

v1 whole, which is shorter than its diff:
```python
import functools
import math

import jax
import jax.numpy as jnp
from jax import lax
from jax.experimental import pallas as pl
from jax.experimental.pallas import tpu as pltpu
from jax.sharding import PartitionSpec as P

DH = 128
BS = 128
GROUPS = ((0, 3), (3, 9), (9, 12))
CROSS = 3
BATCH = 4
TILE = 768
NEG = -1e30
LOG2_SCALE = math.log2(math.e) / math.sqrt(DH)
MIB = 1024 * 1024


def frame_ids():
    frame = lax.axis_index("frame")
    sign = 1 - 2 * lax.rem(frame, 2)
    pair_is_away = lax.rem(lax.div(frame, 2) + lax.rem(frame, 2), 2) == 1
    return frame, sign, pair_is_away


def entry(table_ref, query_frame, key_frame):
    frames = table_ref.shape[0]
    inside = (key_frame >= 0) & (key_frame < frames)
    count = table_ref[query_frame, jnp.clip(key_frame, 0, frames - 1)]
    return jnp.where(inside, count, 0)


def attend(problems):
    scores = []
    for query, parts in problems:
        row = []
        for keys, _, valid in parts:
            raw = lax.dot_general(
                query, keys, (((1,), (1,)), ((), ())), preferred_element_type=jnp.float32
            )
            row.append(raw if valid is None else jnp.where(valid, raw, NEG))
        scores.append(row)
    tops = []
    for row in scores:
        best = None
        for raw in row:
            for at in range(0, raw.shape[1], BS):
                piece = raw[:, at : at + BS]
                best = piece if best is None else jnp.maximum(best, piece)
        tops.append(best.max(axis=1, keepdims=True))
    weights = [
        [jnp.exp2((raw - top) * LOG2_SCALE) for raw in row] for row, top in zip(scores, tops)
    ]
    totals = []
    for row in weights:
        total = None
        for weight in row:
            for at in range(0, weight.shape[1], BS):
                piece = weight[:, at : at + BS]
                total = piece if total is None else total + piece
        totals.append(total.sum(axis=1, keepdims=True))
    results = []
    for (_, parts), row, top, total in zip(problems, weights, tops, totals):
        blended = 0.0
        for (_, values, _), weight in zip(parts, row):
            blended = blended + jnp.dot(
                weight.astype(jnp.bfloat16), values, preferred_element_type=jnp.float32
            )
        results.append((blended / total, top * LOG2_SCALE + jnp.log2(total)))
    return results


def attend_heads(group, blocks, problem, out):
    rows = blocks * BS
    heads = range(*group)
    lanes = lax.broadcasted_iota(jnp.int32, (rows, DH), 1)
    stats = jnp.zeros((rows, DH), jnp.float32)
    items = [(place, head, block) for place, head in enumerate(heads) for block in range(blocks)]
    sums = {}
    for at in range(0, len(items), BATCH):
        chunk = items[at : at + BATCH]
        results = attend([problem(head, block) for _, head, block in chunk])
        for (place, head, block), (blended, logsum) in zip(chunk, results):
            out[block * BS : (block + 1) * BS, head_cols(place)] = blended.astype(out.dtype)
            sums[place, block] = logsum
    for place in range(len(heads)):
        column = jnp.concatenate([sums[place, block] for block in range(blocks)], axis=0)
        stats = jnp.where(lanes == place, column, stats)
    return stats


def head_cols(head):
    return slice(head * DH, (head + 1) * DH)


def stat_rows(heads):
    return (4, 16) if heads <= 4 else (8, 32)


def write_stats(out, stats, heads):
    pad, count = stat_rows(heads)
    rows = stats.shape[0]
    packed, rest = 0.0, stats
    for part in range(3):
        piece = rest.astype(jnp.bfloat16).astype(jnp.float32)
        rest = rest - piece
        packed = packed + (pltpu.roll(piece, part * pad, 1) if part else piece)
    out[rows:, :] = jnp.zeros((count, out.shape[1]), out.dtype)
    out[rows:, :rows] = packed.T[:count].astype(out.dtype)


def read_stats(ref, heads):
    pad, count = stat_rows(heads)
    rows = ref.shape[0] - count
    packed = ref[rows:, :rows].astype(jnp.float32)
    padding = jnp.zeros((DH - count, rows), jnp.float32)
    packed = jnp.concatenate([packed, padding], axis=0).T
    return packed + pltpu.roll(packed, DH - pad, 1) + pltpu.roll(packed, DH - 2 * pad, 1)


def pair(ref, col, block):
    rows = ref.shape[0] // 2
    cols = head_cols(col)
    return (
        ref[block * BS : (block + 1) * BS, cols],
        ref[rows + block * BS : rows + (block + 1) * BS, cols],
    )


class Buffers:
    def __init__(self, refs, pair_is_away):
        self.refs = refs
        self.pair_is_away = pair_is_away

    def choose(self, first, second):
        return tuple(jnp.where(self.pair_is_away, a, b) for a, b in zip(first, second))

    def major(self, step, col, block):
        a, b = self.refs["a%d" % step], self.refs["b%d" % step]
        return self.choose(pair(a, col, block), pair(b, col, block))

    def minor(self, step, col, block):
        a, b = self.refs["a%d" % step], self.refs["b%d" % step]
        return self.choose(pair(b, col, block), pair(a, col, block))

    def away(self, head, block):
        return self.major(1, head, block) if head < 6 else self.major(3, head - 6, block)

    def near(self, head, block):
        return self.minor(1, head - 3, block) if head < 9 else self.minor(2, head - 9, block)

    def near_first(self, head):
        if head < 9:
            return pair(self.refs["first1"], head - 3, 0)
        first = self.refs["first2"]
        return self.choose(pair(first, CROSS + head - 9, 0), pair(first, head - 9, 0))

    def cross_first(self, head):
        first = self.refs["first2"]
        return self.choose(pair(first, head, 0), pair(first, CROSS + head, 0))

    def relay(self, head, block):
        return self.minor(3, head - 3, block) if head < 9 else self.minor(4, head - 9, block)


def partner_kernel(group, names, table_ref, query, keys, values, sib_keys, sib_values, *rest):
    frame, sign, pair_is_away = frame_ids()
    buffers = Buffers(dict(zip(names, rest)), pair_is_away)
    out = rest[len(names)]
    rows = query.shape[0]
    blocks = rows // BS
    partner = frame + sign
    own_count = entry(table_ref, partner, frame)
    near_count = entry(table_ref, partner, frame + 2 * sign)
    away_valid = entry(table_ref, partner, frame - 2 * sign) > 0
    relay_valid = entry(table_ref, partner, frame + 4 * sign) > 0
    cross_valid = entry(table_ref, partner, frame - sign) > 0

    def problem(head, block):
        mine = slice(block * BS, (block + 1) * BS)
        cols = head_cols(head)
        last = block + 1 == blocks
        parts = [(keys[mine, cols], values[mine, cols], None)]
        if last:
            parts.append((sib_keys[:BS, cols], sib_values[:BS, cols], own_count > 1))
        else:
            after = slice((block + 1) * BS, (block + 2) * BS)
            parts.append((keys[after, cols], values[after, cols], own_count > 1))
        parts.append((*buffers.away(head, block), away_valid))
        if head < CROSS:
            parts.append((*buffers.major(2, head, block), cross_valid))
        else:
            parts.append((*buffers.near(head, block), near_count > 0))
            after = buffers.near_first(head) if last else buffers.near(head, block + 1)
            parts.append((*after, near_count > 1))
            parts.append((*buffers.relay(head, block), relay_valid))
        return query[mine, cols], parts

    stats = attend_heads(group, blocks, problem, out)
    write_stats(out, stats, group[1] - group[0])


def own_kernel(group, names, table_ref, query, keys, values, sib_keys, sib_values, *rest):
    frame, sign, pair_is_away = frame_ids()
    buffers = Buffers(dict(zip(names, rest)), pair_is_away)
    out, out_stats = rest[len(names) :]
    rows = query.shape[0]
    blocks = rows // BS
    near_valid = entry(table_ref, frame, frame + 2 * sign) > 0
    away_valid = entry(table_ref, frame, frame - 2 * sign) > 0
    cross_count = entry(table_ref, frame, frame - sign)
    far_valid = entry(table_ref, frame, frame - 3 * sign) > 0

    def problem(head, block):
        mine = slice(block * BS, (block + 1) * BS)
        cols = head_cols(head)
        parts = [
            (keys[:, cols], values[:, cols], None),
            (sib_keys[:, cols], sib_values[:, cols], None),
            (*buffers.away(head, block), away_valid),
        ]
        if head < CROSS:
            last = block + 1 == blocks
            parts.append((*buffers.major(2, head, block), cross_count > 0))
            after = buffers.cross_first(head) if last else buffers.major(2, head, block + 1)
            parts.append((*after, cross_count > 1))
            parts.append((*buffers.major(4, head, block), far_valid))
        else:
            parts.append((*buffers.near(head, block), near_valid))
        return query[mine, cols], parts

    out_stats[...] = attend_heads(group, blocks, problem, out)


def weight_copies(groups, weight, buffer, sems):
    columns = buffer.shape[1]
    copies = []
    for tile in range(columns // TILE):
        cols = slice(tile * TILE, (tile + 1) * TILE)
        at, row = 0, []
        for index, (first, last) in enumerate(groups):
            size = (last - first) * DH
            row.append(
                pltpu.make_async_copy(
                    weight.at[first * DH : last * DH, cols],
                    buffer.at[at : at + size, cols],
                    sems.at[tile, index],
                )
            )
            at += size
        copies.append(row)
    return copies


def project_kernel(groups, has_base, weight, *refs):
    count = len(groups)
    operands, refs = refs[: 3 * count], refs[3 * count :]
    base = refs[0] if has_base else None
    out, attended, buffer, sems = refs[1:] if has_base else refs
    copies = weight_copies(groups, weight, buffer, sems)
    for row in copies:
        for copy in row:
            copy.start()
    rows = out.shape[0]
    at = 0
    for index, (first, last) in enumerate(groups):
        own, own_stats, part = operands[3 * index : 3 * index + 3]
        own_sum = own_stats[...]
        part_sum = read_stats(part, last - first)
        top = jnp.maximum(own_sum, part_sum)
        own_weight = jnp.exp2(own_sum - top)
        part_weight = jnp.exp2(part_sum - top)
        total = own_weight + part_weight
        own_weight = own_weight / total
        part_weight = part_weight / total
        for place in range(last - first):
            cols = head_cols(place)
            mixed = own_weight[:, place : place + 1] * own[:, cols] + part_weight[
                :, place : place + 1
            ] * part[:rows, cols].astype(jnp.float32)
            attended[:, head_cols(at + place)] = mixed.astype(attended.dtype)
        at += last - first
    for tile, row in enumerate(copies):
        cols = slice(tile * TILE, (tile + 1) * TILE)
        for copy in row:
            copy.wait()
        product = jnp.dot(attended[...], buffer[:, cols], preferred_element_type=jnp.float32)
        if has_base:
            product = product + base[:, cols]
        out[:, cols] = product.astype(out.dtype)


def whole(shape):
    return pl.BlockSpec(shape, lambda i: (0,) * len(shape))


def run(body, name, table, operands, out_shapes, flops):
    return pl.pallas_call(
        body,
        grid=(1,),
        in_specs=[pl.BlockSpec(memory_space=pltpu.SMEM)] + [whole(x.shape) for x in operands],
        out_specs=[whole(s.shape) for s in out_shapes],
        out_shape=out_shapes,
        compiler_params=pltpu.CompilerParams(vmem_limit_bytes=40 * MIB),
        cost_estimate=pl.CostEstimate(
            flops=flops, bytes_accessed=4 * MIB, transcendentals=flops // 512
        ),
        name=name,
    )(table, *operands)


def project(groups, weight, operands, base, dtype):
    rows = operands[0].shape[0]
    depth = sum(last - first for first, last in groups) * DH
    columns = weight.shape[1]
    extra = () if base is None else (base,)
    inputs = (*operands, *extra)
    return pl.pallas_call(
        functools.partial(project_kernel, groups, base is not None),
        grid=(1,),
        in_specs=[pl.BlockSpec(memory_space=pl.ANY)] + [whole(x.shape) for x in inputs],
        out_specs=whole((rows, columns)),
        out_shape=jax.ShapeDtypeStruct((rows, columns), dtype),
        scratch_shapes=[
            pltpu.VMEM((rows, depth), jnp.bfloat16),
            pltpu.VMEM((depth, columns), jnp.bfloat16),
            pltpu.SemaphoreType.DMA((columns // TILE, len(groups))),
        ],
        compiler_params=pltpu.CompilerParams(vmem_limit_bytes=40 * MIB),
        cost_estimate=pl.CostEstimate(
            flops=2 * rows * depth * columns, bytes_accessed=8 * MIB, transcendentals=0
        ),
        name="merge_and_project",
    )(weight, *inputs)


def per_device(queries, key_tokens, value_tokens, radial_table, out_weight):
    frames = lax.axis_size("frame")
    cores = lax.axis_size("head")
    rows = queries.shape[0]
    _, _, pair_is_away = frame_ids()

    def moves(target):
        return [(f, target(f)) for f in range(frames) if 0 <= target(f) < frames]

    partner_moves = moves(lambda f: f ^ 1)
    a_moves = moves(lambda f: f ^ 2)
    b_moves = moves(lambda f: f + 2 if f & 2 else f - 2)
    core_moves = [(c, cores - 1 - c) for c in range(cores)]

    def pack(first, last):
        cols = slice(first * DH, last * DH)
        return jnp.concatenate([key_tokens[:, cols], value_tokens[:, cols]], axis=0)

    def firsts(packed):
        return jnp.concatenate([packed[:BS], packed[rows : rows + BS]], axis=0)

    def choose(first, second):
        return jnp.where(pair_is_away, first, second)

    cross = lax.ppermute(pack(0, 3), "frame", partner_moves)
    a1 = lax.ppermute(choose(pack(3, 9), pack(0, 6)), "frame", a_moves)
    b1 = lax.ppermute(choose(pack(0, 6), pack(3, 9)), "frame", b_moves)
    partner_query = lax.ppermute(queries, "frame", partner_moves)
    sib_keys = lax.ppermute(key_tokens, "head", core_moves)
    sib_values = lax.ppermute(value_tokens, "head", core_moves)
    all_weight = lax.all_gather(out_weight, "head", axis=0, tiled=True)
    a2 = lax.ppermute(choose(pack(9, 12), cross), "frame", a_moves)
    b2 = lax.ppermute(choose(cross, pack(9, 12)), "frame", b_moves)
    a3 = lax.ppermute(choose(b1, pack(6, 12)), "frame", a_moves)
    b3 = lax.ppermute(choose(pack(6, 12), a1), "frame", b_moves)
    a4 = lax.ppermute(b2, "frame", a_moves)
    b4 = lax.ppermute(a2, "frame", b_moves)
    first1 = lax.ppermute(firsts(choose(b1, a1)), "head", core_moves)
    first2 = lax.ppermute(firsts(jnp.concatenate([a2, b2], axis=1)), "head", core_moves)
    refs = {
        "a1": a1,
        "a2": a2,
        "a3": a3,
        "a4": a4,
        "b1": b1,
        "b2": b2,
        "b3": b3,
        "b4": b4,
        "first1": first1,
        "first2": first2,
    }
    local = (key_tokens, value_tokens, sib_keys, sib_values)

    def partner_part(group, names):
        heads = group[1] - group[0]
        shape = jax.ShapeDtypeStruct((rows + stat_rows(heads)[1], heads * DH), jnp.bfloat16)
        (part,) = run(
            functools.partial(partner_kernel, group, names),
            "partner_part",
            radial_table,
            (partner_query, *local, *(refs[n] for n in names)),
            [shape],
            heads * rows * 6 * BS * DH * 4,
        )
        return lax.ppermute(part, "frame", partner_moves)

    def own_part(group, names):
        heads = group[1] - group[0]
        return run(
            functools.partial(own_kernel, group, names),
            "own_part",
            radial_table,
            (queries, *local, *(refs[n] for n in names)),
            [
                jax.ShapeDtypeStruct((rows, heads * DH), jnp.float32),
                jax.ShapeDtypeStruct((rows, DH), jnp.float32),
            ],
            heads * rows * 6 * BS * DH * 4,
        )

    low, middle, high = GROUPS
    part_low = partner_part(low, ("a1", "b1", "a2", "b2"))
    part_middle = partner_part(middle, ("a1", "b1", "a3", "b3", "first1"))
    own_middle = own_part(middle, ("a1", "b1", "a3", "b3"))
    own_high = own_part(high, ("a2", "b2", "a3", "b3"))
    part_high = partner_part(high, ("a2", "b2", "a3", "b3", "a4", "b4", "first2"))
    own_low = own_part(low, ("a1", "b1", "a2", "b2", "a4", "b4", "first2"))
    base = project((middle,), all_weight, (*own_middle, part_middle), None, jnp.float32)
    return project(
        (low, high), all_weight, (*own_low, part_low, *own_high, part_high), base, jnp.bfloat16
    )


def solution(mesh):
    in_specs = (
        P(("clip", "frame", "head"), None),
        P(("clip", "frame", "head"), None),
        P(("clip", "frame", "head"), None),
        P(),
        P("head", None),
    )
    out_specs = P(("clip", "frame", "head"), None)
    return jax.shard_map(
        per_device, mesh=mesh, in_specs=in_specs, out_specs=out_specs, check_vma=False
    )
```

time: 115 us -> 110 us (0.957)
  waiting for transfers between devices: 49.6 us -> 32.5 us
  Pallas kernels: 18.9 us -> 27.2 us
  local copies, waits for them, and re-layouts: 5.6 us -> 10.4 us
  starting transfers between devices: 26.9 us -> 25.4 us
    ppermute x8 -> x10, waiting for transfers between devices: 38.4 us -> 17 us  [the longest x1 7.94 us: per_device(): a3 = lax.ppermute(choose(b1, pack(6, 12)), 'frame', a_moves)]
    ppermute x1, waiting for transfers between devices: 0.01 us -> 5.95 us  [per_device(): partner_query = lax.ppermute(queries, 'frame', partner_moves)]
    unnamed x10 -> x33, local copies, waits for them, and re-layouts: 5.17 us -> 9.99 us
    pallas_call x4 -> x6, Pallas kernels: 13.2 us -> 17.5 us  [run(): pl.pallas_call(body, grid=(1,), in_specs=[pl.BlockSpec(memory_space=pltpu...]
    pallas_call x1 -> x2, Pallas kernels: 5.65 us -> 9.66 us  [project(): pl.pallas_call(functools.partial(project_kernel, groups, base is not None...]
    ppermute x1, starting transfers between devices: 4.66 us -> 1.52 us  [per_device(): partner_query = lax.ppermute(queries, 'frame', partner_moves)]
    ppermute x2 -> x3, waiting for transfers between devices: 2.91 us -> 0.01 us  [partner_part(): return lax.ppermute(part, 'frame', partner_moves)]
    ppermute x8 -> x10, starting transfers between devices: 15.7 us -> 18.2 us  [the longest x1 5.86 us: per_device(): a1 = lax.ppermute(choose(pack(3, 9), pack(0, 6)), 'frame', a_moves)]
  transfers between devices with their start and end apart: 15 -> 18, of which waited for: 7 -> 5; matrix products, arithmetic and copies ran while one was open for 1% -> 1% of each run, Pallas kernels for 11% -> 19%
where the time goes in v1:
time: 110 us
  waiting for transfers between devices  32.5 us (30%)
  Pallas kernels  27.2 us (25%)
  starting transfers between devices  25.4 us (23%)
  between operations  13.7 us (12%)
  local copies, waits for them, and re-layouts  10.4 us (9%)
    pallas_call x6, Pallas kernels, run(): pl.pallas_call(body, grid=(1,), in_specs=[pl.BlockSpec(memory_space=pltpu...  17.5 us
    unnamed x33, local copies, waits for them, and re-layouts  9.99 us
    pallas_call x2, Pallas kernels, project(): pl.pallas_call(functools.partial(project_kernel, groups, base is not None...  9.66 us
    ppermute x1, waiting for transfers between devices, per_device(): cross = lax.ppermute(pack(0, 3), 'frame', partner_moves)  8.77 us
    ppermute x1, waiting for transfers between devices, per_device(): a3 = lax.ppermute(choose(b1, pack(6, 12)), 'frame', a_moves)  7.94 us
    ppermute x1, waiting for transfers between devices, per_device(): partner_query = lax.ppermute(queries, 'frame', partner_moves)  5.95 us
    ppermute x1, starting transfers between devices, per_device(): a1 = lax.ppermute(choose(pack(3, 9), pack(0, 6)), 'frame', a_moves)  5.86 us
    ppermute x1, waiting for transfers between devices, per_device(): a2 = lax.ppermute(choose(pack(9, 12), cross), 'frame', a_moves)  4.58 us
  transfers between devices with their start and end apart: 18, of which 5 were waited for; matrix products, arithmetic and copies ran while one was open for 1% of the time, Pallas kernels for 19%

profile of v1, /device:TPU:0, one launch (start us, length us, event | category | flops | bytes accessed | tf_op | source)
XLA Modules:
  0.0 110.2 jit_solution(45697031864724379)
XLA Ops:
  6.5 0.7 all-gather.2.cloned.1.call-update
  7.8 0.7 copy-done.1
  8.8 0.7 collective-permute-start.3
  9.6 5.9 %collective-permute-start.2 = (bf16[512,768]{1,0:T(8,128)(2,1)S(1)}, bf16[512,768]{1,0:T(8,128)(2,1)S(1)}, u32[]{:S(2)}, u32[]{:S(2)}) collective-permute-start(bf16[512,768]{1,0:T(8,128)(2,1)S(1)} %get-tuple-element.18), channel_id=1, source_target_pairs={{0,4},{2,6},{4,0},{6,2},{8,12},{10,14},{12,8},{14,10},{1,5},{3,7},... | collective-permute-start | bytes 2359304 | tf_op jit(solution)/shard_map/ppermute | solution.py:365
  15.6 1.6 %collective-permute-start.4 = (bf16[512,384]{1,0:T(8,128)(2,1)S(1)}, bf16[512,384]{1,0:T(8,128)(2,1)S(1)}, u32[]{:S(2)}, u32[]{:S(2)}) collective-permute-start(bf16[512,384]{1,0:T(8,128)(2,1)S(1)} %pad_maximum_fusion.4), channel_id=1, source_target_pairs={{0,2},{2,0},{4,6},{6,4},{8,10},{10,8},{12,14},{14,12},{1,3},{3,1},... | collective-permute-start | bytes 1179656 | tf_op jit(solution)/shard_map/ppermute | solution.py:364
  17.2 8.8 %collective-permute-done.4 = bf16[512,384]{1,0:T(8,128)(2,1)S(1)} collective-permute-done((bf16[512,384]{1,0:T(8,128)(2,1)S(1)}, bf16[512,384]{1,0:T(8,128)(2,1)S(1)}, u32[]{:S(2)}, u32[]{:S(2)}) %collective-permute-start.4) | collective-permute-done | bytes 393248 | tf_op jit(solution)/shard_map/ppermute | solution.py:364
  26.1 0.7 collective-permute-start.6
  26.8 2.0 %collective-permute-start.5 = (bf16[512,384]{1,0:T(8,128)(2,1)S(1)}, bf16[512,384]{1,0:T(8,128)(2,1)S(1)}, u32[]{:S(2)}, u32[]{:S(2)}) collective-permute-start(bf16[512,384]{1,0:T(8,128)(2,1)S(1)} %get-tuple-element.33), channel_id=1, source_target_pairs={{0,4},{2,6},{4,0},{6,2},{8,12},{10,14},{12,8},{14,10},{1,5},{3,7},... | collective-permute-start | bytes 1179656 | tf_op jit(solution)/shard_map/ppermute | solution.py:371
  29.3 4.5 %collective-permute-done.2.rest_0_ = bf16[512,768]{1,0:T(8,128)(2,1)S(1)} collective-permute-done((bf16[512,768]{1,0:T(8,128)(2,1)S(1)}, bf16[512,768]{1,0:T(8,128)(2,1)S(1)}, u32[]{:S(2)}, u32[]{:S(2)}) %collective-permute-start.2) | collective-permute-done | bytes 786464 | tf_op jit(solution)/shard_map/ppermute | solution.py:365
  33.8 1.5 %collective-permute-start.10 = (bf16[256,1536]{1,0:T(8,128)(2,1)S(1)}, bf16[256,1536]{1,0:T(8,128)(2,1)S(1)}, u32[]{:S(2)}, u32[]{:S(2)}) collective-permute-start(bf16[256,1536]{1,0:T(8,128)(2,1)S(1)} %copy-done.6), channel_id=1, source_target_pairs={{0,2},{2,0},{4,6},{6,4},{8,10},{10,8},{12,14},{14,12},{1,3},{3,1},... | collective-permute-start | bytes 2359304 | tf_op jit(solution)/shard_map/ppermute | solution.py:367
  35.8 0.7 collective-permute-start.13
  36.5 4.6 %collective-permute-done.5.rest_2_.rest_0_ = bf16[512,384]{1,0:T(8,128)(2,1)S(1)} collective-permute-done((bf16[512,384]{1,0:T(8,128)(2,1)S(1)}, bf16[512,384]{1,0:T(8,128)(2,1)S(1)}, u32[]{:S(2)}, u32[]{:S(2)}) %collective-permute-start.5) | collective-permute-done | bytes 393248 | tf_op jit(solution)/shard_map/ppermute | solution.py:371
  41.1 3.9 %collective-permute-start.12 = (bf16[512,768]{1,0:T(8,128)(2,1)S(1)}, bf16[512,768]{1,0:T(8,128)(2,1)S(1)}, u32[]{:S(2)}, u32[]{:S(2)}) collective-permute-start(bf16[512,768]{1,0:T(8,128)(2,1)S(1)} %get-tuple-element.23), channel_id=1, source_target_pairs={{0,4},{2,6},{4,0},{6,2},{8,12},{10,14},{12,8},{14,10},{1,5},{3,7},... | collective-permute-start | bytes 2359304 | tf_op jit(solution)/shard_map/ppermute | solution.py:373
  45.2 5.9 %collective-permute-done.10.query = bf16[256,1536]{1,0:T(8,128)(2,1)S(1)} collective-permute-done((bf16[256,1536]{1,0:T(8,128)(2,1)S(1)}, bf16[256,1536]{1,0:T(8,128)(2,1)S(1)}, u32[]{:S(2)}, u32[]{:S(2)}) %collective-permute-start.10) | collective-permute-done | bytes 786464 | tf_op jit(solution)/shard_map/ppermute | solution.py:367
  51.3 3.1 %collective-permute-start.7 = (bf16[512,384]{1,0:T(8,128)(2,1)S(1)}, bf16[512,384]{1,0:T(8,128)(2,1)S(1)}, u32[]{:S(2)}, u32[]{:S(2)}) collective-permute-start(bf16[512,384]{1,0:T(8,128)(2,1)S(1)} %collective-permute-done.6.rest_3_.rest_1_), channel_id=1, source_target_pairs={{0,4},{2,6},{4,0},{6,2},{8,12},{10,14},{12,8},{14,10},{1,5},{3,7},... | collective-permute-start | bytes 1179656 | tf_op jit(solution)/shard_map/ppermute | solution.py:375
  54.4 0.9 collective-permute-start.8
  55.5 7.9 %collective-permute-done.12.rest_2_ = bf16[512,768]{1,0:T(8,128)(2,1)S(1)} collective-permute-done((bf16[512,768]{1,0:T(8,128)(2,1)S(1)}, bf16[512,768]{1,0:T(8,128)(2,1)S(1)}, u32[]{:S(2)}, u32[]{:S(2)}) %collective-permute-start.12) | collective-permute-done | bytes 786464 | tf_op jit(solution)/shard_map/ppermute | solution.py:373
  63.5 3.9 %partner_part.5 = bf16[288,768]{1,0:T(8,128)(2,1)S(1)} custom-call(s32[8,8]{1,0:T(8,128)S(1)} %copy-done.11, bf16[256,1536]{1,0:T(8,128)(2,1)S(1)} %collective-permute-done.10.query, bf16[256,1536]{1,0:T(8,128)(2,1)S(1)} %copy-done, bf16[256,1536]{1,0:T(8,128)(2,1)S(1)} %copy-done.1, bf16[256,1536]{1,0:T(8,128)(2,1)S(1)} %collective-permute-done.sib_keys, ...), custom_call_target="tpu_custom_call" | custom-call | flops 603979776 | bytes 4194304 | tf_op jit(solution)/shard_map/partner_part/pallas_call | solution.py:301
  67.4 1.6 %collective-permute-start.16 = (bf16[288,768]{1,0:T(8,128)(2,1)S(1)}, bf16[288,768]{1,0:T(8,128)(2,1)S(1)}, u32[]{:S(2)}, u32[]{:S(2)}) collective-permute-start(bf16[288,768]{1,0:T(8,128)(2,1)S(1)} %partner_part.5), channel_id=1, source_target_pairs={{0,2},{2,0},{4,6},{6,4},{8,10},{10,8},{12,14},{14,12},{1,3},{3,1},... | collective-permute-start | bytes 1327112 | tf_op jit(solution)/shard_map/ppermute | solution.py:404
  68.9 2.7 %partner_part.3 = bf16[272,384]{1,0:T(8,128)(2,1)} custom-call(s32[8,8]{1,0:T(8,128)S(1)} %copy-done.11, bf16[256,1536]{1,0:T(8,128)(2,1)S(1)} %collective-permute-done.10.query, bf16[256,1536]{1,0:T(8,128)(2,1)S(1)} %copy-done, bf16[256,1536]{1,0:T(8,128)(2,1)S(1)} %copy-done.1, bf16[256,1536]{1,0:T(8,128)(2,1)S(1)} %collective-permute-done.sib_keys, ...), custom_call_target="tpu_custom_call" | custom-call | flops 301989888 | bytes 4194304 | tf_op jit(solution)/shard_map/partner_part/pallas_call | solution.py:301
  72.2 3.3 %partner_part.4 = bf16[272,384]{1,0:T(8,128)(2,1)} custom-call(s32[8,8]{1,0:T(8,128)S(1)} %copy-done.11, bf16[256,1536]{1,0:T(8,128)(2,1)S(1)} %collective-permute-done.10.query, bf16[256,1536]{1,0:T(8,128)(2,1)S(1)} %copy-done, bf16[256,1536]{1,0:T(8,128)(2,1)S(1)} %copy-done.1, bf16[256,1536]{1,0:T(8,128)(2,1)S(1)} %collective-permute-done.sib_keys, ...), custom_call_target="tpu_custom_call" | custom-call | flops 301989888 | bytes 4194304 | tf_op jit(solution)/shard_map/partner_part/pallas_call | solution.py:301
  75.5 1.5 %collective-permute-start.14 = (bf16[272,384]{1,0:T(8,128)(2,1)}, bf16[272,384]{1,0:T(8,128)(2,1)}, u32[]{:S(2)}, u32[]{:S(2)}) collective-permute-start(bf16[272,384]{1,0:T(8,128)(2,1)} %partner_part.4), channel_id=1, source_target_pairs={{0,2},{2,0},{4,6},{6,4},{8,10},{10,8},{12,14},{14,12},{1,3},{3,1},... | collective-permute-start | bytes 626696 | tf_op jit(solution)/shard_map/ppermute | solution.py:404
  77.0 2.5 %own_part.3 = (f32[256,384]{1,0:T(8,128)S(1)}, f32[256,128]{1,0:T(8,128)S(1)}) custom-call(s32[8,8]{1,0:T(8,128)S(1)} %copy-done.11, bf16[256,1536]{1,0:T(8,128)(2,1)S(1)} %copy-done.6, bf16[256,1536]{1,0:T(8,128)(2,1)S(1)} %copy-done, bf16[256,1536]{1,0:T(8,128)(2,1)S(1)} %copy-done.1, bf16[256,1536]{1,0:T(8,128)(2,1)S(1)} %collective-permute-done.sib_keys, ...), custom_call_target="tpu_custom_call" | custom-call | flops 301989888 | bytes 4194304 | tf_op jit(solution)/shard_map/own_part/pallas_call | solution.py:301
  79.5 2.0 %own_part.4 = (f32[256,384]{1,0:T(8,128)S(1)}, f32[256,128]{1,0:T(8,128)S(1)}) custom-call(s32[8,8]{1,0:T(8,128)S(1)} %copy-done.11, bf16[256,1536]{1,0:T(8,128)(2,1)S(1)} %copy-done.6, bf16[256,1536]{1,0:T(8,128)(2,1)S(1)} %copy-done, bf16[256,1536]{1,0:T(8,128)(2,1)S(1)} %copy-done.1, bf16[256,1536]{1,0:T(8,128)(2,1)S(1)} %collective-permute-done.sib_keys, ...), custom_call_target="tpu_custom_call" | custom-call | flops 301989888 | bytes 4194304 | tf_op jit(solution)/shard_map/own_part/pallas_call | solution.py:301
  81.5 3.2 %own_part.5 = (f32[256,768]{1,0:T(8,128)S(1)}, f32[256,128]{1,0:T(8,128)S(1)}) custom-call(s32[8,8]{1,0:T(8,128)S(1)} %copy-done.11, bf16[256,1536]{1,0:T(8,128)(2,1)S(1)} %copy-done.6, bf16[256,1536]{1,0:T(8,128)(2,1)S(1)} %copy-done, bf16[256,1536]{1,0:T(8,128)(2,1)S(1)} %copy-done.1, bf16[256,1536]{1,0:T(8,128)(2,1)S(1)} %collective-permute-done.sib_keys, ...), custom_call_target="tpu_custom_call" | custom-call | flops 603979776 | bytes 4194304 | tf_op jit(solution)/shard_map/own_part/pallas_call | solution.py:301
  84.7 0.6 copy-done.14
  85.4 3.7 %copy-done.2 = bf16[1536,3072]{1,0:T(8,128)(2,1)S(1)} copy-done((bf16[1536,3072]{1,0:T(8,128)(2,1)S(1)}, bf16[1536,3072]{1,0:T(8,128)(2,1)}, u32[]{:S(2)}) %copy-start.2) | copy-done | bytes 9437208
  89.1 0.9 copy-done.15
  90.0 3.9 %merge_and_project.2.refs_6_ = f32[256,3072]{1,0:T(8,128)S(1)} custom-call(bf16[1536,3072]{1,0:T(8,128)(2,1)S(1)} %copy-done.2, f32[256,768]{1,0:T(8,128)S(1)} %get-tuple-element.15.refs_0_, f32[256,128]{1,0:T(8,128)S(1)} %copy-done.15, bf16[288,768]{1,0:T(8,128)(2,1)S(1)} %collective-permute-done.16.refs_2_), custom_call_target="tpu_custom_call" | custom-call | flops 1207959552 | bytes 8388608 | tf_op jit(solution)/shard_map/merge_and_project/pallas_call | solution.py:321
  93.9 1.7 %copy-done.4 = f32[256,3072]{1,0:T(8,128)} copy-done((f32[256,3072]{1,0:T(8,128)}, f32[256,3072]{1,0:T(8,128)S(1)}, u32[]{:S(2)}) %copy-start.4) | copy-done | bytes 3145752
  95.6 1.9 %copy-done.5 = f32[256,3072]{1,0:T(8,128)S(1)} copy-done((f32[256,3072]{1,0:T(8,128)S(1)}, f32[256,3072]{1,0:T(8,128)}, u32[]{:S(2)}) %copy-start.5) | copy-done | bytes 3145752
  97.5 5.8 %merge_and_project.3 = bf16[256,3072]{1,0:T(8,128)(2,1)} custom-call(bf16[1536,3072]{1,0:T(8,128)(2,1)S(1)} %copy-done.3, f32[256,384]{1,0:T(8,128)S(1)} %copy-done.8, f32[256,128]{1,0:T(8,128)S(1)} %get-tuple-element.12.refs_1_, bf16[272,384]{1,0:T(8,128)(2,1)S(1)} %collective-permute-done.11.refs_2_, f32[256,384]{1,0:T(8,128)S(1)} %copy-done.10, ...), custom_call_target="tpu_custom_call" | custom-call | flops 1207959552 | bytes 8388608 | tf_op jit(solution)/shard_map/merge_and_project/pallas_call | solution.py:321
  (59 shorter events, 3.2 us)
Async XLA Ops:
  6.5 1.1 %copy-start = (bf16[256,1536]{1,0:T(8,128)(2,1)S(1)}, bf16[256,1536]{1,0:T(8,128)(2,1)}, u32[]{:S(2)}) copy-start(bf16[256,1536]{1,0:T(8,128)(2,1)} %keys.11) | copy-start | bytes 2359300
  6.5 78.8 %all-gather.2.cloned.1.call-start = ((), (), s32[]{:S(2)}) async-start(), calls=%async_computation | async-start | bytes 14155776 | tf_op jit(solution)/shard_map/all_gather | solution.py:370
  7.3 1.2 %copy-start.1 = (bf16[256,1536]{1,0:T(8,128)(2,1)S(1)}, bf16[256,1536]{1,0:T(8,128)(2,1)}, u32[]{:S(2)}) copy-start(bf16[256,1536]{1,0:T(8,128)(2,1)} %values.11) | copy-start | bytes 2359300
  8.8 20.0 %collective-permute-start.3 = (bf16[512,768]{1,0:T(8,128)(2,1)S(1)}, bf16[512,768]{1,0:T(8,128)(2,1)S(1)}, u32[]{:S(2)}, u32[]{:S(2)}) collective-permute-start(bf16[512,768]{1,0:T(8,128)(2,1)S(1)} %get-tuple-element.17), channel_id=1, source_target_pairs={{4,8},{6,10},{8,4},{10,6},{5,9},{7,11},{9,5},{11,7},{20,24},{22,26... | collective-permute-start | bytes 2359304 | tf_op jit(solution)/shard_map/ppermute | solution.py:366
  9.6 24.3 %collective-permute-start.2 = (bf16[512,768]{1,0:T(8,128)(2,1)S(1)}, bf16[512,768]{1,0:T(8,128)(2,1)S(1)}, u32[]{:S(2)}, u32[]{:S(2)}) collective-permute-start(bf16[512,768]{1,0:T(8,128)(2,1)S(1)} %get-tuple-element.18), channel_id=1, source_target_pairs={{0,4},{2,6},{4,0},{6,2},{8,12},{10,14},{12,8},{14,10},{1,5},{3,7},... | collective-permute-start | bytes 2359304 | tf_op jit(solution)/shard_map/ppermute | solution.py:365
  15.5 18.4 %copy-start.6 = (bf16[256,1536]{1,0:T(8,128)(2,1)S(1)}, bf16[256,1536]{1,0:T(8,128)(2,1)}, u32[]{:S(2)}) copy-start(bf16[256,1536]{1,0:T(8,128)(2,1)} %query.5) | copy-start | bytes 2359300
  15.6 10.4 %collective-permute-start.4 = (bf16[512,384]{1,0:T(8,128)(2,1)S(1)}, bf16[512,384]{1,0:T(8,128)(2,1)S(1)}, u32[]{:S(2)}, u32[]{:S(2)}) collective-permute-start(bf16[512,384]{1,0:T(8,128)(2,1)S(1)} %pad_maximum_fusion.4), channel_id=1, source_target_pairs={{0,2},{2,0},{4,6},{6,4},{8,10},{10,8},{12,14},{14,12},{1,3},{3,1},... | collective-permute-start | bytes 1179656 | tf_op jit(solution)/shard_map/ppermute | solution.py:364
  26.1 9.7 %collective-permute-start.6 = (bf16[512,384]{1,0:T(8,128)(2,1)S(1)}, bf16[512,384]{1,0:T(8,128)(2,1)S(1)}, u32[]{:S(2)}, u32[]{:S(2)}) collective-permute-start(bf16[512,384]{1,0:T(8,128)(2,1)S(1)} %get-tuple-element.32), channel_id=1, source_target_pairs={{4,8},{6,10},{8,4},{10,6},{5,9},{7,11},{9,5},{11,7},{20,24},{22,26... | collective-permute-start | bytes 1179656 | tf_op jit(solution)/shard_map/ppermute | solution.py:372
  26.8 14.3 %collective-permute-start.5 = (bf16[512,384]{1,0:T(8,128)(2,1)S(1)}, bf16[512,384]{1,0:T(8,128)(2,1)S(1)}, u32[]{:S(2)}, u32[]{:S(2)}) collective-permute-start(bf16[512,384]{1,0:T(8,128)(2,1)S(1)} %get-tuple-element.33), channel_id=1, source_target_pairs={{0,4},{2,6},{4,0},{6,2},{8,12},{10,14},{12,8},{14,10},{1,5},{3,7},... | collective-permute-start | bytes 1179656 | tf_op jit(solution)/shard_map/ppermute | solution.py:371
  28.8 22.4 %collective-permute-start = (bf16[256,1536]{1,0:T(8,128)(2,1)S(1)}, bf16[256,1536]{1,0:T(8,128)(2,1)S(1)}, u32[]{:S(2)}, u32[]{:S(2)}) collective-permute-start(bf16[256,1536]{1,0:T(8,128)(2,1)S(1)} %copy-done), channel_id=1, source_target_pairs={{0,1},{1,0},{2,3},{3,2},{4,5},{5,4},{6,7},{7,6},{8,9},{9,8},{10,11... | collective-permute-start | bytes 2359304 | tf_op jit(solution)/shard_map/ppermute | solution.py:368
  28.8 25.5 %collective-permute-start.1 = (bf16[256,1536]{1,0:T(8,128)(2,1)S(1)}, bf16[256,1536]{1,0:T(8,128)(2,1)S(1)}, u32[]{:S(2)}, u32[]{:S(2)}) collective-permute-start(bf16[256,1536]{1,0:T(8,128)(2,1)S(1)} %copy-done.1), channel_id=1, source_target_pairs={{0,1},{1,0},{2,3},{3,2},{4,5},{5,4},{6,7},{7,6},{8,9},{9,8},{10,11... | collective-permute-start | bytes 2359304 | tf_op jit(solution)/shard_map/ppermute | solution.py:369
  33.8 17.3 %collective-permute-start.10 = (bf16[256,1536]{1,0:T(8,128)(2,1)S(1)}, bf16[256,1536]{1,0:T(8,128)(2,1)S(1)}, u32[]{:S(2)}, u32[]{:S(2)}) collective-permute-start(bf16[256,1536]{1,0:T(8,128)(2,1)S(1)} %copy-done.6), channel_id=1, source_target_pairs={{0,2},{2,0},{4,6},{6,4},{8,10},{10,8},{12,14},{14,12},{1,3},{3,1},... | collective-permute-start | bytes 2359304 | tf_op jit(solution)/shard_map/ppermute | solution.py:367
  35.8 19.7 %collective-permute-start.13 = (bf16[512,768]{1,0:T(8,128)(2,1)S(1)}, bf16[512,768]{1,0:T(8,128)(2,1)S(1)}, u32[]{:S(2)}, u32[]{:S(2)}) collective-permute-start(bf16[512,768]{1,0:T(8,128)(2,1)S(1)} %get-tuple-element.22), channel_id=1, source_target_pairs={{4,8},{6,10},{8,4},{10,6},{5,9},{7,11},{9,5},{11,7},{20,24},{22,26... | collective-permute-start | bytes 2359304 | tf_op jit(solution)/shard_map/ppermute | solution.py:374
  41.1 22.4 %collective-permute-start.12 = (bf16[512,768]{1,0:T(8,128)(2,1)S(1)}, bf16[512,768]{1,0:T(8,128)(2,1)S(1)}, u32[]{:S(2)}, u32[]{:S(2)}) collective-permute-start(bf16[512,768]{1,0:T(8,128)(2,1)S(1)} %get-tuple-element.23), channel_id=1, source_target_pairs={{0,4},{2,6},{4,0},{6,2},{8,12},{10,14},{12,8},{14,10},{1,5},{3,7},... | collective-permute-start | bytes 2359304 | tf_op jit(solution)/shard_map/ppermute | solution.py:373
  45.1 18.4 %copy-start.11 = (s32[8,8]{1,0:T(8,128)S(1)}, s32[8,8]{1,0:T(8,128)}, u32[]{:S(2)}) copy-start(s32[8,8]{1,0:T(8,128)} %table_ref.11) | copy-start | bytes 772
  51.1 4.1 %collective-permute-start.15 = (bf16[256,768]{1,0:T(8,128)(2,1)S(1)}, bf16[256,768]{1,0:T(8,128)(2,1)S(1)}, u32[]{:S(2)}, u32[]{:S(2)}) collective-permute-start(bf16[256,768]{1,0:T(8,128)(2,1)S(1)} %pad_maximum_fusion.6), channel_id=1, source_target_pairs={{0,1},{1,0},{2,3},{3,2},{4,5},{5,4},{6,7},{7,6},{8,9},{9,8},{10,11... | collective-permute-start | bytes 1179656 | tf_op jit(solution)/shard_map/ppermute | solution.py:377
  51.3 20.9 %collective-permute-start.7 = (bf16[512,384]{1,0:T(8,128)(2,1)S(1)}, bf16[512,384]{1,0:T(8,128)(2,1)S(1)}, u32[]{:S(2)}, u32[]{:S(2)}) collective-permute-start(bf16[512,384]{1,0:T(8,128)(2,1)S(1)} %collective-permute-done.6.rest_3_.rest_1_), channel_id=1, source_target_pairs={{0,4},{2,6},{4,0},{6,2},{8,12},{10,14},{12,8},{14,10},{1,5},{3,7},... | collective-permute-start | bytes 1179656 | tf_op jit(solution)/shard_map/ppermute | solution.py:375
  54.4 17.8 %collective-permute-start.8 = (bf16[512,384]{1,0:T(8,128)(2,1)S(1)}, bf16[512,384]{1,0:T(8,128)(2,1)S(1)}, u32[]{:S(2)}, u32[]{:S(2)}) collective-permute-start(bf16[512,384]{1,0:T(8,128)(2,1)S(1)} %collective-permute-done.5.rest_2_.rest_0_), channel_id=1, source_target_pairs={{4,8},{6,10},{8,4},{10,6},{5,9},{7,11},{9,5},{11,7},{20,24},{22,26... | collective-permute-start | bytes 1179656 | tf_op jit(solution)/shard_map/ppermute | solution.py:376
  55.2 16.9 %collective-permute-start.9 = (bf16[256,768]{1,0:T(8,128)(2,1)S(1)}, bf16[256,768]{1,0:T(8,128)(2,1)S(1)}, u32[]{:S(2)}, u32[]{:S(2)}) collective-permute-start(bf16[256,768]{1,0:T(8,128)(2,1)S(1)} %pad_maximum_fusion.5), channel_id=1, source_target_pairs={{0,1},{1,0},{2,3},{3,2},{4,5},{5,4},{6,7},{7,6},{8,9},{9,8},{10,11... | collective-permute-start | bytes 1179656 | tf_op jit(solution)/shard_map/ppermute | solution.py:378
  67.4 18.0 %collective-permute-start.16 = (bf16[288,768]{1,0:T(8,128)(2,1)S(1)}, bf16[288,768]{1,0:T(8,128)(2,1)S(1)}, u32[]{:S(2)}, u32[]{:S(2)}) collective-permute-start(bf16[288,768]{1,0:T(8,128)(2,1)S(1)} %partner_part.5), channel_id=1, source_target_pairs={{0,2},{2,0},{4,6},{6,4},{8,10},{10,8},{12,14},{14,12},{1,3},{3,1},... | collective-permute-start | bytes 1327112 | tf_op jit(solution)/shard_map/ppermute | solution.py:404
  71.7 23.9 %collective-permute-start.11 = (bf16[272,384]{1,0:T(8,128)(2,1)}, bf16[272,384]{1,0:T(8,128)(2,1)S(1)}, u32[]{:S(2)}, u32[]{:S(2)}) collective-permute-start(bf16[272,384]{1,0:T(8,128)(2,1)} %partner_part.3), channel_id=1, source_target_pairs={{0,2},{2,0},{4,6},{6,4},{8,10},{10,8},{12,14},{14,12},{1,3},{3,1},... | collective-permute-start | bytes 626696 | tf_op jit(solution)/shard_map/ppermute | solution.py:404
  75.5 20.1 %collective-permute-start.14 = (bf16[272,384]{1,0:T(8,128)(2,1)}, bf16[272,384]{1,0:T(8,128)(2,1)}, u32[]{:S(2)}, u32[]{:S(2)}) collective-permute-start(bf16[272,384]{1,0:T(8,128)(2,1)} %partner_part.4), channel_id=1, source_target_pairs={{0,2},{2,0},{4,6},{6,4},{8,10},{10,8},{12,14},{14,12},{1,3},{3,1},... | collective-permute-start | bytes 626696 | tf_op jit(solution)/shard_map/ppermute | solution.py:404
  79.4 2.1 %copy-start.7 = (f32[256,384]{1,0:T(8,128)}, f32[256,384]{1,0:T(8,128)S(1)}, u32[]{:S(2)}) copy-start(f32[256,384]{1,0:T(8,128)S(1)} %get-tuple-element.11.refs_0_) | copy-start | bytes 1179652
  81.5 3.2 %copy-start.9 = (f32[256,384]{1,0:T(8,128)}, f32[256,384]{1,0:T(8,128)S(1)}, u32[]{:S(2)}) copy-start(f32[256,384]{1,0:T(8,128)S(1)} %get-tuple-element.13.refs_3_) | copy-start | bytes 1179652
  81.5 3.2 %copy-start.12 = (f32[256,128]{1,0:T(8,128)}, f32[256,128]{1,0:T(8,128)S(1)}, u32[]{:S(2)}) copy-start(f32[256,128]{1,0:T(8,128)S(1)} %get-tuple-element.14.refs_4_) | copy-start | bytes 393220
  85.4 3.7 %copy-start.2 = (bf16[1536,3072]{1,0:T(8,128)(2,1)S(1)}, bf16[1536,3072]{1,0:T(8,128)(2,1)}, u32[]{:S(2)}) copy-start(bf16[1536,3072]{1,0:T(8,128)(2,1)} %all-gather.2.cloned.1.call-done.weight) | copy-start | bytes 28311556
  90.0 5.6 %copy-start.3 = (bf16[1536,3072]{1,0:T(8,128)(2,1)S(1)}, bf16[1536,3072]{1,0:T(8,128)(2,1)}, u32[]{:S(2)}) copy-start(bf16[1536,3072]{1,0:T(8,128)(2,1)} %all-gather.2.cloned.1.call-done.weight) | copy-start | bytes 28311556
  90.0 5.6 %copy-start.8 = (f32[256,384]{1,0:T(8,128)S(1)}, f32[256,384]{1,0:T(8,128)}, u32[]{:S(2)}) copy-start(f32[256,384]{1,0:T(8,128)} %copy-done.7) | copy-start | bytes 1179652
  90.0 5.6 %copy-start.10 = (f32[256,384]{1,0:T(8,128)S(1)}, f32[256,384]{1,0:T(8,128)}, u32[]{:S(2)}) copy-start(f32[256,384]{1,0:T(8,128)} %copy-done.9) | copy-start | bytes 1179652
  90.0 5.6 %copy-start.13 = (f32[256,128]{1,0:T(8,128)S(1)}, f32[256,128]{1,0:T(8,128)}, u32[]{:S(2)}) copy-start(f32[256,128]{1,0:T(8,128)} %copy-done.12) | copy-start | bytes 393220
  93.9 1.7 %copy-start.4 = (f32[256,3072]{1,0:T(8,128)}, f32[256,3072]{1,0:T(8,128)S(1)}, u32[]{:S(2)}) copy-start(f32[256,3072]{1,0:T(8,128)S(1)} %merge_and_project.2.refs_6_) | copy-start | bytes 9437188
  95.6 1.9 %copy-start.5 = (f32[256,3072]{1,0:T(8,128)S(1)}, f32[256,3072]{1,0:T(8,128)}, u32[]{:S(2)}) copy-start(f32[256,3072]{1,0:T(8,128)} %copy-done.4) | copy-start | bytes 9437188
  (2 other events, 1.6 us)
Sparse Core Ops, SparseCore 0:
  8.9 26.7 all-gather.1

commit v2 on v1

--- a/solution.py
+++ b/solution.py
@@ -10,9 +10,8 @@
 
 DH = 128
 BS = 128
-GROUPS = ((0, 3), (3, 9), (9, 12))
 CROSS = 3
-BATCH = 4
+BATCH = 6
 TILE = 768
 NEG = -1e30
 LOG2_SCALE = math.log2(math.e) / math.sqrt(DH)
@@ -36,40 +35,36 @@
 def attend(problems):
     scores = []
     for query, parts in problems:
-        row = []
-        for keys, _, valid in parts:
-            raw = lax.dot_general(
-                query, keys, (((1,), (1,)), ((), ())), preferred_element_type=jnp.float32
-            )
-            row.append(raw if valid is None else jnp.where(valid, raw, NEG))
-        scores.append(row)
+        keys = jnp.concatenate([k for k, _, _ in parts], axis=0)
+        raw = lax.dot_general(
+            query, keys, (((1,), (1,)), ((), ())), preferred_element_type=jnp.float32
+        )
+        pieces, at = [], 0
+        for k, _, valid in parts:
+            for _ in range(k.shape[0] // BS):
+                piece = raw[:, at : at + BS]
+                pieces.append(piece if valid is None else jnp.where(valid, piece, NEG))
+                at += BS
+        scores.append(pieces)
     tops = []
-    for row in scores:
-        best = None
-        for raw in row:
-            for at in range(0, raw.shape[1], BS):
-                piece = raw[:, at : at + BS]
-                best = piece if best is None else jnp.maximum(best, piece)
+    for pieces in scores:
+        best = pieces[0]
+        for piece in pieces[1:]:
+            best = jnp.maximum(best, piece)
         tops.append(best.max(axis=1, keepdims=True))
-    weights = [
-        [jnp.exp2((raw - top) * LOG2_SCALE) for raw in row] for row, top in zip(scores, tops)
-    ]
-    totals = []
-    for row in weights:
-        total = None
-        for weight in row:
-            for at in range(0, weight.shape[1], BS):
-                piece = weight[:, at : at + BS]
-                total = piece if total is None else total + piece
+    weights, totals = [], []
+    for pieces, top in zip(scores, tops):
+        row = [jnp.exp2((piece - top) * LOG2_SCALE) for piece in pieces]
+        total = row[0]
+        for weight in row[1:]:
+            total = total + weight
         totals.append(total.sum(axis=1, keepdims=True))
+        weights.append(jnp.concatenate([w.astype(jnp.bfloat16) for w in row], axis=1))
     results = []
-    for (_, parts), row, top, total in zip(problems, weights, tops, totals):
-        blended = 0.0
-        for (_, values, _), weight in zip(parts, row):
-            blended = blended + jnp.dot(
-                weight.astype(jnp.bfloat16), values, preferred_element_type=jnp.float32
-            )
-        results.append((blended / total, top * LOG2_SCALE + jnp.log2(total)))
+    for (_, parts), weight, top, total in zip(problems, weights, tops, totals):
+        values = jnp.concatenate([v for _, v, _ in parts], axis=0)
+        blended = jnp.dot(weight, values, preferred_element_type=jnp.float32)
+        results.append((blended * (1.0 / total), top * LOG2_SCALE + jnp.log2(total)))
     return results
 
 
@@ -169,7 +164,7 @@
 def partner_kernel(group, names, table_ref, query, keys, values, sib_keys, sib_values, *rest):
     frame, sign, pair_is_away = frame_ids()
     buffers = Buffers(dict(zip(names, rest)), pair_is_away)
-    out = rest[len(names)]
+    out = rest[-1]
     rows = query.shape[0]
     blocks = rows // BS
     partner = frame + sign
@@ -206,7 +201,7 @@
 def own_kernel(group, names, table_ref, query, keys, values, sib_keys, sib_values, *rest):
     frame, sign, pair_is_away = frame_ids()
     buffers = Buffers(dict(zip(names, rest)), pair_is_away)
-    out, out_stats = rest[len(names) :]
+    out, out_stats = rest[-2:]
     rows = query.shape[0]
     blocks = rows // BS
     near_valid = entry(table_ref, frame, frame + 2 * sign) > 0
@@ -235,106 +230,93 @@
     out_stats[...] = attend_heads(group, blocks, problem, out)
 
 
-def weight_copies(groups, weight, buffer, sems):
-    columns = buffer.shape[1]
-    copies = []
-    for tile in range(columns // TILE):
-        cols = slice(tile * TILE, (tile + 1) * TILE)
-        at, row = 0, []
-        for index, (first, last) in enumerate(groups):
-            size = (last - first) * DH
-            row.append(
-                pltpu.make_async_copy(
-                    weight.at[first * DH : last * DH, cols],
-                    buffer.at[at : at + size, cols],
-                    sems.at[tile, index],
-                )
-            )
-            at += size
-        copies.append(row)
-    return copies
-
-
-def project_kernel(groups, has_base, weight, *refs):
-    count = len(groups)
-    operands, refs = refs[: 3 * count], refs[3 * count :]
-    base = refs[0] if has_base else None
-    out, attended, buffer, sems = refs[1:] if has_base else refs
-    copies = weight_copies(groups, weight, buffer, sems)
-    for row in copies:
-        for copy in row:
-            copy.start()
+def project_kernel(own_groups, part_groups, *refs):
+    refs = list(refs)
+    weight = refs.pop(0)
+    owns = [(group, refs.pop(0), refs.pop(0)) for group in own_groups]
+    parts = [(group, refs.pop(0)) for group in part_groups]
+    out, attended = refs
     rows = out.shape[0]
-    at = 0
-    for index, (first, last) in enumerate(groups):
-        own, own_stats, part = operands[3 * index : 3 * index + 3]
-        own_sum = own_stats[...]
-        part_sum = read_stats(part, last - first)
-        top = jnp.maximum(own_sum, part_sum)
-        own_weight = jnp.exp2(own_sum - top)
-        part_weight = jnp.exp2(part_sum - top)
-        total = own_weight + part_weight
-        own_weight = own_weight / total
-        part_weight = part_weight / total
-        for place in range(last - first):
-            cols = head_cols(place)
-            mixed = own_weight[:, place : place + 1] * own[:, cols] + part_weight[
-                :, place : place + 1
-            ] * part[:rows, cols].astype(jnp.float32)
-            attended[:, head_cols(at + place)] = mixed.astype(attended.dtype)
-        at += last - first
-    for tile, row in enumerate(copies):
-        cols = slice(tile * TILE, (tile + 1) * TILE)
-        for copy in row:
-            copy.wait()
-        product = jnp.dot(attended[...], buffer[:, cols], preferred_element_type=jnp.float32)
-        if has_base:
-            product = product + base[:, cols]
-        out[:, cols] = product.astype(out.dtype)
-
-
-def whole(shape):
-    return pl.BlockSpec(shape, lambda i: (0,) * len(shape))
-
-
-def run(body, name, table, operands, out_shapes, flops):
+    lanes = lax.broadcasted_iota(jnp.int32, (rows, DH), 1)
+    own_at, part_at = {}, {}
+    own_sum = part_sum = jnp.zeros((rows, DH), jnp.float32)
+    for (first, last), own, stats in owns:
+        shifted = pltpu.roll(stats[...], first, 1) if first else stats[...]
+        own_sum = jnp.where((lanes >= first) & (lanes < last), shifted, own_sum)
+        own_at.update({head: (own, head - first) for head in range(first, last)})
+    for (first, last), part in parts:
+        stats = read_stats(part, last - first)
+        shifted = pltpu.roll(stats, first, 1) if first else stats
+        part_sum = jnp.where((lanes >= first) & (lanes < last), shifted, part_sum)
+        part_at.update({head: (part, head - first) for head in range(first, last)})
+    top = jnp.maximum(own_sum, part_sum)
+    own_weight = jnp.exp2(own_sum - top)
+    part_weight = jnp.exp2(part_sum - top)
+    inverse = 1.0 / (own_weight + part_weight)
+    own_weight = own_weight * inverse
+    part_weight = part_weight * inverse
+    for head in sorted(own_at):
+        own, own_place = own_at[head]
+        part, part_place = part_at[head]
+        mixed = own_weight[:, head : head + 1] * own[:, head_cols(own_place)] + part_weight[
+            :, head : head + 1
+        ] * part[:rows, head_cols(part_place)].astype(jnp.float32)
+        attended[:, head_cols(head)] = mixed.astype(attended.dtype)
+    for at in range(0, out.shape[1], TILE):
+        out[:, at : at + TILE] = jnp.dot(
+            attended[...], weight[:, at : at + TILE], preferred_element_type=jnp.float32
+        ).astype(out.dtype)
+
+
+def run(body, name, table, operands, out_shapes, flops, after=()):
+    in_vmem = pl.BlockSpec(memory_space=pltpu.VMEM)
     return pl.pallas_call(
         body,
-        grid=(1,),
-        in_specs=[pl.BlockSpec(memory_space=pltpu.SMEM)] + [whole(x.shape) for x in operands],
-        out_specs=[whole(s.shape) for s in out_shapes],
+        in_specs=[pl.BlockSpec(memory_space=pltpu.SMEM)]
+        + [in_vmem] * len(operands)
+        + [pl.BlockSpec(memory_space=pl.ANY)] * len(after),
+        out_specs=[in_vmem] * len(out_shapes),
         out_shape=out_shapes,
-        compiler_params=pltpu.CompilerParams(vmem_limit_bytes=40 * MIB),
+        compiler_params=pltpu.CompilerParams(vmem_limit_bytes=24 * MIB),
         cost_estimate=pl.CostEstimate(
-            flops=flops, bytes_accessed=4 * MIB, transcendentals=flops // 512
+            flops=flops, bytes_accessed=MIB, transcendentals=flops // 512
         ),
         name=name,
-    )(table, *operands)
-
-
-def project(groups, weight, operands, base, dtype):
+    )(table, *operands, *after)
+
+
+def tie_kernel(*refs):
+    del refs
+
+
+def tie(before, *payloads):
+    anywhere = pl.BlockSpec(memory_space=pl.ANY)
+    return pl.pallas_call(
+        tie_kernel,
+        in_specs=[anywhere] * (len(before) + len(payloads)),
+        out_specs=[anywhere] * len(payloads),
+        out_shape=[jax.ShapeDtypeStruct(p.shape, p.dtype) for p in payloads],
+        input_output_aliases={len(before) + i: i for i in range(len(payloads))},
+        name="tie",
+    )(*before, *payloads)
+
+
+def project(own_groups, part_groups, weight, operands):
+    in_vmem = pl.BlockSpec(memory_space=pltpu.VMEM)
     rows = operands[0].shape[0]
-    depth = sum(last - first for first, last in groups) * DH
-    columns = weight.shape[1]
-    extra = () if base is None else (base,)
-    inputs = (*operands, *extra)
+    depth, columns = weight.shape
     return pl.pallas_call(
-        functools.partial(project_kernel, groups, base is not None),
-        grid=(1,),
-        in_specs=[pl.BlockSpec(memory_space=pl.ANY)] + [whole(x.shape) for x in inputs],
-        out_specs=whole((rows, columns)),
-        out_shape=jax.ShapeDtypeStruct((rows, columns), dtype),
-        scratch_shapes=[
-            pltpu.VMEM((rows, depth), jnp.bfloat16),
-            pltpu.VMEM((depth, columns), jnp.bfloat16),
-            pltpu.SemaphoreType.DMA((columns // TILE, len(groups))),
-        ],
-        compiler_params=pltpu.CompilerParams(vmem_limit_bytes=40 * MIB),
+        functools.partial(project_kernel, own_groups, part_groups),
+        in_specs=[in_vmem] * (1 + len(operands)),
+        out_specs=in_vmem,
+        out_shape=jax.ShapeDtypeStruct((rows, columns), jnp.bfloat16),
+        scratch_shapes=[pltpu.VMEM((rows, depth), jnp.bfloat16)],
+        compiler_params=pltpu.CompilerParams(vmem_limit_bytes=24 * MIB),
         cost_estimate=pl.CostEstimate(
-            flops=2 * rows * depth * columns, bytes_accessed=8 * MIB, transcendentals=0
+            flops=2 * rows * depth * columns, bytes_accessed=12 * MIB, transcendentals=0
         ),
         name="merge_and_project",
-    )(weight, *inputs)
+    )(weight, *operands)
 
 
 def per_device(queries, key_tokens, value_tokens, radial_table, out_weight):
@@ -368,29 +350,20 @@
     sib_keys = lax.ppermute(key_tokens, "head", core_moves)
     sib_values = lax.ppermute(value_tokens, "head", core_moves)
     all_weight = lax.all_gather(out_weight, "head", axis=0, tiled=True)
-    a2 = lax.ppermute(choose(pack(9, 12), cross), "frame", a_moves)
-    b2 = lax.ppermute(choose(cross, pack(9, 12)), "frame", b_moves)
+    to_a2, to_b2 = tie(
+        (sib_keys, sib_values), choose(pack(9, 12), cross), choose(cross, pack(9, 12))
+    )
+    a2 = lax.ppermute(to_a2, "frame", a_moves)
+    b2 = lax.ppermute(to_b2, "frame", b_moves)
     a3 = lax.ppermute(choose(b1, pack(6, 12)), "frame", a_moves)
     b3 = lax.ppermute(choose(pack(6, 12), a1), "frame", b_moves)
-    a4 = lax.ppermute(b2, "frame", a_moves)
-    b4 = lax.ppermute(a2, "frame", b_moves)
     first1 = lax.ppermute(firsts(choose(b1, a1)), "head", core_moves)
     first2 = lax.ppermute(firsts(jnp.concatenate([a2, b2], axis=1)), "head", core_moves)
-    refs = {
-        "a1": a1,
-        "a2": a2,
-        "a3": a3,
-        "a4": a4,
-        "b1": b1,
-        "b2": b2,
-        "b3": b3,
-        "b4": b4,
-        "first1": first1,
-        "first2": first2,
-    }
+    refs = {"a1": a1, "a2": a2, "a3": a3, "b1": b1, "b2": b2, "b3": b3}
+    refs.update({"first1": first1, "first2": first2})
     local = (key_tokens, value_tokens, sib_keys, sib_values)
 
-    def partner_part(group, names):
+    def partner_part(group, names, after=()):
         heads = group[1] - group[0]
         shape = jax.ShapeDtypeStruct((rows + stat_rows(heads)[1], heads * DH), jnp.bfloat16)
         (part,) = run(
@@ -400,8 +373,9 @@
             (partner_query, *local, *(refs[n] for n in names)),
             [shape],
             heads * rows * 6 * BS * DH * 4,
+            after,
         )
-        return lax.ppermute(part, "frame", partner_moves)
+        return part
 
     def own_part(group, names):
         heads = group[1] - group[0]
@@ -417,16 +391,27 @@
             heads * rows * 6 * BS * DH * 4,
         )
 
-    low, middle, high = GROUPS
-    part_low = partner_part(low, ("a1", "b1", "a2", "b2"))
-    part_middle = partner_part(middle, ("a1", "b1", "a3", "b3", "first1"))
-    own_middle = own_part(middle, ("a1", "b1", "a3", "b3"))
-    own_high = own_part(high, ("a2", "b2", "a3", "b3"))
-    part_high = partner_part(high, ("a2", "b2", "a3", "b3", "a4", "b4", "first2"))
-    own_low = own_part(low, ("a1", "b1", "a2", "b2", "a4", "b4", "first2"))
-    base = project((middle,), all_weight, (*own_middle, part_middle), None, jnp.float32)
+    own_groups = ((0, 3), (3, 6), (6, 12))
+    part_groups = ((0, 3), (3, 9), (9, 12))
+    part_low = partner_part((0, 3), ("a1", "b1", "a2", "b2"), (all_weight[:16, :DH],))
+    own_early = own_part((3, 6), ("a1", "b1"))
+    to_a4, to_b4 = tie((part_low, own_early[1]), b2, a2)
+    part_low = lax.ppermute(part_low, "frame", partner_moves)
+    refs["a4"] = lax.ppermute(to_a4, "frame", a_moves)
+    refs["b4"] = lax.ppermute(to_b4, "frame", b_moves)
+    part_middle = partner_part((3, 9), ("a1", "b1", "a3", "b3", "first1"))
+    part_middle = lax.ppermute(part_middle, "frame", partner_moves)
+    own_late = own_part((6, 12), ("a1", "b1", "a2", "b2", "a3", "b3"))
+    part_high = partner_part(
+        (9, 12), ("a2", "b2", "a3", "b3", "a4", "b4", "first2"), (own_late[1],)
+    )
+    part_high = lax.ppermute(part_high, "frame", partner_moves)
+    own_low = own_part((0, 3), ("a1", "b1", "a2", "b2", "a4", "b4", "first2"))
     return project(
-        (low, high), all_weight, (*own_low, part_low, *own_high, part_high), base, jnp.bfloat16
+        own_groups,
+        part_groups,
+        all_weight,
+        (*own_low, *own_early, *own_late, part_low, part_middle, part_high),
     )
 
 

time: 110 us -> 97.5 us (0.89)
  waiting for transfers between devices: 32.5 us -> 19.8 us
  other arithmetic: 1 us -> 7.11 us
  starting transfers between devices: 25.4 us -> 21.1 us
  local copies, waits for them, and re-layouts: 10.4 us -> 6.63 us
  Pallas kernels: 27.2 us -> 28.8 us
    ppermute x1, waiting for transfers between devices: 5.95 us -> 0.01 us  [per_device(): partner_query = lax.ppermute(queries, 'frame', partner_moves)]
    unnamed x33 -> x41, local copies, waits for them, and re-layouts: 9.99 us -> 4.83 us
    select_n x3, other arithmetic: 0.9 us -> 5.51 us  [choose(): return jnp.where(pair_is_away, first, second)]
    ppermute x7, starting transfers between devices: 10.3 us -> 5.71 us  [the longest x1 1.58 us: per_device(): part_middle = lax.ppermute(part_middle, 'frame', partner_moves)]
    ppermute x1, waiting for transfers between devices: 7.94 us -> 4.8 us  [per_device(): a3 = lax.ppermute(choose(b1, pack(6, 12)), 'frame', a_moves)]
    ppermute x7, waiting for transfers between devices: 4.6 us -> 2.01 us  [the longest x1 2 us: per_device(): part_high = lax.ppermute(part_high, 'frame', partner_moves)]
    pallas_call x8 -> x9, Pallas kernels: 27.2 us -> 28.8 us  [the longest x6 23.7 us: run(): pl.pallas_call(body, in_specs=[pl.BlockSpec(memory_space=pltpu.SMEM)] + [...]
    concatenate x2, other arithmetic: 0.06 us -> 1.55 us  [firsts(): return jnp.concatenate([packed[:BS], packed[rows:rows + BS]], axis=0)]
  transfers between devices with their start and end apart: 18 -> 18, of which waited for: 5 -> 4; matrix products, arithmetic and copies ran while one was open for 1% -> 11% of each run, Pallas kernels for 19% -> 24%
where the time goes in v2:
time: 97.5 us; the launch traced here: 97 us
  Pallas kernels  28.8 us (30%)
  starting transfers between devices  21.1 us (22%)
  waiting for transfers between devices  19.8 us (20%)
  between operations  13.6 us (14%)
  other arithmetic  7.11 us (7%)
  local copies, waits for them, and re-layouts  6.63 us (7%)
    pallas_call x6, Pallas kernels, run(): pl.pallas_call(body, in_specs=[pl.BlockSpec(memory_space=pltpu.SMEM)] + [...  23.7 us
    ppermute x1, waiting for transfers between devices, per_device(): cross = lax.ppermute(pack(0, 3), 'frame', partner_moves)  9.17 us
    select_n x3, other arithmetic, choose(): return jnp.where(pair_is_away, first, second)  5.51 us
    pallas_call x1, Pallas kernels, project(): pl.pallas_call(functools.partial(project_kernel, own_groups, part_groups)...  5.1 us
    ppermute x1, starting transfers between devices, per_device(): a1 = lax.ppermute(choose(pack(3, 9), pack(0, 6)), 'frame', a_moves)  4.85 us
    unnamed x41, local copies, waits for them, and re-layouts  4.83 us
    ppermute x1, waiting for transfers between devices, per_device(): a3 = lax.ppermute(choose(b1, pack(6, 12)), 'frame', a_moves)  4.8 us
    ppermute x1, waiting for transfers between devices, per_device(): a1 = lax.ppermute(choose(pack(3, 9), pack(0, 6)), 'frame', a_moves)  3.07 us
  transfers between devices with their start and end apart: 18, of which 4 were waited for; matrix products, arithmetic and copies ran while one was open for 11% of the time, Pallas kernels for 24%

profile of v2, /device:TPU:0, one launch (start us, length us, event | category | flops | bytes accessed | tf_op | source)
XLA Modules:
  0.0 97.0 jit_solution(13661620616011743358)
XLA Ops:
  6.5 0.7 all-gather.2.cloned.1.call-update
  8.4 0.8 fusion.2
  9.3 1.5 %broadcast_select_fusion.3 = (bf16[512,768]{1,0:T(8,128)(2,1)}, bf16[512,768]{1,0:T(8,128)(2,1)}) fusion(pred[]{:T(512)S(6)} %eq.3, bf16[256,768]{1,0:T(8,128)(2,1)S(1)} %get-tuple-element.36, bf16[256,768]{1,0:T(8,128)(2,1)S(1)} %get-tuple-element.33, bf16[256,768]{1,0:T(8,128)(2,1)S(1)} %get-tuple-element.37, bf16[256,768]{1,0:T(8,128)(2,1)S(1)} %get-tuple-element.34), kind=kLoop, calls=%fused_computation.6 | loop fusion | flops 3932160 | bytes 3145729 | tf_op jit(solution)/shard_map/jit(_where)/select_n | solution.py:344
  10.7 1.5 %collective-permute-start.3 = (bf16[512,768]{1,0:T(8,128)(2,1)}, bf16[512,768]{1,0:T(8,128)(2,1)}, u32[]{:S(2)}, u32[]{:S(2)}) collective-permute-start(bf16[512,768]{1,0:T(8,128)(2,1)} %get-tuple-element.25), channel_id=1, source_target_pairs={{4,8},{6,10},{8,4},{10,6},{5,9},{7,11},{9,5},{11,7},{20,24},{22,26... | collective-permute-start | bytes 2359304 | tf_op jit(solution)/shard_map/ppermute | solution.py:348
  12.3 4.8 %collective-permute-start.2 = (bf16[512,768]{1,0:T(8,128)(2,1)}, bf16[512,768]{1,0:T(8,128)(2,1)}, u32[]{:S(2)}, u32[]{:S(2)}) collective-permute-start(bf16[512,768]{1,0:T(8,128)(2,1)} %get-tuple-element.26), channel_id=1, source_target_pairs={{0,4},{2,6},{4,0},{6,2},{8,12},{10,14},{12,8},{14,10},{1,5},{3,7},... | collective-permute-start | bytes 2359304 | tf_op jit(solution)/shard_map/ppermute | solution.py:347
  17.3 1.6 %collective-permute-start.4 = (bf16[512,384]{1,0:T(8,128)(2,1)S(1)}, bf16[512,384]{1,0:T(8,128)(2,1)S(1)}, u32[]{:S(2)}, u32[]{:S(2)}) collective-permute-start(bf16[512,384]{1,0:T(8,128)(2,1)S(1)} %pad_maximum_fusion.4), channel_id=1, source_target_pairs={{0,2},{2,0},{4,6},{6,4},{8,10},{10,8},{12,14},{14,12},{1,3},{3,1},... | collective-permute-start | bytes 1179656 | tf_op jit(solution)/shard_map/ppermute | solution.py:346
  18.9 9.2 %collective-permute-done.4 = bf16[512,384]{1,0:T(8,128)(2,1)S(1)} collective-permute-done((bf16[512,384]{1,0:T(8,128)(2,1)S(1)}, bf16[512,384]{1,0:T(8,128)(2,1)S(1)}, u32[]{:S(2)}, u32[]{:S(2)}) %collective-permute-start.4) | collective-permute-done | bytes 393248 | tf_op jit(solution)/shard_map/ppermute | solution.py:346
  28.0 1.5 %collective-permute-start.7 = (bf16[256,1536]{1,0:T(8,128)(2,1)}, bf16[256,1536]{1,0:T(8,128)(2,1)}, u32[]{:S(2)}, u32[]{:S(2)}) collective-permute-start(bf16[256,1536]{1,0:T(8,128)(2,1)} %query.5), channel_id=1, source_target_pairs={{0,2},{2,0},{4,6},{6,4},{8,10},{10,8},{12,14},{14,12},{1,3},{3,1},... | collective-permute-start | bytes 2359304 | tf_op jit(solution)/shard_map/ppermute | solution.py:349
  29.6 1.0 %broadcast_select_fusion.5 = (bf16[512,384]{1,0:T(8,128)(2,1)}, bf16[512,384]{1,0:T(8,128)(2,1)}) fusion(bf16[512,384]{1,0:T(8,128)(2,1)S(1)} %collective-permute-done.4, pred[]{:T(512)S(6)} %eq.3, bf16[256,384]{1,0:T(8,128)(2,1)S(1)} %get-tuple-element.44, bf16[256,384]{1,0:T(8,128)(2,1)S(1)} %get-tuple-element.42), kind=kLoop, calls=%fused_computation.12 | loop fusion | flops 1179648 | bytes 1572865 | tf_op jit(solution)/shard_map/jit(_where)/select_n | solution.py:344
  30.6 0.9 copy-done.2
  32.7 3.1 %collective-permute-done.2.rest_0_ = bf16[512,768]{1,0:T(8,128)(2,1)} collective-permute-done((bf16[512,768]{1,0:T(8,128)(2,1)}, bf16[512,768]{1,0:T(8,128)(2,1)}, u32[]{:S(2)}, u32[]{:S(2)}) %collective-permute-start.2) | collective-permute-done | bytes 786464 | tf_op jit(solution)/shard_map/ppermute | solution.py:347
  35.8 3.0 %broadcast_select_fusion = (bf16[512,768]{1,0:T(8,128)(2,1)S(1)}, bf16[512,768]{1,0:T(8,128)(2,1)}, bf16[512,768]{1,0:T(8,128)(2,1)}) fusion(bf16[512,768]{1,0:T(8,128)(2,1)} %collective-permute-done.3.rest_1_, bf16[512,768]{1,0:T(8,128)(2,1)} %collective-permute-done.2.rest_0_, pred[]{:T(512)S(6)} %eq.3, bf16[256,768]{1,0:T(8,128)(2,1)} %get-tuple-element.35, ...), kind=kLoop, calls=%fused_computation.3 | loop fusion | flops 2752512 | bytes 4718593 | tf_op jit(solution)/shard_map/jit(_where)/select_n | solution.py:344
  38.9 1.7 %collective-permute-start.12 = (bf16[512,768]{1,0:T(8,128)(2,1)}, bf16[512,768]{1,0:T(8,128)(2,1)}, u32[]{:S(2)}, u32[]{:S(2)}) collective-permute-start(bf16[512,768]{1,0:T(8,128)(2,1)} %get-tuple-element.30), channel_id=1, source_target_pairs={{4,8},{6,10},{8,4},{10,6},{5,9},{7,11},{9,5},{11,7},{20,24},{22,26... | collective-permute-start | bytes 2359304 | tf_op jit(solution)/shard_map/ppermute | solution.py:359
  40.6 2.9 %collective-permute-start.11 = (bf16[512,768]{1,0:T(8,128)(2,1)}, bf16[512,768]{1,0:T(8,128)(2,1)}, u32[]{:S(2)}, u32[]{:S(2)}) collective-permute-start(bf16[512,768]{1,0:T(8,128)(2,1)} %get-tuple-element.31), channel_id=1, source_target_pairs={{0,4},{2,6},{4,0},{6,2},{8,12},{10,14},{12,8},{14,10},{1,5},{3,7},... | collective-permute-start | bytes 2359304 | tf_op jit(solution)/shard_map/ppermute | solution.py:358
  43.5 0.8 pad_maximum_fusion.6
  44.3 3.1 %own_part.3 = (f32[256,384]{1,0:T(8,128)S(1)}, f32[256,128]{1,0:T(8,128)S(1)}) custom-call(s32[8,8]{1,0:T(8,128)S(1)} %copy-done.15, bf16[256,1536]{1,0:T(8,128)(2,1)} %query.5, bf16[256,1536]{1,0:T(8,128)(2,1)S(1)} %copy-done, bf16[256,1536]{1,0:T(8,128)(2,1)S(1)} %copy-done.1, bf16[256,1536]{1,0:T(8,128)(2,1)S(1)} %copy-done.3, ...), custom_call_target="tpu_custom_call" | custom-call | flops 301989888 | bytes 1048576 | tf_op jit(solution)/shard_map/own_part/pallas_call | solution.py:273
  47.7 0.8 pad_maximum_fusion.5
  49.0 0.7 copy.13.refs_3_
  49.7 0.8 copy.12.refs_2_
  51.1 1.0 %copy-done.7 = bf16[512,384]{1,0:T(8,128)(2,1)S(1)} copy-done((bf16[512,384]{1,0:T(8,128)(2,1)S(1)}, bf16[512,384]{1,0:T(8,128)(2,1)}, u32[]{:S(2)}) %copy-start.7) | copy-done | bytes 393240
  52.1 3.2 %partner_part.3.refs_0_ = bf16[272,384]{1,0:T(8,128)(2,1)S(1)} custom-call(s32[8,8]{1,0:T(8,128)S(1)} %copy-done.15, bf16[256,1536]{1,0:T(8,128)(2,1)} %collective-permute-done.7.query, bf16[256,1536]{1,0:T(8,128)(2,1)S(1)} %copy-done, bf16[256,1536]{1,0:T(8,128)(2,1)S(1)} %copy-done.1, bf16[256,1536]{1,0:T(8,128)(2,1)S(1)} %copy-done.3, ...), custom_call_target="tpu_custom_call" | custom-call | flops 301989888 | bytes 1048576 | tf_op jit(solution)/shard_map/partner_part/pallas_call | solution.py:273
  55.3 0.7 copy-done.9
  56.0 1.0 %collective-permute-start.9 = (bf16[512,384]{1,0:T(8,128)(2,1)}, bf16[512,384]{1,0:T(8,128)(2,1)S(1)}, u32[]{:S(2)}, u32[]{:S(2)}) collective-permute-start(bf16[512,384]{1,0:T(8,128)(2,1)} %get-tuple-element.19), channel_id=1, source_target_pairs={{4,8},{6,10},{8,4},{10,6},{5,9},{7,11},{9,5},{11,7},{20,24},{22,26... | collective-permute-start | bytes 1179656 | tf_op jit(solution)/shard_map/ppermute | solution.py:401
  57.0 4.8 %collective-permute-done.11.rest_4_.rest_2_ = bf16[512,768]{1,0:T(8,128)(2,1)} collective-permute-done((bf16[512,768]{1,0:T(8,128)(2,1)}, bf16[512,768]{1,0:T(8,128)(2,1)}, u32[]{:S(2)}, u32[]{:S(2)}) %collective-permute-start.11) | collective-permute-done | bytes 786464 | tf_op jit(solution)/shard_map/ppermute | solution.py:358
  61.8 5.4 %partner_part.4 = bf16[288,768]{1,0:T(8,128)(2,1)S(1)} custom-call(s32[8,8]{1,0:T(8,128)S(1)} %copy-done.15, bf16[256,1536]{1,0:T(8,128)(2,1)} %collective-permute-done.7.query, bf16[256,1536]{1,0:T(8,128)(2,1)S(1)} %copy-done, bf16[256,1536]{1,0:T(8,128)(2,1)S(1)} %copy-done.1, bf16[256,1536]{1,0:T(8,128)(2,1)S(1)} %copy-done.3, ...), custom_call_target="tpu_custom_call" | custom-call | flops 603979776 | bytes 1048576 | tf_op jit(solution)/shard_map/partner_part/pallas_call | solution.py:273
  67.2 1.6 %collective-permute-start.15 = (bf16[288,768]{1,0:T(8,128)(2,1)S(1)}, bf16[288,768]{1,0:T(8,128)(2,1)S(1)}, u32[]{:S(2)}, u32[]{:S(2)}) collective-permute-start(bf16[288,768]{1,0:T(8,128)(2,1)S(1)} %partner_part.4), channel_id=1, source_target_pairs={{0,2},{2,0},{4,6},{6,4},{8,10},{10,8},{12,14},{14,12},{1,3},{3,1},... | collective-permute-start | bytes 1327112 | tf_op jit(solution)/shard_map/ppermute | solution.py:403
  68.8 5.0 %own_part.5 = (f32[256,768]{1,0:T(8,128)S(1)}, f32[256,128]{1,0:T(8,128)S(1)}) custom-call(s32[8,8]{1,0:T(8,128)S(1)} %copy-done.15, bf16[256,1536]{1,0:T(8,128)(2,1)} %query.5, bf16[256,1536]{1,0:T(8,128)(2,1)S(1)} %copy-done, bf16[256,1536]{1,0:T(8,128)(2,1)S(1)} %copy-done.1, bf16[256,1536]{1,0:T(8,128)(2,1)S(1)} %copy-done.3, ...), custom_call_target="tpu_custom_call" | custom-call | flops 603979776 | bytes 1048576 | tf_op jit(solution)/shard_map/own_part/pallas_call | solution.py:273
  74.4 3.6 %partner_part.5 = bf16[272,384]{1,0:T(8,128)(2,1)S(1)} custom-call(s32[8,8]{1,0:T(8,128)S(1)} %copy-done.15, bf16[256,1536]{1,0:T(8,128)(2,1)} %collective-permute-done.7.query, bf16[256,1536]{1,0:T(8,128)(2,1)S(1)} %copy-done, bf16[256,1536]{1,0:T(8,128)(2,1)S(1)} %copy-done.1, bf16[256,1536]{1,0:T(8,128)(2,1)S(1)} %copy-done.3, ...), custom_call_target="tpu_custom_call" | custom-call | flops 301989888 | bytes 1048576 | tf_op jit(solution)/shard_map/partner_part/pallas_call | solution.py:273
  78.0 1.6 %collective-permute-start.16 = (bf16[272,384]{1,0:T(8,128)(2,1)S(1)}, bf16[272,384]{1,0:T(8,128)(2,1)S(1)}, u32[]{:S(2)}, u32[]{:S(2)}) collective-permute-start(bf16[272,384]{1,0:T(8,128)(2,1)S(1)} %partner_part.5), channel_id=1, source_target_pairs={{0,2},{2,0},{4,6},{6,4},{8,10},{10,8},{12,14},{14,12},{1,3},{3,1},... | collective-permute-start | bytes 626696 | tf_op jit(solution)/shard_map/ppermute | solution.py:408
  79.6 3.4 %own_part.4 = (f32[256,384]{1,0:T(8,128)S(1)}, f32[256,128]{1,0:T(8,128)S(1)}) custom-call(s32[8,8]{1,0:T(8,128)S(1)} %copy-done.15, bf16[256,1536]{1,0:T(8,128)(2,1)} %query.5, bf16[256,1536]{1,0:T(8,128)(2,1)S(1)} %copy-done, bf16[256,1536]{1,0:T(8,128)(2,1)S(1)} %copy-done.1, bf16[256,1536]{1,0:T(8,128)(2,1)S(1)} %copy-done.3, ...), custom_call_target="tpu_custom_call" | custom-call | flops 301989888 | bytes 1048576 | tf_op jit(solution)/shard_map/own_part/pallas_call | solution.py:273
  83.1 2.0 %collective-permute-done.16.refs_9_ = bf16[272,384]{1,0:T(8,128)(2,1)S(1)} collective-permute-done((bf16[272,384]{1,0:T(8,128)(2,1)S(1)}, bf16[272,384]{1,0:T(8,128)(2,1)S(1)}, u32[]{:S(2)}, u32[]{:S(2)}) %collective-permute-start.16) | collective-permute-done | bytes 208928 | tf_op jit(solution)/shard_map/ppermute | solution.py:408
  85.1 5.1 %merge_and_project.1 = bf16[256,3072]{1,0:T(8,128)(2,1)} custom-call(bf16[1536,3072]{1,0:T(8,128)(2,1)S(1)} %bitcast.1, f32[256,384]{1,0:T(8,128)S(1)} %get-tuple-element.20.refs_1_, f32[256,128]{1,0:T(8,128)S(1)} %get-tuple-element.21.refs_2_, f32[256,384]{1,0:T(8,128)S(1)} %copy-done.14, f32[256,128]{1,0:T(8,128)S(1)} %copy-done.12, ...), custom_call_target="tpu_custom_call" | custom-call | flops 2415919104 | bytes 12582912 | tf_op jit(solution)/shard_map/merge_and_project/pallas_call | solution.py:308
  (70 shorter events, 4.6 us)
Async XLA Ops:
  6.5 1.1 %copy-start = (bf16[256,1536]{1,0:T(8,128)(2,1)S(1)}, bf16[256,1536]{1,0:T(8,128)(2,1)}, u32[]{:S(2)}) copy-start(bf16[256,1536]{1,0:T(8,128)(2,1)} %keys.11) | copy-start | bytes 2359300
  6.5 1.6 %copy-start.1 = (bf16[256,1536]{1,0:T(8,128)(2,1)S(1)}, bf16[256,1536]{1,0:T(8,128)(2,1)}, u32[]{:S(2)}) copy-start(bf16[256,1536]{1,0:T(8,128)(2,1)} %values.11) | copy-start | bytes 2359300
  6.5 43.9 %all-gather.2.cloned.1.call-start = ((), (), s32[]{:S(2)}) async-start(), calls=%async_computation | async-start | bytes 14155776 | tf_op jit(solution)/shard_map/all_gather | solution.py:352
  7.7 22.9 %collective-permute-start = (bf16[256,1536]{1,0:T(8,128)(2,1)S(1)}, bf16[256,1536]{1,0:T(8,128)(2,1)S(1)}, u32[]{:S(2)}, u32[]{:S(2)}) collective-permute-start(bf16[256,1536]{1,0:T(8,128)(2,1)S(1)} %copy-done), channel_id=1, source_target_pairs={{0,1},{1,0},{2,3},{3,2},{4,5},{5,4},{6,7},{7,6},{8,9},{9,8},{10,11... | collective-permute-start | bytes 2359304 | tf_op jit(solution)/shard_map/ppermute | solution.py:350
  8.1 22.5 %collective-permute-start.1 = (bf16[256,1536]{1,0:T(8,128)(2,1)S(1)}, bf16[256,1536]{1,0:T(8,128)(2,1)S(1)}, u32[]{:S(2)}, u32[]{:S(2)}) collective-permute-start(bf16[256,1536]{1,0:T(8,128)(2,1)S(1)} %copy-done.1), channel_id=1, source_target_pairs={{0,1},{1,0},{2,3},{3,2},{4,5},{5,4},{6,7},{7,6},{8,9},{9,8},{10,11... | collective-permute-start | bytes 2359304 | tf_op jit(solution)/shard_map/ppermute | solution.py:351
  10.7 22.0 %collective-permute-start.3 = (bf16[512,768]{1,0:T(8,128)(2,1)}, bf16[512,768]{1,0:T(8,128)(2,1)}, u32[]{:S(2)}, u32[]{:S(2)}) collective-permute-start(bf16[512,768]{1,0:T(8,128)(2,1)} %get-tuple-element.25), channel_id=1, source_target_pairs={{4,8},{6,10},{8,4},{10,6},{5,9},{7,11},{9,5},{11,7},{20,24},{22,26... | collective-permute-start | bytes 2359304 | tf_op jit(solution)/shard_map/ppermute | solution.py:348
  12.3 23.5 %collective-permute-start.2 = (bf16[512,768]{1,0:T(8,128)(2,1)}, bf16[512,768]{1,0:T(8,128)(2,1)}, u32[]{:S(2)}, u32[]{:S(2)}) collective-permute-start(bf16[512,768]{1,0:T(8,128)(2,1)} %get-tuple-element.26), channel_id=1, source_target_pairs={{0,4},{2,6},{4,0},{6,2},{8,12},{10,14},{12,8},{14,10},{1,5},{3,7},... | collective-permute-start | bytes 2359304 | tf_op jit(solution)/shard_map/ppermute | solution.py:347
  17.3 10.8 %collective-permute-start.4 = (bf16[512,384]{1,0:T(8,128)(2,1)S(1)}, bf16[512,384]{1,0:T(8,128)(2,1)S(1)}, u32[]{:S(2)}, u32[]{:S(2)}) collective-permute-start(bf16[512,384]{1,0:T(8,128)(2,1)S(1)} %pad_maximum_fusion.4), channel_id=1, source_target_pairs={{0,2},{2,0},{4,6},{6,4},{8,10},{10,8},{12,14},{14,12},{1,3},{3,1},... | collective-permute-start | bytes 1179656 | tf_op jit(solution)/shard_map/ppermute | solution.py:346
  28.0 23.1 %collective-permute-start.7 = (bf16[256,1536]{1,0:T(8,128)(2,1)}, bf16[256,1536]{1,0:T(8,128)(2,1)}, u32[]{:S(2)}, u32[]{:S(2)}) collective-permute-start(bf16[256,1536]{1,0:T(8,128)(2,1)} %query.5), channel_id=1, source_target_pairs={{0,2},{2,0},{4,6},{6,4},{8,10},{10,8},{12,14},{14,12},{1,3},{3,1},... | collective-permute-start | bytes 2359304 | tf_op jit(solution)/shard_map/ppermute | solution.py:349
  30.6 1.2 %copy-start.4 = (bf16[256,1536]{1,0:T(8,128)(2,1)}, bf16[256,1536]{1,0:T(8,128)(2,1)S(1)}, u32[]{:S(2)}) copy-start(bf16[256,1536]{1,0:T(8,128)(2,1)S(1)} %collective-permute-done.1.refs_1_.sib_values) | copy-start | bytes 2359300
  31.7 15.7 %collective-permute-start.5 = (bf16[512,384]{1,0:T(8,128)(2,1)}, bf16[512,384]{1,0:T(8,128)(2,1)S(1)}, u32[]{:S(2)}, u32[]{:S(2)}) collective-permute-start(bf16[512,384]{1,0:T(8,128)(2,1)} %get-tuple-element.15), channel_id=1, source_target_pairs={{0,4},{2,6},{4,0},{6,2},{8,12},{10,14},{12,8},{14,10},{1,5},{3,7},... | collective-permute-start | bytes 1179656 | tf_op jit(solution)/shard_map/ppermute | solution.py:356
  32.0 15.5 %collective-permute-start.6 = (bf16[512,384]{1,0:T(8,128)(2,1)}, bf16[512,384]{1,0:T(8,128)(2,1)S(1)}, u32[]{:S(2)}, u32[]{:S(2)}) collective-permute-start(bf16[512,384]{1,0:T(8,128)(2,1)} %get-tuple-element.16), channel_id=1, source_target_pairs={{4,8},{6,10},{8,4},{10,6},{5,9},{7,11},{9,5},{11,7},{20,24},{22,26... | collective-permute-start | bytes 1179656 | tf_op jit(solution)/shard_map/ppermute | solution.py:357
  38.9 5.4 %copy-start.3 = (bf16[256,1536]{1,0:T(8,128)(2,1)S(1)}, bf16[256,1536]{1,0:T(8,128)(2,1)}, u32[]{:S(2)}) copy-start(bf16[256,1536]{1,0:T(8,128)(2,1)} %copy-done.2) | copy-start | bytes 2359300
  38.9 5.4 %copy-start.5 = (bf16[256,1536]{1,0:T(8,128)(2,1)S(1)}, bf16[256,1536]{1,0:T(8,128)(2,1)}, u32[]{:S(2)}) copy-start(bf16[256,1536]{1,0:T(8,128)(2,1)} %copy-done.4) | copy-start | bytes 2359300
  38.9 5.4 %copy-start.15 = (s32[8,8]{1,0:T(8,128)S(1)}, s32[8,8]{1,0:T(8,128)}, u32[]{:S(2)}) copy-start(s32[8,8]{1,0:T(8,128)} %table_ref.11) | copy-start | bytes 772
  38.9 18.1 %collective-permute-start.12 = (bf16[512,768]{1,0:T(8,128)(2,1)}, bf16[512,768]{1,0:T(8,128)(2,1)}, u32[]{:S(2)}, u32[]{:S(2)}) collective-permute-start(bf16[512,768]{1,0:T(8,128)(2,1)} %get-tuple-element.30), channel_id=1, source_target_pairs={{4,8},{6,10},{8,4},{10,6},{5,9},{7,11},{9,5},{11,7},{20,24},{22,26... | collective-permute-start | bytes 2359304 | tf_op jit(solution)/shard_map/ppermute | solution.py:359
  40.6 21.2 %collective-permute-start.11 = (bf16[512,768]{1,0:T(8,128)(2,1)}, bf16[512,768]{1,0:T(8,128)(2,1)}, u32[]{:S(2)}, u32[]{:S(2)}) collective-permute-start(bf16[512,768]{1,0:T(8,128)(2,1)} %get-tuple-element.31), channel_id=1, source_target_pairs={{0,4},{2,6},{4,0},{6,2},{8,12},{10,14},{12,8},{14,10},{1,5},{3,7},... | collective-permute-start | bytes 2359304 | tf_op jit(solution)/shard_map/ppermute | solution.py:358
  47.4 8.6 %collective-permute-start.14 = (bf16[256,768]{1,0:T(8,128)(2,1)}, bf16[256,768]{1,0:T(8,128)(2,1)}, u32[]{:S(2)}, u32[]{:S(2)}) collective-permute-start(bf16[256,768]{1,0:T(8,128)(2,1)} %pad_maximum_fusion.6), channel_id=1, source_target_pairs={{0,1},{1,0},{2,3},{3,2},{4,5},{5,4},{6,7},{7,6},{8,9},{9,8},{10,11... | collective-permute-start | bytes 1179656 | tf_op jit(solution)/shard_map/ppermute | solution.py:360
  47.6 2.1 %copy-start.6 = (bf16[512,384]{1,0:T(8,128)(2,1)}, bf16[512,384]{1,0:T(8,128)(2,1)S(1)}, u32[]{:S(2)}) copy-start(bf16[512,384]{1,0:T(8,128)(2,1)S(1)} %collective-permute-done.6.rest_3_.rest_1_) | copy-start | bytes 1179652
  48.5 25.9 %collective-permute-start.10 = (bf16[256,768]{1,0:T(8,128)(2,1)}, bf16[256,768]{1,0:T(8,128)(2,1)}, u32[]{:S(2)}, u32[]{:S(2)}) collective-permute-start(bf16[256,768]{1,0:T(8,128)(2,1)} %pad_maximum_fusion.5), channel_id=1, source_target_pairs={{0,1},{1,0},{2,3},{3,2},{4,5},{5,4},{6,7},{7,6},{8,9},{9,8},{10,11... | collective-permute-start | bytes 1179656 | tf_op jit(solution)/shard_map/ppermute | solution.py:361
  56.0 18.4 %collective-permute-start.8 = (bf16[512,384]{1,0:T(8,128)(2,1)}, bf16[512,384]{1,0:T(8,128)(2,1)S(1)}, u32[]{:S(2)}, u32[]{:S(2)}) collective-permute-start(bf16[512,384]{1,0:T(8,128)(2,1)} %get-tuple-element.18), channel_id=1, source_target_pairs={{0,4},{2,6},{4,0},{6,2},{8,12},{10,14},{12,8},{14,10},{1,5},{3,7},... | collective-permute-start | bytes 1179656 | tf_op jit(solution)/shard_map/ppermute | solution.py:400
  56.0 12.8 %copy-start.8 = (bf16[512,384]{1,0:T(8,128)(2,1)S(1)}, bf16[512,384]{1,0:T(8,128)(2,1)}, u32[]{:S(2)}) copy-start(bf16[512,384]{1,0:T(8,128)(2,1)} %copy-done.6) | copy-start | bytes 1179652
  56.0 18.4 %collective-permute-start.9 = (bf16[512,384]{1,0:T(8,128)(2,1)}, bf16[512,384]{1,0:T(8,128)(2,1)S(1)}, u32[]{:S(2)}, u32[]{:S(2)}) collective-permute-start(bf16[512,384]{1,0:T(8,128)(2,1)} %get-tuple-element.19), channel_id=1, source_target_pairs={{4,8},{6,10},{8,4},{10,6},{5,9},{7,11},{9,5},{11,7},{20,24},{22,26... | collective-permute-start | bytes 1179656 | tf_op jit(solution)/shard_map/ppermute | solution.py:401
  67.2 6.6 %copy-start.10 = (bf16[272,384]{1,0:T(8,128)(2,1)S(1)}, bf16[272,384]{1,0:T(8,128)(2,1)}, u32[]{:S(2)}) copy-start(bf16[272,384]{1,0:T(8,128)(2,1)} %copy-done.9) | copy-start | bytes 626692
  67.2 15.8 %collective-permute-start.15 = (bf16[288,768]{1,0:T(8,128)(2,1)S(1)}, bf16[288,768]{1,0:T(8,128)(2,1)S(1)}, u32[]{:S(2)}, u32[]{:S(2)}) collective-permute-start(bf16[288,768]{1,0:T(8,128)(2,1)S(1)} %partner_part.4), channel_id=1, source_target_pairs={{0,2},{2,0},{4,6},{6,4},{8,10},{10,8},{12,14},{14,12},{1,3},{3,1},... | collective-permute-start | bytes 1327112 | tf_op jit(solution)/shard_map/ppermute | solution.py:403
  68.8 16.3 %slice-start = ((s8[9437184]{0:T(1024)(128)(4,1)}), s8[4194304]{0:T(1024)(128)(4,1)S(1)}, s32[]{:S(2)}) async-start(s8[9437184]{0:T(1024)(128)(4,1)} %bitcast), calls=%async_computation.1 | async-start | bytes 8388608
  68.8 16.3 %slice-start.1 = ((s8[9437184]{0:T(1024)(128)(4,1)}), s8[4194304]{0:T(1024)(128)(4,1)S(1)}, s32[]{:S(2)}) async-start(s8[9437184]{0:T(1024)(128)(4,1)} %bitcast), calls=%async_computation.2 | async-start | bytes 8388608
  73.8 9.3 %collective-permute-start.13 = (bf16[272,384]{1,0:T(8,128)(2,1)S(1)}, bf16[272,384]{1,0:T(8,128)(2,1)S(1)}, u32[]{:S(2)}, u32[]{:S(2)}) collective-permute-start(bf16[272,384]{1,0:T(8,128)(2,1)S(1)} %copy-done.10), channel_id=1, source_target_pairs={{0,2},{2,0},{4,6},{6,4},{8,10},{10,8},{12,14},{14,12},{1,3},{3,1},... | collective-permute-start | bytes 626696 | tf_op jit(solution)/shard_map/ppermute | solution.py:399
  74.4 10.7 %slice-start.2 = ((s8[9437184]{0:T(1024)(128)(4,1)}), s8[1048576]{0:T(1024)(128)(4,1)S(1)}, s32[]{:S(2)}) async-start(s8[9437184]{0:T(1024)(128)(4,1)} %bitcast), calls=%async_computation.3 | async-start | bytes 2097152
  78.0 7.1 %copy-start.12 = (f32[256,128]{1,0:T(8,128)S(1)}, f32[256,128]{1,0:T(8,128)}, u32[]{:S(2)}) copy-start(f32[256,128]{1,0:T(8,128)} %copy-done.11) | copy-start | bytes 393220
  78.0 7.1 %copy-start.14 = (f32[256,384]{1,0:T(8,128)S(1)}, f32[256,384]{1,0:T(8,128)}, u32[]{:S(2)}) copy-start(f32[256,384]{1,0:T(8,128)} %copy-done.13) | copy-start | bytes 1179652
  78.0 7.0 %collective-permute-start.16 = (bf16[272,384]{1,0:T(8,128)(2,1)S(1)}, bf16[272,384]{1,0:T(8,128)(2,1)S(1)}, u32[]{:S(2)}, u32[]{:S(2)}) collective-permute-start(bf16[272,384]{1,0:T(8,128)(2,1)S(1)} %partner_part.5), channel_id=1, source_target_pairs={{0,2},{2,0},{4,6},{6,4},{8,10},{10,8},{12,14},{14,12},{1,3},{3,1},... | collective-permute-start | bytes 626696 | tf_op jit(solution)/shard_map/ppermute | solution.py:408
  (5 other events, 4.7 us)
Sparse Core Ops, SparseCore 0:
  8.9 24.5 all-gather.1

commit v3 on v2

--- a/solution.py
+++ b/solution.py
@@ -11,7 +11,7 @@
 DH = 128
 BS = 128
 CROSS = 3
-BATCH = 6
+BATCH = 4
 TILE = 768
 NEG = -1e30
 LOG2_SCALE = math.log2(math.e) / math.sqrt(DH)
@@ -20,9 +20,7 @@
 
 def frame_ids():
     frame = lax.axis_index("frame")
-    sign = 1 - 2 * lax.rem(frame, 2)
-    pair_is_away = lax.rem(lax.div(frame, 2) + lax.rem(frame, 2), 2) == 1
-    return frame, sign, pair_is_away
+    return frame, 1 - 2 * lax.rem(frame, 2)
 
 
 def entry(table_ref, query_frame, key_frame):
@@ -35,36 +33,40 @@
 def attend(problems):
     scores = []
     for query, parts in problems:
-        keys = jnp.concatenate([k for k, _, _ in parts], axis=0)
-        raw = lax.dot_general(
-            query, keys, (((1,), (1,)), ((), ())), preferred_element_type=jnp.float32
-        )
-        pieces, at = [], 0
-        for k, _, valid in parts:
-            for _ in range(k.shape[0] // BS):
+        row = []
+        for keys, _, valid in parts:
+            raw = lax.dot_general(
+                query, keys, (((1,), (1,)), ((), ())), preferred_element_type=jnp.float32
+            )
+            row.append(raw if valid is None else jnp.where(valid, raw, NEG))
+        scores.append(row)
+    tops = []
+    for row in scores:
+        best = None
+        for raw in row:
+            for at in range(0, raw.shape[1], BS):
                 piece = raw[:, at : at + BS]
-                pieces.append(piece if valid is None else jnp.where(valid, piece, NEG))
-                at += BS
-        scores.append(pieces)
-    tops = []
-    for pieces in scores:
-        best = pieces[0]
-        for piece in pieces[1:]:
-            best = jnp.maximum(best, piece)
+                best = piece if best is None else jnp.maximum(best, piece)
         tops.append(best.max(axis=1, keepdims=True))
-    weights, totals = [], []
-    for pieces, top in zip(scores, tops):
-        row = [jnp.exp2((piece - top) * LOG2_SCALE) for piece in pieces]
-        total = row[0]
-        for weight in row[1:]:
-            total = total + weight
+    weights = [
+        [jnp.exp2((raw - top) * LOG2_SCALE) for raw in row] for row, top in zip(scores, tops)
+    ]
+    totals = []
+    for row in weights:
+        total = None
+        for weight in row:
+            for at in range(0, weight.shape[1], BS):
+                piece = weight[:, at : at + BS]
+                total = piece if total is None else total + piece
         totals.append(total.sum(axis=1, keepdims=True))
-        weights.append(jnp.concatenate([w.astype(jnp.bfloat16) for w in row], axis=1))
     results = []
-    for (_, parts), weight, top, total in zip(problems, weights, tops, totals):
-        values = jnp.concatenate([v for _, v, _ in parts], axis=0)
-        blended = jnp.dot(weight, values, preferred_element_type=jnp.float32)
-        results.append((blended * (1.0 / total), top * LOG2_SCALE + jnp.log2(total)))
+    for (_, parts), row, top, total in zip(problems, weights, tops, totals):
+        blended = 0.0
+        for (_, values, _), weight in zip(parts, row):
+            blended = blended + jnp.dot(
+                weight.astype(jnp.bfloat16), values, preferred_element_type=jnp.float32
+            )
+        results.append((blended / total, top * LOG2_SCALE + jnp.log2(total)))
     return results
 
 
@@ -126,44 +128,42 @@
 
 
 class Buffers:
-    def __init__(self, refs, pair_is_away):
+    def __init__(self, refs):
         self.refs = refs
-        self.pair_is_away = pair_is_away
-
-    def choose(self, first, second):
-        return tuple(jnp.where(self.pair_is_away, a, b) for a, b in zip(first, second))
-
-    def major(self, step, col, block):
-        a, b = self.refs["a%d" % step], self.refs["b%d" % step]
-        return self.choose(pair(a, col, block), pair(b, col, block))
-
-    def minor(self, step, col, block):
-        a, b = self.refs["a%d" % step], self.refs["b%d" % step]
-        return self.choose(pair(b, col, block), pair(a, col, block))
+
+    def cross(self, head, block):
+        return pair(self.refs["major2"], head, block)
+
+    def far(self, head, block):
+        return pair(self.refs["major4"], head, block)
 
     def away(self, head, block):
-        return self.major(1, head, block) if head < 6 else self.major(3, head - 6, block)
+        if head < 6:
+            return pair(self.refs["major1"], head, block)
+        return pair(self.refs["major3"], head - 6, block)
 
     def near(self, head, block):
-        return self.minor(1, head - 3, block) if head < 9 else self.minor(2, head - 9, block)
+        if head < 9:
+            return pair(self.refs["minor1"], head - 3, block)
+        return pair(self.refs["minor2"], head - 9, block)
 
     def near_first(self, head):
         if head < 9:
             return pair(self.refs["first1"], head - 3, 0)
-        first = self.refs["first2"]
-        return self.choose(pair(first, CROSS + head - 9, 0), pair(first, head - 9, 0))
+        return pair(self.refs["first2"], head - 9, 0)
 
     def cross_first(self, head):
-        first = self.refs["first2"]
-        return self.choose(pair(first, head, 0), pair(first, CROSS + head, 0))
+        return pair(self.refs["first2"], CROSS + head, 0)
 
     def relay(self, head, block):
-        return self.minor(3, head - 3, block) if head < 9 else self.minor(4, head - 9, block)
+        if head < 9:
+            return pair(self.refs["minor3"], head - 3, block)
+        return pair(self.refs["minor4"], head - 9, block)
 
 
 def partner_kernel(group, names, table_ref, query, keys, values, sib_keys, sib_values, *rest):
-    frame, sign, pair_is_away = frame_ids()
-    buffers = Buffers(dict(zip(names, rest)), pair_is_away)
+    frame, sign = frame_ids()
+    buffers = Buffers(dict(zip(names, rest)))
     out = rest[-1]
     rows = query.shape[0]
     blocks = rows // BS
@@ -186,7 +186,7 @@
             parts.append((keys[after, cols], values[after, cols], own_count > 1))
         parts.append((*buffers.away(head, block), away_valid))
         if head < CROSS:
-            parts.append((*buffers.major(2, head, block), cross_valid))
+            parts.append((*buffers.cross(head, block), cross_valid))
         else:
             parts.append((*buffers.near(head, block), near_count > 0))
             after = buffers.near_first(head) if last else buffers.near(head, block + 1)
@@ -199,8 +199,8 @@
 
 
 def own_kernel(group, names, table_ref, query, keys, values, sib_keys, sib_values, *rest):
-    frame, sign, pair_is_away = frame_ids()
-    buffers = Buffers(dict(zip(names, rest)), pair_is_away)
+    frame, sign = frame_ids()
+    buffers = Buffers(dict(zip(names, rest)))
     out, out_stats = rest[-2:]
     rows = query.shape[0]
     blocks = rows // BS
@@ -219,10 +219,10 @@
         ]
         if head < CROSS:
             last = block + 1 == blocks
-            parts.append((*buffers.major(2, head, block), cross_count > 0))
-            after = buffers.cross_first(head) if last else buffers.major(2, head, block + 1)
+            parts.append((*buffers.cross(head, block), cross_count > 0))
+            after = buffers.cross_first(head) if last else buffers.cross(head, block + 1)
             parts.append((*after, cross_count > 1))
-            parts.append((*buffers.major(4, head, block), far_valid))
+            parts.append((*buffers.far(head, block), far_valid))
         else:
             parts.append((*buffers.near(head, block), near_valid))
         return query[mine, cols], parts
@@ -268,14 +268,18 @@
         ).astype(out.dtype)
 
 
+def whole(shape):
+    return pl.BlockSpec(shape, lambda i: (0,) * len(shape))
+
+
 def run(body, name, table, operands, out_shapes, flops, after=()):
-    in_vmem = pl.BlockSpec(memory_space=pltpu.VMEM)
     return pl.pallas_call(
         body,
+        grid=(1,),
         in_specs=[pl.BlockSpec(memory_space=pltpu.SMEM)]
-        + [in_vmem] * len(operands)
+        + [whole(x.shape) for x in operands]
         + [pl.BlockSpec(memory_space=pl.ANY)] * len(after),
-        out_specs=[in_vmem] * len(out_shapes),
+        out_specs=[whole(s.shape) for s in out_shapes],
         out_shape=out_shapes,
         compiler_params=pltpu.CompilerParams(vmem_limit_bytes=24 * MIB),
         cost_estimate=pl.CostEstimate(
@@ -302,13 +306,13 @@
 
 
 def project(own_groups, part_groups, weight, operands):
-    in_vmem = pl.BlockSpec(memory_space=pltpu.VMEM)
     rows = operands[0].shape[0]
     depth, columns = weight.shape
     return pl.pallas_call(
         functools.partial(project_kernel, own_groups, part_groups),
-        in_specs=[in_vmem] * (1 + len(operands)),
-        out_specs=in_vmem,
+        grid=(1,),
+        in_specs=[whole(x.shape) for x in (weight, *operands)],
+        out_specs=whole((rows, columns)),
         out_shape=jax.ShapeDtypeStruct((rows, columns), jnp.bfloat16),
         scratch_shapes=[pltpu.VMEM((rows, depth), jnp.bfloat16)],
         compiler_params=pltpu.CompilerParams(vmem_limit_bytes=24 * MIB),
@@ -323,44 +327,54 @@
     frames = lax.axis_size("frame")
     cores = lax.axis_size("head")
     rows = queries.shape[0]
-    _, _, pair_is_away = frame_ids()
 
     def moves(target):
         return [(f, target(f)) for f in range(frames) if 0 <= target(f) < frames]
 
     partner_moves = moves(lambda f: f ^ 1)
-    a_moves = moves(lambda f: f ^ 2)
-    b_moves = moves(lambda f: f + 2 if f & 2 else f - 2)
+    near_moves = moves(lambda f: f - 2 if f % 2 == 0 else f + 2)
+    away_moves = moves(lambda f: f + 2 if f % 2 == 0 else f - 2)
     core_moves = [(c, cores - 1 - c) for c in range(cores)]
 
     def pack(first, last):
         cols = slice(first * DH, last * DH)
         return jnp.concatenate([key_tokens[:, cols], value_tokens[:, cols]], axis=0)
 
-    def firsts(packed):
-        return jnp.concatenate([packed[:BS], packed[rows : rows + BS]], axis=0)
-
-    def choose(first, second):
-        return jnp.where(pair_is_away, first, second)
+    def firsts(*packed):
+        return jnp.concatenate(
+            [jnp.concatenate([p[at : at + BS] for p in packed], axis=1) for at in (0, rows)],
+            axis=0,
+        )
 
     cross = lax.ppermute(pack(0, 3), "frame", partner_moves)
-    a1 = lax.ppermute(choose(pack(3, 9), pack(0, 6)), "frame", a_moves)
-    b1 = lax.ppermute(choose(pack(0, 6), pack(3, 9)), "frame", b_moves)
-    partner_query = lax.ppermute(queries, "frame", partner_moves)
+    major1 = lax.ppermute(pack(0, 6), "frame", away_moves)
+    minor1 = lax.ppermute(pack(3, 9), "frame", near_moves)
     sib_keys = lax.ppermute(key_tokens, "head", core_moves)
     sib_values = lax.ppermute(value_tokens, "head", core_moves)
+    partner_query = lax.ppermute(queries, "frame", partner_moves)
     all_weight = lax.all_gather(out_weight, "head", axis=0, tiled=True)
-    to_a2, to_b2 = tie(
-        (sib_keys, sib_values), choose(pack(9, 12), cross), choose(cross, pack(9, 12))
-    )
-    a2 = lax.ppermute(to_a2, "frame", a_moves)
-    b2 = lax.ppermute(to_b2, "frame", b_moves)
-    a3 = lax.ppermute(choose(b1, pack(6, 12)), "frame", a_moves)
-    b3 = lax.ppermute(choose(pack(6, 12), a1), "frame", b_moves)
-    first1 = lax.ppermute(firsts(choose(b1, a1)), "head", core_moves)
-    first2 = lax.ppermute(firsts(jnp.concatenate([a2, b2], axis=1)), "head", core_moves)
-    refs = {"a1": a1, "a2": a2, "a3": a3, "b1": b1, "b2": b2, "b3": b3}
-    refs.update({"first1": first1, "first2": first2})
+    cross, to_minor2 = tie((sib_keys, sib_values), cross, pack(9, 12))
+    minor2 = lax.ppermute(to_minor2, "frame", near_moves)
+    major2 = lax.ppermute(cross, "frame", away_moves)
+    (to_major3,) = tie((major1,), pack(6, 12))
+    major3 = lax.ppermute(to_major3, "frame", away_moves)
+    minor3 = lax.ppermute(minor1, "frame", near_moves)
+    first1 = lax.ppermute(firsts(minor1), "head", core_moves)
+    major4 = lax.ppermute(major2, "frame", away_moves)
+    minor4 = lax.ppermute(minor2, "frame", near_moves)
+    first2 = lax.ppermute(firsts(minor2, major2), "head", core_moves)
+    refs = {
+        "major1": major1,
+        "major2": major2,
+        "major3": major3,
+        "major4": major4,
+        "minor1": minor1,
+        "minor2": minor2,
+        "minor3": minor3,
+        "minor4": minor4,
+        "first1": first1,
+        "first2": first2,
+    }
     local = (key_tokens, value_tokens, sib_keys, sib_values)
 
     def partner_part(group, names, after=()):
@@ -377,7 +391,7 @@
         )
         return part
 
-    def own_part(group, names):
+    def own_part(group, names, after=()):
         heads = group[1] - group[0]
         return run(
             functools.partial(own_kernel, group, names),
@@ -389,24 +403,24 @@
                 jax.ShapeDtypeStruct((rows, DH), jnp.float32),
             ],
             heads * rows * 6 * BS * DH * 4,
+            after,
         )
 
     own_groups = ((0, 3), (3, 6), (6, 12))
     part_groups = ((0, 3), (3, 9), (9, 12))
-    part_low = partner_part((0, 3), ("a1", "b1", "a2", "b2"), (all_weight[:16, :DH],))
-    own_early = own_part((3, 6), ("a1", "b1"))
-    to_a4, to_b4 = tie((part_low, own_early[1]), b2, a2)
+    part_low = partner_part((0, 3), ("major1", "major2"), (all_weight[:16, :DH],))
+    own_early = own_part((3, 6), ("major1", "minor1"))
+    part_middle = partner_part(
+        (3, 9), ("major1", "major3", "minor1", "minor3", "first1"), (part_low, own_early[1])
+    )
     part_low = lax.ppermute(part_low, "frame", partner_moves)
-    refs["a4"] = lax.ppermute(to_a4, "frame", a_moves)
-    refs["b4"] = lax.ppermute(to_b4, "frame", b_moves)
-    part_middle = partner_part((3, 9), ("a1", "b1", "a3", "b3", "first1"))
     part_middle = lax.ppermute(part_middle, "frame", partner_moves)
-    own_late = own_part((6, 12), ("a1", "b1", "a2", "b2", "a3", "b3"))
+    own_late = own_part((6, 12), ("major3", "minor1", "minor2"))
     part_high = partner_part(
-        (9, 12), ("a2", "b2", "a3", "b3", "a4", "b4", "first2"), (own_late[1],)
+        (9, 12), ("major3", "minor2", "minor4", "first2"), (own_late[1], major4, part_low)
     )
     part_high = lax.ppermute(part_high, "frame", partner_moves)
-    own_low = own_part((0, 3), ("a1", "b1", "a2", "b2", "a4", "b4", "first2"))
+    own_low = own_part((0, 3), ("major1", "major2", "major4", "first2"))
     return project(
         own_groups,
         part_groups,

time: 97.5 us -> 103 us (1.056)
  starting transfers between devices: 21.1 us -> 32 us
  waiting for transfers between devices: 19.8 us -> 15.9 us
  other arithmetic: 7.11 us -> 5.47 us
  Pallas kernels: 28.8 us -> 27.2 us
  local copies, waits for them, and re-layouts: 6.63 us -> 8.13 us
    ppermute x10, starting transfers between devices: 13.5 us -> 24.8 us  [the longest x1 6.03 us: per_device(): major3 = lax.ppermute(to_major3, 'frame', away_moves)]
    select_n x3 -> x0, other arithmetic: 5.51 us -> none  [choose(): return jnp.where(pair_is_away, first, second)]
    concatenate x1 -> x5, other arithmetic: 0.04 us -> 4.67 us  [pack(): return jnp.concatenate([key_tokens[:, cols], value_tokens[:, cols]], axis=0)]
    ppermute x10, waiting for transfers between devices: 7.89 us -> 4.27 us  [the longest x1 3.22 us: per_device(): minor2 = lax.ppermute(to_minor2, 'frame', near_moves)]
    slice x2 -> x3, local copies, waits for them, and re-layouts: 0.05 us -> 2.03 us  [firsts(): p[at:at + BS]]
    pallas_call x6, Pallas kernels: 23.7 us -> 22 us  [run(): pl.pallas_call(body, grid=(1,), in_specs=[pl.BlockSpec(memory_space=pltpu...]
    ppermute x1, starting transfers between devices: 1.58 us -> 2.63 us  [per_device(): cross = lax.ppermute(pack(0, 3), 'frame', partner_moves)]
    unnamed x41 -> x32, local copies, waits for them, and re-layouts: 4.83 us -> 4.41 us
  transfers between devices with their start and end apart: 18 -> 18, of which waited for: 4 -> 4; matrix products, arithmetic and copies ran while one was open for 11% -> 9% of each run, Pallas kernels for 24% -> 21%
where the time goes in v3:
time: 103 us; the launch traced here: 102 us
  starting transfers between devices  32 us (31%)
  Pallas kernels  27.2 us (26%)
  waiting for transfers between devices  15.9 us (15%)
  between operations  13.7 us (13%)
  local copies, waits for them, and re-layouts  8.13 us (8%)
  other arithmetic  5.47 us (5%)
    pallas_call x6, Pallas kernels, run(): pl.pallas_call(body, grid=(1,), in_specs=[pl.BlockSpec(memory_space=pltpu...  22 us
    ppermute x1, waiting for transfers between devices, per_device(): cross = lax.ppermute(pack(0, 3), 'frame', partner_moves)  8.25 us
    ppermute x1, starting transfers between devices, per_device(): major3 = lax.ppermute(to_major3, 'frame', away_moves)  6.03 us
    ppermute x1, starting transfers between devices, per_device(): major1 = lax.ppermute(pack(0, 6), 'frame', away_moves)  5.66 us
    ppermute x1, starting transfers between devices, per_device(): major4 = lax.ppermute(major2, 'frame', away_moves)  5.28 us
    pallas_call x1, Pallas kernels, project(): pl.pallas_call(functools.partial(project_kernel, own_groups, part_groups)...  5.25 us
    concatenate x5, other arithmetic, pack(): return jnp.concatenate([key_tokens[:, cols], value_tokens[:, cols]], axis=0)  4.67 us
    unnamed x32, local copies, waits for them, and re-layouts  4.41 us
  transfers between devices with their start and end apart: 18, of which 4 were waited for; matrix products, arithmetic and copies ran while one was open for 9% of the time, Pallas kernels for 21%

profile of v3, /device:TPU:0, one launch (start us, length us, event | category | flops | bytes accessed | tf_op | source)
XLA Modules:
  0.0 102.4 jit_solution(2433147691692534764)
XLA Ops:
  8.4 0.8 fusion.2
  9.3 0.9 pad_maximum_fusion
  10.2 5.7 %collective-permute-start.2 = (bf16[512,768]{1,0:T(8,128)(2,1)}, bf16[512,768]{1,0:T(8,128)(2,1)}, u32[]{:S(2)}, u32[]{:S(2)}) collective-permute-start(bf16[512,768]{1,0:T(8,128)(2,1)} %pad_maximum_fusion), channel_id=1, source_target_pairs={{0,4},{4,8},{6,2},{8,12},{10,6},{14,10},{1,5},{5,9},{7,3},{9,13},{... | collective-permute-start | bytes 2359304 | tf_op jit(solution)/shard_map/ppermute | solution.py:350
  15.9 0.9 pad_maximum_fusion.1
  16.8 1.3 %collective-permute-start.8 = (bf16[512,768]{1,0:T(8,128)(2,1)}, bf16[512,768]{1,0:T(8,128)(2,1)}, u32[]{:S(2)}, u32[]{:S(2)}) collective-permute-start(bf16[512,768]{1,0:T(8,128)(2,1)} %pad_maximum_fusion.1), channel_id=1, source_target_pairs={{2,6},{4,0},{6,10},{8,4},{10,14},{12,8},{3,7},{5,1},{7,11},{9,5},{... | collective-permute-start | bytes 2359304 | tf_op jit(solution)/shard_map/ppermute | solution.py:351
  18.3 2.6 %collective-permute-start.3 = (bf16[512,384]{1,0:T(8,128)(2,1)S(1)}, bf16[512,384]{1,0:T(8,128)(2,1)}, u32[]{:S(2)}, u32[]{:S(2)}) collective-permute-start(bf16[512,384]{1,0:T(8,128)(2,1)S(1)} %pad_maximum_fusion.3), channel_id=1, source_target_pairs={{0,2},{2,0},{4,6},{6,4},{8,10},{10,8},{12,14},{14,12},{1,3},{3,1},... | collective-permute-start | bytes 1179656 | tf_op jit(solution)/shard_map/ppermute | solution.py:349
  20.9 0.8 pad_maximum_fusion.4.refs_3_
  21.7 8.3 %collective-permute-done.3.refs_2_ = bf16[512,384]{1,0:T(8,128)(2,1)} collective-permute-done((bf16[512,384]{1,0:T(8,128)(2,1)S(1)}, bf16[512,384]{1,0:T(8,128)(2,1)}, u32[]{:S(2)}, u32[]{:S(2)}) %collective-permute-start.3) | collective-permute-done | bytes 393248 | tf_op jit(solution)/shard_map/ppermute | solution.py:349
  29.9 1.7 %collective-permute-start.10 = (bf16[256,1536]{1,0:T(8,128)(2,1)}, bf16[256,1536]{1,0:T(8,128)(2,1)}, u32[]{:S(2)}, u32[]{:S(2)}) collective-permute-start(bf16[256,1536]{1,0:T(8,128)(2,1)} %query.5), channel_id=1, source_target_pairs={{0,2},{2,0},{4,6},{6,4},{8,10},{10,8},{12,14},{14,12},{1,3},{3,1},... | collective-permute-start | bytes 2359304 | tf_op jit(solution)/shard_map/ppermute | solution.py:354
  31.7 0.9 copy-done.2
  32.6 0.9 copy-done.4
  33.5 2.6 %collective-permute-start.4 = (bf16[512,384]{1,0:T(8,128)(2,1)}, bf16[512,384]{1,0:T(8,128)(2,1)S(1)}, u32[]{:S(2)}, u32[]{:S(2)}) collective-permute-start(bf16[512,384]{1,0:T(8,128)(2,1)} %get-tuple-element.13), channel_id=1, source_target_pairs={{0,4},{4,8},{6,2},{8,12},{10,6},{14,10},{1,5},{5,9},{7,3},{9,13},{... | collective-permute-start | bytes 1179656 | tf_op jit(solution)/shard_map/ppermute | solution.py:358
  36.1 2.0 %pad_maximum_fusion.2.refs_1_ = bf16[512,768]{1,0:T(8,128)(2,1)} fusion(bf16[256,768]{1,0:T(8,128)(2,1)} %get-tuple-element.26, bf16[256,768]{1,0:T(8,128)(2,1)S(1)} %get-tuple-element.23), kind=kLoop, calls=%fused_computation.2 | loop fusion | flops 1572864 | bytes 1572864 | tf_op jit(solution)/shard_map/concatenate | solution.py:341
  38.1 1.3 %collective-permute-start.6 = (bf16[512,384]{1,0:T(8,128)(2,1)}, bf16[512,384]{1,0:T(8,128)(2,1)}, u32[]{:S(2)}, u32[]{:S(2)}) collective-permute-start(bf16[512,384]{1,0:T(8,128)(2,1)} %get-tuple-element.14), channel_id=1, source_target_pairs={{2,6},{4,0},{6,10},{8,4},{10,14},{12,8},{3,7},{5,1},{7,11},{9,5},{... | collective-permute-start | bytes 1179656 | tf_op jit(solution)/shard_map/ppermute | solution.py:357
  39.4 6.0 %collective-permute-start.9 = (bf16[512,768]{1,0:T(8,128)(2,1)}, bf16[512,768]{1,0:T(8,128)(2,1)}, u32[]{:S(2)}, u32[]{:S(2)}) collective-permute-start(bf16[512,768]{1,0:T(8,128)(2,1)} %tie.3), channel_id=1, source_target_pairs={{0,4},{4,8},{6,2},{8,12},{10,6},{14,10},{1,5},{5,9},{7,3},{9,13},{... | collective-permute-start | bytes 2359304 | tf_op jit(solution)/shard_map/ppermute | solution.py:360
  45.4 1.0 %fusion = (bf16[128,768]{1,0:T(8,128)(2,1)S(1)}, bf16[128,768]{1,0:T(8,128)(2,1)S(1)}) fusion(bf16[512,768]{1,0:T(8,128)(2,1)} %collective-permute-done.8.rest_1_.rest_2_), kind=kLoop, calls=%fused_computation.7 | loop fusion | bytes 786432 | tf_op jit(solution)/shard_map/slice | solution.py:345
  46.5 1.3 %collective-permute-start.12 = (bf16[512,768]{1,0:T(8,128)(2,1)}, bf16[512,768]{1,0:T(8,128)(2,1)}, u32[]{:S(2)}, u32[]{:S(2)}) collective-permute-start(bf16[512,768]{1,0:T(8,128)(2,1)} %collective-permute-done.8.rest_1_.rest_2_), channel_id=1, source_target_pairs={{2,6},{4,0},{6,10},{8,4},{10,14},{12,8},{3,7},{5,1},{7,11},{9,5},{... | collective-permute-start | bytes 2359304 | tf_op jit(solution)/shard_map/ppermute | solution.py:361
  47.9 3.2 %collective-permute-done.6.rest_2_.rest_1_ = bf16[512,384]{1,0:T(8,128)(2,1)} collective-permute-done((bf16[512,384]{1,0:T(8,128)(2,1)}, bf16[512,384]{1,0:T(8,128)(2,1)}, u32[]{:S(2)}, u32[]{:S(2)}) %collective-permute-start.6) | collective-permute-done | bytes 393248 | tf_op jit(solution)/shard_map/ppermute | solution.py:357
  51.2 1.0 fusion.5
  52.9 5.3 %collective-permute-start.5 = (bf16[512,384]{1,0:T(8,128)(2,1)S(1)}, bf16[512,384]{1,0:T(8,128)(2,1)}, u32[]{:S(2)}, u32[]{:S(2)}) collective-permute-start(bf16[512,384]{1,0:T(8,128)(2,1)S(1)} %collective-permute-done.4.rest_1_), channel_id=1, source_target_pairs={{0,4},{4,8},{6,2},{8,12},{10,6},{14,10},{1,5},{5,9},{7,3},{9,13},{... | collective-permute-start | bytes 1179656 | tf_op jit(solution)/shard_map/ppermute | solution.py:363
  58.9 1.3 %collective-permute-start.15 = (bf16[512,384]{1,0:T(8,128)(2,1)}, bf16[512,384]{1,0:T(8,128)(2,1)}, u32[]{:S(2)}, u32[]{:S(2)}) collective-permute-start(bf16[512,384]{1,0:T(8,128)(2,1)} %collective-permute-done.6.rest_2_.rest_1_), channel_id=1, source_target_pairs={{2,6},{4,0},{6,10},{8,4},{10,14},{12,8},{3,7},{5,1},{7,11},{9,5},{... | collective-permute-start | bytes 1179656 | tf_op jit(solution)/shard_map/ppermute | solution.py:364
  60.3 2.9 %own_part.4 = (f32[256,384]{1,0:T(8,128)S(1)}, f32[256,128]{1,0:T(8,128)S(1)}) custom-call(s32[8,8]{1,0:T(8,128)S(1)} %copy-done.12, bf16[256,1536]{1,0:T(8,128)(2,1)} %query.5, bf16[256,1536]{1,0:T(8,128)(2,1)S(1)} %copy-done, bf16[256,1536]{1,0:T(8,128)(2,1)S(1)} %copy-done.1, bf16[256,1536]{1,0:T(8,128)(2,1)S(1)} %copy-done.3, ...), custom_call_target="tpu_custom_call" | custom-call | flops 301989888 | bytes 1048576 | tf_op jit(solution)/shard_map/own_part/pallas_call | solution.py:276
  65.3 2.8 %partner_part.3.rest_5_ = bf16[272,384]{1,0:T(8,128)(2,1)S(1)} custom-call(s32[8,8]{1,0:T(8,128)S(1)} %copy-done.12, bf16[256,1536]{1,0:T(8,128)(2,1)} %collective-permute-done.10.query, bf16[256,1536]{1,0:T(8,128)(2,1)S(1)} %copy-done, bf16[256,1536]{1,0:T(8,128)(2,1)S(1)} %copy-done.1, bf16[256,1536]{1,0:T(8,128)(2,1)S(1)} %copy-done.3, ...), custom_call_target="tpu_custom_call" | custom-call | flops 301989888 | bytes 1048576 | tf_op jit(solution)/shard_map/partner_part/pallas_call | solution.py:276
  68.1 1.0 %collective-permute-done.12.rest_3_ = bf16[512,768]{1,0:T(8,128)(2,1)} collective-permute-done((bf16[512,768]{1,0:T(8,128)(2,1)}, bf16[512,768]{1,0:T(8,128)(2,1)}, u32[]{:S(2)}, u32[]{:S(2)}) %collective-permute-start.12) | collective-permute-done | bytes 786464 | tf_op jit(solution)/shard_map/ppermute | solution.py:361
  69.2 5.2 %partner_part.4 = bf16[288,768]{1,0:T(8,128)(2,1)S(1)} custom-call(s32[8,8]{1,0:T(8,128)S(1)} %copy-done.12, bf16[256,1536]{1,0:T(8,128)(2,1)} %collective-permute-done.10.query, bf16[256,1536]{1,0:T(8,128)(2,1)S(1)} %copy-done, bf16[256,1536]{1,0:T(8,128)(2,1)S(1)} %copy-done.1, bf16[256,1536]{1,0:T(8,128)(2,1)S(1)} %copy-done.3, ...), custom_call_target="tpu_custom_call" | custom-call | flops 603979776 | bytes 1048576 | tf_op jit(solution)/shard_map/partner_part/pallas_call | solution.py:276
  74.4 1.1 %collective-permute-start.14 = (bf16[288,768]{1,0:T(8,128)(2,1)S(1)}, bf16[288,768]{1,0:T(8,128)(2,1)S(1)}, u32[]{:S(2)}, u32[]{:S(2)}) collective-permute-start(bf16[288,768]{1,0:T(8,128)(2,1)S(1)} %partner_part.4), channel_id=1, source_target_pairs={{0,2},{2,0},{4,6},{6,4},{8,10},{10,8},{12,14},{14,12},{1,3},{3,1},... | collective-permute-start | bytes 1327112 | tf_op jit(solution)/shard_map/ppermute | solution.py:417
  75.5 4.1 %own_part.5 = (f32[256,768]{1,0:T(8,128)S(1)}, f32[256,128]{1,0:T(8,128)S(1)}) custom-call(s32[8,8]{1,0:T(8,128)S(1)} %copy-done.12, bf16[256,1536]{1,0:T(8,128)(2,1)} %query.5, bf16[256,1536]{1,0:T(8,128)(2,1)S(1)} %copy-done, bf16[256,1536]{1,0:T(8,128)(2,1)S(1)} %copy-done.1, bf16[256,1536]{1,0:T(8,128)(2,1)S(1)} %copy-done.3, ...), custom_call_target="tpu_custom_call" | custom-call | flops 603979776 | bytes 1048576 | tf_op jit(solution)/shard_map/own_part/pallas_call | solution.py:276
  79.7 3.6 %partner_part.5 = bf16[272,384]{1,0:T(8,128)(2,1)S(1)} custom-call(s32[8,8]{1,0:T(8,128)S(1)} %copy-done.12, bf16[256,1536]{1,0:T(8,128)(2,1)} %collective-permute-done.10.query, bf16[256,1536]{1,0:T(8,128)(2,1)S(1)} %copy-done, bf16[256,1536]{1,0:T(8,128)(2,1)S(1)} %copy-done.1, bf16[256,1536]{1,0:T(8,128)(2,1)S(1)} %copy-done.3, ...), custom_call_target="tpu_custom_call" | custom-call | flops 301989888 | bytes 1048576 | tf_op jit(solution)/shard_map/partner_part/pallas_call | solution.py:276
  83.3 1.1 %collective-permute-start.16 = (bf16[272,384]{1,0:T(8,128)(2,1)S(1)}, bf16[272,384]{1,0:T(8,128)(2,1)S(1)}, u32[]{:S(2)}, u32[]{:S(2)}) collective-permute-start(bf16[272,384]{1,0:T(8,128)(2,1)S(1)} %partner_part.5), channel_id=1, source_target_pairs={{0,2},{2,0},{4,6},{6,4},{8,10},{10,8},{12,14},{14,12},{1,3},{3,1},... | collective-permute-start | bytes 626696 | tf_op jit(solution)/shard_map/ppermute | solution.py:422
  84.3 3.3 %own_part.3 = (f32[256,384]{1,0:T(8,128)S(1)}, f32[256,128]{1,0:T(8,128)S(1)}) custom-call(s32[8,8]{1,0:T(8,128)S(1)} %copy-done.12, bf16[256,1536]{1,0:T(8,128)(2,1)} %query.5, bf16[256,1536]{1,0:T(8,128)(2,1)S(1)} %copy-done, bf16[256,1536]{1,0:T(8,128)(2,1)S(1)} %copy-done.1, bf16[256,1536]{1,0:T(8,128)(2,1)S(1)} %copy-done.3, ...), custom_call_target="tpu_custom_call" | custom-call | flops 301989888 | bytes 1048576 | tf_op jit(solution)/shard_map/own_part/pallas_call | solution.py:276
  87.7 2.6 %collective-permute-done.16.refs_9_ = bf16[272,384]{1,0:T(8,128)(2,1)S(1)} collective-permute-done((bf16[272,384]{1,0:T(8,128)(2,1)S(1)}, bf16[272,384]{1,0:T(8,128)(2,1)S(1)}, u32[]{:S(2)}, u32[]{:S(2)}) %collective-permute-start.16) | collective-permute-done | bytes 208928 | tf_op jit(solution)/shard_map/ppermute | solution.py:422
  90.3 5.3 %merge_and_project.1 = bf16[256,3072]{1,0:T(8,128)(2,1)} custom-call(bf16[1536,3072]{1,0:T(8,128)(2,1)S(1)} %bitcast.1, f32[256,384]{1,0:T(8,128)S(1)} %get-tuple-element.15.refs_1_, f32[256,128]{1,0:T(8,128)S(1)} %get-tuple-element.16.refs_2_, f32[256,384]{1,0:T(8,128)S(1)} %copy-done.9, f32[256,128]{1,0:T(8,128)S(1)} %copy-done.7, ...), custom_call_target="tpu_custom_call" | custom-call | flops 2415919104 | bytes 12582912 | tf_op jit(solution)/shard_map/merge_and_project/pallas_call | solution.py:311
  (62 shorter events, 5.9 us)
Async XLA Ops:
  6.5 1.1 %copy-start = (bf16[256,1536]{1,0:T(8,128)(2,1)S(1)}, bf16[256,1536]{1,0:T(8,128)(2,1)}, u32[]{:S(2)}) copy-start(bf16[256,1536]{1,0:T(8,128)(2,1)} %keys.11) | copy-start | bytes 2359300
  6.5 1.6 %copy-start.1 = (bf16[256,1536]{1,0:T(8,128)(2,1)S(1)}, bf16[256,1536]{1,0:T(8,128)(2,1)}, u32[]{:S(2)}) copy-start(bf16[256,1536]{1,0:T(8,128)(2,1)} %values.11) | copy-start | bytes 2359300
  6.5 58.0 %all-gather.2.cloned.1.call-start = ((), (), s32[]{:S(2)}) async-start(), calls=%async_computation | async-start | bytes 14155776 | tf_op jit(solution)/shard_map/all_gather | solution.py:355
  7.7 24.0 %collective-permute-start = (bf16[256,1536]{1,0:T(8,128)(2,1)S(1)}, bf16[256,1536]{1,0:T(8,128)(2,1)S(1)}, u32[]{:S(2)}, u32[]{:S(2)}) collective-permute-start(bf16[256,1536]{1,0:T(8,128)(2,1)S(1)} %copy-done), channel_id=1, source_target_pairs={{0,1},{1,0},{2,3},{3,2},{4,5},{5,4},{6,7},{7,6},{8,9},{9,8},{10,11... | collective-permute-start | bytes 2359304 | tf_op jit(solution)/shard_map/ppermute | solution.py:352
  8.1 23.6 %collective-permute-start.1 = (bf16[256,1536]{1,0:T(8,128)(2,1)S(1)}, bf16[256,1536]{1,0:T(8,128)(2,1)S(1)}, u32[]{:S(2)}, u32[]{:S(2)}) collective-permute-start(bf16[256,1536]{1,0:T(8,128)(2,1)S(1)} %copy-done.1), channel_id=1, source_target_pairs={{0,1},{1,0},{2,3},{3,2},{4,5},{5,4},{6,7},{7,6},{8,9},{9,8},{10,11... | collective-permute-start | bytes 2359304 | tf_op jit(solution)/shard_map/ppermute | solution.py:353
  10.2 29.1 %collective-permute-start.2 = (bf16[512,768]{1,0:T(8,128)(2,1)}, bf16[512,768]{1,0:T(8,128)(2,1)}, u32[]{:S(2)}, u32[]{:S(2)}) collective-permute-start(bf16[512,768]{1,0:T(8,128)(2,1)} %pad_maximum_fusion), channel_id=1, source_target_pairs={{0,4},{4,8},{6,2},{8,12},{10,6},{14,10},{1,5},{5,9},{7,3},{9,13},{... | collective-permute-start | bytes 2359304 | tf_op jit(solution)/shard_map/ppermute | solution.py:350
  16.8 28.6 %collective-permute-start.8 = (bf16[512,768]{1,0:T(8,128)(2,1)}, bf16[512,768]{1,0:T(8,128)(2,1)}, u32[]{:S(2)}, u32[]{:S(2)}) collective-permute-start(bf16[512,768]{1,0:T(8,128)(2,1)} %pad_maximum_fusion.1), channel_id=1, source_target_pairs={{2,6},{4,0},{6,10},{8,4},{10,14},{12,8},{3,7},{5,1},{7,11},{9,5},{... | collective-permute-start | bytes 2359304 | tf_op jit(solution)/shard_map/ppermute | solution.py:351
  18.3 11.7 %collective-permute-start.3 = (bf16[512,384]{1,0:T(8,128)(2,1)S(1)}, bf16[512,384]{1,0:T(8,128)(2,1)}, u32[]{:S(2)}, u32[]{:S(2)}) collective-permute-start(bf16[512,384]{1,0:T(8,128)(2,1)S(1)} %pad_maximum_fusion.3), channel_id=1, source_target_pairs={{0,2},{2,0},{4,6},{6,4},{8,10},{10,8},{12,14},{14,12},{1,3},{3,1},... | collective-permute-start | bytes 1179656 | tf_op jit(solution)/shard_map/ppermute | solution.py:349
  29.9 22.9 %collective-permute-start.10 = (bf16[256,1536]{1,0:T(8,128)(2,1)}, bf16[256,1536]{1,0:T(8,128)(2,1)}, u32[]{:S(2)}, u32[]{:S(2)}) collective-permute-start(bf16[256,1536]{1,0:T(8,128)(2,1)} %query.5), channel_id=1, source_target_pairs={{0,2},{2,0},{4,6},{6,4},{8,10},{10,8},{12,14},{14,12},{1,3},{3,1},... | collective-permute-start | bytes 2359304 | tf_op jit(solution)/shard_map/ppermute | solution.py:354
  31.7 0.9 copy-start.2
  32.6 0.9 copy-start.4
  33.5 14.3 %collective-permute-start.4 = (bf16[512,384]{1,0:T(8,128)(2,1)}, bf16[512,384]{1,0:T(8,128)(2,1)S(1)}, u32[]{:S(2)}, u32[]{:S(2)}) collective-permute-start(bf16[512,384]{1,0:T(8,128)(2,1)} %get-tuple-element.13), channel_id=1, source_target_pairs={{0,4},{4,8},{6,2},{8,12},{10,6},{14,10},{1,5},{5,9},{7,3},{9,13},{... | collective-permute-start | bytes 1179656 | tf_op jit(solution)/shard_map/ppermute | solution.py:358
  38.1 13.1 %collective-permute-start.6 = (bf16[512,384]{1,0:T(8,128)(2,1)}, bf16[512,384]{1,0:T(8,128)(2,1)}, u32[]{:S(2)}, u32[]{:S(2)}) collective-permute-start(bf16[512,384]{1,0:T(8,128)(2,1)} %get-tuple-element.14), channel_id=1, source_target_pairs={{2,6},{4,0},{6,10},{8,4},{10,14},{12,8},{3,7},{5,1},{7,11},{9,5},{... | collective-permute-start | bytes 1179656 | tf_op jit(solution)/shard_map/ppermute | solution.py:357
  39.4 20.9 %copy-start.3 = (bf16[256,1536]{1,0:T(8,128)(2,1)S(1)}, bf16[256,1536]{1,0:T(8,128)(2,1)}, u32[]{:S(2)}) copy-start(bf16[256,1536]{1,0:T(8,128)(2,1)} %copy-done.2) | copy-start | bytes 2359300
  39.4 20.9 %copy-start.5 = (bf16[256,1536]{1,0:T(8,128)(2,1)S(1)}, bf16[256,1536]{1,0:T(8,128)(2,1)}, u32[]{:S(2)}) copy-start(bf16[256,1536]{1,0:T(8,128)(2,1)} %copy-done.4) | copy-start | bytes 2359300
  39.4 20.9 %copy-start.12 = (s32[8,8]{1,0:T(8,128)S(1)}, s32[8,8]{1,0:T(8,128)}, u32[]{:S(2)}) copy-start(s32[8,8]{1,0:T(8,128)} %table_ref.11) | copy-start | bytes 772
  39.4 28.7 %collective-permute-start.9 = (bf16[512,768]{1,0:T(8,128)(2,1)}, bf16[512,768]{1,0:T(8,128)(2,1)}, u32[]{:S(2)}, u32[]{:S(2)}) collective-permute-start(bf16[512,768]{1,0:T(8,128)(2,1)} %tie.3), channel_id=1, source_target_pairs={{0,4},{4,8},{6,2},{8,12},{10,6},{14,10},{1,5},{5,9},{7,3},{9,13},{... | collective-permute-start | bytes 2359304 | tf_op jit(solution)/shard_map/ppermute | solution.py:360
  46.5 22.7 %collective-permute-start.12 = (bf16[512,768]{1,0:T(8,128)(2,1)}, bf16[512,768]{1,0:T(8,128)(2,1)}, u32[]{:S(2)}, u32[]{:S(2)}) collective-permute-start(bf16[512,768]{1,0:T(8,128)(2,1)} %collective-permute-done.8.rest_1_.rest_2_), channel_id=1, source_target_pairs={{2,6},{4,0},{6,10},{8,4},{10,14},{12,8},{3,7},{5,1},{7,11},{9,5},{... | collective-permute-start | bytes 2359304 | tf_op jit(solution)/shard_map/ppermute | solution.py:361
  47.8 10.4 %collective-permute-start.13 = (bf16[256,768]{1,0:T(8,128)(2,1)S(1)}, bf16[256,768]{1,0:T(8,128)(2,1)S(1)}, u32[]{:S(2)}, u32[]{:S(2)}) collective-permute-start(bf16[256,768]{1,0:T(8,128)(2,1)S(1)} %pad_maximum_fusion.5), channel_id=1, source_target_pairs={{0,1},{1,0},{2,3},{3,2},{4,5},{5,4},{6,7},{7,6},{8,9},{9,8},{10,11... | collective-permute-start | bytes 1179656 | tf_op jit(solution)/shard_map/ppermute | solution.py:362
  52.9 26.8 %collective-permute-start.7 = (bf16[256,768]{1,0:T(8,128)(2,1)}, bf16[256,768]{1,0:T(8,128)(2,1)}, u32[]{:S(2)}, u32[]{:S(2)}) collective-permute-start(bf16[256,768]{1,0:T(8,128)(2,1)} %maximum_maximum_fusion), channel_id=1, source_target_pairs={{0,1},{1,0},{2,3},{3,2},{4,5},{5,4},{6,7},{7,6},{8,9},{9,8},{10,11... | collective-permute-start | bytes 1179656 | tf_op jit(solution)/shard_map/ppermute | solution.py:365
  52.9 26.7 %collective-permute-start.5 = (bf16[512,384]{1,0:T(8,128)(2,1)S(1)}, bf16[512,384]{1,0:T(8,128)(2,1)}, u32[]{:S(2)}, u32[]{:S(2)}) collective-permute-start(bf16[512,384]{1,0:T(8,128)(2,1)S(1)} %collective-permute-done.4.rest_1_), channel_id=1, source_target_pairs={{0,4},{4,8},{6,2},{8,12},{10,6},{14,10},{1,5},{5,9},{7,3},{9,13},{... | collective-permute-start | bytes 1179656 | tf_op jit(solution)/shard_map/ppermute | solution.py:363
  58.2 0.8 copy-start.10
  58.9 20.7 %collective-permute-start.15 = (bf16[512,384]{1,0:T(8,128)(2,1)}, bf16[512,384]{1,0:T(8,128)(2,1)}, u32[]{:S(2)}, u32[]{:S(2)}) collective-permute-start(bf16[512,384]{1,0:T(8,128)(2,1)} %collective-permute-done.6.rest_2_.rest_1_), channel_id=1, source_target_pairs={{2,6},{4,0},{6,10},{8,4},{10,14},{12,8},{3,7},{5,1},{7,11},{9,5},{... | collective-permute-start | bytes 1179656 | tf_op jit(solution)/shard_map/ppermute | solution.py:364
  65.3 3.9 %copy-start.7 = (f32[256,128]{1,0:T(8,128)S(1)}, f32[256,128]{1,0:T(8,128)}, u32[]{:S(2)}) copy-start(f32[256,128]{1,0:T(8,128)} %copy-done.6) | copy-start | bytes 393220
  65.3 3.9 %copy-start.11 = (bf16[256,768]{1,0:T(8,128)(2,1)S(1)}, bf16[256,768]{1,0:T(8,128)(2,1)}, u32[]{:S(2)}) copy-start(bf16[256,768]{1,0:T(8,128)(2,1)} %copy-done.10) | copy-start | bytes 1179652
  68.1 11.6 %collective-permute-start.11 = (bf16[272,384]{1,0:T(8,128)(2,1)S(1)}, bf16[272,384]{1,0:T(8,128)(2,1)S(1)}, u32[]{:S(2)}, u32[]{:S(2)}) collective-permute-start(bf16[272,384]{1,0:T(8,128)(2,1)S(1)} %partner_part.3.rest_5_), channel_id=1, source_target_pairs={{0,2},{2,0},{4,6},{6,4},{8,10},{10,8},{12,14},{14,12},{1,3},{3,1},... | collective-permute-start | bytes 626696 | tf_op jit(solution)/shard_map/ppermute | solution.py:416
  69.2 21.1 %slice-start = ((s8[9437184]{0:T(1024)(128)(4,1)}), s8[4194304]{0:T(1024)(128)(4,1)S(1)}, s32[]{:S(2)}) async-start(s8[9437184]{0:T(1024)(128)(4,1)} %bitcast), calls=%async_computation.1 | async-start | bytes 8388608
  74.4 15.9 %slice-start.1 = ((s8[9437184]{0:T(1024)(128)(4,1)}), s8[4194304]{0:T(1024)(128)(4,1)S(1)}, s32[]{:S(2)}) async-start(s8[9437184]{0:T(1024)(128)(4,1)} %bitcast), calls=%async_computation.2 | async-start | bytes 8388608
  74.4 15.9 %collective-permute-start.14 = (bf16[288,768]{1,0:T(8,128)(2,1)S(1)}, bf16[288,768]{1,0:T(8,128)(2,1)S(1)}, u32[]{:S(2)}, u32[]{:S(2)}) collective-permute-start(bf16[288,768]{1,0:T(8,128)(2,1)S(1)} %partner_part.4), channel_id=1, source_target_pairs={{0,2},{2,0},{4,6},{6,4},{8,10},{10,8},{12,14},{14,12},{1,3},{3,1},... | collective-permute-start | bytes 1327112 | tf_op jit(solution)/shard_map/ppermute | solution.py:417
  79.7 10.6 %slice-start.2 = ((s8[9437184]{0:T(1024)(128)(4,1)}), s8[1048576]{0:T(1024)(128)(4,1)S(1)}, s32[]{:S(2)}) async-start(s8[9437184]{0:T(1024)(128)(4,1)} %bitcast), calls=%async_computation.3 | async-start | bytes 2097152
  83.3 7.0 %copy-start.9 = (f32[256,384]{1,0:T(8,128)S(1)}, f32[256,384]{1,0:T(8,128)}, u32[]{:S(2)}) copy-start(f32[256,384]{1,0:T(8,128)} %copy-done.8) | copy-start | bytes 1179652
  83.3 7.0 %collective-permute-start.16 = (bf16[272,384]{1,0:T(8,128)(2,1)S(1)}, bf16[272,384]{1,0:T(8,128)(2,1)S(1)}, u32[]{:S(2)}, u32[]{:S(2)}) collective-permute-start(bf16[272,384]{1,0:T(8,128)(2,1)S(1)} %partner_part.5), channel_id=1, source_target_pairs={{0,2},{2,0},{4,6},{6,4},{8,10},{10,8},{12,14},{14,12},{1,3},{3,1},... | collective-permute-start | bytes 626696 | tf_op jit(solution)/shard_map/ppermute | solution.py:422
  (2 other events, 1.4 us)
Sparse Core Ops, SparseCore 0:
  8.9 24.5 all-gather.1

commit v4 on v3

--- a/solution.py
+++ b/solution.py
@@ -281,7 +281,7 @@
         + [pl.BlockSpec(memory_space=pl.ANY)] * len(after),
         out_specs=[whole(s.shape) for s in out_shapes],
         out_shape=out_shapes,
-        compiler_params=pltpu.CompilerParams(vmem_limit_bytes=24 * MIB),
+        compiler_params=pltpu.CompilerParams(vmem_limit_bytes=8 * MIB),
         cost_estimate=pl.CostEstimate(
             flops=flops, bytes_accessed=MIB, transcendentals=flops // 512
         ),
@@ -301,6 +301,7 @@
         out_specs=[anywhere] * len(payloads),
         out_shape=[jax.ShapeDtypeStruct(p.shape, p.dtype) for p in payloads],
         input_output_aliases={len(before) + i: i for i in range(len(payloads))},
+        compiler_params=pltpu.CompilerParams(vmem_limit_bytes=MIB),
         name="tie",
     )(*before, *payloads)
 
@@ -315,7 +316,7 @@
         out_specs=whole((rows, columns)),
         out_shape=jax.ShapeDtypeStruct((rows, columns), jnp.bfloat16),
         scratch_shapes=[pltpu.VMEM((rows, depth), jnp.bfloat16)],
-        compiler_params=pltpu.CompilerParams(vmem_limit_bytes=24 * MIB),
+        compiler_params=pltpu.CompilerParams(vmem_limit_bytes=8 * MIB),
         cost_estimate=pl.CostEstimate(
             flops=2 * rows * depth * columns, bytes_accessed=12 * MIB, transcendentals=0
         ),

time: 103 us -> 97.9 us (0.950)
  other arithmetic: 5.47 us -> 1.93 us
  Pallas kernels: 27.2 us -> 24.5 us
    concatenate x5, other arithmetic: 4.67 us -> 1.12 us  [pack(): return jnp.concatenate([key_tokens[:, cols], value_tokens[:, cols]], axis=0)]
    pallas_call x6, Pallas kernels: 22 us -> 19.4 us  [run(): pl.pallas_call(body, grid=(1,), in_specs=[pl.BlockSpec(memory_space=pltpu...]
    ppermute x1, starting transfers between devices: 0.06 us -> 1.53 us  [per_device(): part_low = lax.ppermute(part_low, 'frame', partner_moves)]
    unnamed x32 -> x38, local copies, waits for them, and re-layouts: 4.41 us -> 5.83 us
    ppermute x1, waiting for transfers between devices: 2.63 us -> 3.67 us  [per_device(): part_high = lax.ppermute(part_high, 'frame', partner_moves)]
  transfers between devices with their start and end apart: 18 -> 18, of which waited for: 4 -> 3; matrix products, arithmetic and copies ran while one was open for 9% -> 5% of each run, Pallas kernels for 21% -> 20%
where the time goes in v4:
time: 97.9 us; the launch traced here: 97.2 us
  starting transfers between devices  32.3 us (33%)
  Pallas kernels  24.5 us (25%)
  waiting for transfers between devices  16 us (16%)
  between operations  13.7 us (14%)
  local copies, waits for them, and re-layouts  8.8 us (9%)
  other arithmetic  1.93 us (2%)
    pallas_call x6, Pallas kernels, run(): pl.pallas_call(body, grid=(1,), in_specs=[pl.BlockSpec(memory_space=pltpu...  19.4 us
    ppermute x1, waiting for transfers between devices, per_device(): cross = lax.ppermute(pack(0, 3), 'frame', partner_moves)  8.91 us
    unnamed x38, local copies, waits for them, and re-layouts  5.83 us
    ppermute x1, starting transfers between devices, per_device(): major3 = lax.ppermute(to_major3, 'frame', away_moves)  5.58 us
    pallas_call x1, Pallas kernels, project(): pl.pallas_call(functools.partial(project_kernel, own_groups, part_groups)...  5.13 us
    ppermute x1, starting transfers between devices, per_device(): major1 = lax.ppermute(pack(0, 6), 'frame', away_moves)  4.8 us
    ppermute x1, starting transfers between devices, per_device(): major4 = lax.ppermute(major2, 'frame', away_moves)  4.64 us
    ppermute x1, waiting for transfers between devices, per_device(): part_high = lax.ppermute(part_high, 'frame', partner_moves)  3.67 us
  transfers between devices with their start and end apart: 18, of which 3 were waited for; matrix products, arithmetic and copies ran while one was open for 5% of the time, Pallas kernels for 20%

profile of v4, /device:TPU:0, one launch (start us, length us, event | category | flops | bytes accessed | tf_op | source)
XLA Modules:
  0.0 97.2 jit_solution(10477064920153931553)
XLA Ops:
  6.5 0.7 all-gather.2.cloned.1.call-update
  8.6 4.8 %collective-permute-start.2 = (bf16[512,768]{1,0:T(8,128)(2,1)S(1)}, bf16[512,768]{1,0:T(8,128)(2,1)S(1)}, u32[]{:S(2)}, u32[]{:S(2)}) collective-permute-start(bf16[512,768]{1,0:T(8,128)(2,1)S(1)} %pad_maximum_fusion), channel_id=1, source_target_pairs={{0,4},{4,8},{6,2},{8,12},{10,6},{14,10},{1,5},{5,9},{7,3},{9,13},{... | collective-permute-start | bytes 2359304 | tf_op jit(solution)/shard_map/ppermute | solution.py:351
  13.5 1.4 %collective-permute-start.8 = (bf16[512,768]{1,0:T(8,128)(2,1)S(1)}, bf16[512,768]{1,0:T(8,128)(2,1)}, u32[]{:S(2)}, u32[]{:S(2)}) collective-permute-start(bf16[512,768]{1,0:T(8,128)(2,1)S(1)} %pad_maximum_fusion.1), channel_id=1, source_target_pairs={{2,6},{4,0},{6,10},{8,4},{10,14},{12,8},{3,7},{5,1},{7,11},{9,5},{... | collective-permute-start | bytes 2359304 | tf_op jit(solution)/shard_map/ppermute | solution.py:352
  15.1 3.5 %collective-permute-start.3 = (bf16[512,384]{1,0:T(8,128)(2,1)S(1)}, bf16[512,384]{1,0:T(8,128)(2,1)S(1)}, u32[]{:S(2)}, u32[]{:S(2)}) collective-permute-start(bf16[512,384]{1,0:T(8,128)(2,1)S(1)} %pad_maximum_fusion.3), channel_id=1, source_target_pairs={{0,2},{2,0},{4,6},{6,4},{8,10},{10,8},{12,14},{14,12},{1,3},{3,1},... | collective-permute-start | bytes 1179656 | tf_op jit(solution)/shard_map/ppermute | solution.py:350
  18.6 8.9 %collective-permute-done.3.refs_2_ = bf16[512,384]{1,0:T(8,128)(2,1)S(1)} collective-permute-done((bf16[512,384]{1,0:T(8,128)(2,1)S(1)}, bf16[512,384]{1,0:T(8,128)(2,1)S(1)}, u32[]{:S(2)}, u32[]{:S(2)}) %collective-permute-start.3) | collective-permute-done | bytes 393248 | tf_op jit(solution)/shard_map/ppermute | solution.py:350
  27.5 1.7 %collective-permute-start.10 = (bf16[256,1536]{1,0:T(8,128)(2,1)S(1)}, bf16[256,1536]{1,0:T(8,128)(2,1)S(1)}, u32[]{:S(2)}, u32[]{:S(2)}) collective-permute-start(bf16[256,1536]{1,0:T(8,128)(2,1)S(1)} %copy-done.4), channel_id=1, source_target_pairs={{0,2},{2,0},{4,6},{6,4},{8,10},{10,8},{12,14},{14,12},{1,3},{3,1},... | collective-permute-start | bytes 2359304 | tf_op jit(solution)/shard_map/ppermute | solution.py:355
  29.3 2.6 %collective-permute-start.4 = (bf16[512,384]{1,0:T(8,128)(2,1)S(1)}, bf16[512,384]{1,0:T(8,128)(2,1)S(1)}, u32[]{:S(2)}, u32[]{:S(2)}) collective-permute-start(bf16[512,384]{1,0:T(8,128)(2,1)S(1)} %get-tuple-element.13), channel_id=1, source_target_pairs={{0,4},{4,8},{6,2},{8,12},{10,6},{14,10},{1,5},{5,9},{7,3},{9,13},{... | collective-permute-start | bytes 1179656 | tf_op jit(solution)/shard_map/ppermute | solution.py:359
  31.9 0.9 pad_maximum_fusion.2.refs_1_
  32.8 1.3 %collective-permute-start.6 = (bf16[512,384]{1,0:T(8,128)(2,1)S(1)}, bf16[512,384]{1,0:T(8,128)(2,1)}, u32[]{:S(2)}, u32[]{:S(2)}) collective-permute-start(bf16[512,384]{1,0:T(8,128)(2,1)S(1)} %get-tuple-element.14), channel_id=1, source_target_pairs={{2,6},{4,0},{6,10},{8,4},{10,14},{12,8},{3,7},{5,1},{7,11},{9,5},{... | collective-permute-start | bytes 1179656 | tf_op jit(solution)/shard_map/ppermute | solution.py:358
  34.1 5.6 %collective-permute-start.9 = (bf16[512,768]{1,0:T(8,128)(2,1)}, bf16[512,768]{1,0:T(8,128)(2,1)}, u32[]{:S(2)}, u32[]{:S(2)}) collective-permute-start(bf16[512,768]{1,0:T(8,128)(2,1)} %tie.3), channel_id=1, source_target_pairs={{0,4},{4,8},{6,2},{8,12},{10,6},{14,10},{1,5},{5,9},{7,3},{9,13},{... | collective-permute-start | bytes 2359304 | tf_op jit(solution)/shard_map/ppermute | solution.py:361
  39.7 1.0 %fusion = (bf16[128,768]{1,0:T(8,128)(2,1)S(1)}, bf16[128,768]{1,0:T(8,128)(2,1)S(1)}) fusion(bf16[512,768]{1,0:T(8,128)(2,1)} %collective-permute-done.8.rest_1_.rest_2_), kind=kLoop, calls=%fused_computation.7 | loop fusion | bytes 786432 | tf_op jit(solution)/shard_map/slice | solution.py:346
  40.8 1.3 %collective-permute-start.12 = (bf16[512,768]{1,0:T(8,128)(2,1)}, bf16[512,768]{1,0:T(8,128)(2,1)}, u32[]{:S(2)}, u32[]{:S(2)}) collective-permute-start(bf16[512,768]{1,0:T(8,128)(2,1)} %collective-permute-done.8.rest_1_.rest_2_), channel_id=1, source_target_pairs={{2,6},{4,0},{6,10},{8,4},{10,14},{12,8},{3,7},{5,1},{7,11},{9,5},{... | collective-permute-start | bytes 2359304 | tf_op jit(solution)/shard_map/ppermute | solution.py:362
  42.2 2.6 %collective-permute-done.6.rest_2_.rest_1_ = bf16[512,384]{1,0:T(8,128)(2,1)} collective-permute-done((bf16[512,384]{1,0:T(8,128)(2,1)S(1)}, bf16[512,384]{1,0:T(8,128)(2,1)}, u32[]{:S(2)}, u32[]{:S(2)}) %collective-permute-start.6) | collective-permute-done | bytes 393248 | tf_op jit(solution)/shard_map/ppermute | solution.py:358
  44.9 1.0 fusion.5
  45.8 0.8 maximum_maximum_fusion
  46.6 0.9 copy-done.6
  47.6 4.6 %collective-permute-start.5 = (bf16[512,384]{1,0:T(8,128)(2,1)S(1)}, bf16[512,384]{1,0:T(8,128)(2,1)}, u32[]{:S(2)}, u32[]{:S(2)}) collective-permute-start(bf16[512,384]{1,0:T(8,128)(2,1)S(1)} %collective-permute-done.4.rest_1_), channel_id=1, source_target_pairs={{0,4},{4,8},{6,2},{8,12},{10,6},{14,10},{1,5},{5,9},{7,3},{9,13},{... | collective-permute-start | bytes 1179656 | tf_op jit(solution)/shard_map/ppermute | solution.py:364
  52.2 0.8 copy-done.13
  53.0 1.3 %collective-permute-start.15 = (bf16[512,384]{1,0:T(8,128)(2,1)}, bf16[512,384]{1,0:T(8,128)(2,1)}, u32[]{:S(2)}, u32[]{:S(2)}) collective-permute-start(bf16[512,384]{1,0:T(8,128)(2,1)} %collective-permute-done.6.rest_2_.rest_1_), channel_id=1, source_target_pairs={{2,6},{4,0},{6,10},{8,4},{10,14},{12,8},{3,7},{5,1},{7,11},{9,5},{... | collective-permute-start | bytes 1179656 | tf_op jit(solution)/shard_map/ppermute | solution.py:365
  54.3 2.4 %own_part.4 = (f32[256,384]{1,0:T(8,128)S(1)}, f32[256,128]{1,0:T(8,128)S(1)}) custom-call(s32[8,8]{1,0:T(8,128)S(1)} %copy-done.15, bf16[256,1536]{1,0:T(8,128)(2,1)S(1)} %copy-done.4, bf16[256,1536]{1,0:T(8,128)(2,1)S(1)} %copy-done, bf16[256,1536]{1,0:T(8,128)(2,1)S(1)} %copy-done.1, bf16[256,1536]{1,0:T(8,128)(2,1)S(1)} %collective-permute-done.refs_0_.sib_keys, ...), custom_call_target="tpu_custom_call" | custom-call | flops 301989888 | bytes 1048576 | tf_op jit(solution)/shard_map/own_part/pallas_call | solution.py:276
  57.4 0.7 copy-done.11
  58.8 1.1 %copy-done.3 = bf16[512,768]{1,0:T(8,128)(2,1)S(1)} copy-done((bf16[512,768]{1,0:T(8,128)(2,1)S(1)}, bf16[512,768]{1,0:T(8,128)(2,1)}, u32[]{:S(2)}) %copy-start.3) | copy-done | bytes 786456
  60.0 1.1 %copy-done.7 = bf16[256,1536]{1,0:T(8,128)(2,1)S(1)} copy-done((bf16[256,1536]{1,0:T(8,128)(2,1)S(1)}, bf16[256,1536]{1,0:T(8,128)(2,1)}, u32[]{:S(2)}) %copy-start.7) | copy-done | bytes 786456
  61.1 2.0 %partner_part.3.rest_5_ = bf16[272,384]{1,0:T(8,128)(2,1)S(1)} custom-call(s32[8,8]{1,0:T(8,128)S(1)} %copy-done.15, bf16[256,1536]{1,0:T(8,128)(2,1)S(1)} %copy-done.7, bf16[256,1536]{1,0:T(8,128)(2,1)S(1)} %copy-done, bf16[256,1536]{1,0:T(8,128)(2,1)S(1)} %copy-done.1, bf16[256,1536]{1,0:T(8,128)(2,1)S(1)} %collective-permute-done.refs_0_.sib_keys, ...), custom_call_target="tpu_custom_call" | custom-call | flops 301989888 | bytes 1048576 | tf_op jit(solution)/shard_map/partner_part/pallas_call | solution.py:276
  63.1 1.5 %collective-permute-start.11 = (bf16[272,384]{1,0:T(8,128)(2,1)S(1)}, bf16[272,384]{1,0:T(8,128)(2,1)S(1)}, u32[]{:S(2)}, u32[]{:S(2)}) collective-permute-start(bf16[272,384]{1,0:T(8,128)(2,1)S(1)} %partner_part.3.rest_5_), channel_id=1, source_target_pairs={{0,2},{2,0},{4,6},{6,4},{8,10},{10,8},{12,14},{14,12},{1,3},{3,1},... | collective-permute-start | bytes 626696 | tf_op jit(solution)/shard_map/ppermute | solution.py:417
  64.6 4.8 %partner_part.4 = bf16[288,768]{1,0:T(8,128)(2,1)S(1)} custom-call(s32[8,8]{1,0:T(8,128)S(1)} %copy-done.15, bf16[256,1536]{1,0:T(8,128)(2,1)S(1)} %copy-done.8, bf16[256,1536]{1,0:T(8,128)(2,1)S(1)} %copy-done, bf16[256,1536]{1,0:T(8,128)(2,1)S(1)} %copy-done.1, bf16[256,1536]{1,0:T(8,128)(2,1)S(1)} %collective-permute-done.refs_0_.sib_keys, ...), custom_call_target="tpu_custom_call" | custom-call | flops 603979776 | bytes 1048576 | tf_op jit(solution)/shard_map/partner_part/pallas_call | solution.py:276
  70.0 4.0 %own_part.5 = (f32[256,768]{1,0:T(8,128)S(1)}, f32[256,128]{1,0:T(8,128)S(1)}) custom-call(s32[8,8]{1,0:T(8,128)S(1)} %copy-done.15, bf16[256,1536]{1,0:T(8,128)(2,1)S(1)} %copy-done.5, bf16[256,1536]{1,0:T(8,128)(2,1)S(1)} %copy-done, bf16[256,1536]{1,0:T(8,128)(2,1)S(1)} %copy-done.1, bf16[256,1536]{1,0:T(8,128)(2,1)S(1)} %collective-permute-done.refs_0_.sib_keys, ...), custom_call_target="tpu_custom_call" | custom-call | flops 603979776 | bytes 1048576 | tf_op jit(solution)/shard_map/own_part/pallas_call | solution.py:276
  74.1 3.4 %partner_part.5 = bf16[272,384]{1,0:T(8,128)(2,1)S(1)} custom-call(s32[8,8]{1,0:T(8,128)S(1)} %copy-done.15, bf16[256,1536]{1,0:T(8,128)(2,1)S(1)} %copy-done.8, bf16[256,1536]{1,0:T(8,128)(2,1)S(1)} %copy-done, bf16[256,1536]{1,0:T(8,128)(2,1)S(1)} %copy-done.1, bf16[256,1536]{1,0:T(8,128)(2,1)S(1)} %collective-permute-done.refs_0_.sib_keys, ...), custom_call_target="tpu_custom_call" | custom-call | flops 301989888 | bytes 1048576 | tf_op jit(solution)/shard_map/partner_part/pallas_call | solution.py:276
  77.5 1.2 %collective-permute-start.16 = (bf16[272,384]{1,0:T(8,128)(2,1)S(1)}, bf16[272,384]{1,0:T(8,128)(2,1)S(1)}, u32[]{:S(2)}, u32[]{:S(2)}) collective-permute-start(bf16[272,384]{1,0:T(8,128)(2,1)S(1)} %partner_part.5), channel_id=1, source_target_pairs={{0,2},{2,0},{4,6},{6,4},{8,10},{10,8},{12,14},{14,12},{1,3},{3,1},... | collective-permute-start | bytes 626696 | tf_op jit(solution)/shard_map/ppermute | solution.py:423
  78.7 2.8 %own_part.3 = (f32[256,384]{1,0:T(8,128)S(1)}, f32[256,128]{1,0:T(8,128)S(1)}) custom-call(s32[8,8]{1,0:T(8,128)S(1)} %copy-done.15, bf16[256,1536]{1,0:T(8,128)(2,1)S(1)} %copy-done.5, bf16[256,1536]{1,0:T(8,128)(2,1)S(1)} %copy-done, bf16[256,1536]{1,0:T(8,128)(2,1)S(1)} %copy-done.1, bf16[256,1536]{1,0:T(8,128)(2,1)S(1)} %collective-permute-done.refs_0_.sib_keys, ...), custom_call_target="tpu_custom_call" | custom-call | flops 301989888 | bytes 1048576 | tf_op jit(solution)/shard_map/own_part/pallas_call | solution.py:276
  81.5 3.7 %collective-permute-done.16.refs_9_ = bf16[272,384]{1,0:T(8,128)(2,1)S(1)} collective-permute-done((bf16[272,384]{1,0:T(8,128)(2,1)S(1)}, bf16[272,384]{1,0:T(8,128)(2,1)S(1)}, u32[]{:S(2)}, u32[]{:S(2)}) %collective-permute-start.16) | collective-permute-done | bytes 208928 | tf_op jit(solution)/shard_map/ppermute | solution.py:423
  85.3 5.1 %merge_and_project.1 = bf16[256,3072]{1,0:T(8,128)(2,1)} custom-call(bf16[1536,3072]{1,0:T(8,128)(2,1)S(1)} %bitcast.1, f32[256,384]{1,0:T(8,128)S(1)} %get-tuple-element.15.refs_1_, f32[256,128]{1,0:T(8,128)S(1)} %get-tuple-element.16.refs_2_, f32[256,384]{1,0:T(8,128)S(1)} %copy-done.12, f32[256,128]{1,0:T(8,128)S(1)} %copy-done.10, ...), custom_call_target="tpu_custom_call" | custom-call | flops 2415919104 | bytes 12582912 | tf_op jit(solution)/shard_map/merge_and_project/pallas_call | solution.py:312
  (68 shorter events, 3.7 us)
Async XLA Ops:
  6.5 1.1 %copy-start = (bf16[256,1536]{1,0:T(8,128)(2,1)S(1)}, bf16[256,1536]{1,0:T(8,128)(2,1)}, u32[]{:S(2)}) copy-start(bf16[256,1536]{1,0:T(8,128)(2,1)} %keys.11) | copy-start | bytes 2359300
  6.5 1.6 %copy-start.1 = (bf16[256,1536]{1,0:T(8,128)(2,1)S(1)}, bf16[256,1536]{1,0:T(8,128)(2,1)}, u32[]{:S(2)}) copy-start(bf16[256,1536]{1,0:T(8,128)(2,1)} %values.11) | copy-start | bytes 2359300
  6.5 51.6 %all-gather.2.cloned.1.call-start = ((), (), s32[]{:S(2)}) async-start(), calls=%async_computation | async-start | bytes 14155776 | tf_op jit(solution)/shard_map/all_gather | solution.py:356
  7.7 21.6 %collective-permute-start = (bf16[256,1536]{1,0:T(8,128)(2,1)S(1)}, bf16[256,1536]{1,0:T(8,128)(2,1)S(1)}, u32[]{:S(2)}, u32[]{:S(2)}) collective-permute-start(bf16[256,1536]{1,0:T(8,128)(2,1)S(1)} %copy-done), channel_id=1, source_target_pairs={{0,1},{1,0},{2,3},{3,2},{4,5},{5,4},{6,7},{7,6},{8,9},{9,8},{10,11... | collective-permute-start | bytes 2359304 | tf_op jit(solution)/shard_map/ppermute | solution.py:353
  8.1 21.1 %collective-permute-start.1 = (bf16[256,1536]{1,0:T(8,128)(2,1)S(1)}, bf16[256,1536]{1,0:T(8,128)(2,1)S(1)}, u32[]{:S(2)}, u32[]{:S(2)}) collective-permute-start(bf16[256,1536]{1,0:T(8,128)(2,1)S(1)} %copy-done.1), channel_id=1, source_target_pairs={{0,1},{1,0},{2,3},{3,2},{4,5},{5,4},{6,7},{7,6},{8,9},{9,8},{10,11... | collective-permute-start | bytes 2359304 | tf_op jit(solution)/shard_map/ppermute | solution.py:354
  8.6 25.5 %collective-permute-start.2 = (bf16[512,768]{1,0:T(8,128)(2,1)S(1)}, bf16[512,768]{1,0:T(8,128)(2,1)S(1)}, u32[]{:S(2)}, u32[]{:S(2)}) collective-permute-start(bf16[512,768]{1,0:T(8,128)(2,1)S(1)} %pad_maximum_fusion), channel_id=1, source_target_pairs={{0,4},{4,8},{6,2},{8,12},{10,6},{14,10},{1,5},{5,9},{7,3},{9,13},{... | collective-permute-start | bytes 2359304 | tf_op jit(solution)/shard_map/ppermute | solution.py:351
  13.5 14.0 %copy-start.4 = (bf16[256,1536]{1,0:T(8,128)(2,1)S(1)}, bf16[256,1536]{1,0:T(8,128)(2,1)}, u32[]{:S(2)}) copy-start(bf16[256,1536]{1,0:T(8,128)(2,1)} %query.5) | copy-start | bytes 2359300
  13.5 26.2 %collective-permute-start.8 = (bf16[512,768]{1,0:T(8,128)(2,1)S(1)}, bf16[512,768]{1,0:T(8,128)(2,1)}, u32[]{:S(2)}, u32[]{:S(2)}) collective-permute-start(bf16[512,768]{1,0:T(8,128)(2,1)S(1)} %pad_maximum_fusion.1), channel_id=1, source_target_pairs={{2,6},{4,0},{6,10},{8,4},{10,14},{12,8},{3,7},{5,1},{7,11},{9,5},{... | collective-permute-start | bytes 2359304 | tf_op jit(solution)/shard_map/ppermute | solution.py:352
  15.1 12.4 %collective-permute-start.3 = (bf16[512,384]{1,0:T(8,128)(2,1)S(1)}, bf16[512,384]{1,0:T(8,128)(2,1)S(1)}, u32[]{:S(2)}, u32[]{:S(2)}) collective-permute-start(bf16[512,384]{1,0:T(8,128)(2,1)S(1)} %pad_maximum_fusion.3), channel_id=1, source_target_pairs={{0,2},{2,0},{4,6},{6,4},{8,10},{10,8},{12,14},{14,12},{1,3},{3,1},... | collective-permute-start | bytes 1179656 | tf_op jit(solution)/shard_map/ppermute | solution.py:350
  27.5 19.1 %collective-permute-start.10 = (bf16[256,1536]{1,0:T(8,128)(2,1)S(1)}, bf16[256,1536]{1,0:T(8,128)(2,1)S(1)}, u32[]{:S(2)}, u32[]{:S(2)}) collective-permute-start(bf16[256,1536]{1,0:T(8,128)(2,1)S(1)} %copy-done.4), channel_id=1, source_target_pairs={{0,2},{2,0},{4,6},{6,4},{8,10},{10,8},{12,14},{14,12},{1,3},{3,1},... | collective-permute-start | bytes 2359304 | tf_op jit(solution)/shard_map/ppermute | solution.py:355
  29.3 12.8 %collective-permute-start.4 = (bf16[512,384]{1,0:T(8,128)(2,1)S(1)}, bf16[512,384]{1,0:T(8,128)(2,1)S(1)}, u32[]{:S(2)}, u32[]{:S(2)}) collective-permute-start(bf16[512,384]{1,0:T(8,128)(2,1)S(1)} %get-tuple-element.13), channel_id=1, source_target_pairs={{0,4},{4,8},{6,2},{8,12},{10,6},{14,10},{1,5},{5,9},{7,3},{9,13},{... | collective-permute-start | bytes 1179656 | tf_op jit(solution)/shard_map/ppermute | solution.py:359
  32.8 12.1 %collective-permute-start.6 = (bf16[512,384]{1,0:T(8,128)(2,1)S(1)}, bf16[512,384]{1,0:T(8,128)(2,1)}, u32[]{:S(2)}, u32[]{:S(2)}) collective-permute-start(bf16[512,384]{1,0:T(8,128)(2,1)S(1)} %get-tuple-element.14), channel_id=1, source_target_pairs={{2,6},{4,0},{6,10},{8,4},{10,14},{12,8},{3,7},{5,1},{7,11},{9,5},{... | collective-permute-start | bytes 1179656 | tf_op jit(solution)/shard_map/ppermute | solution.py:358
  34.1 20.2 %copy-start.2 = (bf16[512,768]{1,0:T(8,128)(2,1)}, bf16[512,768]{1,0:T(8,128)(2,1)S(1)}, u32[]{:S(2)}) copy-start(bf16[512,768]{1,0:T(8,128)(2,1)S(1)} %collective-permute-done.2.rest_0_.refs_0_) | copy-start | bytes 2359300
  34.1 20.1 %copy-start.15 = (s32[8,8]{1,0:T(8,128)S(1)}, s32[8,8]{1,0:T(8,128)}, u32[]{:S(2)}) copy-start(s32[8,8]{1,0:T(8,128)} %table_ref.11) | copy-start | bytes 772
  34.1 28.9 %collective-permute-start.9 = (bf16[512,768]{1,0:T(8,128)(2,1)}, bf16[512,768]{1,0:T(8,128)(2,1)}, u32[]{:S(2)}, u32[]{:S(2)}) collective-permute-start(bf16[512,768]{1,0:T(8,128)(2,1)} %tie.3), channel_id=1, source_target_pairs={{0,4},{4,8},{6,2},{8,12},{10,6},{14,10},{1,5},{5,9},{7,3},{9,13},{... | collective-permute-start | bytes 2359304 | tf_op jit(solution)/shard_map/ppermute | solution.py:361
  40.8 23.8 %collective-permute-start.12 = (bf16[512,768]{1,0:T(8,128)(2,1)}, bf16[512,768]{1,0:T(8,128)(2,1)}, u32[]{:S(2)}, u32[]{:S(2)}) collective-permute-start(bf16[512,768]{1,0:T(8,128)(2,1)} %collective-permute-done.8.rest_1_.rest_2_), channel_id=1, source_target_pairs={{2,6},{4,0},{6,10},{8,4},{10,14},{12,8},{3,7},{5,1},{7,11},{9,5},{... | collective-permute-start | bytes 2359304 | tf_op jit(solution)/shard_map/ppermute | solution.py:362
  42.1 10.1 %collective-permute-start.13 = (bf16[256,768]{1,0:T(8,128)(2,1)S(1)}, bf16[256,768]{1,0:T(8,128)(2,1)S(1)}, u32[]{:S(2)}, u32[]{:S(2)}) collective-permute-start(bf16[256,768]{1,0:T(8,128)(2,1)S(1)} %pad_maximum_fusion.5), channel_id=1, source_target_pairs={{0,1},{1,0},{2,3},{3,2},{4,5},{5,4},{6,7},{7,6},{8,9},{9,8},{10,11... | collective-permute-start | bytes 1179656 | tf_op jit(solution)/shard_map/ppermute | solution.py:363
  46.6 27.4 %collective-permute-start.7 = (bf16[256,768]{1,0:T(8,128)(2,1)}, bf16[256,768]{1,0:T(8,128)(2,1)}, u32[]{:S(2)}, u32[]{:S(2)}) collective-permute-start(bf16[256,768]{1,0:T(8,128)(2,1)} %maximum_maximum_fusion), channel_id=1, source_target_pairs={{0,1},{1,0},{2,3},{3,2},{4,5},{5,4},{6,7},{7,6},{8,9},{9,8},{10,11... | collective-permute-start | bytes 1179656 | tf_op jit(solution)/shard_map/ppermute | solution.py:366
  47.6 26.5 %collective-permute-start.5 = (bf16[512,384]{1,0:T(8,128)(2,1)S(1)}, bf16[512,384]{1,0:T(8,128)(2,1)}, u32[]{:S(2)}, u32[]{:S(2)}) collective-permute-start(bf16[512,384]{1,0:T(8,128)(2,1)S(1)} %collective-permute-done.4.rest_1_), channel_id=1, source_target_pairs={{0,4},{4,8},{6,2},{8,12},{10,6},{14,10},{1,5},{5,9},{7,3},{9,13},{... | collective-permute-start | bytes 1179656 | tf_op jit(solution)/shard_map/ppermute | solution.py:364
  53.0 21.1 %collective-permute-start.15 = (bf16[512,384]{1,0:T(8,128)(2,1)}, bf16[512,384]{1,0:T(8,128)(2,1)}, u32[]{:S(2)}, u32[]{:S(2)}) collective-permute-start(bf16[512,384]{1,0:T(8,128)(2,1)} %collective-permute-done.6.rest_2_.rest_1_), channel_id=1, source_target_pairs={{2,6},{4,0},{6,10},{8,4},{10,14},{12,8},{3,7},{5,1},{7,11},{9,5},{... | collective-permute-start | bytes 1179656 | tf_op jit(solution)/shard_map/ppermute | solution.py:365
  58.8 1.1 %copy-start.3 = (bf16[512,768]{1,0:T(8,128)(2,1)S(1)}, bf16[512,768]{1,0:T(8,128)(2,1)}, u32[]{:S(2)}) copy-start(bf16[512,768]{1,0:T(8,128)(2,1)} %copy-done.2) | copy-start | bytes 2359300
  61.1 3.5 %copy-start.8 = (bf16[256,1536]{1,0:T(8,128)(2,1)S(1)}, bf16[256,1536]{1,0:T(8,128)(2,1)}, u32[]{:S(2)}) copy-start(bf16[256,1536]{1,0:T(8,128)(2,1)} %copy-done.6) | copy-start | bytes 2359300
  61.1 3.5 %copy-start.10 = (f32[256,128]{1,0:T(8,128)S(1)}, f32[256,128]{1,0:T(8,128)}, u32[]{:S(2)}) copy-start(f32[256,128]{1,0:T(8,128)} %copy-done.9) | copy-start | bytes 393220
  61.1 3.5 %copy-start.14 = (bf16[256,768]{1,0:T(8,128)(2,1)S(1)}, bf16[256,768]{1,0:T(8,128)(2,1)}, u32[]{:S(2)}) copy-start(bf16[256,768]{1,0:T(8,128)(2,1)} %copy-done.13) | copy-start | bytes 1179652
  63.1 11.0 %collective-permute-start.11 = (bf16[272,384]{1,0:T(8,128)(2,1)S(1)}, bf16[272,384]{1,0:T(8,128)(2,1)S(1)}, u32[]{:S(2)}, u32[]{:S(2)}) collective-permute-start(bf16[272,384]{1,0:T(8,128)(2,1)S(1)} %partner_part.3.rest_5_), channel_id=1, source_target_pairs={{0,2},{2,0},{4,6},{6,4},{8,10},{10,8},{12,14},{14,12},{1,3},{3,1},... | collective-permute-start | bytes 626696 | tf_op jit(solution)/shard_map/ppermute | solution.py:417
  64.6 5.4 %copy-start.5 = (bf16[256,1536]{1,0:T(8,128)(2,1)S(1)}, bf16[256,1536]{1,0:T(8,128)(2,1)}, u32[]{:S(2)}) copy-start(bf16[256,1536]{1,0:T(8,128)(2,1)} %query.5) | copy-start | bytes 2359300
  64.6 20.6 %slice-start = ((s8[9437184]{0:T(1024)(128)(4,1)}), s8[4194304]{0:T(1024)(128)(4,1)S(1)}, s32[]{:S(2)}) async-start(s8[9437184]{0:T(1024)(128)(4,1)} %bitcast), calls=%async_computation.1 | async-start | bytes 8388608
  69.4 15.8 %slice-start.1 = ((s8[9437184]{0:T(1024)(128)(4,1)}), s8[4194304]{0:T(1024)(128)(4,1)S(1)}, s32[]{:S(2)}) async-start(s8[9437184]{0:T(1024)(128)(4,1)} %bitcast), calls=%async_computation.2 | async-start | bytes 8388608
  69.4 15.8 %collective-permute-start.14 = (bf16[288,768]{1,0:T(8,128)(2,1)S(1)}, bf16[288,768]{1,0:T(8,128)(2,1)S(1)}, u32[]{:S(2)}, u32[]{:S(2)}) collective-permute-start(bf16[288,768]{1,0:T(8,128)(2,1)S(1)} %partner_part.4), channel_id=1, source_target_pairs={{0,2},{2,0},{4,6},{6,4},{8,10},{10,8},{12,14},{14,12},{1,3},{3,1},... | collective-permute-start | bytes 1327112 | tf_op jit(solution)/shard_map/ppermute | solution.py:418
  74.1 11.1 %slice-start.2 = ((s8[9437184]{0:T(1024)(128)(4,1)}), s8[1048576]{0:T(1024)(128)(4,1)S(1)}, s32[]{:S(2)}) async-start(s8[9437184]{0:T(1024)(128)(4,1)} %bitcast), calls=%async_computation.3 | async-start | bytes 2097152
  77.5 7.8 %copy-start.12 = (f32[256,384]{1,0:T(8,128)S(1)}, f32[256,384]{1,0:T(8,128)}, u32[]{:S(2)}) copy-start(f32[256,384]{1,0:T(8,128)} %copy-done.11) | copy-start | bytes 1179652
  77.5 7.7 %collective-permute-start.16 = (bf16[272,384]{1,0:T(8,128)(2,1)S(1)}, bf16[272,384]{1,0:T(8,128)(2,1)S(1)}, u32[]{:S(2)}, u32[]{:S(2)}) collective-permute-start(bf16[272,384]{1,0:T(8,128)(2,1)S(1)} %partner_part.5), channel_id=1, source_target_pairs={{0,2},{2,0},{4,6},{6,4},{8,10},{10,8},{12,14},{14,12},{1,3},{3,1},... | collective-permute-start | bytes 626696 | tf_op jit(solution)/shard_map/ppermute | solution.py:423
  (5 other events, 4.2 us)
Sparse Core Ops, SparseCore 0:
  8.9 24.5 all-gather.1

commit v5 on v4

--- a/solution.py
+++ b/solution.py
@@ -148,12 +148,10 @@
         return pair(self.refs["minor2"], head - 9, block)
 
     def near_first(self, head):
-        if head < 9:
-            return pair(self.refs["first1"], head - 3, 0)
-        return pair(self.refs["first2"], head - 9, 0)
+        return pair(self.refs["nearest"], head - 3, 0)
 
     def cross_first(self, head):
-        return pair(self.refs["first2"], CROSS + head, 0)
+        return pair(self.refs["nearest"], 9 + head, 0)
 
     def relay(self, head, block):
         if head < 9:
@@ -230,9 +228,10 @@
     out_stats[...] = attend_heads(group, blocks, problem, out)
 
 
-def project_kernel(own_groups, part_groups, *refs):
+def project_kernel(own_groups, part_groups, chunks, *refs):
     refs = list(refs)
-    weight = refs.pop(0)
+    weights = [refs.pop(0) for _ in range(chunks)]
+    sib_weights = [refs.pop(0) for _ in range(chunks)]
     owns = [(group, refs.pop(0), refs.pop(0)) for group in own_groups]
     parts = [(group, refs.pop(0)) for group in part_groups]
     out, attended = refs
@@ -262,10 +261,20 @@
             :, head : head + 1
         ] * part[:rows, head_cols(part_place)].astype(jnp.float32)
         attended[:, head_cols(head)] = mixed.astype(attended.dtype)
+    core = lax.axis_index("head")
+    chunk = weights[0].shape[0]
+    pieces = []
+    for index in range(chunks):
+        for weight, side in ((weights[index], core), (sib_weights[index], 1 - core)):
+            at = pl.multiple_of((side * chunks + index) * chunk, DH)
+            pieces.append((attended[:, pl.ds(at, chunk)], weight))
     for at in range(0, out.shape[1], TILE):
-        out[:, at : at + TILE] = jnp.dot(
-            attended[...], weight[:, at : at + TILE], preferred_element_type=jnp.float32
-        ).astype(out.dtype)
+        product = 0.0
+        for piece, weight in pieces:
+            product = product + jnp.dot(
+                piece, weight[:, at : at + TILE], preferred_element_type=jnp.float32
+            )
+        out[:, at : at + TILE] = product.astype(out.dtype)
 
 
 def whole(shape):
@@ -294,6 +303,7 @@
 
 
 def tie(before, *payloads):
+    before = tuple(before)
     anywhere = pl.BlockSpec(memory_space=pl.ANY)
     return pl.pallas_call(
         tie_kernel,
@@ -306,13 +316,13 @@
     )(*before, *payloads)
 
 
-def project(own_groups, part_groups, weight, operands):
-    rows = operands[0].shape[0]
-    depth, columns = weight.shape
+def project(own_groups, part_groups, weights, operands):
+    rows, columns = operands[0].shape[0], weights[0].shape[1]
+    depth = sum(weight.shape[0] for weight in weights)
     return pl.pallas_call(
-        functools.partial(project_kernel, own_groups, part_groups),
+        functools.partial(project_kernel, own_groups, part_groups, len(weights) // 2),
         grid=(1,),
-        in_specs=[whole(x.shape) for x in (weight, *operands)],
+        in_specs=[whole(x.shape) for x in (*weights, *operands)],
         out_specs=whole((rows, columns)),
         out_shape=jax.ShapeDtypeStruct((rows, columns), jnp.bfloat16),
         scratch_shapes=[pltpu.VMEM((rows, depth), jnp.bfloat16)],
@@ -321,7 +331,7 @@
             flops=2 * rows * depth * columns, bytes_accessed=12 * MIB, transcendentals=0
         ),
         name="merge_and_project",
-    )(weight, *operands)
+    )(*weights, *operands)
 
 
 def per_device(queries, key_tokens, value_tokens, radial_table, out_weight):
@@ -335,6 +345,7 @@
     partner_moves = moves(lambda f: f ^ 1)
     near_moves = moves(lambda f: f - 2 if f % 2 == 0 else f + 2)
     away_moves = moves(lambda f: f + 2 if f % 2 == 0 else f - 2)
+    cross_moves = moves(lambda f: f - 1 if f % 2 == 0 else f + 1)
     core_moves = [(c, cores - 1 - c) for c in range(cores)]
 
     def pack(first, last):
@@ -347,23 +358,24 @@
             axis=0,
         )
 
-    cross = lax.ppermute(pack(0, 3), "frame", partner_moves)
     major1 = lax.ppermute(pack(0, 6), "frame", away_moves)
     minor1 = lax.ppermute(pack(3, 9), "frame", near_moves)
     sib_keys = lax.ppermute(key_tokens, "head", core_moves)
     sib_values = lax.ppermute(value_tokens, "head", core_moves)
-    partner_query = lax.ppermute(queries, "frame", partner_moves)
-    all_weight = lax.all_gather(out_weight, "head", axis=0, tiled=True)
-    cross, to_minor2 = tie((sib_keys, sib_values), cross, pack(9, 12))
+    own_weight = [out_weight]
+    sib_weight = [lax.ppermute(out_weight, "head", core_moves)]
+    to_minor2, to_major2, to_partner = tie(
+        (sib_keys, sib_values, *sib_weight), pack(9, 12), pack(0, 3), queries
+    )
+    partner_query = lax.ppermute(to_partner, "frame", partner_moves)
     minor2 = lax.ppermute(to_minor2, "frame", near_moves)
-    major2 = lax.ppermute(cross, "frame", away_moves)
+    major2 = lax.ppermute(to_major2, "frame", cross_moves)
+    minor3 = lax.ppermute(minor1, "frame", near_moves)
     (to_major3,) = tie((major1,), pack(6, 12))
     major3 = lax.ppermute(to_major3, "frame", away_moves)
-    minor3 = lax.ppermute(minor1, "frame", near_moves)
-    first1 = lax.ppermute(firsts(minor1), "head", core_moves)
     major4 = lax.ppermute(major2, "frame", away_moves)
     minor4 = lax.ppermute(minor2, "frame", near_moves)
-    first2 = lax.ppermute(firsts(minor2, major2), "head", core_moves)
+    nearest = lax.ppermute(firsts(minor1, minor2, major2), "head", core_moves)
     refs = {
         "major1": major1,
         "major2": major2,
@@ -373,8 +385,7 @@
         "minor2": minor2,
         "minor3": minor3,
         "minor4": minor4,
-        "first1": first1,
-        "first2": first2,
+        "nearest": nearest,
     }
     local = (key_tokens, value_tokens, sib_keys, sib_values)
 
@@ -409,23 +420,23 @@
 
     own_groups = ((0, 3), (3, 6), (6, 12))
     part_groups = ((0, 3), (3, 9), (9, 12))
-    part_low = partner_part((0, 3), ("major1", "major2"), (all_weight[:16, :DH],))
+    part_low = partner_part((0, 3), ("major1", "major2"))
     own_early = own_part((3, 6), ("major1", "minor1"))
     part_middle = partner_part(
-        (3, 9), ("major1", "major3", "minor1", "minor3", "first1"), (part_low, own_early[1])
+        (3, 9), ("major1", "major3", "minor1", "minor3", "nearest"), (part_low, own_early[1])
     )
     part_low = lax.ppermute(part_low, "frame", partner_moves)
     part_middle = lax.ppermute(part_middle, "frame", partner_moves)
     own_late = own_part((6, 12), ("major3", "minor1", "minor2"))
     part_high = partner_part(
-        (9, 12), ("major3", "minor2", "minor4", "first2"), (own_late[1], major4, part_low)
+        (9, 12), ("major3", "minor2", "minor4", "nearest"), (own_late[1], major4, part_low, *sib_weight)
     )
     part_high = lax.ppermute(part_high, "frame", partner_moves)
-    own_low = own_part((0, 3), ("major1", "major2", "major4", "first2"))
+    own_low = own_part((0, 3), ("major1", "major2", "major4", "nearest"))
     return project(
         own_groups,
         part_groups,
-        all_weight,
+        (*own_weight, *sib_weight),
         (*own_low, *own_early, *own_late, part_low, part_middle, part_high),
     )
 

time: 97.9 us -> 99.9 us (1.020)
  starting transfers between devices: 32.3 us -> 54.4 us
  between operations: 13.7 us -> 0.31 us
  local copies, waits for them, and re-layouts: 8.8 us -> 1.66 us
  waiting for transfers between devices: 16 us -> 22.2 us
  Pallas kernels: 24.5 us -> 20.7 us
  other arithmetic: 1.93 us -> 0.3 us
    ppermute x1, starting transfers between devices: 4.64 us -> 27.8 us  [per_device(): major4 = lax.ppermute(major2, 'frame', away_moves)]
    ppermute x1, waiting for transfers between devices: 0.01 us -> 12.7 us  [per_device(): major1 = lax.ppermute(pack(0, 6), 'frame', away_moves)]
    ppermute x5 -> x4, waiting for transfers between devices: 8.92 us -> 0.01 us  [the longest x1 0.01 us: per_device(): major2 = lax.ppermute(to_major2, 'frame', cross_moves)]
    unnamed x38 -> x13, local copies, waits for them, and re-layouts: 5.83 us -> 0.09 us
    pallas_call x6, Pallas kernels: 19.4 us -> 15.5 us  [run(): pl.pallas_call(body, grid=(1,), in_specs=[pl.BlockSpec(memory_space=pltpu...]
    ppermute x1, waiting for transfers between devices: 3.67 us -> 6.2 us  [per_device(): part_high = lax.ppermute(part_high, 'frame', partner_moves)]
    slice x3, local copies, waits for them, and re-layouts: 2.03 us -> 0.07 us  [firsts(): p[at:at + BS]]
    ppermute x1, waiting for transfers between devices: 2.65 us -> 1 us  [per_device(): minor2 = lax.ppermute(to_minor2, 'frame', near_moves)]
  transfers between devices with their start and end apart: 18 -> 16, of which waited for: 3 -> 6; matrix products, arithmetic and copies ran while one was open for 5% -> 2% of each run, Pallas kernels for 20% -> 16%
where the time goes in v5:
time: 99.9 us; the launch traced here: 99.5 us
  starting transfers between devices  54.4 us (54%)
  waiting for transfers between devices  22.2 us (22%)
  Pallas kernels  20.7 us (21%)
  local copies, waits for them, and re-layouts  1.66 us (2%)
    ppermute x1, starting transfers between devices, per_device(): major4 = lax.ppermute(major2, 'frame', away_moves)  27.8 us
    pallas_call x6, Pallas kernels, run(): pl.pallas_call(body, grid=(1,), in_specs=[pl.BlockSpec(memory_space=pltpu...  15.5 us
    ppermute x1, waiting for transfers between devices, per_device(): major1 = lax.ppermute(pack(0, 6), 'frame', away_moves)  12.7 us
    ppermute x1, waiting for transfers between devices, per_device(): part_high = lax.ppermute(part_high, 'frame', partner_moves)  6.2 us
    ppermute x1, starting transfers between devices, per_device(): partner_query = lax.ppermute(to_partner, 'frame', partner_moves)  5.39 us
    pallas_call x1, Pallas kernels, project(): pl.pallas_call(functools.partial(project_kernel, own_groups, part_groups,...  5.23 us
    ppermute x1, starting transfers between devices, per_device(): major1 = lax.ppermute(pack(0, 6), 'frame', away_moves)  4.72 us
    ppermute x1, starting transfers between devices, per_device(): major3 = lax.ppermute(to_major3, 'frame', away_moves)  4.42 us
  transfers between devices with their start and end apart: 16, of which 6 were waited for; matrix products, arithmetic and copies ran while one was open for 2% of the time, Pallas kernels for 16%

profile of v5, /device:TPU:0, one launch (start us, length us, event | category | flops | bytes accessed | tf_op | source)
XLA Modules:
  0.0 99.5 jit_solution(17230874125832630970)
XLA Ops:
  0.0 0.5 collective-permute-start
  0.5 0.1 collective-permute-start.1
  0.5 0.4 collective-permute-start.2
  1.0 1.3 %fusion = (bf16[256,768]{1,0:T(8,128)(2,1)S(1)}, bf16[256,768]{1,0:T(8,128)(2,1)S(1)}, bf16[256,768]{1,0:T(8,128)(2,1)S(1)}) fusion(bf16[256,1536]{1,0:T(8,128)(2,1)} %keys.11), kind=kLoop, calls=%fused_computation.6 | loop fusion | bytes 2359296 | tf_op jit(solution)/shard_map/slice | solution.py:353
  2.3 0.1 fusion.1
  2.5 4.7 %collective-permute-start.3 = (bf16[512,768]{1,0:T(8,128)(2,1)S(1)}, bf16[512,768]{1,0:T(8,128)(2,1)S(1)}, u32[]{:S(2)}, u32[]{:S(2)}) collective-permute-start(bf16[512,768]{1,0:T(8,128)(2,1)S(1)} %pad_maximum_fusion), channel_id=1, source_target_pairs={{0,4},{4,8},{6,2},{8,12},{10,6},{14,10},{1,5},{5,9},{7,3},{9,13},{... | collective-permute-start | bytes 2359304 | tf_op jit(solution)/shard_map/ppermute | solution.py:361
  7.3 1.4 %collective-permute-start.6 = (bf16[512,768]{1,0:T(8,128)(2,1)S(1)}, bf16[512,768]{1,0:T(8,128)(2,1)S(1)}, u32[]{:S(2)}, u32[]{:S(2)}) collective-permute-start(bf16[512,768]{1,0:T(8,128)(2,1)S(1)} %pad_maximum_fusion.1), channel_id=1, source_target_pairs={{2,6},{4,0},{6,10},{8,4},{10,14},{12,8},{3,7},{5,1},{7,11},{9,5},{... | collective-permute-start | bytes 2359304 | tf_op jit(solution)/shard_map/ppermute | solution.py:362
  8.9 0.1 pad_maximum_fusion.3
  9.0 0.3 collective-permute-done.1.refs_0_.sib_keys
  9.3 1.1 %collective-permute-done.2.refs_1_.sib_values = bf16[256,1536]{1,0:T(8,128)(2,1)S(1)} collective-permute-done((bf16[256,1536]{1,0:T(8,128)(2,1)}, bf16[256,1536]{1,0:T(8,128)(2,1)S(1)}, u32[]{:S(2)}, u32[]{:S(2)}) %collective-permute-start.2) | collective-permute-done | bytes 786464 | tf_op jit(solution)/shard_map/ppermute | solution.py:364
  10.5 1.3 %collective-permute-start.7 = (bf16[512,384]{1,0:T(8,128)(2,1)S(1)}, bf16[512,384]{1,0:T(8,128)(2,1)S(1)}, u32[]{:S(2)}, u32[]{:S(2)}) collective-permute-start(bf16[512,384]{1,0:T(8,128)(2,1)S(1)} %get-tuple-element.15), channel_id=1, source_target_pairs={{2,6},{4,0},{6,10},{8,4},{10,14},{12,8},{3,7},{5,1},{7,11},{9,5},{... | collective-permute-start | bytes 1179656 | tf_op jit(solution)/shard_map/ppermute | solution.py:371
  11.8 12.7 %collective-permute-done.3.rest_0_.refs_0_ = bf16[512,768]{1,0:T(8,128)(2,1)S(1)} collective-permute-done((bf16[512,768]{1,0:T(8,128)(2,1)S(1)}, bf16[512,768]{1,0:T(8,128)(2,1)S(1)}, u32[]{:S(2)}, u32[]{:S(2)}) %collective-permute-start.3) | collective-permute-done | bytes 786464 | tf_op jit(solution)/shard_map/ppermute | solution.py:361
  24.5 4.4 %collective-permute-start.9 = (bf16[512,768]{1,0:T(8,128)(2,1)S(1)}, bf16[512,768]{1,0:T(8,128)(2,1)S(1)}, u32[]{:S(2)}, u32[]{:S(2)}) collective-permute-start(bf16[512,768]{1,0:T(8,128)(2,1)S(1)} %tie.3), channel_id=1, source_target_pairs={{0,4},{4,8},{6,2},{8,12},{10,6},{14,10},{1,5},{5,9},{7,3},{9,13},{... | collective-permute-start | bytes 2359304 | tf_op jit(solution)/shard_map/ppermute | solution.py:375
  29.0 0.7 collective-permute-done.6.rest_1_.rest_2_
  29.7 1.3 %collective-permute-start.12 = (bf16[512,768]{1,0:T(8,128)(2,1)S(1)}, bf16[512,768]{1,0:T(8,128)(2,1)S(1)}, u32[]{:S(2)}, u32[]{:S(2)}) collective-permute-start(bf16[512,768]{1,0:T(8,128)(2,1)S(1)} %collective-permute-done.6.rest_1_.rest_2_), channel_id=1, source_target_pairs={{2,6},{4,0},{6,10},{8,4},{10,14},{12,8},{3,7},{5,1},{7,11},{9,5},{... | collective-permute-start | bytes 2359304 | tf_op jit(solution)/shard_map/ppermute | solution.py:373
  31.0 0.7 collective-permute-start.4
  31.7 5.4 %collective-permute-start.10 = (bf16[256,1536]{1,0:T(8,128)(2,1)S(1)}, bf16[256,1536]{1,0:T(8,128)(2,1)S(1)}, u32[]{:S(2)}, u32[]{:S(2)}) collective-permute-start(bf16[256,1536]{1,0:T(8,128)(2,1)S(1)} %get-tuple-element.22), channel_id=1, source_target_pairs={{0,2},{2,0},{4,6},{6,4},{8,10},{10,8},{12,14},{14,12},{1,3},{3,1},... | collective-permute-start | bytes 2359304 | tf_op jit(solution)/shard_map/ppermute | solution.py:370
  37.1 1.0 %collective-permute-done.7.rest_2_.rest_1_ = bf16[512,384]{1,0:T(8,128)(2,1)S(1)} collective-permute-done((bf16[512,384]{1,0:T(8,128)(2,1)S(1)}, bf16[512,384]{1,0:T(8,128)(2,1)S(1)}, u32[]{:S(2)}, u32[]{:S(2)}) %collective-permute-start.7) | collective-permute-done | bytes 393248 | tf_op jit(solution)/shard_map/ppermute | solution.py:371
  38.2 0.1 collective-permute-start.8
  38.3 27.8 %collective-permute-start.5 = (bf16[512,384]{1,0:T(8,128)(2,1)S(1)}, bf16[512,384]{1,0:T(8,128)(2,1)S(1)}, u32[]{:S(2)}, u32[]{:S(2)}) collective-permute-start(bf16[512,384]{1,0:T(8,128)(2,1)S(1)} %collective-permute-done.4.rest_1_), channel_id=1, source_target_pairs={{0,4},{4,8},{6,2},{8,12},{10,6},{14,10},{1,5},{5,9},{7,3},{9,13},{... | collective-permute-start | bytes 1179656 | tf_op jit(solution)/shard_map/ppermute | solution.py:376
  66.1 1.5 %collective-permute-start.14 = (bf16[512,384]{1,0:T(8,128)(2,1)S(1)}, bf16[512,384]{1,0:T(8,128)(2,1)S(1)}, u32[]{:S(2)}, u32[]{:S(2)}) collective-permute-start(bf16[512,384]{1,0:T(8,128)(2,1)S(1)} %collective-permute-done.7.rest_2_.rest_1_), channel_id=1, source_target_pairs={{2,6},{4,0},{6,10},{8,4},{10,14},{12,8},{3,7},{5,1},{7,11},{9,5},{... | collective-permute-start | bytes 1179656 | tf_op jit(solution)/shard_map/ppermute | solution.py:377
  67.6 1.9 %own_part.4 = (f32[256,384]{1,0:T(8,128)S(1)}, f32[256,128]{1,0:T(8,128)S(1)}) custom-call(s32[8,8]{1,0:T(8,128)S(1)} %copy-done.3, bf16[256,1536]{1,0:T(8,128)(2,1)S(1)} %copy-done.2, bf16[256,1536]{1,0:T(8,128)(2,1)S(1)} %copy-done, bf16[256,1536]{1,0:T(8,128)(2,1)S(1)} %copy-done.1, bf16[256,1536]{1,0:T(8,128)(2,1)S(1)} %collective-permute-done.1.refs_0_.sib_keys, ...), custom_call_target="tpu_custom_call" | custom-call | flops 301989888 | bytes 1048576 | tf_op jit(solution)/shard_map/own_part/pallas_call | solution.py:285
  69.5 2.0 %partner_part.3.rest_5_ = bf16[272,384]{1,0:T(8,128)(2,1)S(1)} custom-call(s32[8,8]{1,0:T(8,128)S(1)} %copy-done.3, bf16[256,1536]{1,0:T(8,128)(2,1)S(1)} %collective-permute-done.10.query, bf16[256,1536]{1,0:T(8,128)(2,1)S(1)} %copy-done, bf16[256,1536]{1,0:T(8,128)(2,1)S(1)} %copy-done.1, bf16[256,1536]{1,0:T(8,128)(2,1)S(1)} %collective-permute-done.1.refs_0_.sib_keys, ...), custom_call_target="tpu_custom_call" | custom-call | flops 301989888 | bytes 1048576 | tf_op jit(solution)/shard_map/partner_part/pallas_call | solution.py:285
  71.6 2.8 %collective-permute-start.11 = (bf16[272,384]{1,0:T(8,128)(2,1)S(1)}, bf16[272,384]{1,0:T(8,128)(2,1)S(1)}, u32[]{:S(2)}, u32[]{:S(2)}) collective-permute-start(bf16[272,384]{1,0:T(8,128)(2,1)S(1)} %partner_part.3.rest_5_), channel_id=1, source_target_pairs={{0,2},{2,0},{4,6},{6,4},{8,10},{10,8},{12,14},{14,12},{1,3},{3,1},... | collective-permute-start | bytes 626696 | tf_op jit(solution)/shard_map/ppermute | solution.py:428
  74.4 3.7 %partner_part.4 = bf16[288,768]{1,0:T(8,128)(2,1)S(1)} custom-call(s32[8,8]{1,0:T(8,128)S(1)} %copy-done.3, bf16[256,1536]{1,0:T(8,128)(2,1)S(1)} %collective-permute-done.10.query, bf16[256,1536]{1,0:T(8,128)(2,1)S(1)} %copy-done, bf16[256,1536]{1,0:T(8,128)(2,1)S(1)} %copy-done.1, bf16[256,1536]{1,0:T(8,128)(2,1)S(1)} %collective-permute-done.1.refs_0_.sib_keys, ...), custom_call_target="tpu_custom_call" | custom-call | flops 603979776 | bytes 1048576 | tf_op jit(solution)/shard_map/partner_part/pallas_call | solution.py:285
  78.1 0.1 collective-permute-start.13
  78.1 3.0 %own_part.5 = (f32[256,768]{1,0:T(8,128)S(1)}, f32[256,128]{1,0:T(8,128)S(1)}) custom-call(s32[8,8]{1,0:T(8,128)S(1)} %copy-done.3, bf16[256,1536]{1,0:T(8,128)(2,1)S(1)} %copy-done.2, bf16[256,1536]{1,0:T(8,128)(2,1)S(1)} %copy-done, bf16[256,1536]{1,0:T(8,128)(2,1)S(1)} %copy-done.1, bf16[256,1536]{1,0:T(8,128)(2,1)S(1)} %collective-permute-done.1.refs_0_.sib_keys, ...), custom_call_target="tpu_custom_call" | custom-call | flops 603979776 | bytes 1048576 | tf_op jit(solution)/shard_map/own_part/pallas_call | solution.py:285
  81.2 2.5 %partner_part.5 = bf16[272,384]{1,0:T(8,128)(2,1)S(1)} custom-call(s32[8,8]{1,0:T(8,128)S(1)} %copy-done.3, bf16[256,1536]{1,0:T(8,128)(2,1)S(1)} %collective-permute-done.10.query, bf16[256,1536]{1,0:T(8,128)(2,1)S(1)} %copy-done, bf16[256,1536]{1,0:T(8,128)(2,1)S(1)} %copy-done.1, bf16[256,1536]{1,0:T(8,128)(2,1)S(1)} %collective-permute-done.1.refs_0_.sib_keys, ...), custom_call_target="tpu_custom_call" | custom-call | flops 301989888 | bytes 1048576 | tf_op jit(solution)/shard_map/partner_part/pallas_call | solution.py:285
  83.6 2.0 %collective-permute-start.15 = (bf16[272,384]{1,0:T(8,128)(2,1)S(1)}, bf16[272,384]{1,0:T(8,128)(2,1)S(1)}, u32[]{:S(2)}, u32[]{:S(2)}) collective-permute-start(bf16[272,384]{1,0:T(8,128)(2,1)S(1)} %partner_part.5), channel_id=1, source_target_pairs={{0,2},{2,0},{4,6},{6,4},{8,10},{10,8},{12,14},{14,12},{1,3},{3,1},... | collective-permute-start | bytes 626696 | tf_op jit(solution)/shard_map/ppermute | solution.py:434
  85.7 2.4 %own_part.3 = (f32[256,384]{1,0:T(8,128)S(1)}, f32[256,128]{1,0:T(8,128)S(1)}) custom-call(s32[8,8]{1,0:T(8,128)S(1)} %copy-done.3, bf16[256,1536]{1,0:T(8,128)(2,1)S(1)} %copy-done.2, bf16[256,1536]{1,0:T(8,128)(2,1)S(1)} %copy-done, bf16[256,1536]{1,0:T(8,128)(2,1)S(1)} %copy-done.1, bf16[256,1536]{1,0:T(8,128)(2,1)S(1)} %collective-permute-done.1.refs_0_.sib_keys, ...), custom_call_target="tpu_custom_call" | custom-call | flops 301989888 | bytes 1048576 | tf_op jit(solution)/shard_map/own_part/pallas_call | solution.py:285
  88.1 6.2 %collective-permute-done.15.refs_10_ = bf16[272,384]{1,0:T(8,128)(2,1)S(1)} collective-permute-done((bf16[272,384]{1,0:T(8,128)(2,1)S(1)}, bf16[272,384]{1,0:T(8,128)(2,1)S(1)}, u32[]{:S(2)}, u32[]{:S(2)}) %collective-permute-start.15) | collective-permute-done | bytes 208928 | tf_op jit(solution)/shard_map/ppermute | solution.py:434
  94.3 5.2 %merge_and_project.1 = bf16[256,3072]{1,0:T(8,128)(2,1)} custom-call(bf16[768,3072]{1,0:T(8,128)(2,1)S(1)} %bitcast.1, bf16[768,3072]{1,0:T(8,128)(2,1)S(1)} %collective-permute-done.refs_2_.rest_7_.refs_1_, f32[256,384]{1,0:T(8,128)S(1)} %get-tuple-element.16.refs_2_, f32[256,128]{1,0:T(8,128)S(1)} %get-tuple-element.17.refs_3_, ...), custom_call_target="tpu_custom_call" | custom-call | flops 2415919104 | bytes 12582912 | tf_op jit(solution)/shard_map/merge_and_project/pallas_call | solution.py:322
  (35 shorter events, 0.5 us)
Async XLA Ops:
  0.0 2.3 %copy-start.1 = (bf16[256,1536]{1,0:T(8,128)(2,1)S(1)}, bf16[256,1536]{1,0:T(8,128)(2,1)}, u32[]{:S(2)}) copy-start(bf16[256,1536]{1,0:T(8,128)(2,1)} %values.11) | copy-start | bytes 2359300
  0.0 10.5 %collective-permute-start = (bf16[768,3072]{1,0:T(8,128)(2,1)}, bf16[768,3072]{1,0:T(8,128)(2,1)S(1)}, u32[]{:S(2)}, u32[]{:S(2)}) collective-permute-start(bf16[768,3072]{1,0:T(8,128)(2,1)} %refs_0_.1), channel_id=1, source_target_pairs={{0,1},{1,0},{2,3},{3,2},{4,5},{5,4},{6,7},{7,6},{8,9},{9,8},{10,11... | collective-permute-start | bytes 14155784 | tf_op jit(solution)/shard_map/ppermute | solution.py:366
  0.5 8.9 %collective-permute-start.1 = (bf16[256,1536]{1,0:T(8,128)(2,1)}, bf16[256,1536]{1,0:T(8,128)(2,1)S(1)}, u32[]{:S(2)}, u32[]{:S(2)}) collective-permute-start(bf16[256,1536]{1,0:T(8,128)(2,1)} %keys.11), channel_id=1, source_target_pairs={{0,1},{1,0},{2,3},{3,2},{4,5},{5,4},{6,7},{7,6},{8,9},{9,8},{10,11... | collective-permute-start | bytes 2359304 | tf_op jit(solution)/shard_map/ppermute | solution.py:363
  0.5 9.9 %collective-permute-start.2 = (bf16[256,1536]{1,0:T(8,128)(2,1)}, bf16[256,1536]{1,0:T(8,128)(2,1)S(1)}, u32[]{:S(2)}, u32[]{:S(2)}) collective-permute-start(bf16[256,1536]{1,0:T(8,128)(2,1)} %values.11), channel_id=1, source_target_pairs={{0,1},{1,0},{2,3},{3,2},{4,5},{5,4},{6,7},{7,6},{8,9},{9,8},{10,11... | collective-permute-start | bytes 2359304 | tf_op jit(solution)/shard_map/ppermute | solution.py:364
  2.4 6.3 %copy-start.2 = (bf16[256,1536]{1,0:T(8,128)(2,1)S(1)}, bf16[256,1536]{1,0:T(8,128)(2,1)}, u32[]{:S(2)}) copy-start(bf16[256,1536]{1,0:T(8,128)(2,1)} %query.5) | copy-start | bytes 2359300
  2.5 22.1 %collective-permute-start.3 = (bf16[512,768]{1,0:T(8,128)(2,1)S(1)}, bf16[512,768]{1,0:T(8,128)(2,1)S(1)}, u32[]{:S(2)}, u32[]{:S(2)}) collective-permute-start(bf16[512,768]{1,0:T(8,128)(2,1)S(1)} %pad_maximum_fusion), channel_id=1, source_target_pairs={{0,4},{4,8},{6,2},{8,12},{10,6},{14,10},{1,5},{5,9},{7,3},{9,13},{... | collective-permute-start | bytes 2359304 | tf_op jit(solution)/shard_map/ppermute | solution.py:361
  7.2 1.6 %copy-start = (bf16[256,1536]{1,0:T(8,128)(2,1)S(1)}, bf16[256,1536]{1,0:T(8,128)(2,1)}, u32[]{:S(2)}) copy-start(bf16[256,1536]{1,0:T(8,128)(2,1)} %keys.11) | copy-start | bytes 2359300
  7.3 22.4 %collective-permute-start.6 = (bf16[512,768]{1,0:T(8,128)(2,1)S(1)}, bf16[512,768]{1,0:T(8,128)(2,1)S(1)}, u32[]{:S(2)}, u32[]{:S(2)}) collective-permute-start(bf16[512,768]{1,0:T(8,128)(2,1)S(1)} %pad_maximum_fusion.1), channel_id=1, source_target_pairs={{2,6},{4,0},{6,10},{8,4},{10,14},{12,8},{3,7},{5,1},{7,11},{9,5},{... | collective-permute-start | bytes 2359304 | tf_op jit(solution)/shard_map/ppermute | solution.py:362
  10.5 27.7 %collective-permute-start.7 = (bf16[512,384]{1,0:T(8,128)(2,1)S(1)}, bf16[512,384]{1,0:T(8,128)(2,1)S(1)}, u32[]{:S(2)}, u32[]{:S(2)}) collective-permute-start(bf16[512,384]{1,0:T(8,128)(2,1)S(1)} %get-tuple-element.15), channel_id=1, source_target_pairs={{2,6},{4,0},{6,10},{8,4},{10,14},{12,8},{3,7},{5,1},{7,11},{9,5},{... | collective-permute-start | bytes 1179656 | tf_op jit(solution)/shard_map/ppermute | solution.py:371
  24.5 47.0 %collective-permute-start.9 = (bf16[512,768]{1,0:T(8,128)(2,1)S(1)}, bf16[512,768]{1,0:T(8,128)(2,1)S(1)}, u32[]{:S(2)}, u32[]{:S(2)}) collective-permute-start(bf16[512,768]{1,0:T(8,128)(2,1)S(1)} %tie.3), channel_id=1, source_target_pairs={{0,4},{4,8},{6,2},{8,12},{10,6},{14,10},{1,5},{5,9},{7,3},{9,13},{... | collective-permute-start | bytes 2359304 | tf_op jit(solution)/shard_map/ppermute | solution.py:375
  29.7 44.7 %collective-permute-start.12 = (bf16[512,768]{1,0:T(8,128)(2,1)S(1)}, bf16[512,768]{1,0:T(8,128)(2,1)S(1)}, u32[]{:S(2)}, u32[]{:S(2)}) collective-permute-start(bf16[512,768]{1,0:T(8,128)(2,1)S(1)} %collective-permute-done.6.rest_1_.rest_2_), channel_id=1, source_target_pairs={{2,6},{4,0},{6,10},{8,4},{10,14},{12,8},{3,7},{5,1},{7,11},{9,5},{... | collective-permute-start | bytes 2359304 | tf_op jit(solution)/shard_map/ppermute | solution.py:373
  31.0 36.6 %copy-start.3 = (s32[8,8]{1,0:T(8,128)S(1)}, s32[8,8]{1,0:T(8,128)}, u32[]{:S(2)}) copy-start(s32[8,8]{1,0:T(8,128)} %table_ref.11) | copy-start | bytes 772
  31.0 7.2 %collective-permute-start.4 = (bf16[512,384]{1,0:T(8,128)(2,1)S(1)}, bf16[512,384]{1,0:T(8,128)(2,1)S(1)}, u32[]{:S(2)}, u32[]{:S(2)}) collective-permute-start(bf16[512,384]{1,0:T(8,128)(2,1)S(1)} %get-tuple-element.14), channel_id=1, source_target_pairs={{2,4},{4,2},{6,8},{8,6},{10,12},{12,10},{3,5},{5,3},{7,9},{9,7},{1... | collective-permute-start | bytes 1179656 | tf_op jit(solution)/shard_map/ppermute | solution.py:372
  31.7 34.4 %collective-permute-start.10 = (bf16[256,1536]{1,0:T(8,128)(2,1)S(1)}, bf16[256,1536]{1,0:T(8,128)(2,1)S(1)}, u32[]{:S(2)}, u32[]{:S(2)}) collective-permute-start(bf16[256,1536]{1,0:T(8,128)(2,1)S(1)} %get-tuple-element.22), channel_id=1, source_target_pairs={{0,2},{2,0},{4,6},{6,4},{8,10},{10,8},{12,14},{14,12},{1,3},{3,1},... | collective-permute-start | bytes 2359304 | tf_op jit(solution)/shard_map/ppermute | solution.py:370
  38.2 36.1 %collective-permute-start.8 = (bf16[256,1536]{1,0:T(8,128)(2,1)S(1)}, bf16[256,1536]{1,0:T(8,128)(2,1)S(1)}, u32[]{:S(2)}, u32[]{:S(2)}) collective-permute-start(bf16[256,1536]{1,0:T(8,128)(2,1)S(1)} %maximum_maximum_fusion), channel_id=1, source_target_pairs={{0,1},{1,0},{2,3},{3,2},{4,5},{5,4},{6,7},{7,6},{8,9},{9,8},{10,11... | collective-permute-start | bytes 2359304 | tf_op jit(solution)/shard_map/ppermute | solution.py:378
  38.3 42.8 %collective-permute-start.5 = (bf16[512,384]{1,0:T(8,128)(2,1)S(1)}, bf16[512,384]{1,0:T(8,128)(2,1)S(1)}, u32[]{:S(2)}, u32[]{:S(2)}) collective-permute-start(bf16[512,384]{1,0:T(8,128)(2,1)S(1)} %collective-permute-done.4.rest_1_), channel_id=1, source_target_pairs={{0,4},{4,8},{6,2},{8,12},{10,6},{14,10},{1,5},{5,9},{7,3},{9,13},{... | collective-permute-start | bytes 1179656 | tf_op jit(solution)/shard_map/ppermute | solution.py:376
  66.1 15.0 %collective-permute-start.14 = (bf16[512,384]{1,0:T(8,128)(2,1)S(1)}, bf16[512,384]{1,0:T(8,128)(2,1)S(1)}, u32[]{:S(2)}, u32[]{:S(2)}) collective-permute-start(bf16[512,384]{1,0:T(8,128)(2,1)S(1)} %collective-permute-done.7.rest_2_.rest_1_), channel_id=1, source_target_pairs={{2,6},{4,0},{6,10},{8,4},{10,14},{12,8},{3,7},{5,1},{7,11},{9,5},{... | collective-permute-start | bytes 1179656 | tf_op jit(solution)/shard_map/ppermute | solution.py:377
  71.6 9.6 %collective-permute-start.11 = (bf16[272,384]{1,0:T(8,128)(2,1)S(1)}, bf16[272,384]{1,0:T(8,128)(2,1)S(1)}, u32[]{:S(2)}, u32[]{:S(2)}) collective-permute-start(bf16[272,384]{1,0:T(8,128)(2,1)S(1)} %partner_part.3.rest_5_), channel_id=1, source_target_pairs={{0,2},{2,0},{4,6},{6,4},{8,10},{10,8},{12,14},{14,12},{1,3},{3,1},... | collective-permute-start | bytes 626696 | tf_op jit(solution)/shard_map/ppermute | solution.py:428
  78.1 16.2 %collective-permute-start.13 = (bf16[288,768]{1,0:T(8,128)(2,1)S(1)}, bf16[288,768]{1,0:T(8,128)(2,1)S(1)}, u32[]{:S(2)}, u32[]{:S(2)}) collective-permute-start(bf16[288,768]{1,0:T(8,128)(2,1)S(1)} %partner_part.4), channel_id=1, source_target_pairs={{0,2},{2,0},{4,6},{6,4},{8,10},{10,8},{12,14},{14,12},{1,3},{3,1},... | collective-permute-start | bytes 1327112 | tf_op jit(solution)/shard_map/ppermute | solution.py:429
  81.1 13.2 %slice-start = ((s8[4718592]{0:T(1024)(128)(4,1)}), s8[4194304]{0:T(1024)(128)(4,1)S(1)}, s32[]{:S(2)}) async-start(s8[4718592]{0:T(1024)(128)(4,1)} %bitcast), calls=%async_computation | async-start | bytes 8388608
  81.2 13.1 %slice-start.1 = ((s8[4718592]{0:T(1024)(128)(4,1)}), s8[524288]{0:T(1024)(128)(4,1)S(1)}, s32[]{:S(2)}) async-start(s8[4718592]{0:T(1024)(128)(4,1)} %bitcast), calls=%async_computation.1 | async-start | bytes 1048576
  83.6 10.7 %collective-permute-start.15 = (bf16[272,384]{1,0:T(8,128)(2,1)S(1)}, bf16[272,384]{1,0:T(8,128)(2,1)S(1)}, u32[]{:S(2)}, u32[]{:S(2)}) collective-permute-start(bf16[272,384]{1,0:T(8,128)(2,1)S(1)} %partner_part.5), channel_id=1, source_target_pairs={{0,2},{2,0},{4,6},{6,4},{8,10},{10,8},{12,14},{14,12},{1,3},{3,1},... | collective-permute-start | bytes 626696 | tf_op jit(solution)/shard_map/ppermute | solution.py:434

commit v6 on v5

--- a/solution.py
+++ b/solution.py
@@ -358,24 +358,26 @@
             axis=0,
         )
 
+    sib_keys = lax.ppermute(key_tokens, "head", core_moves)
+    sib_values = lax.ppermute(value_tokens, "head", core_moves)
     major1 = lax.ppermute(pack(0, 6), "frame", away_moves)
     minor1 = lax.ppermute(pack(3, 9), "frame", near_moves)
-    sib_keys = lax.ppermute(key_tokens, "head", core_moves)
-    sib_values = lax.ppermute(value_tokens, "head", core_moves)
-    own_weight = [out_weight]
-    sib_weight = [lax.ppermute(out_weight, "head", core_moves)]
-    to_minor2, to_major2, to_partner = tie(
-        (sib_keys, sib_values, *sib_weight), pack(9, 12), pack(0, 3), queries
-    )
+    to_minor2, to_major2, to_sib = tie(
+        (sib_keys, sib_values), pack(9, 12), pack(0, 3), out_weight
+    )
+    own_weight = [to_sib]
+    sib_weight = [lax.ppermute(to_sib, "head", core_moves)]
+    (to_partner,) = tie(sib_weight, queries)
     partner_query = lax.ppermute(to_partner, "frame", partner_moves)
     minor2 = lax.ppermute(to_minor2, "frame", near_moves)
     major2 = lax.ppermute(to_major2, "frame", cross_moves)
     minor3 = lax.ppermute(minor1, "frame", near_moves)
-    (to_major3,) = tie((major1,), pack(6, 12))
+    (to_major3,) = tie((major2,), pack(6, 12))
     major3 = lax.ppermute(to_major3, "frame", away_moves)
     major4 = lax.ppermute(major2, "frame", away_moves)
     minor4 = lax.ppermute(minor2, "frame", near_moves)
-    nearest = lax.ppermute(firsts(minor1, minor2, major2), "head", core_moves)
+    (to_nearest,) = tie((partner_query,), firsts(minor1, minor2, major2))
+    nearest = lax.ppermute(to_nearest, "head", core_moves)
     refs = {
         "major1": major1,
         "major2": major2,

time: 99.9 us -> 89.6 us (0.90)
  starting transfers between devices: 54.4 us -> 37.9 us
  waiting for transfers between devices: 22.2 us -> 27.6 us
  local copies, waits for them, and re-layouts: 1.66 us -> 2.94 us
    ppermute x1, starting transfers between devices: 27.8 us -> 4.69 us  [per_device(): major4 = lax.ppermute(major2, 'frame', away_moves)]
    ppermute x1, waiting for transfers between devices: 12.7 us -> 0.01 us  [per_device(): major1 = lax.ppermute(pack(0, 6), 'frame', away_moves)]
    ppermute x1, waiting for transfers between devices: 0.71 us -> 8.71 us  [per_device(): minor1 = lax.ppermute(pack(3, 9), 'frame', near_moves)]
    ppermute x1, starting transfers between devices: 4.42 us -> 12 us  [per_device(): major3 = lax.ppermute(to_major3, 'frame', away_moves)]
    ppermute x1, waiting for transfers between devices: 0.01 us -> 6.57 us  [per_device(): minor3 = lax.ppermute(minor1, 'frame', near_moves)]
    ppermute x1, starting transfers between devices: 4.72 us -> 9.54 us  [per_device(): major1 = lax.ppermute(pack(0, 6), 'frame', away_moves)]
    ppermute x1, starting transfers between devices: 5.39 us -> 1.23 us  [per_device(): partner_query = lax.ppermute(to_partner, 'frame', partner_moves)]
    unnamed x13 -> x10, local copies, waits for them, and re-layouts: 0.09 us -> 2.62 us
  transfers between devices with their start and end apart: 16 -> 16, of which waited for: 6 -> 6; matrix products, arithmetic and copies ran while one was open for 2% -> 1% of each run, Pallas kernels for 16% -> 17%
where the time goes in v6:
time: 89.6 us; the launch traced here: 89.3 us
  starting transfers between devices  37.9 us (42%)
  waiting for transfers between devices  27.6 us (31%)
  Pallas kernels  20.3 us (23%)
  local copies, waits for them, and re-layouts  2.94 us (3%)
    pallas_call x6, Pallas kernels, run(): pl.pallas_call(body, grid=(1,), in_specs=[pl.BlockSpec(memory_space=pltpu...  15.1 us
    ppermute x1, starting transfers between devices, per_device(): major3 = lax.ppermute(to_major3, 'frame', away_moves)  12 us
    ppermute x1, starting transfers between devices, per_device(): major1 = lax.ppermute(pack(0, 6), 'frame', away_moves)  9.54 us
    ppermute x1, waiting for transfers between devices, per_device(): minor1 = lax.ppermute(pack(3, 9), 'frame', near_moves)  8.71 us
    ppermute x1, waiting for transfers between devices, per_device(): minor3 = lax.ppermute(minor1, 'frame', near_moves)  6.57 us
    ppermute x1, waiting for transfers between devices, per_device(): part_high = lax.ppermute(part_high, 'frame', partner_moves)  6.12 us
    pallas_call x1, Pallas kernels, project(): pl.pallas_call(functools.partial(project_kernel, own_groups, part_groups,...  5.22 us
    ppermute x1, starting transfers between devices, per_device(): major4 = lax.ppermute(major2, 'frame', away_moves)  4.69 us
  transfers between devices with their start and end apart: 16, of which 6 were waited for; matrix products, arithmetic and copies ran while one was open for 1% of the time, Pallas kernels for 17%

profile of v6, /device:TPU:0, one launch (start us, length us, event | category | flops | bytes accessed | tf_op | source)
XLA Modules:
  0.0 89.3 jit_solution(4081224368409755579)
XLA Ops:
  0.0 2.5 %copy.19.refs_4_ = bf16[768,3072]{1,0:T(8,128)(2,1)S(1)} copy(bf16[768,3072]{1,0:T(8,128)(2,1)} %param.9) | data formatting | bytes 9437184
  2.5 0.1 copy-done
  2.6 0.5 collective-permute-start
  3.0 0.2 collective-permute-start.1
  3.4 1.5 %collective-permute-done.refs_0_.sib_keys = bf16[256,1536]{1,0:T(8,128)(2,1)S(1)} collective-permute-done((bf16[256,1536]{1,0:T(8,128)(2,1)S(1)}, bf16[256,1536]{1,0:T(8,128)(2,1)S(1)}, u32[]{:S(2)}, u32[]{:S(2)}) %collective-permute-start) | collective-permute-done | bytes 786464 | tf_op jit(solution)/shard_map/ppermute | solution.py:361
  4.9 1.1 %collective-permute-done.1.refs_1_.sib_values = bf16[256,1536]{1,0:T(8,128)(2,1)S(1)} collective-permute-done((bf16[256,1536]{1,0:T(8,128)(2,1)S(1)}, bf16[256,1536]{1,0:T(8,128)(2,1)S(1)}, u32[]{:S(2)}, u32[]{:S(2)}) %collective-permute-start.1) | collective-permute-done | bytes 786464 | tf_op jit(solution)/shard_map/ppermute | solution.py:362
  6.0 0.4 collective-permute-start.2
  6.4 0.1 fusion
  6.5 0.1 fusion.1
  6.7 1.4 %collective-permute-start.7 = (bf16[512,768]{1,0:T(8,128)(2,1)S(1)}, bf16[512,768]{1,0:T(8,128)(2,1)S(1)}, u32[]{:S(2)}, u32[]{:S(2)}) collective-permute-start(bf16[512,768]{1,0:T(8,128)(2,1)S(1)} %pad_maximum_fusion.1), channel_id=1, source_target_pairs={{2,6},{4,0},{6,10},{8,4},{10,14},{12,8},{3,7},{5,1},{7,11},{9,5},{... | collective-permute-start | bytes 2359304 | tf_op jit(solution)/shard_map/ppermute | solution.py:364
  8.1 0.7 collective-permute-start.4
  8.9 9.5 %collective-permute-start.3 = (bf16[512,768]{1,0:T(8,128)(2,1)S(1)}, bf16[512,768]{1,0:T(8,128)(2,1)S(1)}, u32[]{:S(2)}, u32[]{:S(2)}) collective-permute-start(bf16[512,768]{1,0:T(8,128)(2,1)S(1)} %pad_maximum_fusion), channel_id=1, source_target_pairs={{0,4},{4,8},{6,2},{8,12},{10,6},{14,10},{1,5},{5,9},{7,3},{9,13},{... | collective-permute-start | bytes 2359304 | tf_op jit(solution)/shard_map/ppermute | solution.py:363
  18.5 1.3 %collective-permute-start.8 = (bf16[512,384]{1,0:T(8,128)(2,1)S(1)}, bf16[512,384]{1,0:T(8,128)(2,1)S(1)}, u32[]{:S(2)}, u32[]{:S(2)}) collective-permute-start(bf16[512,384]{1,0:T(8,128)(2,1)S(1)} %get-tuple-element.16), channel_id=1, source_target_pairs={{2,6},{4,0},{6,10},{8,4},{10,14},{12,8},{3,7},{5,1},{7,11},{9,5},{... | collective-permute-start | bytes 1179656 | tf_op jit(solution)/shard_map/ppermute | solution.py:372
  19.9 1.2 %collective-permute-start.6 = (bf16[256,1536]{1,0:T(8,128)(2,1)S(1)}, bf16[256,1536]{1,0:T(8,128)(2,1)S(1)}, u32[]{:S(2)}, u32[]{:S(2)}) collective-permute-start(bf16[256,1536]{1,0:T(8,128)(2,1)S(1)} %tie.5), channel_id=1, source_target_pairs={{0,2},{2,0},{4,6},{6,4},{8,10},{10,8},{12,14},{14,12},{1,3},{3,1},... | collective-permute-start | bytes 2359304 | tf_op jit(solution)/shard_map/ppermute | solution.py:371
  21.1 8.7 %collective-permute-done.7.rest_1_.rest_2_ = bf16[512,768]{1,0:T(8,128)(2,1)S(1)} collective-permute-done((bf16[512,768]{1,0:T(8,128)(2,1)S(1)}, bf16[512,768]{1,0:T(8,128)(2,1)S(1)}, u32[]{:S(2)}, u32[]{:S(2)}) %collective-permute-start.7) | collective-permute-done | bytes 786464 | tf_op jit(solution)/shard_map/ppermute | solution.py:364
  29.8 1.3 %collective-permute-start.12 = (bf16[512,768]{1,0:T(8,128)(2,1)S(1)}, bf16[512,768]{1,0:T(8,128)(2,1)S(1)}, u32[]{:S(2)}, u32[]{:S(2)}) collective-permute-start(bf16[512,768]{1,0:T(8,128)(2,1)S(1)} %collective-permute-done.7.rest_1_.rest_2_), channel_id=1, source_target_pairs={{2,6},{4,0},{6,10},{8,4},{10,14},{12,8},{3,7},{5,1},{7,11},{9,5},{... | collective-permute-start | bytes 2359304 | tf_op jit(solution)/shard_map/ppermute | solution.py:374
  31.2 12.0 %collective-permute-start.10 = (bf16[512,768]{1,0:T(8,128)(2,1)S(1)}, bf16[512,768]{1,0:T(8,128)(2,1)S(1)}, u32[]{:S(2)}, u32[]{:S(2)}) collective-permute-start(bf16[512,768]{1,0:T(8,128)(2,1)S(1)} %tie.7), channel_id=1, source_target_pairs={{0,4},{4,8},{6,2},{8,12},{10,6},{14,10},{1,5},{5,9},{7,3},{9,13},{... | collective-permute-start | bytes 2359304 | tf_op jit(solution)/shard_map/ppermute | solution.py:376
  43.2 3.5 %collective-permute-done.8.rest_2_.rest_1_ = bf16[512,384]{1,0:T(8,128)(2,1)S(1)} collective-permute-done((bf16[512,384]{1,0:T(8,128)(2,1)S(1)}, bf16[512,384]{1,0:T(8,128)(2,1)S(1)}, u32[]{:S(2)}, u32[]{:S(2)}) %collective-permute-start.8) | collective-permute-done | bytes 393248 | tf_op jit(solution)/shard_map/ppermute | solution.py:372
  46.9 4.7 %collective-permute-start.5 = (bf16[512,384]{1,0:T(8,128)(2,1)S(1)}, bf16[512,384]{1,0:T(8,128)(2,1)S(1)}, u32[]{:S(2)}, u32[]{:S(2)}) collective-permute-start(bf16[512,384]{1,0:T(8,128)(2,1)S(1)} %collective-permute-done.4.rest_1_.refs_0_), channel_id=1, source_target_pairs={{0,4},{4,8},{6,2},{8,12},{10,6},{14,10},{1,5},{5,9},{7,3},{9,13},{... | collective-permute-start | bytes 1179656 | tf_op jit(solution)/shard_map/ppermute | solution.py:377
  51.6 1.5 %collective-permute-start.14 = (bf16[512,384]{1,0:T(8,128)(2,1)S(1)}, bf16[512,384]{1,0:T(8,128)(2,1)S(1)}, u32[]{:S(2)}, u32[]{:S(2)}) collective-permute-start(bf16[512,384]{1,0:T(8,128)(2,1)S(1)} %collective-permute-done.8.rest_2_.rest_1_), channel_id=1, source_target_pairs={{2,6},{4,0},{6,10},{8,4},{10,14},{12,8},{3,7},{5,1},{7,11},{9,5},{... | collective-permute-start | bytes 1179656 | tf_op jit(solution)/shard_map/ppermute | solution.py:378
  53.1 1.9 %own_part.4 = (f32[256,384]{1,0:T(8,128)S(1)}, f32[256,128]{1,0:T(8,128)S(1)}) custom-call(s32[8,8]{1,0:T(8,128)S(1)} %copy-done.3, bf16[256,1536]{1,0:T(8,128)(2,1)S(1)} %copy-done.2, bf16[256,1536]{1,0:T(8,128)(2,1)S(1)} %copy-done, bf16[256,1536]{1,0:T(8,128)(2,1)S(1)} %copy-done.1, bf16[256,1536]{1,0:T(8,128)(2,1)S(1)} %collective-permute-done.refs_0_.sib_keys, ...), custom_call_target="tpu_custom_call" | custom-call | flops 301989888 | bytes 1048576 | tf_op jit(solution)/shard_map/own_part/pallas_call | solution.py:285
  55.0 2.0 %partner_part.3.rest_5_ = bf16[272,384]{1,0:T(8,128)(2,1)S(1)} custom-call(s32[8,8]{1,0:T(8,128)S(1)} %copy-done.3, bf16[256,1536]{1,0:T(8,128)(2,1)S(1)} %collective-permute-done.6.refs_0_.query, bf16[256,1536]{1,0:T(8,128)(2,1)S(1)} %copy-done, bf16[256,1536]{1,0:T(8,128)(2,1)S(1)} %copy-done.1, ...), custom_call_target="tpu_custom_call" | custom-call | flops 301989888 | bytes 1048576 | tf_op jit(solution)/shard_map/partner_part/pallas_call | solution.py:285
  57.0 6.6 %collective-permute-done.12.rest_3_ = bf16[512,768]{1,0:T(8,128)(2,1)S(1)} collective-permute-done((bf16[512,768]{1,0:T(8,128)(2,1)S(1)}, bf16[512,768]{1,0:T(8,128)(2,1)S(1)}, u32[]{:S(2)}, u32[]{:S(2)}) %collective-permute-start.12) | collective-permute-done | bytes 786464 | tf_op jit(solution)/shard_map/ppermute | solution.py:374
  63.6 1.0 %collective-permute-start.11 = (bf16[272,384]{1,0:T(8,128)(2,1)S(1)}, bf16[272,384]{1,0:T(8,128)(2,1)S(1)}, u32[]{:S(2)}, u32[]{:S(2)}) collective-permute-start(bf16[272,384]{1,0:T(8,128)(2,1)S(1)} %partner_part.3.rest_5_), channel_id=1, source_target_pairs={{0,2},{2,0},{4,6},{6,4},{8,10},{10,8},{12,14},{14,12},{1,3},{3,1},... | collective-permute-start | bytes 626696 | tf_op jit(solution)/shard_map/ppermute | solution.py:430
  64.6 3.6 %partner_part.4 = bf16[288,768]{1,0:T(8,128)(2,1)S(1)} custom-call(s32[8,8]{1,0:T(8,128)S(1)} %copy-done.3, bf16[256,1536]{1,0:T(8,128)(2,1)S(1)} %collective-permute-done.6.refs_0_.query, bf16[256,1536]{1,0:T(8,128)(2,1)S(1)} %copy-done, bf16[256,1536]{1,0:T(8,128)(2,1)S(1)} %copy-done.1, bf16[256,1536]{1,0:T(8,128)(2,1)S(1)} %collective-permute-done.refs_0_.sib_keys, ...), custom_call_target="tpu_custom_call" | custom-call | flops 603979776 | bytes 1048576 | tf_op jit(solution)/shard_map/partner_part/pallas_call | solution.py:285
  68.2 1.1 %collective-permute-start.13 = (bf16[288,768]{1,0:T(8,128)(2,1)S(1)}, bf16[288,768]{1,0:T(8,128)(2,1)S(1)}, u32[]{:S(2)}, u32[]{:S(2)}) collective-permute-start(bf16[288,768]{1,0:T(8,128)(2,1)S(1)} %partner_part.4), channel_id=1, source_target_pairs={{0,2},{2,0},{4,6},{6,4},{8,10},{10,8},{12,14},{14,12},{1,3},{3,1},... | collective-permute-start | bytes 1327112 | tf_op jit(solution)/shard_map/ppermute | solution.py:431
  69.3 2.8 %own_part.5 = (f32[256,768]{1,0:T(8,128)S(1)}, f32[256,128]{1,0:T(8,128)S(1)}) custom-call(s32[8,8]{1,0:T(8,128)S(1)} %copy-done.3, bf16[256,1536]{1,0:T(8,128)(2,1)S(1)} %copy-done.2, bf16[256,1536]{1,0:T(8,128)(2,1)S(1)} %copy-done, bf16[256,1536]{1,0:T(8,128)(2,1)S(1)} %copy-done.1, bf16[256,1536]{1,0:T(8,128)(2,1)S(1)} %collective-permute-done.refs_0_.sib_keys, ...), custom_call_target="tpu_custom_call" | custom-call | flops 603979776 | bytes 1048576 | tf_op jit(solution)/shard_map/own_part/pallas_call | solution.py:285
  72.1 2.4 %partner_part.5 = bf16[272,384]{1,0:T(8,128)(2,1)S(1)} custom-call(s32[8,8]{1,0:T(8,128)S(1)} %copy-done.3, bf16[256,1536]{1,0:T(8,128)(2,1)S(1)} %collective-permute-done.6.refs_0_.query, bf16[256,1536]{1,0:T(8,128)(2,1)S(1)} %copy-done, bf16[256,1536]{1,0:T(8,128)(2,1)S(1)} %copy-done.1, bf16[256,1536]{1,0:T(8,128)(2,1)S(1)} %collective-permute-done.refs_0_.sib_keys, ...), custom_call_target="tpu_custom_call" | custom-call | flops 301989888 | bytes 1048576 | tf_op jit(solution)/shard_map/partner_part/pallas_call | solution.py:285
  74.6 1.1 %collective-permute-start.15 = (bf16[272,384]{1,0:T(8,128)(2,1)S(1)}, bf16[272,384]{1,0:T(8,128)(2,1)S(1)}, u32[]{:S(2)}, u32[]{:S(2)}) collective-permute-start(bf16[272,384]{1,0:T(8,128)(2,1)S(1)} %partner_part.5), channel_id=1, source_target_pairs={{0,2},{2,0},{4,6},{6,4},{8,10},{10,8},{12,14},{14,12},{1,3},{3,1},... | collective-permute-start | bytes 626696 | tf_op jit(solution)/shard_map/ppermute | solution.py:436
  75.6 2.3 %own_part.3 = (f32[256,384]{1,0:T(8,128)S(1)}, f32[256,128]{1,0:T(8,128)S(1)}) custom-call(s32[8,8]{1,0:T(8,128)S(1)} %copy-done.3, bf16[256,1536]{1,0:T(8,128)(2,1)S(1)} %copy-done.2, bf16[256,1536]{1,0:T(8,128)(2,1)S(1)} %copy-done, bf16[256,1536]{1,0:T(8,128)(2,1)S(1)} %copy-done.1, bf16[256,1536]{1,0:T(8,128)(2,1)S(1)} %collective-permute-done.refs_0_.sib_keys, ...), custom_call_target="tpu_custom_call" | custom-call | flops 301989888 | bytes 1048576 | tf_op jit(solution)/shard_map/own_part/pallas_call | solution.py:285
  78.0 6.1 %collective-permute-done.15.refs_10_ = bf16[272,384]{1,0:T(8,128)(2,1)S(1)} collective-permute-done((bf16[272,384]{1,0:T(8,128)(2,1)S(1)}, bf16[272,384]{1,0:T(8,128)(2,1)S(1)}, u32[]{:S(2)}, u32[]{:S(2)}) %collective-permute-start.15) | collective-permute-done | bytes 208928 | tf_op jit(solution)/shard_map/ppermute | solution.py:436
  84.1 5.2 %merge_and_project.1 = bf16[256,3072]{1,0:T(8,128)(2,1)} custom-call(bf16[768,3072]{1,0:T(8,128)(2,1)S(1)} %get-tuple-element.14.refs_0_, bf16[768,3072]{1,0:T(8,128)(2,1)S(1)} %collective-permute-done.2.refs_0_.rest_7_.refs_1_, f32[256,384]{1,0:T(8,128)S(1)} %get-tuple-element.17.refs_2_, f32[256,128]{1,0:T(8,128)S(1)} %get-tuple-element.18.refs_3_, ...), custom_call_target="tpu_custom_call" | custom-call | flops 2415919104 | bytes 12582912 | tf_op jit(solution)/shard_map/merge_and_project/pallas_call | solution.py:322
  (33 shorter events, 0.6 us)
Async XLA Ops:
  0.0 2.6 %copy-start = (bf16[256,1536]{1,0:T(8,128)(2,1)S(1)}, bf16[256,1536]{1,0:T(8,128)(2,1)}, u32[]{:S(2)}) copy-start(bf16[256,1536]{1,0:T(8,128)(2,1)} %keys.11) | copy-start | bytes 2359300
  0.0 3.0 %copy-start.1 = (bf16[256,1536]{1,0:T(8,128)(2,1)S(1)}, bf16[256,1536]{1,0:T(8,128)(2,1)}, u32[]{:S(2)}) copy-start(bf16[256,1536]{1,0:T(8,128)(2,1)} %values.11) | copy-start | bytes 2359300
  2.6 2.4 %collective-permute-start = (bf16[256,1536]{1,0:T(8,128)(2,1)S(1)}, bf16[256,1536]{1,0:T(8,128)(2,1)S(1)}, u32[]{:S(2)}, u32[]{:S(2)}) collective-permute-start(bf16[256,1536]{1,0:T(8,128)(2,1)S(1)} %copy-done), channel_id=1, source_target_pairs={{0,1},{1,0},{2,3},{3,2},{4,5},{5,4},{6,7},{7,6},{8,9},{9,8},{10,11... | collective-permute-start | bytes 2359304 | tf_op jit(solution)/shard_map/ppermute | solution.py:361
  3.0 3.0 %collective-permute-start.1 = (bf16[256,1536]{1,0:T(8,128)(2,1)S(1)}, bf16[256,1536]{1,0:T(8,128)(2,1)S(1)}, u32[]{:S(2)}, u32[]{:S(2)}) collective-permute-start(bf16[256,1536]{1,0:T(8,128)(2,1)S(1)} %copy-done.1), channel_id=1, source_target_pairs={{0,1},{1,0},{2,3},{3,2},{4,5},{5,4},{6,7},{7,6},{8,9},{9,8},{10,11... | collective-permute-start | bytes 2359304 | tf_op jit(solution)/shard_map/ppermute | solution.py:362
  6.0 13.8 %collective-permute-start.2 = (bf16[768,3072]{1,0:T(8,128)(2,1)S(1)}, bf16[768,3072]{1,0:T(8,128)(2,1)S(1)}, u32[]{:S(2)}, u32[]{:S(2)}) collective-permute-start(bf16[768,3072]{1,0:T(8,128)(2,1)S(1)} %get-tuple-element.14.refs_0_), channel_id=1, source_target_pairs={{0,1},{1,0},{2,3},{3,2},{4,5},{5,4},{6,7},{7,6},{8,9},{9,8},{10,11... | collective-permute-start | bytes 14155784 | tf_op jit(solution)/shard_map/ppermute | solution.py:369
  6.6 11.8 %copy-start.2 = (bf16[256,1536]{1,0:T(8,128)(2,1)S(1)}, bf16[256,1536]{1,0:T(8,128)(2,1)}, u32[]{:S(2)}) copy-start(bf16[256,1536]{1,0:T(8,128)(2,1)} %query.5) | copy-start | bytes 2359300
  6.7 23.1 %collective-permute-start.7 = (bf16[512,768]{1,0:T(8,128)(2,1)S(1)}, bf16[512,768]{1,0:T(8,128)(2,1)S(1)}, u32[]{:S(2)}, u32[]{:S(2)}) collective-permute-start(bf16[512,768]{1,0:T(8,128)(2,1)S(1)} %pad_maximum_fusion.1), channel_id=1, source_target_pairs={{2,6},{4,0},{6,10},{8,4},{10,14},{12,8},{3,7},{5,1},{7,11},{9,5},{... | collective-permute-start | bytes 2359304 | tf_op jit(solution)/shard_map/ppermute | solution.py:364
  8.1 23.0 %collective-permute-start.4 = (bf16[512,384]{1,0:T(8,128)(2,1)S(1)}, bf16[512,384]{1,0:T(8,128)(2,1)S(1)}, u32[]{:S(2)}, u32[]{:S(2)}) collective-permute-start(bf16[512,384]{1,0:T(8,128)(2,1)S(1)} %get-tuple-element.15), channel_id=1, source_target_pairs={{2,4},{4,2},{6,8},{8,6},{10,12},{12,10},{3,5},{5,3},{7,9},{9,7},{1... | collective-permute-start | bytes 1179656 | tf_op jit(solution)/shard_map/ppermute | solution.py:373
  8.9 42.8 %collective-permute-start.3 = (bf16[512,768]{1,0:T(8,128)(2,1)S(1)}, bf16[512,768]{1,0:T(8,128)(2,1)S(1)}, u32[]{:S(2)}, u32[]{:S(2)}) collective-permute-start(bf16[512,768]{1,0:T(8,128)(2,1)S(1)} %pad_maximum_fusion), channel_id=1, source_target_pairs={{0,4},{4,8},{6,2},{8,12},{10,6},{14,10},{1,5},{5,9},{7,3},{9,13},{... | collective-permute-start | bytes 2359304 | tf_op jit(solution)/shard_map/ppermute | solution.py:363
  18.5 28.2 %collective-permute-start.8 = (bf16[512,384]{1,0:T(8,128)(2,1)S(1)}, bf16[512,384]{1,0:T(8,128)(2,1)S(1)}, u32[]{:S(2)}, u32[]{:S(2)}) collective-permute-start(bf16[512,384]{1,0:T(8,128)(2,1)S(1)} %get-tuple-element.16), channel_id=1, source_target_pairs={{2,6},{4,0},{6,10},{8,4},{10,14},{12,8},{3,7},{5,1},{7,11},{9,5},{... | collective-permute-start | bytes 1179656 | tf_op jit(solution)/shard_map/ppermute | solution.py:372
  19.9 27.0 %collective-permute-start.6 = (bf16[256,1536]{1,0:T(8,128)(2,1)S(1)}, bf16[256,1536]{1,0:T(8,128)(2,1)S(1)}, u32[]{:S(2)}, u32[]{:S(2)}) collective-permute-start(bf16[256,1536]{1,0:T(8,128)(2,1)S(1)} %tie.5), channel_id=1, source_target_pairs={{0,2},{2,0},{4,6},{6,4},{8,10},{10,8},{12,14},{14,12},{1,3},{3,1},... | collective-permute-start | bytes 2359304 | tf_op jit(solution)/shard_map/ppermute | solution.py:371
  29.8 33.7 %collective-permute-start.12 = (bf16[512,768]{1,0:T(8,128)(2,1)S(1)}, bf16[512,768]{1,0:T(8,128)(2,1)S(1)}, u32[]{:S(2)}, u32[]{:S(2)}) collective-permute-start(bf16[512,768]{1,0:T(8,128)(2,1)S(1)} %collective-permute-done.7.rest_1_.rest_2_), channel_id=1, source_target_pairs={{2,6},{4,0},{6,10},{8,4},{10,14},{12,8},{3,7},{5,1},{7,11},{9,5},{... | collective-permute-start | bytes 2359304 | tf_op jit(solution)/shard_map/ppermute | solution.py:374
  31.2 33.4 %collective-permute-start.10 = (bf16[512,768]{1,0:T(8,128)(2,1)S(1)}, bf16[512,768]{1,0:T(8,128)(2,1)S(1)}, u32[]{:S(2)}, u32[]{:S(2)}) collective-permute-start(bf16[512,768]{1,0:T(8,128)(2,1)S(1)} %tie.7), channel_id=1, source_target_pairs={{0,4},{4,8},{6,2},{8,12},{10,6},{14,10},{1,5},{5,9},{7,3},{9,13},{... | collective-permute-start | bytes 2359304 | tf_op jit(solution)/shard_map/ppermute | solution.py:376
  46.8 6.3 %copy-start.3 = (s32[8,8]{1,0:T(8,128)S(1)}, s32[8,8]{1,0:T(8,128)}, u32[]{:S(2)}) copy-start(s32[8,8]{1,0:T(8,128)} %table_ref.11) | copy-start | bytes 772
  46.8 17.7 %collective-permute-start.9 = (bf16[256,1536]{1,0:T(8,128)(2,1)S(1)}, bf16[256,1536]{1,0:T(8,128)(2,1)S(1)}, u32[]{:S(2)}, u32[]{:S(2)}) collective-permute-start(bf16[256,1536]{1,0:T(8,128)(2,1)S(1)} %tie.6), channel_id=1, source_target_pairs={{0,1},{1,0},{2,3},{3,2},{4,5},{5,4},{6,7},{7,6},{8,9},{9,8},{10,11... | collective-permute-start | bytes 2359304 | tf_op jit(solution)/shard_map/ppermute | solution.py:380
  46.9 25.2 %collective-permute-start.5 = (bf16[512,384]{1,0:T(8,128)(2,1)S(1)}, bf16[512,384]{1,0:T(8,128)(2,1)S(1)}, u32[]{:S(2)}, u32[]{:S(2)}) collective-permute-start(bf16[512,384]{1,0:T(8,128)(2,1)S(1)} %collective-permute-done.4.rest_1_.refs_0_), channel_id=1, source_target_pairs={{0,4},{4,8},{6,2},{8,12},{10,6},{14,10},{1,5},{5,9},{7,3},{9,13},{... | collective-permute-start | bytes 1179656 | tf_op jit(solution)/shard_map/ppermute | solution.py:377
  51.6 20.5 %collective-permute-start.14 = (bf16[512,384]{1,0:T(8,128)(2,1)S(1)}, bf16[512,384]{1,0:T(8,128)(2,1)S(1)}, u32[]{:S(2)}, u32[]{:S(2)}) collective-permute-start(bf16[512,384]{1,0:T(8,128)(2,1)S(1)} %collective-permute-done.8.rest_2_.rest_1_), channel_id=1, source_target_pairs={{2,6},{4,0},{6,10},{8,4},{10,14},{12,8},{3,7},{5,1},{7,11},{9,5},{... | collective-permute-start | bytes 1179656 | tf_op jit(solution)/shard_map/ppermute | solution.py:378
  63.6 8.6 %collective-permute-start.11 = (bf16[272,384]{1,0:T(8,128)(2,1)S(1)}, bf16[272,384]{1,0:T(8,128)(2,1)S(1)}, u32[]{:S(2)}, u32[]{:S(2)}) collective-permute-start(bf16[272,384]{1,0:T(8,128)(2,1)S(1)} %partner_part.3.rest_5_), channel_id=1, source_target_pairs={{0,2},{2,0},{4,6},{6,4},{8,10},{10,8},{12,14},{14,12},{1,3},{3,1},... | collective-permute-start | bytes 626696 | tf_op jit(solution)/shard_map/ppermute | solution.py:430
  68.2 15.9 %collective-permute-start.13 = (bf16[288,768]{1,0:T(8,128)(2,1)S(1)}, bf16[288,768]{1,0:T(8,128)(2,1)S(1)}, u32[]{:S(2)}, u32[]{:S(2)}) collective-permute-start(bf16[288,768]{1,0:T(8,128)(2,1)S(1)} %partner_part.4), channel_id=1, source_target_pairs={{0,2},{2,0},{4,6},{6,4},{8,10},{10,8},{12,14},{14,12},{1,3},{3,1},... | collective-permute-start | bytes 1327112 | tf_op jit(solution)/shard_map/ppermute | solution.py:431
  74.6 9.5 %collective-permute-start.15 = (bf16[272,384]{1,0:T(8,128)(2,1)S(1)}, bf16[272,384]{1,0:T(8,128)(2,1)S(1)}, u32[]{:S(2)}, u32[]{:S(2)}) collective-permute-start(bf16[272,384]{1,0:T(8,128)(2,1)S(1)} %partner_part.5), channel_id=1, source_target_pairs={{0,2},{2,0},{4,6},{6,4},{8,10},{10,8},{12,14},{14,12},{1,3},{3,1},... | collective-permute-start | bytes 626696 | tf_op jit(solution)/shard_map/ppermute | solution.py:436

commit v7 on v5

--- a/solution.py
+++ b/solution.py
@@ -360,22 +360,24 @@
 
     major1 = lax.ppermute(pack(0, 6), "frame", away_moves)
     minor1 = lax.ppermute(pack(3, 9), "frame", near_moves)
-    sib_keys = lax.ppermute(key_tokens, "head", core_moves)
-    sib_values = lax.ppermute(value_tokens, "head", core_moves)
     own_weight = [out_weight]
     sib_weight = [lax.ppermute(out_weight, "head", core_moves)]
-    to_minor2, to_major2, to_partner = tie(
-        (sib_keys, sib_values, *sib_weight), pack(9, 12), pack(0, 3), queries
-    )
+    cross = lax.ppermute(pack(0, 3), "frame", partner_moves)
+    (to_minor2,) = tie((cross, *sib_weight), pack(9, 12))
+    minor2 = lax.ppermute(to_minor2, "frame", near_moves)
+    (to_partner,) = tie(sib_weight, queries)
     partner_query = lax.ppermute(to_partner, "frame", partner_moves)
-    minor2 = lax.ppermute(to_minor2, "frame", near_moves)
-    major2 = lax.ppermute(to_major2, "frame", cross_moves)
+    major2 = lax.ppermute(cross, "frame", away_moves)
     minor3 = lax.ppermute(minor1, "frame", near_moves)
     (to_major3,) = tie((major1,), pack(6, 12))
     major3 = lax.ppermute(to_major3, "frame", away_moves)
     major4 = lax.ppermute(major2, "frame", away_moves)
     minor4 = lax.ppermute(minor2, "frame", near_moves)
-    nearest = lax.ppermute(firsts(minor1, minor2, major2), "head", core_moves)
+    to_sib_keys, to_sib_values = tie((minor2,), key_tokens, value_tokens)
+    sib_keys = lax.ppermute(to_sib_keys, "head", core_moves)
+    sib_values = lax.ppermute(to_sib_values, "head", core_moves)
+    (to_nearest,) = tie((partner_query,), firsts(minor1, minor2, major2))
+    nearest = lax.ppermute(to_nearest, "head", core_moves)
     refs = {
         "major1": major1,
         "major2": major2,

time: 99.9 us -> 86.9 us (0.87)
  starting transfers between devices: 54.4 us -> 30.2 us
  waiting for transfers between devices: 22.2 us -> 33.2 us
    ppermute x1, starting transfers between devices: 27.8 us -> 3.75 us  [per_device(): major4 = lax.ppermute(major2, 'frame', away_moves)]
    ppermute x1, waiting for transfers between devices: 12.7 us -> 2.56 us  [per_device(): major1 = lax.ppermute(pack(0, 6), 'frame', away_moves)]
    ppermute x4 -> x5, waiting for transfers between devices: 1.48 us -> 9.77 us  [the longest x1 9.73 us: per_device(): cross = lax.ppermute(pack(0, 3), 'frame', partner_moves)]
    ppermute x1, waiting for transfers between devices: 1 us -> 8.6 us  [per_device(): minor2 = lax.ppermute(to_minor2, 'frame', near_moves)]
    ppermute x1, waiting for transfers between devices: 0.01 us -> 5.86 us  [per_device(): partner_query = lax.ppermute(to_partner, 'frame', partner_moves)]
    ppermute x1, starting transfers between devices: 5.39 us -> 2.63 us  [per_device(): partner_query = lax.ppermute(to_partner, 'frame', partner_moves)]
    ppermute x4 -> x5, starting transfers between devices: 1.27 us -> 4.03 us  [the longest x1 3.45 us: per_device(): major2 = lax.ppermute(cross, 'frame', away_moves)]
  transfers between devices with their start and end apart: 16 -> 17, of which waited for: 6 -> 5; matrix products, arithmetic and copies ran while one was open for 2% -> 3% of each run, Pallas kernels for 16% -> 18%
where the time goes in v7:
time: 86.9 us; the launch traced here: 86.6 us
  waiting for transfers between devices  33.2 us (38%)
  starting transfers between devices  30.2 us (35%)
  Pallas kernels  20.5 us (24%)
  local copies, waits for them, and re-layouts  2.09 us (2%)
    pallas_call x6, Pallas kernels, run(): pl.pallas_call(body, grid=(1,), in_specs=[pl.BlockSpec(memory_space=pltpu...  15.2 us
    ppermute x1, waiting for transfers between devices, per_device(): cross = lax.ppermute(pack(0, 3), 'frame', partner_moves)  9.73 us
    ppermute x1, waiting for transfers between devices, per_device(): minor2 = lax.ppermute(to_minor2, 'frame', near_moves)  8.6 us
    ppermute x1, waiting for transfers between devices, per_device(): part_high = lax.ppermute(part_high, 'frame', partner_moves)  6.39 us
    ppermute x1, waiting for transfers between devices, per_device(): partner_query = lax.ppermute(to_partner, 'frame', partner_moves)  5.86 us
    pallas_call x1, Pallas kernels, project(): pl.pallas_call(functools.partial(project_kernel, own_groups, part_groups,...  5.23 us
    ppermute x1, starting transfers between devices, per_device(): major1 = lax.ppermute(pack(0, 6), 'frame', away_moves)  4.66 us
    ppermute x1, starting transfers between devices, per_device(): major3 = lax.ppermute(to_major3, 'frame', away_moves)  4.42 us
  transfers between devices with their start and end apart: 17, of which 5 were waited for; matrix products, arithmetic and copies ran while one was open for 3% of the time, Pallas kernels for 18%

profile of v7, /device:TPU:0, one launch (start us, length us, event | category | flops | bytes accessed | tf_op | source)
XLA Modules:
  0.0 86.6 jit_solution(8430057670441835135)
XLA Ops:
  0.0 0.5 collective-permute-start
  0.5 1.7 %fusion = (bf16[256,768]{1,0:T(8,128)(2,1)S(1)}, bf16[256,768]{1,0:T(8,128)(2,1)S(1)}, bf16[256,768]{1,0:T(8,128)(2,1)S(1)}, bf16[256,768]{1,0:T(8,128)(2,1)S(1)...) fusion(bf16[256,1536]{1,0:T(8,128)(2,1)} %keys.11, bf16[256,1536]{1,0:T(8,128)(2,1)} %values.11), kind=kLoop, calls=%fused_computation.6 | loop fusion | bytes 4718592 | tf_op jit(solution)/shard_map/slice | solution.py:353
  2.2 0.1 pad_maximum_fusion
  2.3 4.7 %collective-permute-start.5 = (bf16[512,768]{1,0:T(8,128)(2,1)S(1)}, bf16[512,768]{1,0:T(8,128)(2,1)S(1)}, u32[]{:S(2)}, u32[]{:S(2)}) collective-permute-start(bf16[512,768]{1,0:T(8,128)(2,1)S(1)} %pad_maximum_fusion), channel_id=1, source_target_pairs={{0,4},{4,8},{6,2},{8,12},{10,6},{14,10},{1,5},{5,9},{7,3},{9,13},{... | collective-permute-start | bytes 2359304 | tf_op jit(solution)/shard_map/ppermute | solution.py:361
  7.0 0.1 fusion.3
  7.1 0.1 collective-permute-start.1
  7.2 0.1 pad_maximum_fusion.1
  7.3 1.4 %collective-permute-start.9 = (bf16[512,768]{1,0:T(8,128)(2,1)S(1)}, bf16[512,768]{1,0:T(8,128)(2,1)S(1)}, u32[]{:S(2)}, u32[]{:S(2)}) collective-permute-start(bf16[512,768]{1,0:T(8,128)(2,1)S(1)} %pad_maximum_fusion.1), channel_id=1, source_target_pairs={{2,6},{4,0},{6,10},{8,4},{10,14},{12,8},{3,7},{5,1},{7,11},{9,5},{... | collective-permute-start | bytes 2359304 | tf_op jit(solution)/shard_map/ppermute | solution.py:362
  8.7 9.7 %collective-permute-done.1.refs_0_ = bf16[512,384]{1,0:T(8,128)(2,1)S(1)} collective-permute-done((bf16[512,384]{1,0:T(8,128)(2,1)S(1)}, bf16[512,384]{1,0:T(8,128)(2,1)S(1)}, u32[]{:S(2)}, u32[]{:S(2)}) %collective-permute-start.1) | collective-permute-done | bytes 393248 | tf_op jit(solution)/shard_map/ppermute | solution.py:365
  18.4 3.4 %collective-permute-start.6 = (bf16[512,384]{1,0:T(8,128)(2,1)S(1)}, bf16[512,384]{1,0:T(8,128)(2,1)S(1)}, u32[]{:S(2)}, u32[]{:S(2)}) collective-permute-start(bf16[512,384]{1,0:T(8,128)(2,1)S(1)} %collective-permute-done.1.refs_0_), channel_id=1, source_target_pairs={{0,4},{4,8},{6,2},{8,12},{10,6},{14,10},{1,5},{5,9},{7,3},{9,13},{... | collective-permute-start | bytes 1179656 | tf_op jit(solution)/shard_map/ppermute | solution.py:370
  22.2 2.6 %collective-permute-done.5.rest_0_.refs_0_ = bf16[512,768]{1,0:T(8,128)(2,1)S(1)} collective-permute-done((bf16[512,768]{1,0:T(8,128)(2,1)S(1)}, bf16[512,768]{1,0:T(8,128)(2,1)S(1)}, u32[]{:S(2)}, u32[]{:S(2)}) %collective-permute-start.5) | collective-permute-done | bytes 786464 | tf_op jit(solution)/shard_map/ppermute | solution.py:361
  24.7 4.4 %collective-permute-start.11 = (bf16[512,768]{1,0:T(8,128)(2,1)S(1)}, bf16[512,768]{1,0:T(8,128)(2,1)S(1)}, u32[]{:S(2)}, u32[]{:S(2)}) collective-permute-start(bf16[512,768]{1,0:T(8,128)(2,1)S(1)} %tie.9), channel_id=1, source_target_pairs={{0,4},{4,8},{6,2},{8,12},{10,6},{14,10},{1,5},{5,9},{7,3},{9,13},{... | collective-permute-start | bytes 2359304 | tf_op jit(solution)/shard_map/ppermute | solution.py:373
  29.2 1.3 %collective-permute-start.2 = (bf16[512,384]{1,0:T(8,128)(2,1)S(1)}, bf16[512,384]{1,0:T(8,128)(2,1)S(1)}, u32[]{:S(2)}, u32[]{:S(2)}) collective-permute-start(bf16[512,384]{1,0:T(8,128)(2,1)S(1)} %tie.5), channel_id=1, source_target_pairs={{2,6},{4,0},{6,10},{8,4},{10,14},{12,8},{3,7},{5,1},{7,11},{9,5},{... | collective-permute-start | bytes 1179656 | tf_op jit(solution)/shard_map/ppermute | solution.py:367
  30.5 2.6 %collective-permute-start.8 = (bf16[256,1536]{1,0:T(8,128)(2,1)S(1)}, bf16[256,1536]{1,0:T(8,128)(2,1)S(1)}, u32[]{:S(2)}, u32[]{:S(2)}) collective-permute-start(bf16[256,1536]{1,0:T(8,128)(2,1)S(1)} %tie.7), channel_id=1, source_target_pairs={{0,2},{2,0},{4,6},{6,4},{8,10},{10,8},{12,14},{14,12},{1,3},{3,1},... | collective-permute-start | bytes 2359304 | tf_op jit(solution)/shard_map/ppermute | solution.py:369
  33.2 1.3 %collective-permute-start.13 = (bf16[512,768]{1,0:T(8,128)(2,1)S(1)}, bf16[512,768]{1,0:T(8,128)(2,1)S(1)}, u32[]{:S(2)}, u32[]{:S(2)}) collective-permute-start(bf16[512,768]{1,0:T(8,128)(2,1)S(1)} %collective-permute-done.9.rest_1_.rest_2_), channel_id=1, source_target_pairs={{2,6},{4,0},{6,10},{8,4},{10,14},{12,8},{3,7},{5,1},{7,11},{9,5},{... | collective-permute-start | bytes 2359304 | tf_op jit(solution)/shard_map/ppermute | solution.py:371
  34.5 8.6 %collective-permute-done.2.refs_0_.rest_2_.rest_1_ = bf16[512,384]{1,0:T(8,128)(2,1)S(1)} collective-permute-done((bf16[512,384]{1,0:T(8,128)(2,1)S(1)}, bf16[512,384]{1,0:T(8,128)(2,1)S(1)}, u32[]{:S(2)}, u32[]{:S(2)}) %collective-permute-start.2) | collective-permute-done | bytes 393248 | tf_op jit(solution)/shard_map/ppermute | solution.py:367
  43.1 0.5 collective-permute-start.4
  43.7 0.1 maximum_maximum_fusion.refs_1_
  43.8 5.9 %collective-permute-done.8.refs_0_.query = bf16[256,1536]{1,0:T(8,128)(2,1)S(1)} collective-permute-done((bf16[256,1536]{1,0:T(8,128)(2,1)S(1)}, bf16[256,1536]{1,0:T(8,128)(2,1)S(1)}, u32[]{:S(2)}, u32[]{:S(2)}) %collective-permute-start.8) | collective-permute-done | bytes 786464 | tf_op jit(solution)/shard_map/ppermute | solution.py:369
  49.6 3.7 %collective-permute-start.7 = (bf16[512,384]{1,0:T(8,128)(2,1)S(1)}, bf16[512,384]{1,0:T(8,128)(2,1)S(1)}, u32[]{:S(2)}, u32[]{:S(2)}) collective-permute-start(bf16[512,384]{1,0:T(8,128)(2,1)S(1)} %collective-permute-done.6.rest_1_), channel_id=1, source_target_pairs={{0,4},{4,8},{6,2},{8,12},{10,6},{14,10},{1,5},{5,9},{7,3},{9,13},{... | collective-permute-start | bytes 1179656 | tf_op jit(solution)/shard_map/ppermute | solution.py:374
  53.4 1.5 %collective-permute-start.15 = (bf16[512,384]{1,0:T(8,128)(2,1)S(1)}, bf16[512,384]{1,0:T(8,128)(2,1)S(1)}, u32[]{:S(2)}, u32[]{:S(2)}) collective-permute-start(bf16[512,384]{1,0:T(8,128)(2,1)S(1)} %collective-permute-done.2.refs_0_.rest_2_.rest_1_), channel_id=1, source_target_pairs={{2,6},{4,0},{6,10},{8,4},{10,14},{12,8},{3,7},{5,1},{7,11},{9,5},{... | collective-permute-start | bytes 1179656 | tf_op jit(solution)/shard_map/ppermute | solution.py:375
  54.9 2.0 %partner_part.3.rest_5_ = bf16[272,384]{1,0:T(8,128)(2,1)S(1)} custom-call(s32[8,8]{1,0:T(8,128)S(1)} %copy-done.3, bf16[256,1536]{1,0:T(8,128)(2,1)S(1)} %collective-permute-done.8.refs_0_.query, bf16[256,1536]{1,0:T(8,128)(2,1)S(1)} %copy-done, bf16[256,1536]{1,0:T(8,128)(2,1)S(1)} %copy-done.1, bf16[256,1536]{1,0:T(8,128)(2,1)S(1)} %collective-permute-done.3.sib_keys, ...), custom_call_target="tpu_custom_call" | custom-call | flops 301989888 | bytes 1048576 | tf_op jit(solution)/shard_map/partner_part/pallas_call | solution.py:285
  56.9 1.9 %own_part.4 = (f32[256,384]{1,0:T(8,128)S(1)}, f32[256,128]{1,0:T(8,128)S(1)}) custom-call(s32[8,8]{1,0:T(8,128)S(1)} %copy-done.3, bf16[256,1536]{1,0:T(8,128)(2,1)S(1)} %copy-done.2, bf16[256,1536]{1,0:T(8,128)(2,1)S(1)} %copy-done, bf16[256,1536]{1,0:T(8,128)(2,1)S(1)} %copy-done.1, bf16[256,1536]{1,0:T(8,128)(2,1)S(1)} %collective-permute-done.3.sib_keys, ...), custom_call_target="tpu_custom_call" | custom-call | flops 301989888 | bytes 1048576 | tf_op jit(solution)/shard_map/own_part/pallas_call | solution.py:285
  58.8 2.6 %collective-permute-start.12 = (bf16[272,384]{1,0:T(8,128)(2,1)S(1)}, bf16[272,384]{1,0:T(8,128)(2,1)S(1)}, u32[]{:S(2)}, u32[]{:S(2)}) collective-permute-start(bf16[272,384]{1,0:T(8,128)(2,1)S(1)} %partner_part.3.rest_5_), channel_id=1, source_target_pairs={{0,2},{2,0},{4,6},{6,4},{8,10},{10,8},{12,14},{14,12},{1,3},{3,1},... | collective-permute-start | bytes 626696 | tf_op jit(solution)/shard_map/ppermute | solution.py:430
  61.4 3.7 %partner_part.4 = bf16[288,768]{1,0:T(8,128)(2,1)S(1)} custom-call(s32[8,8]{1,0:T(8,128)S(1)} %copy-done.3, bf16[256,1536]{1,0:T(8,128)(2,1)S(1)} %collective-permute-done.8.refs_0_.query, bf16[256,1536]{1,0:T(8,128)(2,1)S(1)} %copy-done, bf16[256,1536]{1,0:T(8,128)(2,1)S(1)} %copy-done.1, bf16[256,1536]{1,0:T(8,128)(2,1)S(1)} %collective-permute-done.3.sib_keys, ...), custom_call_target="tpu_custom_call" | custom-call | flops 603979776 | bytes 1048576 | tf_op jit(solution)/shard_map/partner_part/pallas_call | solution.py:285
  65.1 0.1 collective-permute-start.14
  65.2 2.9 %own_part.5 = (f32[256,768]{1,0:T(8,128)S(1)}, f32[256,128]{1,0:T(8,128)S(1)}) custom-call(s32[8,8]{1,0:T(8,128)S(1)} %copy-done.3, bf16[256,1536]{1,0:T(8,128)(2,1)S(1)} %copy-done.2, bf16[256,1536]{1,0:T(8,128)(2,1)S(1)} %copy-done, bf16[256,1536]{1,0:T(8,128)(2,1)S(1)} %copy-done.1, bf16[256,1536]{1,0:T(8,128)(2,1)S(1)} %collective-permute-done.3.sib_keys, ...), custom_call_target="tpu_custom_call" | custom-call | flops 603979776 | bytes 1048576 | tf_op jit(solution)/shard_map/own_part/pallas_call | solution.py:285
  68.1 2.4 %partner_part.5 = bf16[272,384]{1,0:T(8,128)(2,1)S(1)} custom-call(s32[8,8]{1,0:T(8,128)S(1)} %copy-done.3, bf16[256,1536]{1,0:T(8,128)(2,1)S(1)} %collective-permute-done.8.refs_0_.query, bf16[256,1536]{1,0:T(8,128)(2,1)S(1)} %copy-done, bf16[256,1536]{1,0:T(8,128)(2,1)S(1)} %copy-done.1, bf16[256,1536]{1,0:T(8,128)(2,1)S(1)} %collective-permute-done.3.sib_keys, ...), custom_call_target="tpu_custom_call" | custom-call | flops 301989888 | bytes 1048576 | tf_op jit(solution)/shard_map/partner_part/pallas_call | solution.py:285
  70.6 2.0 %collective-permute-start.16 = (bf16[272,384]{1,0:T(8,128)(2,1)S(1)}, bf16[272,384]{1,0:T(8,128)(2,1)S(1)}, u32[]{:S(2)}, u32[]{:S(2)}) collective-permute-start(bf16[272,384]{1,0:T(8,128)(2,1)S(1)} %partner_part.5), channel_id=1, source_target_pairs={{0,2},{2,0},{4,6},{6,4},{8,10},{10,8},{12,14},{14,12},{1,3},{3,1},... | collective-permute-start | bytes 626696 | tf_op jit(solution)/shard_map/ppermute | solution.py:436
  72.6 2.4 %own_part.3 = (f32[256,384]{1,0:T(8,128)S(1)}, f32[256,128]{1,0:T(8,128)S(1)}) custom-call(s32[8,8]{1,0:T(8,128)S(1)} %copy-done.3, bf16[256,1536]{1,0:T(8,128)(2,1)S(1)} %copy-done.2, bf16[256,1536]{1,0:T(8,128)(2,1)S(1)} %copy-done, bf16[256,1536]{1,0:T(8,128)(2,1)S(1)} %copy-done.1, bf16[256,1536]{1,0:T(8,128)(2,1)S(1)} %collective-permute-done.3.sib_keys, ...), custom_call_target="tpu_custom_call" | custom-call | flops 301989888 | bytes 1048576 | tf_op jit(solution)/shard_map/own_part/pallas_call | solution.py:285
  75.0 6.4 %collective-permute-done.16.refs_10_ = bf16[272,384]{1,0:T(8,128)(2,1)S(1)} collective-permute-done((bf16[272,384]{1,0:T(8,128)(2,1)S(1)}, bf16[272,384]{1,0:T(8,128)(2,1)S(1)}, u32[]{:S(2)}, u32[]{:S(2)}) %collective-permute-start.16) | collective-permute-done | bytes 208928 | tf_op jit(solution)/shard_map/ppermute | solution.py:436
  81.4 5.2 %merge_and_project.1 = bf16[256,3072]{1,0:T(8,128)(2,1)} custom-call(bf16[768,3072]{1,0:T(8,128)(2,1)S(1)} %bitcast.1, bf16[768,3072]{1,0:T(8,128)(2,1)S(1)} %collective-permute-done.refs_1_.refs_0_.rest_7_, f32[256,384]{1,0:T(8,128)S(1)} %get-tuple-element.15.refs_2_, f32[256,128]{1,0:T(8,128)S(1)} %get-tuple-element.16.refs_3_, ...), custom_call_target="tpu_custom_call" | custom-call | flops 2415919104 | bytes 12582912 | tf_op jit(solution)/shard_map/merge_and_project/pallas_call | solution.py:322
  (41 shorter events, 0.5 us)
Async XLA Ops:
  0.0 29.2 %collective-permute-start = (bf16[768,3072]{1,0:T(8,128)(2,1)}, bf16[768,3072]{1,0:T(8,128)(2,1)S(1)}, u32[]{:S(2)}, u32[]{:S(2)}) collective-permute-start(bf16[768,3072]{1,0:T(8,128)(2,1)} %refs_0_.1), channel_id=1, source_target_pairs={{0,1},{1,0},{2,3},{3,2},{4,5},{5,4},{6,7},{7,6},{8,9},{9,8},{10,11... | collective-permute-start | bytes 14155784 | tf_op jit(solution)/shard_map/ppermute | solution.py:364
  2.2 4.8 %copy-start = (bf16[256,1536]{1,0:T(8,128)(2,1)S(1)}, bf16[256,1536]{1,0:T(8,128)(2,1)}, u32[]{:S(2)}) copy-start(bf16[256,1536]{1,0:T(8,128)(2,1)} %keys.11) | copy-start | bytes 2359300
  2.2 4.8 %copy-start.1 = (bf16[256,1536]{1,0:T(8,128)(2,1)S(1)}, bf16[256,1536]{1,0:T(8,128)(2,1)}, u32[]{:S(2)}) copy-start(bf16[256,1536]{1,0:T(8,128)(2,1)} %values.11) | copy-start | bytes 2359300
  2.3 22.5 %collective-permute-start.5 = (bf16[512,768]{1,0:T(8,128)(2,1)S(1)}, bf16[512,768]{1,0:T(8,128)(2,1)S(1)}, u32[]{:S(2)}, u32[]{:S(2)}) collective-permute-start(bf16[512,768]{1,0:T(8,128)(2,1)S(1)} %pad_maximum_fusion), channel_id=1, source_target_pairs={{0,4},{4,8},{6,2},{8,12},{10,6},{14,10},{1,5},{5,9},{7,3},{9,13},{... | collective-permute-start | bytes 2359304 | tf_op jit(solution)/shard_map/ppermute | solution.py:361
  7.1 11.3 %collective-permute-start.1 = (bf16[512,384]{1,0:T(8,128)(2,1)S(1)}, bf16[512,384]{1,0:T(8,128)(2,1)S(1)}, u32[]{:S(2)}, u32[]{:S(2)}) collective-permute-start(bf16[512,384]{1,0:T(8,128)(2,1)S(1)} %pad_maximum_fusion.3), channel_id=1, source_target_pairs={{0,2},{2,0},{4,6},{6,4},{8,10},{10,8},{12,14},{14,12},{1,3},{3,1},... | collective-permute-start | bytes 1179656 | tf_op jit(solution)/shard_map/ppermute | solution.py:365
  7.3 14.8 %copy-start.2 = (bf16[256,1536]{1,0:T(8,128)(2,1)S(1)}, bf16[256,1536]{1,0:T(8,128)(2,1)}, u32[]{:S(2)}) copy-start(bf16[256,1536]{1,0:T(8,128)(2,1)} %query.5) | copy-start | bytes 2359300
  7.3 25.9 %collective-permute-start.9 = (bf16[512,768]{1,0:T(8,128)(2,1)S(1)}, bf16[512,768]{1,0:T(8,128)(2,1)S(1)}, u32[]{:S(2)}, u32[]{:S(2)}) collective-permute-start(bf16[512,768]{1,0:T(8,128)(2,1)S(1)} %pad_maximum_fusion.1), channel_id=1, source_target_pairs={{2,6},{4,0},{6,10},{8,4},{10,14},{12,8},{3,7},{5,1},{7,11},{9,5},{... | collective-permute-start | bytes 2359304 | tf_op jit(solution)/shard_map/ppermute | solution.py:362
  18.4 14.7 %collective-permute-start.6 = (bf16[512,384]{1,0:T(8,128)(2,1)S(1)}, bf16[512,384]{1,0:T(8,128)(2,1)S(1)}, u32[]{:S(2)}, u32[]{:S(2)}) collective-permute-start(bf16[512,384]{1,0:T(8,128)(2,1)S(1)} %collective-permute-done.1.refs_0_), channel_id=1, source_target_pairs={{0,4},{4,8},{6,2},{8,12},{10,6},{14,10},{1,5},{5,9},{7,3},{9,13},{... | collective-permute-start | bytes 1179656 | tf_op jit(solution)/shard_map/ppermute | solution.py:370
  24.7 34.0 %collective-permute-start.11 = (bf16[512,768]{1,0:T(8,128)(2,1)S(1)}, bf16[512,768]{1,0:T(8,128)(2,1)S(1)}, u32[]{:S(2)}, u32[]{:S(2)}) collective-permute-start(bf16[512,768]{1,0:T(8,128)(2,1)S(1)} %tie.9), channel_id=1, source_target_pairs={{0,4},{4,8},{6,2},{8,12},{10,6},{14,10},{1,5},{5,9},{7,3},{9,13},{... | collective-permute-start | bytes 2359304 | tf_op jit(solution)/shard_map/ppermute | solution.py:373
  29.2 13.9 %collective-permute-start.2 = (bf16[512,384]{1,0:T(8,128)(2,1)S(1)}, bf16[512,384]{1,0:T(8,128)(2,1)S(1)}, u32[]{:S(2)}, u32[]{:S(2)}) collective-permute-start(bf16[512,384]{1,0:T(8,128)(2,1)S(1)} %tie.5), channel_id=1, source_target_pairs={{2,6},{4,0},{6,10},{8,4},{10,14},{12,8},{3,7},{5,1},{7,11},{9,5},{... | collective-permute-start | bytes 1179656 | tf_op jit(solution)/shard_map/ppermute | solution.py:367
  30.5 19.1 %collective-permute-start.8 = (bf16[256,1536]{1,0:T(8,128)(2,1)S(1)}, bf16[256,1536]{1,0:T(8,128)(2,1)S(1)}, u32[]{:S(2)}, u32[]{:S(2)}) collective-permute-start(bf16[256,1536]{1,0:T(8,128)(2,1)S(1)} %tie.7), channel_id=1, source_target_pairs={{0,2},{2,0},{4,6},{6,4},{8,10},{10,8},{12,14},{14,12},{1,3},{3,1},... | collective-permute-start | bytes 2359304 | tf_op jit(solution)/shard_map/ppermute | solution.py:369
  33.2 28.2 %collective-permute-start.13 = (bf16[512,768]{1,0:T(8,128)(2,1)S(1)}, bf16[512,768]{1,0:T(8,128)(2,1)S(1)}, u32[]{:S(2)}, u32[]{:S(2)}) collective-permute-start(bf16[512,768]{1,0:T(8,128)(2,1)S(1)} %collective-permute-done.9.rest_1_.rest_2_), channel_id=1, source_target_pairs={{2,6},{4,0},{6,10},{8,4},{10,14},{12,8},{3,7},{5,1},{7,11},{9,5},{... | collective-permute-start | bytes 2359304 | tf_op jit(solution)/shard_map/ppermute | solution.py:371
  43.1 6.5 %collective-permute-start.3 = (bf16[256,1536]{1,0:T(8,128)(2,1)S(1)}, bf16[256,1536]{1,0:T(8,128)(2,1)S(1)}, u32[]{:S(2)}, u32[]{:S(2)}) collective-permute-start(bf16[256,1536]{1,0:T(8,128)(2,1)S(1)} %get-tuple-element.13), channel_id=1, source_target_pairs={{0,1},{1,0},{2,3},{3,2},{4,5},{5,4},{6,7},{7,6},{8,9},{9,8},{10,11... | collective-permute-start | bytes 2359304 | tf_op jit(solution)/shard_map/ppermute | solution.py:377
  43.1 10.2 %collective-permute-start.4 = (bf16[256,1536]{1,0:T(8,128)(2,1)S(1)}, bf16[256,1536]{1,0:T(8,128)(2,1)S(1)}, u32[]{:S(2)}, u32[]{:S(2)}) collective-permute-start(bf16[256,1536]{1,0:T(8,128)(2,1)S(1)} %get-tuple-element.14), channel_id=1, source_target_pairs={{0,1},{1,0},{2,3},{3,2},{4,5},{5,4},{6,7},{7,6},{8,9},{9,8},{10,11... | collective-permute-start | bytes 2359304 | tf_op jit(solution)/shard_map/ppermute | solution.py:378
  43.7 11.1 %copy-start.3 = (s32[8,8]{1,0:T(8,128)S(1)}, s32[8,8]{1,0:T(8,128)}, u32[]{:S(2)}) copy-start(s32[8,8]{1,0:T(8,128)} %table_ref.11) | copy-start | bytes 772
  49.6 11.8 %collective-permute-start.10 = (bf16[256,1536]{1,0:T(8,128)(2,1)S(1)}, bf16[256,1536]{1,0:T(8,128)(2,1)S(1)}, u32[]{:S(2)}, u32[]{:S(2)}) collective-permute-start(bf16[256,1536]{1,0:T(8,128)(2,1)S(1)} %tie.8), channel_id=1, source_target_pairs={{0,1},{1,0},{2,3},{3,2},{4,5},{5,4},{6,7},{7,6},{8,9},{9,8},{10,11... | collective-permute-start | bytes 2359304 | tf_op jit(solution)/shard_map/ppermute | solution.py:380
  49.6 18.4 %collective-permute-start.7 = (bf16[512,384]{1,0:T(8,128)(2,1)S(1)}, bf16[512,384]{1,0:T(8,128)(2,1)S(1)}, u32[]{:S(2)}, u32[]{:S(2)}) collective-permute-start(bf16[512,384]{1,0:T(8,128)(2,1)S(1)} %collective-permute-done.6.rest_1_), channel_id=1, source_target_pairs={{0,4},{4,8},{6,2},{8,12},{10,6},{14,10},{1,5},{5,9},{7,3},{9,13},{... | collective-permute-start | bytes 1179656 | tf_op jit(solution)/shard_map/ppermute | solution.py:374
  53.4 14.7 %collective-permute-start.15 = (bf16[512,384]{1,0:T(8,128)(2,1)S(1)}, bf16[512,384]{1,0:T(8,128)(2,1)S(1)}, u32[]{:S(2)}, u32[]{:S(2)}) collective-permute-start(bf16[512,384]{1,0:T(8,128)(2,1)S(1)} %collective-permute-done.2.refs_0_.rest_2_.rest_1_), channel_id=1, source_target_pairs={{2,6},{4,0},{6,10},{8,4},{10,14},{12,8},{3,7},{5,1},{7,11},{9,5},{... | collective-permute-start | bytes 1179656 | tf_op jit(solution)/shard_map/ppermute | solution.py:375
  58.8 9.3 %collective-permute-start.12 = (bf16[272,384]{1,0:T(8,128)(2,1)S(1)}, bf16[272,384]{1,0:T(8,128)(2,1)S(1)}, u32[]{:S(2)}, u32[]{:S(2)}) collective-permute-start(bf16[272,384]{1,0:T(8,128)(2,1)S(1)} %partner_part.3.rest_5_), channel_id=1, source_target_pairs={{0,2},{2,0},{4,6},{6,4},{8,10},{10,8},{12,14},{14,12},{1,3},{3,1},... | collective-permute-start | bytes 626696 | tf_op jit(solution)/shard_map/ppermute | solution.py:430
  65.1 16.3 %collective-permute-start.14 = (bf16[288,768]{1,0:T(8,128)(2,1)S(1)}, bf16[288,768]{1,0:T(8,128)(2,1)S(1)}, u32[]{:S(2)}, u32[]{:S(2)}) collective-permute-start(bf16[288,768]{1,0:T(8,128)(2,1)S(1)} %partner_part.4), channel_id=1, source_target_pairs={{0,2},{2,0},{4,6},{6,4},{8,10},{10,8},{12,14},{14,12},{1,3},{3,1},... | collective-permute-start | bytes 1327112 | tf_op jit(solution)/shard_map/ppermute | solution.py:431
  68.1 13.3 %slice-start = ((s8[4718592]{0:T(1024)(128)(4,1)}), s8[4194304]{0:T(1024)(128)(4,1)S(1)}, s32[]{:S(2)}) async-start(s8[4718592]{0:T(1024)(128)(4,1)} %bitcast), calls=%async_computation | async-start | bytes 8388608
  68.1 13.3 %slice-start.1 = ((s8[4718592]{0:T(1024)(128)(4,1)}), s8[524288]{0:T(1024)(128)(4,1)S(1)}, s32[]{:S(2)}) async-start(s8[4718592]{0:T(1024)(128)(4,1)} %bitcast), calls=%async_computation.1 | async-start | bytes 1048576
  70.6 10.8 %collective-permute-start.16 = (bf16[272,384]{1,0:T(8,128)(2,1)S(1)}, bf16[272,384]{1,0:T(8,128)(2,1)S(1)}, u32[]{:S(2)}, u32[]{:S(2)}) collective-permute-start(bf16[272,384]{1,0:T(8,128)(2,1)S(1)} %partner_part.5), channel_id=1, source_target_pairs={{0,2},{2,0},{4,6},{6,4},{8,10},{10,8},{12,14},{14,12},{1,3},{3,1},... | collective-permute-start | bytes 626696 | tf_op jit(solution)/shard_map/ppermute | solution.py:436

commit v8 on v7

--- a/solution.py
+++ b/solution.py
@@ -363,21 +363,19 @@
     own_weight = [out_weight]
     sib_weight = [lax.ppermute(out_weight, "head", core_moves)]
     cross = lax.ppermute(pack(0, 3), "frame", partner_moves)
-    (to_minor2,) = tie((cross, *sib_weight), pack(9, 12))
+    cross, to_minor2 = tie(sib_weight, cross, pack(9, 12))
     minor2 = lax.ppermute(to_minor2, "frame", near_moves)
-    (to_partner,) = tie(sib_weight, queries)
-    partner_query = lax.ppermute(to_partner, "frame", partner_moves)
+    partner_query = lax.ppermute(queries, "frame", partner_moves)
     major2 = lax.ppermute(cross, "frame", away_moves)
     minor3 = lax.ppermute(minor1, "frame", near_moves)
     (to_major3,) = tie((major1,), pack(6, 12))
     major3 = lax.ppermute(to_major3, "frame", away_moves)
     major4 = lax.ppermute(major2, "frame", away_moves)
     minor4 = lax.ppermute(minor2, "frame", near_moves)
-    to_sib_keys, to_sib_values = tie((minor2,), key_tokens, value_tokens)
+    to_sib_keys, to_sib_values = tie((major2,), key_tokens, value_tokens)
     sib_keys = lax.ppermute(to_sib_keys, "head", core_moves)
     sib_values = lax.ppermute(to_sib_values, "head", core_moves)
-    (to_nearest,) = tie((partner_query,), firsts(minor1, minor2, major2))
-    nearest = lax.ppermute(to_nearest, "head", core_moves)
+    nearest = lax.ppermute(firsts(minor1, minor2, major2), "head", core_moves)
     refs = {
         "major1": major1,
         "major2": major2,

time: 86.9 us -> 82.1 us (0.945)
  waiting for transfers between devices: 33.2 us -> 29.8 us
  starting transfers between devices: 30.2 us -> 28.5 us
    ppermute x1, waiting for transfers between devices: 0.01 us -> 6.19 us  [per_device(): minor3 = lax.ppermute(minor1, 'frame', near_moves)]
    ppermute x2, waiting for transfers between devices: 5.86 us -> 0.01 us  [the longest x1 0.01 us: per_device(): partner_query = lax.ppermute(queries, 'frame', partner_moves)]
    ppermute x1, waiting for transfers between devices: 6.39 us -> 2.8 us  [per_device(): part_high = lax.ppermute(part_high, 'frame', partner_moves)]
    ppermute x1, starting transfers between devices: 0.07 us -> 2.65 us  [per_device(): cross = lax.ppermute(pack(0, 3), 'frame', partner_moves)]
    ppermute x1, waiting for transfers between devices: 2.56 us -> 0.39 us  [per_device(): major1 = lax.ppermute(pack(0, 6), 'frame', away_moves)]
    ppermute x2, starting transfers between devices: 2.63 us -> 0.64 us  [the longest x1 0.57 us: per_device(): nearest = lax.ppermute(firsts(minor1, minor2, major2), 'head', core_moves)]
    ppermute x1, waiting for transfers between devices: 0.04 us -> 1.79 us  [per_device(): major2 = lax.ppermute(cross, 'frame', away_moves)]
    ppermute x1, starting transfers between devices: 2.63 us -> 1.06 us  [per_device(): part_low = lax.ppermute(part_low, 'frame', partner_moves)]
  transfers between devices with their start and end apart: 17 -> 17, of which waited for: 5 -> 6; matrix products, arithmetic and copies ran while one was open for 3% -> 3% of each run, Pallas kernels for 18% -> 19%
where the time goes in v8:
time: 82.1 us; the launch traced here: 81.8 us
  waiting for transfers between devices  29.8 us (36%)
  starting transfers between devices  28.5 us (35%)
  Pallas kernels  20.8 us (25%)
  local copies, waits for them, and re-layouts  2.04 us (2%)
    pallas_call x6, Pallas kernels, run(): pl.pallas_call(body, grid=(1,), in_specs=[pl.BlockSpec(memory_space=pltpu...  15.5 us
    ppermute x1, waiting for transfers between devices, per_device(): minor2 = lax.ppermute(to_minor2, 'frame', near_moves)  9.48 us
    ppermute x1, waiting for transfers between devices, per_device(): cross = lax.ppermute(pack(0, 3), 'frame', partner_moves)  9.17 us
    ppermute x1, waiting for transfers between devices, per_device(): minor3 = lax.ppermute(minor1, 'frame', near_moves)  6.19 us
    pallas_call x1, Pallas kernels, project(): pl.pallas_call(functools.partial(project_kernel, own_groups, part_groups,...  5.23 us
    ppermute x1, starting transfers between devices, per_device(): major1 = lax.ppermute(pack(0, 6), 'frame', away_moves)  4.66 us
    ppermute x1, starting transfers between devices, per_device(): major3 = lax.ppermute(to_major3, 'frame', away_moves)  4.42 us
    ppermute x1, starting transfers between devices, per_device(): major2 = lax.ppermute(cross, 'frame', away_moves)  3.71 us
  transfers between devices with their start and end apart: 17, of which 6 were waited for; matrix products, arithmetic and copies ran while one was open for 3% of the time, Pallas kernels for 19%

profile of v8, /device:TPU:0, one launch (start us, length us, event | category | flops | bytes accessed | tf_op | source)
XLA Modules:
  0.0 81.8 jit_solution(12282085157301825217)
XLA Ops:
  0.0 0.5 collective-permute-start
  0.5 1.7 %fusion = (bf16[256,768]{1,0:T(8,128)(2,1)S(1)}, bf16[256,768]{1,0:T(8,128)(2,1)S(1)}, bf16[256,768]{1,0:T(8,128)(2,1)S(1)}, bf16[256,768]{1,0:T(8,128)(2,1)S(1)...) fusion(bf16[256,1536]{1,0:T(8,128)(2,1)} %keys.11, bf16[256,1536]{1,0:T(8,128)(2,1)} %values.11), kind=kLoop, calls=%fused_computation.6 | loop fusion | bytes 4718592 | tf_op jit(solution)/shard_map/slice | solution.py:353
  2.2 0.1 pad_maximum_fusion
  2.3 4.7 %collective-permute-start.5 = (bf16[512,768]{1,0:T(8,128)(2,1)S(1)}, bf16[512,768]{1,0:T(8,128)(2,1)S(1)}, u32[]{:S(2)}, u32[]{:S(2)}) collective-permute-start(bf16[512,768]{1,0:T(8,128)(2,1)S(1)} %pad_maximum_fusion), channel_id=1, source_target_pairs={{0,4},{4,8},{6,2},{8,12},{10,6},{14,10},{1,5},{5,9},{7,3},{9,13},{... | collective-permute-start | bytes 2359304 | tf_op jit(solution)/shard_map/ppermute | solution.py:361
  7.0 0.1 pad_maximum_fusion.1
  7.0 1.3 %collective-permute-start.7 = (bf16[512,768]{1,0:T(8,128)(2,1)S(1)}, bf16[512,768]{1,0:T(8,128)(2,1)S(1)}, u32[]{:S(2)}, u32[]{:S(2)}) collective-permute-start(bf16[512,768]{1,0:T(8,128)(2,1)S(1)} %pad_maximum_fusion.1), channel_id=1, source_target_pairs={{2,6},{4,0},{6,10},{8,4},{10,14},{12,8},{3,7},{5,1},{7,11},{9,5},{... | collective-permute-start | bytes 2359304 | tf_op jit(solution)/shard_map/ppermute | solution.py:362
  8.3 0.1 fusion.3
  8.5 2.7 %collective-permute-start.1 = (bf16[512,384]{1,0:T(8,128)(2,1)S(1)}, bf16[512,384]{1,0:T(8,128)(2,1)S(1)}, u32[]{:S(2)}, u32[]{:S(2)}) collective-permute-start(bf16[512,384]{1,0:T(8,128)(2,1)S(1)} %pad_maximum_fusion.3), channel_id=1, source_target_pairs={{0,2},{2,0},{4,6},{6,4},{8,10},{10,8},{12,14},{14,12},{1,3},{3,1},... | collective-permute-start | bytes 1179656 | tf_op jit(solution)/shard_map/ppermute | solution.py:365
  11.2 9.2 %collective-permute-done.1.refs_1_ = bf16[512,384]{1,0:T(8,128)(2,1)S(1)} collective-permute-done((bf16[512,384]{1,0:T(8,128)(2,1)S(1)}, bf16[512,384]{1,0:T(8,128)(2,1)S(1)}, u32[]{:S(2)}, u32[]{:S(2)}) %collective-permute-start.1) | collective-permute-done | bytes 393248 | tf_op jit(solution)/shard_map/ppermute | solution.py:365
  20.4 3.7 %collective-permute-start.2 = (bf16[512,384]{1,0:T(8,128)(2,1)S(1)}, bf16[512,384]{1,0:T(8,128)(2,1)S(1)}, u32[]{:S(2)}, u32[]{:S(2)}) collective-permute-start(bf16[512,384]{1,0:T(8,128)(2,1)S(1)} %get-tuple-element.15), channel_id=1, source_target_pairs={{0,4},{4,8},{6,2},{8,12},{10,6},{14,10},{1,5},{5,9},{7,3},{9,13},{... | collective-permute-start | bytes 1179656 | tf_op jit(solution)/shard_map/ppermute | solution.py:369
  24.1 0.1 collective-permute-start.11
  24.4 0.4 collective-permute-done.5.rest_0_.refs_0_
  24.7 4.4 %collective-permute-start.10 = (bf16[512,768]{1,0:T(8,128)(2,1)S(1)}, bf16[512,768]{1,0:T(8,128)(2,1)S(1)}, u32[]{:S(2)}, u32[]{:S(2)}) collective-permute-start(bf16[512,768]{1,0:T(8,128)(2,1)S(1)} %tie.5), channel_id=1, source_target_pairs={{0,4},{4,8},{6,2},{8,12},{10,6},{14,10},{1,5},{5,9},{7,3},{9,13},{... | collective-permute-start | bytes 2359304 | tf_op jit(solution)/shard_map/ppermute | solution.py:372
  29.2 1.3 %collective-permute-start.8 = (bf16[512,384]{1,0:T(8,128)(2,1)S(1)}, bf16[512,384]{1,0:T(8,128)(2,1)S(1)}, u32[]{:S(2)}, u32[]{:S(2)}) collective-permute-start(bf16[512,384]{1,0:T(8,128)(2,1)S(1)} %get-tuple-element.18), channel_id=1, source_target_pairs={{2,6},{4,0},{6,10},{8,4},{10,14},{12,8},{3,7},{5,1},{7,11},{9,5},{... | collective-permute-start | bytes 1179656 | tf_op jit(solution)/shard_map/ppermute | solution.py:367
  30.5 1.3 %collective-permute-start.13 = (bf16[512,768]{1,0:T(8,128)(2,1)S(1)}, bf16[512,768]{1,0:T(8,128)(2,1)S(1)}, u32[]{:S(2)}, u32[]{:S(2)}) collective-permute-start(bf16[512,768]{1,0:T(8,128)(2,1)S(1)} %collective-permute-done.7.rest_1_.rest_2_), channel_id=1, source_target_pairs={{2,6},{4,0},{6,10},{8,4},{10,14},{12,8},{3,7},{5,1},{7,11},{9,5},{... | collective-permute-start | bytes 2359304 | tf_op jit(solution)/shard_map/ppermute | solution.py:370
  31.8 1.8 %collective-permute-done.2.refs_0_.rest_1_ = bf16[512,384]{1,0:T(8,128)(2,1)S(1)} collective-permute-done((bf16[512,384]{1,0:T(8,128)(2,1)S(1)}, bf16[512,384]{1,0:T(8,128)(2,1)S(1)}, u32[]{:S(2)}, u32[]{:S(2)}) %collective-permute-start.2) | collective-permute-done | bytes 393248 | tf_op jit(solution)/shard_map/ppermute | solution.py:369
  33.6 9.5 %collective-permute-done.8.rest_2_.rest_1_ = bf16[512,384]{1,0:T(8,128)(2,1)S(1)} collective-permute-done((bf16[512,384]{1,0:T(8,128)(2,1)S(1)}, bf16[512,384]{1,0:T(8,128)(2,1)S(1)}, u32[]{:S(2)}, u32[]{:S(2)}) %collective-permute-start.8) | collective-permute-done | bytes 393248 | tf_op jit(solution)/shard_map/ppermute | solution.py:367
  43.2 0.1 maximum_maximum_fusion
  43.2 0.6 collective-permute-start.9
  43.8 3.4 %collective-permute-start.6 = (bf16[512,384]{1,0:T(8,128)(2,1)S(1)}, bf16[512,384]{1,0:T(8,128)(2,1)S(1)}, u32[]{:S(2)}, u32[]{:S(2)}) collective-permute-start(bf16[512,384]{1,0:T(8,128)(2,1)S(1)} %collective-permute-done.2.refs_0_.rest_1_), channel_id=1, source_target_pairs={{0,4},{4,8},{6,2},{8,12},{10,6},{14,10},{1,5},{5,9},{7,3},{9,13},{... | collective-permute-start | bytes 1179656 | tf_op jit(solution)/shard_map/ppermute | solution.py:373
  47.3 1.5 %collective-permute-start.15 = (bf16[512,384]{1,0:T(8,128)(2,1)S(1)}, bf16[512,384]{1,0:T(8,128)(2,1)S(1)}, u32[]{:S(2)}, u32[]{:S(2)}) collective-permute-start(bf16[512,384]{1,0:T(8,128)(2,1)S(1)} %collective-permute-done.8.rest_2_.rest_1_), channel_id=1, source_target_pairs={{2,6},{4,0},{6,10},{8,4},{10,14},{12,8},{3,7},{5,1},{7,11},{9,5},{... | collective-permute-start | bytes 1179656 | tf_op jit(solution)/shard_map/ppermute | solution.py:374
  48.8 2.0 %own_part.4 = (f32[256,384]{1,0:T(8,128)S(1)}, f32[256,128]{1,0:T(8,128)S(1)}) custom-call(s32[8,8]{1,0:T(8,128)S(1)} %copy-done.3, bf16[256,1536]{1,0:T(8,128)(2,1)S(1)} %copy-done.2, bf16[256,1536]{1,0:T(8,128)(2,1)S(1)} %copy-done, bf16[256,1536]{1,0:T(8,128)(2,1)S(1)} %copy-done.1, bf16[256,1536]{1,0:T(8,128)(2,1)S(1)} %collective-permute-done.3.sib_keys, ...), custom_call_target="tpu_custom_call" | custom-call | flops 301989888 | bytes 1048576 | tf_op jit(solution)/shard_map/own_part/pallas_call | solution.py:285
  50.7 2.0 %partner_part.3.rest_5_ = bf16[272,384]{1,0:T(8,128)(2,1)S(1)} custom-call(s32[8,8]{1,0:T(8,128)S(1)} %copy-done.3, bf16[256,1536]{1,0:T(8,128)(2,1)S(1)} %collective-permute-done.11.query, bf16[256,1536]{1,0:T(8,128)(2,1)S(1)} %copy-done, bf16[256,1536]{1,0:T(8,128)(2,1)S(1)} %copy-done.1, bf16[256,1536]{1,0:T(8,128)(2,1)S(1)} %collective-permute-done.3.sib_keys, ...), custom_call_target="tpu_custom_call" | custom-call | flops 301989888 | bytes 1048576 | tf_op jit(solution)/shard_map/partner_part/pallas_call | solution.py:285
  52.7 1.1 %collective-permute-start.12 = (bf16[272,384]{1,0:T(8,128)(2,1)S(1)}, bf16[272,384]{1,0:T(8,128)(2,1)S(1)}, u32[]{:S(2)}, u32[]{:S(2)}) collective-permute-start(bf16[272,384]{1,0:T(8,128)(2,1)S(1)} %partner_part.3.rest_5_), channel_id=1, source_target_pairs={{0,2},{2,0},{4,6},{6,4},{8,10},{10,8},{12,14},{14,12},{1,3},{3,1},... | collective-permute-start | bytes 626696 | tf_op jit(solution)/shard_map/ppermute | solution.py:428
  53.8 6.2 %collective-permute-done.13.rest_3_ = bf16[512,768]{1,0:T(8,128)(2,1)S(1)} collective-permute-done((bf16[512,768]{1,0:T(8,128)(2,1)S(1)}, bf16[512,768]{1,0:T(8,128)(2,1)S(1)}, u32[]{:S(2)}, u32[]{:S(2)}) %collective-permute-start.13) | collective-permute-done | bytes 786464 | tf_op jit(solution)/shard_map/ppermute | solution.py:370
  60.0 3.7 %partner_part.4 = bf16[288,768]{1,0:T(8,128)(2,1)S(1)} custom-call(s32[8,8]{1,0:T(8,128)S(1)} %copy-done.3, bf16[256,1536]{1,0:T(8,128)(2,1)S(1)} %collective-permute-done.11.query, bf16[256,1536]{1,0:T(8,128)(2,1)S(1)} %copy-done, bf16[256,1536]{1,0:T(8,128)(2,1)S(1)} %copy-done.1, bf16[256,1536]{1,0:T(8,128)(2,1)S(1)} %collective-permute-done.3.sib_keys, ...), custom_call_target="tpu_custom_call" | custom-call | flops 603979776 | bytes 1048576 | tf_op jit(solution)/shard_map/partner_part/pallas_call | solution.py:285
  63.7 3.0 %own_part.5 = (f32[256,768]{1,0:T(8,128)S(1)}, f32[256,128]{1,0:T(8,128)S(1)}) custom-call(s32[8,8]{1,0:T(8,128)S(1)} %copy-done.3, bf16[256,1536]{1,0:T(8,128)(2,1)S(1)} %copy-done.2, bf16[256,1536]{1,0:T(8,128)(2,1)S(1)} %copy-done, bf16[256,1536]{1,0:T(8,128)(2,1)S(1)} %copy-done.1, bf16[256,1536]{1,0:T(8,128)(2,1)S(1)} %collective-permute-done.3.sib_keys, ...), custom_call_target="tpu_custom_call" | custom-call | flops 603979776 | bytes 1048576 | tf_op jit(solution)/shard_map/own_part/pallas_call | solution.py:285
  66.8 2.4 %partner_part.5 = bf16[272,384]{1,0:T(8,128)(2,1)S(1)} custom-call(s32[8,8]{1,0:T(8,128)S(1)} %copy-done.3, bf16[256,1536]{1,0:T(8,128)(2,1)S(1)} %collective-permute-done.11.query, bf16[256,1536]{1,0:T(8,128)(2,1)S(1)} %copy-done, bf16[256,1536]{1,0:T(8,128)(2,1)S(1)} %copy-done.1, bf16[256,1536]{1,0:T(8,128)(2,1)S(1)} %collective-permute-done.3.sib_keys, ...), custom_call_target="tpu_custom_call" | custom-call | flops 301989888 | bytes 1048576 | tf_op jit(solution)/shard_map/partner_part/pallas_call | solution.py:285
  69.2 2.0 %collective-permute-start.16 = (bf16[272,384]{1,0:T(8,128)(2,1)S(1)}, bf16[272,384]{1,0:T(8,128)(2,1)S(1)}, u32[]{:S(2)}, u32[]{:S(2)}) collective-permute-start(bf16[272,384]{1,0:T(8,128)(2,1)S(1)} %partner_part.5), channel_id=1, source_target_pairs={{0,2},{2,0},{4,6},{6,4},{8,10},{10,8},{12,14},{14,12},{1,3},{3,1},... | collective-permute-start | bytes 626696 | tf_op jit(solution)/shard_map/ppermute | solution.py:434
  71.3 2.4 %own_part.3 = (f32[256,384]{1,0:T(8,128)S(1)}, f32[256,128]{1,0:T(8,128)S(1)}) custom-call(s32[8,8]{1,0:T(8,128)S(1)} %copy-done.3, bf16[256,1536]{1,0:T(8,128)(2,1)S(1)} %copy-done.2, bf16[256,1536]{1,0:T(8,128)(2,1)S(1)} %copy-done, bf16[256,1536]{1,0:T(8,128)(2,1)S(1)} %copy-done.1, bf16[256,1536]{1,0:T(8,128)(2,1)S(1)} %collective-permute-done.3.sib_keys, ...), custom_call_target="tpu_custom_call" | custom-call | flops 301989888 | bytes 1048576 | tf_op jit(solution)/shard_map/own_part/pallas_call | solution.py:285
  73.7 2.8 %collective-permute-done.16.refs_10_ = bf16[272,384]{1,0:T(8,128)(2,1)S(1)} collective-permute-done((bf16[272,384]{1,0:T(8,128)(2,1)S(1)}, bf16[272,384]{1,0:T(8,128)(2,1)S(1)}, u32[]{:S(2)}, u32[]{:S(2)}) %collective-permute-start.16) | collective-permute-done | bytes 208928 | tf_op jit(solution)/shard_map/ppermute | solution.py:434
  76.5 5.2 %merge_and_project.1 = bf16[256,3072]{1,0:T(8,128)(2,1)} custom-call(bf16[768,3072]{1,0:T(8,128)(2,1)S(1)} %bitcast.1, bf16[768,3072]{1,0:T(8,128)(2,1)S(1)} %collective-permute-done.refs_0_.rest_7_.refs_1_, f32[256,384]{1,0:T(8,128)S(1)} %get-tuple-element.19.refs_2_, f32[256,128]{1,0:T(8,128)S(1)} %get-tuple-element.20.refs_3_, ...), custom_call_target="tpu_custom_call" | custom-call | flops 2415919104 | bytes 12582912 | tf_op jit(solution)/shard_map/merge_and_project/pallas_call | solution.py:322
  (38 shorter events, 0.4 us)
Async XLA Ops:
  0.0 20.4 %collective-permute-start = (bf16[768,3072]{1,0:T(8,128)(2,1)}, bf16[768,3072]{1,0:T(8,128)(2,1)S(1)}, u32[]{:S(2)}, u32[]{:S(2)}) collective-permute-start(bf16[768,3072]{1,0:T(8,128)(2,1)} %refs_0_.1), channel_id=1, source_target_pairs={{0,1},{1,0},{2,3},{3,2},{4,5},{5,4},{6,7},{7,6},{8,9},{9,8},{10,11... | collective-permute-start | bytes 14155784 | tf_op jit(solution)/shard_map/ppermute | solution.py:364
  2.2 6.1 %copy-start = (bf16[256,1536]{1,0:T(8,128)(2,1)S(1)}, bf16[256,1536]{1,0:T(8,128)(2,1)}, u32[]{:S(2)}) copy-start(bf16[256,1536]{1,0:T(8,128)(2,1)} %keys.11) | copy-start | bytes 2359300
  2.2 6.1 %copy-start.1 = (bf16[256,1536]{1,0:T(8,128)(2,1)S(1)}, bf16[256,1536]{1,0:T(8,128)(2,1)}, u32[]{:S(2)}) copy-start(bf16[256,1536]{1,0:T(8,128)(2,1)} %values.11) | copy-start | bytes 2359300
  2.3 22.5 %collective-permute-start.5 = (bf16[512,768]{1,0:T(8,128)(2,1)S(1)}, bf16[512,768]{1,0:T(8,128)(2,1)S(1)}, u32[]{:S(2)}, u32[]{:S(2)}) collective-permute-start(bf16[512,768]{1,0:T(8,128)(2,1)S(1)} %pad_maximum_fusion), channel_id=1, source_target_pairs={{0,4},{4,8},{6,2},{8,12},{10,6},{14,10},{1,5},{5,9},{7,3},{9,13},{... | collective-permute-start | bytes 2359304 | tf_op jit(solution)/shard_map/ppermute | solution.py:361
  7.0 23.5 %collective-permute-start.7 = (bf16[512,768]{1,0:T(8,128)(2,1)S(1)}, bf16[512,768]{1,0:T(8,128)(2,1)S(1)}, u32[]{:S(2)}, u32[]{:S(2)}) collective-permute-start(bf16[512,768]{1,0:T(8,128)(2,1)S(1)} %pad_maximum_fusion.1), channel_id=1, source_target_pairs={{2,6},{4,0},{6,10},{8,4},{10,14},{12,8},{3,7},{5,1},{7,11},{9,5},{... | collective-permute-start | bytes 2359304 | tf_op jit(solution)/shard_map/ppermute | solution.py:362
  8.5 11.9 %collective-permute-start.1 = (bf16[512,384]{1,0:T(8,128)(2,1)S(1)}, bf16[512,384]{1,0:T(8,128)(2,1)S(1)}, u32[]{:S(2)}, u32[]{:S(2)}) collective-permute-start(bf16[512,384]{1,0:T(8,128)(2,1)S(1)} %pad_maximum_fusion.3), channel_id=1, source_target_pairs={{0,2},{2,0},{4,6},{6,4},{8,10},{10,8},{12,14},{14,12},{1,3},{3,1},... | collective-permute-start | bytes 1179656 | tf_op jit(solution)/shard_map/ppermute | solution.py:365
  11.2 12.9 %copy-start.2 = (bf16[256,1536]{1,0:T(8,128)(2,1)S(1)}, bf16[256,1536]{1,0:T(8,128)(2,1)}, u32[]{:S(2)}) copy-start(bf16[256,1536]{1,0:T(8,128)(2,1)} %query.5) | copy-start | bytes 2359300
  20.4 13.3 %collective-permute-start.2 = (bf16[512,384]{1,0:T(8,128)(2,1)S(1)}, bf16[512,384]{1,0:T(8,128)(2,1)S(1)}, u32[]{:S(2)}, u32[]{:S(2)}) collective-permute-start(bf16[512,384]{1,0:T(8,128)(2,1)S(1)} %get-tuple-element.15), channel_id=1, source_target_pairs={{0,4},{4,8},{6,2},{8,12},{10,6},{14,10},{1,5},{5,9},{7,3},{9,13},{... | collective-permute-start | bytes 1179656 | tf_op jit(solution)/shard_map/ppermute | solution.py:369
  24.1 19.1 %collective-permute-start.11 = (bf16[256,1536]{1,0:T(8,128)(2,1)S(1)}, bf16[256,1536]{1,0:T(8,128)(2,1)S(1)}, u32[]{:S(2)}, u32[]{:S(2)}) collective-permute-start(bf16[256,1536]{1,0:T(8,128)(2,1)S(1)} %copy-done.2), channel_id=1, source_target_pairs={{0,2},{2,0},{4,6},{6,4},{8,10},{10,8},{12,14},{14,12},{1,3},{3,1},... | collective-permute-start | bytes 2359304 | tf_op jit(solution)/shard_map/ppermute | solution.py:368
  24.7 28.0 %collective-permute-start.10 = (bf16[512,768]{1,0:T(8,128)(2,1)S(1)}, bf16[512,768]{1,0:T(8,128)(2,1)S(1)}, u32[]{:S(2)}, u32[]{:S(2)}) collective-permute-start(bf16[512,768]{1,0:T(8,128)(2,1)S(1)} %tie.5), channel_id=1, source_target_pairs={{0,4},{4,8},{6,2},{8,12},{10,6},{14,10},{1,5},{5,9},{7,3},{9,13},{... | collective-permute-start | bytes 2359304 | tf_op jit(solution)/shard_map/ppermute | solution.py:372
  29.2 13.9 %collective-permute-start.8 = (bf16[512,384]{1,0:T(8,128)(2,1)S(1)}, bf16[512,384]{1,0:T(8,128)(2,1)S(1)}, u32[]{:S(2)}, u32[]{:S(2)}) collective-permute-start(bf16[512,384]{1,0:T(8,128)(2,1)S(1)} %get-tuple-element.18), channel_id=1, source_target_pairs={{2,6},{4,0},{6,10},{8,4},{10,14},{12,8},{3,7},{5,1},{7,11},{9,5},{... | collective-permute-start | bytes 1179656 | tf_op jit(solution)/shard_map/ppermute | solution.py:367
  30.5 29.5 %collective-permute-start.13 = (bf16[512,768]{1,0:T(8,128)(2,1)S(1)}, bf16[512,768]{1,0:T(8,128)(2,1)S(1)}, u32[]{:S(2)}, u32[]{:S(2)}) collective-permute-start(bf16[512,768]{1,0:T(8,128)(2,1)S(1)} %collective-permute-done.7.rest_1_.rest_2_), channel_id=1, source_target_pairs={{2,6},{4,0},{6,10},{8,4},{10,14},{12,8},{3,7},{5,1},{7,11},{9,5},{... | collective-permute-start | bytes 2359304 | tf_op jit(solution)/shard_map/ppermute | solution.py:370
  33.6 15.1 %copy-start.3 = (s32[8,8]{1,0:T(8,128)S(1)}, s32[8,8]{1,0:T(8,128)}, u32[]{:S(2)}) copy-start(s32[8,8]{1,0:T(8,128)} %table_ref.11) | copy-start | bytes 772
  33.6 10.2 %collective-permute-start.3 = (bf16[256,1536]{1,0:T(8,128)(2,1)S(1)}, bf16[256,1536]{1,0:T(8,128)(2,1)S(1)}, u32[]{:S(2)}, u32[]{:S(2)}) collective-permute-start(bf16[256,1536]{1,0:T(8,128)(2,1)S(1)} %get-tuple-element.16), channel_id=1, source_target_pairs={{0,1},{1,0},{2,3},{3,2},{4,5},{5,4},{6,7},{7,6},{8,9},{9,8},{10,11... | collective-permute-start | bytes 2359304 | tf_op jit(solution)/shard_map/ppermute | solution.py:376
  43.1 4.1 %collective-permute-start.4 = (bf16[256,1536]{1,0:T(8,128)(2,1)S(1)}, bf16[256,1536]{1,0:T(8,128)(2,1)S(1)}, u32[]{:S(2)}, u32[]{:S(2)}) collective-permute-start(bf16[256,1536]{1,0:T(8,128)(2,1)S(1)} %get-tuple-element.17), channel_id=1, source_target_pairs={{0,1},{1,0},{2,3},{3,2},{4,5},{5,4},{6,7},{7,6},{8,9},{9,8},{10,11... | collective-permute-start | bytes 2359304 | tf_op jit(solution)/shard_map/ppermute | solution.py:377
  43.2 16.7 %collective-permute-start.9 = (bf16[256,1536]{1,0:T(8,128)(2,1)S(1)}, bf16[256,1536]{1,0:T(8,128)(2,1)S(1)}, u32[]{:S(2)}, u32[]{:S(2)}) collective-permute-start(bf16[256,1536]{1,0:T(8,128)(2,1)S(1)} %maximum_maximum_fusion), channel_id=1, source_target_pairs={{0,1},{1,0},{2,3},{3,2},{4,5},{5,4},{6,7},{7,6},{8,9},{9,8},{10,11... | collective-permute-start | bytes 2359304 | tf_op jit(solution)/shard_map/ppermute | solution.py:378
  43.8 22.9 %collective-permute-start.6 = (bf16[512,384]{1,0:T(8,128)(2,1)S(1)}, bf16[512,384]{1,0:T(8,128)(2,1)S(1)}, u32[]{:S(2)}, u32[]{:S(2)}) collective-permute-start(bf16[512,384]{1,0:T(8,128)(2,1)S(1)} %collective-permute-done.2.refs_0_.rest_1_), channel_id=1, source_target_pairs={{0,4},{4,8},{6,2},{8,12},{10,6},{14,10},{1,5},{5,9},{7,3},{9,13},{... | collective-permute-start | bytes 1179656 | tf_op jit(solution)/shard_map/ppermute | solution.py:373
  47.3 19.5 %collective-permute-start.15 = (bf16[512,384]{1,0:T(8,128)(2,1)S(1)}, bf16[512,384]{1,0:T(8,128)(2,1)S(1)}, u32[]{:S(2)}, u32[]{:S(2)}) collective-permute-start(bf16[512,384]{1,0:T(8,128)(2,1)S(1)} %collective-permute-done.8.rest_2_.rest_1_), channel_id=1, source_target_pairs={{2,6},{4,0},{6,10},{8,4},{10,14},{12,8},{3,7},{5,1},{7,11},{9,5},{... | collective-permute-start | bytes 1179656 | tf_op jit(solution)/shard_map/ppermute | solution.py:374
  52.7 14.0 %collective-permute-start.12 = (bf16[272,384]{1,0:T(8,128)(2,1)S(1)}, bf16[272,384]{1,0:T(8,128)(2,1)S(1)}, u32[]{:S(2)}, u32[]{:S(2)}) collective-permute-start(bf16[272,384]{1,0:T(8,128)(2,1)S(1)} %partner_part.3.rest_5_), channel_id=1, source_target_pairs={{0,2},{2,0},{4,6},{6,4},{8,10},{10,8},{12,14},{14,12},{1,3},{3,1},... | collective-permute-start | bytes 626696 | tf_op jit(solution)/shard_map/ppermute | solution.py:428
  63.7 12.8 %collective-permute-start.14 = (bf16[288,768]{1,0:T(8,128)(2,1)S(1)}, bf16[288,768]{1,0:T(8,128)(2,1)S(1)}, u32[]{:S(2)}, u32[]{:S(2)}) collective-permute-start(bf16[288,768]{1,0:T(8,128)(2,1)S(1)} %partner_part.4), channel_id=1, source_target_pairs={{0,2},{2,0},{4,6},{6,4},{8,10},{10,8},{12,14},{14,12},{1,3},{3,1},... | collective-permute-start | bytes 1327112 | tf_op jit(solution)/shard_map/ppermute | solution.py:429
  66.8 9.7 %slice-start = ((s8[4718592]{0:T(1024)(128)(4,1)}), s8[4194304]{0:T(1024)(128)(4,1)S(1)}, s32[]{:S(2)}) async-start(s8[4718592]{0:T(1024)(128)(4,1)} %bitcast), calls=%async_computation | async-start | bytes 8388608
  66.8 9.7 %slice-start.1 = ((s8[4718592]{0:T(1024)(128)(4,1)}), s8[524288]{0:T(1024)(128)(4,1)S(1)}, s32[]{:S(2)}) async-start(s8[4718592]{0:T(1024)(128)(4,1)} %bitcast), calls=%async_computation.1 | async-start | bytes 1048576
  69.2 7.3 %collective-permute-start.16 = (bf16[272,384]{1,0:T(8,128)(2,1)S(1)}, bf16[272,384]{1,0:T(8,128)(2,1)S(1)}, u32[]{:S(2)}, u32[]{:S(2)}) collective-permute-start(bf16[272,384]{1,0:T(8,128)(2,1)S(1)} %partner_part.5), channel_id=1, source_target_pairs={{0,2},{2,0},{4,6},{6,4},{8,10},{10,8},{12,14},{14,12},{1,3},{3,1},... | collective-permute-start | bytes 626696 | tf_op jit(solution)/shard_map/ppermute | solution.py:434

commit v9 on v8

--- a/solution.py
+++ b/solution.py
@@ -372,7 +372,7 @@
     major3 = lax.ppermute(to_major3, "frame", away_moves)
     major4 = lax.ppermute(major2, "frame", away_moves)
     minor4 = lax.ppermute(minor2, "frame", near_moves)
-    to_sib_keys, to_sib_values = tie((major2,), key_tokens, value_tokens)
+    to_sib_keys, to_sib_values = tie((major2, minor2), key_tokens, value_tokens)
     sib_keys = lax.ppermute(to_sib_keys, "head", core_moves)
     sib_values = lax.ppermute(to_sib_values, "head", core_moves)
     nearest = lax.ppermute(firsts(minor1, minor2, major2), "head", core_moves)
@@ -422,12 +422,12 @@
     part_groups = ((0, 3), (3, 9), (9, 12))
     part_low = partner_part((0, 3), ("major1", "major2"))
     own_early = own_part((3, 6), ("major1", "minor1"))
+    own_late = own_part((6, 12), ("major3", "minor1", "minor2"))
     part_middle = partner_part(
-        (3, 9), ("major1", "major3", "minor1", "minor3", "nearest"), (part_low, own_early[1])
+        (3, 9), ("major1", "major3", "minor1", "minor3", "nearest"), (part_low, own_early[1], own_late[1])
     )
     part_low = lax.ppermute(part_low, "frame", partner_moves)
     part_middle = lax.ppermute(part_middle, "frame", partner_moves)
-    own_late = own_part((6, 12), ("major3", "minor1", "minor2"))
     part_high = partner_part(
         (9, 12), ("major3", "minor2", "minor4", "nearest"), (own_late[1], major4, part_low, *sib_weight)
     )

time: 82.1 us -> 84.7 us (1.032)
  starting transfers between devices: 28.5 us -> 31.9 us
    ppermute x1, waiting for transfers between devices: 2.8 us -> 9.27 us  [per_device(): part_high = lax.ppermute(part_high, 'frame', partner_moves)]
    ppermute x1, waiting for transfers between devices: 6.19 us -> 0.01 us  [per_device(): minor3 = lax.ppermute(minor1, 'frame', near_moves)]
    ppermute x1, waiting for transfers between devices: 0.01 us -> 5.61 us  [per_device(): partner_query = lax.ppermute(queries, 'frame', partner_moves)]
    ppermute x1, waiting for transfers between devices: 9.48 us -> 4.42 us  [per_device(): minor2 = lax.ppermute(to_minor2, 'frame', near_moves)]
    ppermute x1, starting transfers between devices: 0.07 us -> 2.65 us  [per_device(): partner_query = lax.ppermute(queries, 'frame', partner_moves)]
    ppermute x1, starting transfers between devices: 1.06 us -> 2.63 us  [per_device(): part_low = lax.ppermute(part_low, 'frame', partner_moves)]
    ppermute x1, waiting for transfers between devices: 1.79 us -> 0.55 us  [per_device(): major2 = lax.ppermute(cross, 'frame', away_moves)]
    ppermute x1, starting transfers between devices: 4.42 us -> 3.46 us  [per_device(): major3 = lax.ppermute(to_major3, 'frame', away_moves)]
  transfers between devices with their start and end apart: 17 -> 17, of which waited for: 6 -> 5; matrix products, arithmetic and copies ran while one was open for 3% -> 3% of each run, Pallas kernels for 19% -> 18%
where the time goes in v9:
time: 84.7 us; the launch traced here: 84.4 us
  starting transfers between devices  31.9 us (38%)
  waiting for transfers between devices  29.1 us (34%)
  Pallas kernels  20.7 us (24%)
  local copies, waits for them, and re-layouts  2.04 us (2%)
    pallas_call x6, Pallas kernels, run(): pl.pallas_call(body, grid=(1,), in_specs=[pl.BlockSpec(memory_space=pltpu...  15.5 us
    ppermute x1, waiting for transfers between devices, per_device(): part_high = lax.ppermute(part_high, 'frame', partner_moves)  9.27 us
    ppermute x1, waiting for transfers between devices, per_device(): cross = lax.ppermute(pack(0, 3), 'frame', partner_moves)  9.17 us
    ppermute x1, waiting for transfers between devices, per_device(): partner_query = lax.ppermute(queries, 'frame', partner_moves)  5.61 us
    pallas_call x1, Pallas kernels, project(): pl.pallas_call(functools.partial(project_kernel, own_groups, part_groups,...  5.23 us
    ppermute x1, starting transfers between devices, per_device(): major1 = lax.ppermute(pack(0, 6), 'frame', away_moves)  4.66 us
    ppermute x1, waiting for transfers between devices, per_device(): minor2 = lax.ppermute(to_minor2, 'frame', near_moves)  4.42 us
    ppermute x1, starting transfers between devices, per_device(): major4 = lax.ppermute(major2, 'frame', away_moves)  3.72 us
  transfers between devices with their start and end apart: 17, of which 5 were waited for; matrix products, arithmetic and copies ran while one was open for 3% of the time, Pallas kernels for 18%

profile of v9, /device:TPU:0, one launch (start us, length us, event | category | flops | bytes accessed | tf_op | source)
XLA Modules:
  0.0 84.4 jit_solution(12697869672969533809)
XLA Ops:
  0.0 0.5 collective-permute-start
  0.5 1.7 %fusion = (bf16[256,768]{1,0:T(8,128)(2,1)S(1)}, bf16[256,768]{1,0:T(8,128)(2,1)S(1)}, bf16[256,768]{1,0:T(8,128)(2,1)S(1)}, bf16[256,768]{1,0:T(8,128)(2,1)S(1)...) fusion(bf16[256,1536]{1,0:T(8,128)(2,1)} %keys.11, bf16[256,1536]{1,0:T(8,128)(2,1)} %values.11), kind=kLoop, calls=%fused_computation.6 | loop fusion | bytes 4718592 | tf_op jit(solution)/shard_map/slice | solution.py:353
  2.2 0.1 pad_maximum_fusion
  2.3 4.7 %collective-permute-start.6 = (bf16[512,768]{1,0:T(8,128)(2,1)S(1)}, bf16[512,768]{1,0:T(8,128)(2,1)S(1)}, u32[]{:S(2)}, u32[]{:S(2)}) collective-permute-start(bf16[512,768]{1,0:T(8,128)(2,1)S(1)} %pad_maximum_fusion), channel_id=1, source_target_pairs={{0,4},{4,8},{6,2},{8,12},{10,6},{14,10},{1,5},{5,9},{7,3},{9,13},{... | collective-permute-start | bytes 2359304 | tf_op jit(solution)/shard_map/ppermute | solution.py:361
  7.0 0.1 pad_maximum_fusion.1
  7.0 1.3 %collective-permute-start.8 = (bf16[512,768]{1,0:T(8,128)(2,1)S(1)}, bf16[512,768]{1,0:T(8,128)(2,1)S(1)}, u32[]{:S(2)}, u32[]{:S(2)}) collective-permute-start(bf16[512,768]{1,0:T(8,128)(2,1)S(1)} %pad_maximum_fusion.1), channel_id=1, source_target_pairs={{2,6},{4,0},{6,10},{8,4},{10,14},{12,8},{3,7},{5,1},{7,11},{9,5},{... | collective-permute-start | bytes 2359304 | tf_op jit(solution)/shard_map/ppermute | solution.py:362
  8.3 0.1 fusion.3
  8.5 2.7 %collective-permute-start.1 = (bf16[512,384]{1,0:T(8,128)(2,1)S(1)}, bf16[512,384]{1,0:T(8,128)(2,1)S(1)}, u32[]{:S(2)}, u32[]{:S(2)}) collective-permute-start(bf16[512,384]{1,0:T(8,128)(2,1)S(1)} %pad_maximum_fusion.3), channel_id=1, source_target_pairs={{0,2},{2,0},{4,6},{6,4},{8,10},{10,8},{12,14},{14,12},{1,3},{3,1},... | collective-permute-start | bytes 1179656 | tf_op jit(solution)/shard_map/ppermute | solution.py:365
  11.2 9.2 %collective-permute-done.1.refs_1_ = bf16[512,384]{1,0:T(8,128)(2,1)S(1)} collective-permute-done((bf16[512,384]{1,0:T(8,128)(2,1)S(1)}, bf16[512,384]{1,0:T(8,128)(2,1)S(1)}, u32[]{:S(2)}, u32[]{:S(2)}) %collective-permute-start.1) | collective-permute-done | bytes 393248 | tf_op jit(solution)/shard_map/ppermute | solution.py:365
  20.4 3.7 %collective-permute-start.2 = (bf16[512,384]{1,0:T(8,128)(2,1)S(1)}, bf16[512,384]{1,0:T(8,128)(2,1)S(1)}, u32[]{:S(2)}, u32[]{:S(2)}) collective-permute-start(bf16[512,384]{1,0:T(8,128)(2,1)S(1)} %get-tuple-element.15), channel_id=1, source_target_pairs={{0,4},{4,8},{6,2},{8,12},{10,6},{14,10},{1,5},{5,9},{7,3},{9,13},{... | collective-permute-start | bytes 1179656 | tf_op jit(solution)/shard_map/ppermute | solution.py:369
  24.1 1.3 %collective-permute-start.3 = (bf16[512,384]{1,0:T(8,128)(2,1)S(1)}, bf16[512,384]{1,0:T(8,128)(2,1)S(1)}, u32[]{:S(2)}, u32[]{:S(2)}) collective-permute-start(bf16[512,384]{1,0:T(8,128)(2,1)S(1)} %get-tuple-element.16), channel_id=1, source_target_pairs={{2,6},{4,0},{6,10},{8,4},{10,14},{12,8},{3,7},{5,1},{7,11},{9,5},{... | collective-permute-start | bytes 1179656 | tf_op jit(solution)/shard_map/ppermute | solution.py:367
  25.4 2.7 %collective-permute-start.11 = (bf16[256,1536]{1,0:T(8,128)(2,1)S(1)}, bf16[256,1536]{1,0:T(8,128)(2,1)S(1)}, u32[]{:S(2)}, u32[]{:S(2)}) collective-permute-start(bf16[256,1536]{1,0:T(8,128)(2,1)S(1)} %copy-done.2), channel_id=1, source_target_pairs={{0,2},{2,0},{4,6},{6,4},{8,10},{10,8},{12,14},{14,12},{1,3},{3,1},... | collective-permute-start | bytes 2359304 | tf_op jit(solution)/shard_map/ppermute | solution.py:368
  28.2 3.5 %collective-permute-start.10 = (bf16[512,768]{1,0:T(8,128)(2,1)S(1)}, bf16[512,768]{1,0:T(8,128)(2,1)S(1)}, u32[]{:S(2)}, u32[]{:S(2)}) collective-permute-start(bf16[512,768]{1,0:T(8,128)(2,1)S(1)} %tie.5), channel_id=1, source_target_pairs={{0,4},{4,8},{6,2},{8,12},{10,6},{14,10},{1,5},{5,9},{7,3},{9,13},{... | collective-permute-start | bytes 2359304 | tf_op jit(solution)/shard_map/ppermute | solution.py:372
  31.8 1.3 %collective-permute-start.13 = (bf16[512,768]{1,0:T(8,128)(2,1)S(1)}, bf16[512,768]{1,0:T(8,128)(2,1)S(1)}, u32[]{:S(2)}, u32[]{:S(2)}) collective-permute-start(bf16[512,768]{1,0:T(8,128)(2,1)S(1)} %collective-permute-done.8.rest_1_.rest_2_), channel_id=1, source_target_pairs={{2,6},{4,0},{6,10},{8,4},{10,14},{12,8},{3,7},{5,1},{7,11},{9,5},{... | collective-permute-start | bytes 2359304 | tf_op jit(solution)/shard_map/ppermute | solution.py:370
  33.1 0.6 collective-permute-done.2.refs_0_.rest_1_
  33.6 4.4 %collective-permute-done.3.refs_1_.rest_2_.rest_1_ = bf16[512,384]{1,0:T(8,128)(2,1)S(1)} collective-permute-done((bf16[512,384]{1,0:T(8,128)(2,1)S(1)}, bf16[512,384]{1,0:T(8,128)(2,1)S(1)}, u32[]{:S(2)}, u32[]{:S(2)}) %collective-permute-start.3) | collective-permute-done | bytes 393248 | tf_op jit(solution)/shard_map/ppermute | solution.py:367
  38.0 0.5 collective-permute-start.5
  38.6 0.1 maximum_maximum_fusion
  38.7 5.6 %collective-permute-done.11.query = bf16[256,1536]{1,0:T(8,128)(2,1)S(1)} collective-permute-done((bf16[256,1536]{1,0:T(8,128)(2,1)S(1)}, bf16[256,1536]{1,0:T(8,128)(2,1)S(1)}, u32[]{:S(2)}, u32[]{:S(2)}) %collective-permute-start.11) | collective-permute-done | bytes 786464 | tf_op jit(solution)/shard_map/ppermute | solution.py:368
  44.3 3.7 %collective-permute-start.7 = (bf16[512,384]{1,0:T(8,128)(2,1)S(1)}, bf16[512,384]{1,0:T(8,128)(2,1)S(1)}, u32[]{:S(2)}, u32[]{:S(2)}) collective-permute-start(bf16[512,384]{1,0:T(8,128)(2,1)S(1)} %collective-permute-done.2.refs_0_.rest_1_), channel_id=1, source_target_pairs={{0,4},{4,8},{6,2},{8,12},{10,6},{14,10},{1,5},{5,9},{7,3},{9,13},{... | collective-permute-start | bytes 1179656 | tf_op jit(solution)/shard_map/ppermute | solution.py:373
  48.0 1.5 %collective-permute-start.15 = (bf16[512,384]{1,0:T(8,128)(2,1)S(1)}, bf16[512,384]{1,0:T(8,128)(2,1)S(1)}, u32[]{:S(2)}, u32[]{:S(2)}) collective-permute-start(bf16[512,384]{1,0:T(8,128)(2,1)S(1)} %collective-permute-done.3.refs_1_.rest_2_.rest_1_), channel_id=1, source_target_pairs={{2,6},{4,0},{6,10},{8,4},{10,14},{12,8},{3,7},{5,1},{7,11},{9,5},{... | collective-permute-start | bytes 1179656 | tf_op jit(solution)/shard_map/ppermute | solution.py:374
  49.5 1.9 %own_part.4 = (f32[256,384]{1,0:T(8,128)S(1)}, f32[256,128]{1,0:T(8,128)S(1)}) custom-call(s32[8,8]{1,0:T(8,128)S(1)} %copy-done.3, bf16[256,1536]{1,0:T(8,128)(2,1)S(1)} %copy-done.2, bf16[256,1536]{1,0:T(8,128)(2,1)S(1)} %copy-done, bf16[256,1536]{1,0:T(8,128)(2,1)S(1)} %copy-done.1, bf16[256,1536]{1,0:T(8,128)(2,1)S(1)} %collective-permute-done.4.sib_keys, ...), custom_call_target="tpu_custom_call" | custom-call | flops 301989888 | bytes 1048576 | tf_op jit(solution)/shard_map/own_part/pallas_call | solution.py:285
  51.5 2.0 %partner_part.3.rest_5_ = bf16[272,384]{1,0:T(8,128)(2,1)S(1)} custom-call(s32[8,8]{1,0:T(8,128)S(1)} %copy-done.3, bf16[256,1536]{1,0:T(8,128)(2,1)S(1)} %collective-permute-done.11.query, bf16[256,1536]{1,0:T(8,128)(2,1)S(1)} %copy-done, bf16[256,1536]{1,0:T(8,128)(2,1)S(1)} %copy-done.1, bf16[256,1536]{1,0:T(8,128)(2,1)S(1)} %collective-permute-done.4.sib_keys, ...), custom_call_target="tpu_custom_call" | custom-call | flops 301989888 | bytes 1048576 | tf_op jit(solution)/shard_map/partner_part/pallas_call | solution.py:285
  53.5 2.6 %collective-permute-start.12 = (bf16[272,384]{1,0:T(8,128)(2,1)S(1)}, bf16[272,384]{1,0:T(8,128)(2,1)S(1)}, u32[]{:S(2)}, u32[]{:S(2)}) collective-permute-start(bf16[272,384]{1,0:T(8,128)(2,1)S(1)} %partner_part.3.rest_5_), channel_id=1, source_target_pairs={{0,2},{2,0},{4,6},{6,4},{8,10},{10,8},{12,14},{14,12},{1,3},{3,1},... | collective-permute-start | bytes 626696 | tf_op jit(solution)/shard_map/ppermute | solution.py:429
  56.1 3.0 %own_part.5 = (f32[256,768]{1,0:T(8,128)S(1)}, f32[256,128]{1,0:T(8,128)S(1)}) custom-call(s32[8,8]{1,0:T(8,128)S(1)} %copy-done.3, bf16[256,1536]{1,0:T(8,128)(2,1)S(1)} %copy-done.2, bf16[256,1536]{1,0:T(8,128)(2,1)S(1)} %copy-done, bf16[256,1536]{1,0:T(8,128)(2,1)S(1)} %copy-done.1, bf16[256,1536]{1,0:T(8,128)(2,1)S(1)} %collective-permute-done.4.sib_keys, ...), custom_call_target="tpu_custom_call" | custom-call | flops 603979776 | bytes 1048576 | tf_op jit(solution)/shard_map/own_part/pallas_call | solution.py:285
  59.1 3.7 %partner_part.4 = bf16[288,768]{1,0:T(8,128)(2,1)S(1)} custom-call(s32[8,8]{1,0:T(8,128)S(1)} %copy-done.3, bf16[256,1536]{1,0:T(8,128)(2,1)S(1)} %collective-permute-done.11.query, bf16[256,1536]{1,0:T(8,128)(2,1)S(1)} %copy-done, bf16[256,1536]{1,0:T(8,128)(2,1)S(1)} %copy-done.1, bf16[256,1536]{1,0:T(8,128)(2,1)S(1)} %collective-permute-done.4.sib_keys, ...), custom_call_target="tpu_custom_call" | custom-call | flops 603979776 | bytes 1048576 | tf_op jit(solution)/shard_map/partner_part/pallas_call | solution.py:285
  62.8 0.1 collective-permute-start.14
  62.9 2.4 %partner_part.5 = bf16[272,384]{1,0:T(8,128)(2,1)S(1)} custom-call(s32[8,8]{1,0:T(8,128)S(1)} %copy-done.3, bf16[256,1536]{1,0:T(8,128)(2,1)S(1)} %collective-permute-done.11.query, bf16[256,1536]{1,0:T(8,128)(2,1)S(1)} %copy-done, bf16[256,1536]{1,0:T(8,128)(2,1)S(1)} %copy-done.1, bf16[256,1536]{1,0:T(8,128)(2,1)S(1)} %collective-permute-done.4.sib_keys, ...), custom_call_target="tpu_custom_call" | custom-call | flops 301989888 | bytes 1048576 | tf_op jit(solution)/shard_map/partner_part/pallas_call | solution.py:285
  65.4 2.0 %collective-permute-start.16 = (bf16[272,384]{1,0:T(8,128)(2,1)S(1)}, bf16[272,384]{1,0:T(8,128)(2,1)S(1)}, u32[]{:S(2)}, u32[]{:S(2)}) collective-permute-start(bf16[272,384]{1,0:T(8,128)(2,1)S(1)} %partner_part.5), channel_id=1, source_target_pairs={{0,2},{2,0},{4,6},{6,4},{8,10},{10,8},{12,14},{14,12},{1,3},{3,1},... | collective-permute-start | bytes 626696 | tf_op jit(solution)/shard_map/ppermute | solution.py:434
  67.4 2.4 %own_part.3 = (f32[256,384]{1,0:T(8,128)S(1)}, f32[256,128]{1,0:T(8,128)S(1)}) custom-call(s32[8,8]{1,0:T(8,128)S(1)} %copy-done.3, bf16[256,1536]{1,0:T(8,128)(2,1)S(1)} %copy-done.2, bf16[256,1536]{1,0:T(8,128)(2,1)S(1)} %copy-done, bf16[256,1536]{1,0:T(8,128)(2,1)S(1)} %copy-done.1, bf16[256,1536]{1,0:T(8,128)(2,1)S(1)} %collective-permute-done.4.sib_keys, ...), custom_call_target="tpu_custom_call" | custom-call | flops 301989888 | bytes 1048576 | tf_op jit(solution)/shard_map/own_part/pallas_call | solution.py:285
  69.9 9.3 %collective-permute-done.16.refs_10_ = bf16[272,384]{1,0:T(8,128)(2,1)S(1)} collective-permute-done((bf16[272,384]{1,0:T(8,128)(2,1)S(1)}, bf16[272,384]{1,0:T(8,128)(2,1)S(1)}, u32[]{:S(2)}, u32[]{:S(2)}) %collective-permute-start.16) | collective-permute-done | bytes 208928 | tf_op jit(solution)/shard_map/ppermute | solution.py:434
  79.1 5.2 %merge_and_project.1 = bf16[256,3072]{1,0:T(8,128)(2,1)} custom-call(bf16[768,3072]{1,0:T(8,128)(2,1)S(1)} %bitcast.1, bf16[768,3072]{1,0:T(8,128)(2,1)S(1)} %collective-permute-done.refs_0_.rest_7_.refs_1_, f32[256,384]{1,0:T(8,128)S(1)} %get-tuple-element.19.refs_2_, f32[256,128]{1,0:T(8,128)S(1)} %get-tuple-element.20.refs_3_, ...), custom_call_target="tpu_custom_call" | custom-call | flops 2415919104 | bytes 12582912 | tf_op jit(solution)/shard_map/merge_and_project/pallas_call | solution.py:322
  (38 shorter events, 0.4 us)
Async XLA Ops:
  0.0 20.4 %collective-permute-start = (bf16[768,3072]{1,0:T(8,128)(2,1)}, bf16[768,3072]{1,0:T(8,128)(2,1)S(1)}, u32[]{:S(2)}, u32[]{:S(2)}) collective-permute-start(bf16[768,3072]{1,0:T(8,128)(2,1)} %refs_0_.1), channel_id=1, source_target_pairs={{0,1},{1,0},{2,3},{3,2},{4,5},{5,4},{6,7},{7,6},{8,9},{9,8},{10,11... | collective-permute-start | bytes 14155784 | tf_op jit(solution)/shard_map/ppermute | solution.py:364
  2.2 6.1 %copy-start = (bf16[256,1536]{1,0:T(8,128)(2,1)S(1)}, bf16[256,1536]{1,0:T(8,128)(2,1)}, u32[]{:S(2)}) copy-start(bf16[256,1536]{1,0:T(8,128)(2,1)} %keys.11) | copy-start | bytes 2359300
  2.2 6.1 %copy-start.1 = (bf16[256,1536]{1,0:T(8,128)(2,1)S(1)}, bf16[256,1536]{1,0:T(8,128)(2,1)}, u32[]{:S(2)}) copy-start(bf16[256,1536]{1,0:T(8,128)(2,1)} %values.11) | copy-start | bytes 2359300
  2.3 25.9 %collective-permute-start.6 = (bf16[512,768]{1,0:T(8,128)(2,1)S(1)}, bf16[512,768]{1,0:T(8,128)(2,1)S(1)}, u32[]{:S(2)}, u32[]{:S(2)}) collective-permute-start(bf16[512,768]{1,0:T(8,128)(2,1)S(1)} %pad_maximum_fusion), channel_id=1, source_target_pairs={{0,4},{4,8},{6,2},{8,12},{10,6},{14,10},{1,5},{5,9},{7,3},{9,13},{... | collective-permute-start | bytes 2359304 | tf_op jit(solution)/shard_map/ppermute | solution.py:361
  7.0 24.7 %collective-permute-start.8 = (bf16[512,768]{1,0:T(8,128)(2,1)S(1)}, bf16[512,768]{1,0:T(8,128)(2,1)S(1)}, u32[]{:S(2)}, u32[]{:S(2)}) collective-permute-start(bf16[512,768]{1,0:T(8,128)(2,1)S(1)} %pad_maximum_fusion.1), channel_id=1, source_target_pairs={{2,6},{4,0},{6,10},{8,4},{10,14},{12,8},{3,7},{5,1},{7,11},{9,5},{... | collective-permute-start | bytes 2359304 | tf_op jit(solution)/shard_map/ppermute | solution.py:362
  8.5 11.9 %collective-permute-start.1 = (bf16[512,384]{1,0:T(8,128)(2,1)S(1)}, bf16[512,384]{1,0:T(8,128)(2,1)S(1)}, u32[]{:S(2)}, u32[]{:S(2)}) collective-permute-start(bf16[512,384]{1,0:T(8,128)(2,1)S(1)} %pad_maximum_fusion.3), channel_id=1, source_target_pairs={{0,2},{2,0},{4,6},{6,4},{8,10},{10,8},{12,14},{14,12},{1,3},{3,1},... | collective-permute-start | bytes 1179656 | tf_op jit(solution)/shard_map/ppermute | solution.py:365
  11.2 14.2 %copy-start.2 = (bf16[256,1536]{1,0:T(8,128)(2,1)S(1)}, bf16[256,1536]{1,0:T(8,128)(2,1)}, u32[]{:S(2)}) copy-start(bf16[256,1536]{1,0:T(8,128)(2,1)} %query.5) | copy-start | bytes 2359300
  20.4 13.3 %collective-permute-start.2 = (bf16[512,384]{1,0:T(8,128)(2,1)S(1)}, bf16[512,384]{1,0:T(8,128)(2,1)S(1)}, u32[]{:S(2)}, u32[]{:S(2)}) collective-permute-start(bf16[512,384]{1,0:T(8,128)(2,1)S(1)} %get-tuple-element.15), channel_id=1, source_target_pairs={{0,4},{4,8},{6,2},{8,12},{10,6},{14,10},{1,5},{5,9},{7,3},{9,13},{... | collective-permute-start | bytes 1179656 | tf_op jit(solution)/shard_map/ppermute | solution.py:369
  24.1 13.9 %collective-permute-start.3 = (bf16[512,384]{1,0:T(8,128)(2,1)S(1)}, bf16[512,384]{1,0:T(8,128)(2,1)S(1)}, u32[]{:S(2)}, u32[]{:S(2)}) collective-permute-start(bf16[512,384]{1,0:T(8,128)(2,1)S(1)} %get-tuple-element.16), channel_id=1, source_target_pairs={{2,6},{4,0},{6,10},{8,4},{10,14},{12,8},{3,7},{5,1},{7,11},{9,5},{... | collective-permute-start | bytes 1179656 | tf_op jit(solution)/shard_map/ppermute | solution.py:367
  25.4 18.9 %collective-permute-start.11 = (bf16[256,1536]{1,0:T(8,128)(2,1)S(1)}, bf16[256,1536]{1,0:T(8,128)(2,1)S(1)}, u32[]{:S(2)}, u32[]{:S(2)}) collective-permute-start(bf16[256,1536]{1,0:T(8,128)(2,1)S(1)} %copy-done.2), channel_id=1, source_target_pairs={{0,2},{2,0},{4,6},{6,4},{8,10},{10,8},{12,14},{14,12},{1,3},{3,1},... | collective-permute-start | bytes 2359304 | tf_op jit(solution)/shard_map/ppermute | solution.py:368
  28.2 25.2 %collective-permute-start.10 = (bf16[512,768]{1,0:T(8,128)(2,1)S(1)}, bf16[512,768]{1,0:T(8,128)(2,1)S(1)}, u32[]{:S(2)}, u32[]{:S(2)}) collective-permute-start(bf16[512,768]{1,0:T(8,128)(2,1)S(1)} %tie.5), channel_id=1, source_target_pairs={{0,4},{4,8},{6,2},{8,12},{10,6},{14,10},{1,5},{5,9},{7,3},{9,13},{... | collective-permute-start | bytes 2359304 | tf_op jit(solution)/shard_map/ppermute | solution.py:372
  31.8 27.3 %collective-permute-start.13 = (bf16[512,768]{1,0:T(8,128)(2,1)S(1)}, bf16[512,768]{1,0:T(8,128)(2,1)S(1)}, u32[]{:S(2)}, u32[]{:S(2)}) collective-permute-start(bf16[512,768]{1,0:T(8,128)(2,1)S(1)} %collective-permute-done.8.rest_1_.rest_2_), channel_id=1, source_target_pairs={{2,6},{4,0},{6,10},{8,4},{10,14},{12,8},{3,7},{5,1},{7,11},{9,5},{... | collective-permute-start | bytes 2359304 | tf_op jit(solution)/shard_map/ppermute | solution.py:370
  38.0 11.5 %copy-start.3 = (s32[8,8]{1,0:T(8,128)S(1)}, s32[8,8]{1,0:T(8,128)}, u32[]{:S(2)}) copy-start(s32[8,8]{1,0:T(8,128)} %table_ref.11) | copy-start | bytes 772
  38.0 6.3 %collective-permute-start.4 = (bf16[256,1536]{1,0:T(8,128)(2,1)S(1)}, bf16[256,1536]{1,0:T(8,128)(2,1)S(1)}, u32[]{:S(2)}, u32[]{:S(2)}) collective-permute-start(bf16[256,1536]{1,0:T(8,128)(2,1)S(1)} %get-tuple-element.17), channel_id=1, source_target_pairs={{0,1},{1,0},{2,3},{3,2},{4,5},{5,4},{6,7},{7,6},{8,9},{9,8},{10,11... | collective-permute-start | bytes 2359304 | tf_op jit(solution)/shard_map/ppermute | solution.py:376
  38.0 10.0 %collective-permute-start.5 = (bf16[256,1536]{1,0:T(8,128)(2,1)S(1)}, bf16[256,1536]{1,0:T(8,128)(2,1)S(1)}, u32[]{:S(2)}, u32[]{:S(2)}) collective-permute-start(bf16[256,1536]{1,0:T(8,128)(2,1)S(1)} %get-tuple-element.18), channel_id=1, source_target_pairs={{0,1},{1,0},{2,3},{3,2},{4,5},{5,4},{6,7},{7,6},{8,9},{9,8},{10,11... | collective-permute-start | bytes 2359304 | tf_op jit(solution)/shard_map/ppermute | solution.py:377
  44.3 14.8 %collective-permute-start.9 = (bf16[256,1536]{1,0:T(8,128)(2,1)S(1)}, bf16[256,1536]{1,0:T(8,128)(2,1)S(1)}, u32[]{:S(2)}, u32[]{:S(2)}) collective-permute-start(bf16[256,1536]{1,0:T(8,128)(2,1)S(1)} %maximum_maximum_fusion), channel_id=1, source_target_pairs={{0,1},{1,0},{2,3},{3,2},{4,5},{5,4},{6,7},{7,6},{8,9},{9,8},{10,11... | collective-permute-start | bytes 2359304 | tf_op jit(solution)/shard_map/ppermute | solution.py:378
  44.3 18.6 %collective-permute-start.7 = (bf16[512,384]{1,0:T(8,128)(2,1)S(1)}, bf16[512,384]{1,0:T(8,128)(2,1)S(1)}, u32[]{:S(2)}, u32[]{:S(2)}) collective-permute-start(bf16[512,384]{1,0:T(8,128)(2,1)S(1)} %collective-permute-done.2.refs_0_.rest_1_), channel_id=1, source_target_pairs={{0,4},{4,8},{6,2},{8,12},{10,6},{14,10},{1,5},{5,9},{7,3},{9,13},{... | collective-permute-start | bytes 1179656 | tf_op jit(solution)/shard_map/ppermute | solution.py:373
  48.0 14.9 %collective-permute-start.15 = (bf16[512,384]{1,0:T(8,128)(2,1)S(1)}, bf16[512,384]{1,0:T(8,128)(2,1)S(1)}, u32[]{:S(2)}, u32[]{:S(2)}) collective-permute-start(bf16[512,384]{1,0:T(8,128)(2,1)S(1)} %collective-permute-done.3.refs_1_.rest_2_.rest_1_), channel_id=1, source_target_pairs={{2,6},{4,0},{6,10},{8,4},{10,14},{12,8},{3,7},{5,1},{7,11},{9,5},{... | collective-permute-start | bytes 1179656 | tf_op jit(solution)/shard_map/ppermute | solution.py:374
  53.5 9.5 %collective-permute-start.12 = (bf16[272,384]{1,0:T(8,128)(2,1)S(1)}, bf16[272,384]{1,0:T(8,128)(2,1)S(1)}, u32[]{:S(2)}, u32[]{:S(2)}) collective-permute-start(bf16[272,384]{1,0:T(8,128)(2,1)S(1)} %partner_part.3.rest_5_), channel_id=1, source_target_pairs={{0,2},{2,0},{4,6},{6,4},{8,10},{10,8},{12,14},{14,12},{1,3},{3,1},... | collective-permute-start | bytes 626696 | tf_op jit(solution)/shard_map/ppermute | solution.py:429
  59.1 20.0 %slice-start = ((s8[4718592]{0:T(1024)(128)(4,1)}), s8[4194304]{0:T(1024)(128)(4,1)S(1)}, s32[]{:S(2)}) async-start(s8[4718592]{0:T(1024)(128)(4,1)} %bitcast), calls=%async_computation | async-start | bytes 8388608
  62.8 16.3 %slice-start.1 = ((s8[4718592]{0:T(1024)(128)(4,1)}), s8[524288]{0:T(1024)(128)(4,1)S(1)}, s32[]{:S(2)}) async-start(s8[4718592]{0:T(1024)(128)(4,1)} %bitcast), calls=%async_computation.1 | async-start | bytes 1048576
  62.8 16.3 %collective-permute-start.14 = (bf16[288,768]{1,0:T(8,128)(2,1)S(1)}, bf16[288,768]{1,0:T(8,128)(2,1)S(1)}, u32[]{:S(2)}, u32[]{:S(2)}) collective-permute-start(bf16[288,768]{1,0:T(8,128)(2,1)S(1)} %partner_part.4), channel_id=1, source_target_pairs={{0,2},{2,0},{4,6},{6,4},{8,10},{10,8},{12,14},{14,12},{1,3},{3,1},... | collective-permute-start | bytes 1327112 | tf_op jit(solution)/shard_map/ppermute | solution.py:430
  65.4 13.7 %collective-permute-start.16 = (bf16[272,384]{1,0:T(8,128)(2,1)S(1)}, bf16[272,384]{1,0:T(8,128)(2,1)S(1)}, u32[]{:S(2)}, u32[]{:S(2)}) collective-permute-start(bf16[272,384]{1,0:T(8,128)(2,1)S(1)} %partner_part.5), channel_id=1, source_target_pairs={{0,2},{2,0},{4,6},{6,4},{8,10},{10,8},{12,14},{14,12},{1,3},{3,1},... | collective-permute-start | bytes 626696 | tf_op jit(solution)/shard_map/ppermute | solution.py:434

commit v10 on v8

--- a/solution.py
+++ b/solution.py
@@ -228,12 +228,12 @@
     out_stats[...] = attend_heads(group, blocks, problem, out)
 
 
-def project_kernel(own_groups, part_groups, chunks, *refs):
+def project_kernel(span, own_groups, part_groups, has_base, *refs):
     refs = list(refs)
-    weights = [refs.pop(0) for _ in range(chunks)]
-    sib_weights = [refs.pop(0) for _ in range(chunks)]
+    weight, sib_weight = refs.pop(0), refs.pop(0)
     owns = [(group, refs.pop(0), refs.pop(0)) for group in own_groups]
     parts = [(group, refs.pop(0)) for group in part_groups]
+    base = refs.pop(0) if has_base else None
     out, attended = refs
     rows = out.shape[0]
     lanes = lax.broadcasted_iota(jnp.int32, (rows, DH), 1)
@@ -254,27 +254,39 @@
     inverse = 1.0 / (own_weight + part_weight)
     own_weight = own_weight * inverse
     part_weight = part_weight * inverse
-    for head in sorted(own_at):
+    for head in range(*span):
         own, own_place = own_at[head]
         part, part_place = part_at[head]
         mixed = own_weight[:, head : head + 1] * own[:, head_cols(own_place)] + part_weight[
             :, head : head + 1
         ] * part[:rows, head_cols(part_place)].astype(jnp.float32)
-        attended[:, head_cols(head)] = mixed.astype(attended.dtype)
+        attended[:, head_cols(head - span[0])] = mixed.astype(attended.dtype)
+
+    depth = weight.shape[0]
+    start, stop = span[0] * DH, span[1] * DH
+
+    def multiply(halves):
+        for at in range(0, out.shape[1], TILE):
+            product = base[:, at : at + TILE] if has_base else 0.0
+            for index, half in enumerate(halves):
+                low, high = max(start, index * depth), min(stop, (index + 1) * depth)
+                if low < high:
+                    product = product + jnp.dot(
+                        attended[:, low - start : high - start],
+                        half[low - index * depth : high - index * depth, at : at + TILE],
+                        preferred_element_type=jnp.float32,
+                    )
+            out[:, at : at + TILE] = product.astype(out.dtype)
+
     core = lax.axis_index("head")
-    chunk = weights[0].shape[0]
-    pieces = []
-    for index in range(chunks):
-        for weight, side in ((weights[index], core), (sib_weights[index], 1 - core)):
-            at = pl.multiple_of((side * chunks + index) * chunk, DH)
-            pieces.append((attended[:, pl.ds(at, chunk)], weight))
-    for at in range(0, out.shape[1], TILE):
-        product = 0.0
-        for piece, weight in pieces:
-            product = product + jnp.dot(
-                piece, weight[:, at : at + TILE], preferred_element_type=jnp.float32
-            )
-        out[:, at : at + TILE] = product.astype(out.dtype)
+
+    @pl.when(core == 0)
+    def _():
+        multiply((weight, sib_weight))
+
+    @pl.when(core != 0)
+    def _():
+        multiply((sib_weight, weight))
 
 
 def whole(shape):
@@ -316,22 +328,34 @@
     )(*before, *payloads)
 
 
-def project(own_groups, part_groups, weights, operands):
-    rows, columns = operands[0].shape[0], weights[0].shape[1]
-    depth = sum(weight.shape[0] for weight in weights)
+def project(span, owns, parts, weights, base, dtype):
+    rows, columns = owns[0][1][0].shape[0], weights[0].shape[1]
+    depth = (span[1] - span[0]) * DH
+    operands = [*weights]
+    for _, own in owns:
+        operands += own
+    operands += [part for _, part in parts]
+    if base is not None:
+        operands.append(base)
     return pl.pallas_call(
-        functools.partial(project_kernel, own_groups, part_groups, len(weights) // 2),
+        functools.partial(
+            project_kernel,
+            span,
+            tuple(group for group, _ in owns),
+            tuple(group for group, _ in parts),
+            base is not None,
+        ),
         grid=(1,),
-        in_specs=[whole(x.shape) for x in (*weights, *operands)],
+        in_specs=[whole(x.shape) for x in operands],
         out_specs=whole((rows, columns)),
-        out_shape=jax.ShapeDtypeStruct((rows, columns), jnp.bfloat16),
+        out_shape=jax.ShapeDtypeStruct((rows, columns), dtype),
         scratch_shapes=[pltpu.VMEM((rows, depth), jnp.bfloat16)],
         compiler_params=pltpu.CompilerParams(vmem_limit_bytes=8 * MIB),
         cost_estimate=pl.CostEstimate(
-            flops=2 * rows * depth * columns, bytes_accessed=12 * MIB, transcendentals=0
+            flops=2 * rows * depth * columns, bytes_accessed=4 * MIB, transcendentals=0
         ),
         name="merge_and_project",
-    )(*weights, *operands)
+    )(*operands)
 
 
 def per_device(queries, key_tokens, value_tokens, radial_table, out_weight):
@@ -372,7 +396,7 @@
     major3 = lax.ppermute(to_major3, "frame", away_moves)
     major4 = lax.ppermute(major2, "frame", away_moves)
     minor4 = lax.ppermute(minor2, "frame", near_moves)
-    to_sib_keys, to_sib_values = tie((major2,), key_tokens, value_tokens)
+    to_sib_keys, to_sib_values = tie((major2, partner_query, minor2), key_tokens, value_tokens)
     sib_keys = lax.ppermute(to_sib_keys, "head", core_moves)
     sib_values = lax.ppermute(to_sib_values, "head", core_moves)
     nearest = lax.ppermute(firsts(minor1, minor2, major2), "head", core_moves)
@@ -418,26 +442,35 @@
             after,
         )
 
-    own_groups = ((0, 3), (3, 6), (6, 12))
-    part_groups = ((0, 3), (3, 9), (9, 12))
     part_low = partner_part((0, 3), ("major1", "major2"))
     own_early = own_part((3, 6), ("major1", "minor1"))
     part_middle = partner_part(
-        (3, 9), ("major1", "major3", "minor1", "minor3", "nearest"), (part_low, own_early[1])
-    )
+        (3, 6), ("major1", "minor1", "minor3", "nearest"), (part_low, own_early[1], major3)
+    )
+    part_late = partner_part((6, 9), ("major3", "minor1", "minor3", "nearest"), (part_middle,))
     part_low = lax.ppermute(part_low, "frame", partner_moves)
     part_middle = lax.ppermute(part_middle, "frame", partner_moves)
+    part_late = lax.ppermute(part_late, "frame", partner_moves)
     own_late = own_part((6, 12), ("major3", "minor1", "minor2"))
     part_high = partner_part(
-        (9, 12), ("major3", "minor2", "minor4", "nearest"), (own_late[1], major4, part_low, *sib_weight)
+        (9, 12),
+        ("major3", "minor2", "minor4", "nearest"),
+        (own_late[1], major4, part_low, *sib_weight),
     )
     part_high = lax.ppermute(part_high, "frame", partner_moves)
     own_low = own_part((0, 3), ("major1", "major2", "major4", "nearest"))
+    weights = (*own_weight, *sib_weight)
+    owns = (((0, 3), own_low), ((3, 6), own_early), ((6, 12), own_late))
+    base = project(
+        (0, 9),
+        owns,
+        (((0, 3), part_low), ((3, 6), part_middle), ((6, 9), part_late)),
+        weights,
+        None,
+        jnp.float32,
+    )
     return project(
-        own_groups,
-        part_groups,
-        (*own_weight, *sib_weight),
-        (*own_low, *own_early, *own_late, part_low, part_middle, part_high),
+        (9, 12), (((6, 12), own_late),), (((9, 12), part_high),), weights, base, jnp.bfloat16
     )
 
 

time: 82.1 us -> 77.8 us (0.948)
  waiting for transfers between devices: 29.8 us -> 20 us
  starting transfers between devices: 28.5 us -> 31.7 us
  Pallas kernels: 20.8 us -> 23.1 us
    ppermute x1, waiting for transfers between devices: 9.48 us -> 1.84 us  [per_device(): minor2 = lax.ppermute(to_minor2, 'frame', near_moves)]
    ppermute x1, waiting for transfers between devices: 6.19 us -> 0.04 us  [per_device(): minor3 = lax.ppermute(minor1, 'frame', near_moves)]
    ppermute x1, waiting for transfers between devices: 0.01 us -> 4.65 us  [per_device(): partner_query = lax.ppermute(queries, 'frame', partner_moves)]
    ppermute x1, waiting for transfers between devices: 2.8 us -> 0.01 us  [per_device(): part_high = lax.ppermute(part_high, 'frame', partner_moves)]
    ppermute x1, waiting for transfers between devices: 0.01 us -> 2.07 us  [per_device(): major3 = lax.ppermute(to_major3, 'frame', away_moves)]
    ppermute x0 -> x1, starting transfers between devices: none -> 2.05 us  [per_device(): part_late = lax.ppermute(part_late, 'frame', partner_moves)]
    ppermute x1, starting transfers between devices: 2.04 us -> 0.06 us  [per_device(): part_high = lax.ppermute(part_high, 'frame', partner_moves)]
    ppermute x1, waiting for transfers between devices: 1.79 us -> 0.01 us  [per_device(): major2 = lax.ppermute(cross, 'frame', away_moves)]
  transfers between devices with their start and end apart: 17 -> 18, of which waited for: 6 -> 5; matrix products, arithmetic and copies ran while one was open for 3% -> 3% of each run, Pallas kernels for 19% -> 26%
where the time goes in v10:
time: 77.8 us; the launch traced here: 77.5 us
  starting transfers between devices  31.7 us (41%)
  Pallas kernels  23.1 us (30%)
  waiting for transfers between devices  20 us (26%)
  local copies, waits for them, and re-layouts  2.05 us (3%)
    pallas_call x7, Pallas kernels, run(): pl.pallas_call(body, grid=(1,), in_specs=[pl.BlockSpec(memory_space=pltpu...  16.7 us
    ppermute x1, waiting for transfers between devices, per_device(): cross = lax.ppermute(pack(0, 3), 'frame', partner_moves)  9.8 us
    pallas_call x2, Pallas kernels, project(): pl.pallas_call(functools.partial(project_kernel, span, tuple((group for g...  6.4 us
    ppermute x1, starting transfers between devices, per_device(): major4 = lax.ppermute(major2, 'frame', away_moves)  4.75 us
    ppermute x1, starting transfers between devices, per_device(): major1 = lax.ppermute(pack(0, 6), 'frame', away_moves)  4.66 us
    ppermute x1, waiting for transfers between devices, per_device(): partner_query = lax.ppermute(queries, 'frame', partner_moves)  4.65 us
    ppermute x1, starting transfers between devices, per_device(): major3 = lax.ppermute(to_major3, 'frame', away_moves)  4.6 us
    ppermute x1, starting transfers between devices, per_device(): major2 = lax.ppermute(cross, 'frame', away_moves)  4.03 us
  transfers between devices with their start and end apart: 18, of which 5 were waited for; matrix products, arithmetic and copies ran while one was open for 3% of the time, Pallas kernels for 26%

profile of v10, /device:TPU:0, one launch (start us, length us, event | category | flops | bytes accessed | tf_op | source)
XLA Modules:
  0.0 77.5 jit_solution(9387671337919853023)
XLA Ops:
  0.0 0.5 collective-permute-start
  0.5 1.8 %fusion.1 = (bf16[256,768]{1,0:T(8,128)(2,1)S(1)}, bf16[256,768]{1,0:T(8,128)(2,1)S(1)}, bf16[256,768]{1,0:T(8,128)(2,1)S(1)}, bf16[256,768]{1,0:T(8,128)(2,1)S(...) fusion(bf16[256,1536]{1,0:T(8,128)(2,1)} %keys.13, bf16[256,1536]{1,0:T(8,128)(2,1)} %values.13), kind=kLoop, calls=%fused_computation.7 | loop fusion | bytes 4718592 | tf_op jit(solution)/shard_map/slice | solution.py:377
  2.3 4.7 %collective-permute-start.7 = (bf16[512,768]{1,0:T(8,128)(2,1)S(1)}, bf16[512,768]{1,0:T(8,128)(2,1)S(1)}, u32[]{:S(2)}, u32[]{:S(2)}) collective-permute-start(bf16[512,768]{1,0:T(8,128)(2,1)S(1)} %pad_maximum_fusion), channel_id=1, source_target_pairs={{0,4},{4,8},{6,2},{8,12},{10,6},{14,10},{1,5},{5,9},{7,3},{9,13},{... | collective-permute-start | bytes 2359304 | tf_op jit(solution)/shard_map/ppermute | solution.py:385
  7.0 1.4 %collective-permute-start.9 = (bf16[512,768]{1,0:T(8,128)(2,1)S(1)}, bf16[512,768]{1,0:T(8,128)(2,1)S(1)}, u32[]{:S(2)}, u32[]{:S(2)}) collective-permute-start(bf16[512,768]{1,0:T(8,128)(2,1)S(1)} %pad_maximum_fusion.2), channel_id=1, source_target_pairs={{2,6},{4,0},{6,10},{8,4},{10,14},{12,8},{3,7},{5,1},{7,11},{9,5},{... | collective-permute-start | bytes 2359304 | tf_op jit(solution)/shard_map/ppermute | solution.py:386
  8.5 0.1 fusion.3
  8.6 2.7 %collective-permute-start.1 = (bf16[512,384]{1,0:T(8,128)(2,1)S(1)}, bf16[512,384]{1,0:T(8,128)(2,1)S(1)}, u32[]{:S(2)}, u32[]{:S(2)}) collective-permute-start(bf16[512,384]{1,0:T(8,128)(2,1)S(1)} %pad_maximum_fusion.3), channel_id=1, source_target_pairs={{0,2},{2,0},{4,6},{6,4},{8,10},{10,8},{12,14},{14,12},{1,3},{3,1},... | collective-permute-start | bytes 1179656 | tf_op jit(solution)/shard_map/ppermute | solution.py:389
  11.3 0.1 collective-permute-start.3
  11.4 9.8 %collective-permute-done.1.refs_1_ = bf16[512,384]{1,0:T(8,128)(2,1)S(1)} collective-permute-done((bf16[512,384]{1,0:T(8,128)(2,1)S(1)}, bf16[512,384]{1,0:T(8,128)(2,1)S(1)}, u32[]{:S(2)}, u32[]{:S(2)}) %collective-permute-start.1) | collective-permute-done | bytes 393248 | tf_op jit(solution)/shard_map/ppermute | solution.py:389
  21.2 4.0 %collective-permute-start.2 = (bf16[512,384]{1,0:T(8,128)(2,1)S(1)}, bf16[512,384]{1,0:T(8,128)(2,1)S(1)}, u32[]{:S(2)}, u32[]{:S(2)}) collective-permute-start(bf16[512,384]{1,0:T(8,128)(2,1)S(1)} %get-tuple-element.15), channel_id=1, source_target_pairs={{0,4},{4,8},{6,2},{8,12},{10,6},{14,10},{1,5},{5,9},{7,3},{9,13},{... | collective-permute-start | bytes 1179656 | tf_op jit(solution)/shard_map/ppermute | solution.py:393
  25.3 1.3 %collective-permute-start.4 = (bf16[512,384]{1,0:T(8,128)(2,1)S(1)}, bf16[512,384]{1,0:T(8,128)(2,1)S(1)}, u32[]{:S(2)}, u32[]{:S(2)}) collective-permute-start(bf16[512,384]{1,0:T(8,128)(2,1)S(1)} %get-tuple-element.16), channel_id=1, source_target_pairs={{2,6},{4,0},{6,10},{8,4},{10,14},{12,8},{3,7},{5,1},{7,11},{9,5},{... | collective-permute-start | bytes 1179656 | tf_op jit(solution)/shard_map/ppermute | solution.py:391
  26.8 4.6 %collective-permute-start.8 = (bf16[512,768]{1,0:T(8,128)(2,1)S(1)}, bf16[512,768]{1,0:T(8,128)(2,1)S(1)}, u32[]{:S(2)}, u32[]{:S(2)}) collective-permute-start(bf16[512,768]{1,0:T(8,128)(2,1)S(1)} %tie.5), channel_id=1, source_target_pairs={{0,4},{4,8},{6,2},{8,12},{10,6},{14,10},{1,5},{5,9},{7,3},{9,13},{... | collective-permute-start | bytes 2359304 | tf_op jit(solution)/shard_map/ppermute | solution.py:396
  31.4 1.3 %collective-permute-start.15 = (bf16[512,768]{1,0:T(8,128)(2,1)S(1)}, bf16[512,768]{1,0:T(8,128)(2,1)S(1)}, u32[]{:S(2)}, u32[]{:S(2)}) collective-permute-start(bf16[512,768]{1,0:T(8,128)(2,1)S(1)} %collective-permute-done.9.rest_1_), channel_id=1, source_target_pairs={{2,6},{4,0},{6,10},{8,4},{10,14},{12,8},{3,7},{5,1},{7,11},{9,5},{... | collective-permute-start | bytes 2359304 | tf_op jit(solution)/shard_map/ppermute | solution.py:394
  32.7 4.7 %collective-permute-done.3.refs_1_.query = bf16[256,1536]{1,0:T(8,128)(2,1)S(1)} collective-permute-done((bf16[256,1536]{1,0:T(8,128)(2,1)S(1)}, bf16[256,1536]{1,0:T(8,128)(2,1)S(1)}, u32[]{:S(2)}, u32[]{:S(2)}) %collective-permute-start.3) | collective-permute-done | bytes 786464 | tf_op jit(solution)/shard_map/ppermute | solution.py:392
  37.4 1.8 %collective-permute-done.4.refs_2_.rest_2_.rest_1_ = bf16[512,384]{1,0:T(8,128)(2,1)S(1)} collective-permute-done((bf16[512,384]{1,0:T(8,128)(2,1)S(1)}, bf16[512,384]{1,0:T(8,128)(2,1)S(1)}, u32[]{:S(2)}, u32[]{:S(2)}) %collective-permute-start.4) | collective-permute-done | bytes 393248 | tf_op jit(solution)/shard_map/ppermute | solution.py:391
  39.2 0.5 collective-permute-start.6
  39.8 0.1 collective-permute-start.11
  39.9 1.6 %collective-permute-done.5.sib_keys = bf16[256,1536]{1,0:T(8,128)(2,1)S(1)} collective-permute-done((bf16[256,1536]{1,0:T(8,128)(2,1)S(1)}, bf16[256,1536]{1,0:T(8,128)(2,1)S(1)}, u32[]{:S(2)}, u32[]{:S(2)}) %collective-permute-start.5) | collective-permute-done | bytes 786464 | tf_op jit(solution)/shard_map/ppermute | solution.py:400
  41.5 1.3 %collective-permute-start.10 = (bf16[512,384]{1,0:T(8,128)(2,1)S(1)}, bf16[512,384]{1,0:T(8,128)(2,1)S(1)}, u32[]{:S(2)}, u32[]{:S(2)}) collective-permute-start(bf16[512,384]{1,0:T(8,128)(2,1)S(1)} %collective-permute-done.4.refs_2_.rest_2_.rest_1_), channel_id=1, source_target_pairs={{2,6},{4,0},{6,10},{8,4},{10,14},{12,8},{3,7},{5,1},{7,11},{9,5},{... | collective-permute-start | bytes 1179656 | tf_op jit(solution)/shard_map/ppermute | solution.py:398
  42.8 4.8 %collective-permute-start.12 = (bf16[512,384]{1,0:T(8,128)(2,1)S(1)}, bf16[512,384]{1,0:T(8,128)(2,1)S(1)}, u32[]{:S(2)}, u32[]{:S(2)}) collective-permute-start(bf16[512,384]{1,0:T(8,128)(2,1)S(1)} %collective-permute-done.2.refs_0_.rest_1_), channel_id=1, source_target_pairs={{0,4},{4,8},{6,2},{8,12},{10,6},{14,10},{1,5},{5,9},{7,3},{9,13},{... | collective-permute-start | bytes 1179656 | tf_op jit(solution)/shard_map/ppermute | solution.py:397
  47.6 2.0 %partner_part.4.rest_4_ = bf16[272,384]{1,0:T(8,128)(2,1)S(1)} custom-call(s32[8,8]{1,0:T(8,128)S(1)} %copy-done.3, bf16[256,1536]{1,0:T(8,128)(2,1)S(1)} %collective-permute-done.3.refs_1_.query, bf16[256,1536]{1,0:T(8,128)(2,1)S(1)} %copy-done, bf16[256,1536]{1,0:T(8,128)(2,1)S(1)} %copy-done.1, bf16[256,1536]{1,0:T(8,128)(2,1)S(1)} %collective-permute-done.5.sib_keys, ...), custom_call_target="tpu_custom_call" | custom-call | flops 301989888 | bytes 1048576 | tf_op jit(solution)/shard_map/partner_part/pallas_call | solution.py:297
  49.6 2.1 %collective-permute-done.8.rest_0_.rest_6_ = bf16[512,768]{1,0:T(8,128)(2,1)S(1)} collective-permute-done((bf16[512,768]{1,0:T(8,128)(2,1)S(1)}, bf16[512,768]{1,0:T(8,128)(2,1)S(1)}, u32[]{:S(2)}, u32[]{:S(2)}) %collective-permute-start.8) | collective-permute-done | bytes 786464 | tf_op jit(solution)/shard_map/ppermute | solution.py:396
  51.6 2.4 %collective-permute-start.13 = (bf16[272,384]{1,0:T(8,128)(2,1)S(1)}, bf16[272,384]{1,0:T(8,128)(2,1)S(1)}, u32[]{:S(2)}, u32[]{:S(2)}) collective-permute-start(bf16[272,384]{1,0:T(8,128)(2,1)S(1)} %partner_part.4.rest_4_), channel_id=1, source_target_pairs={{0,2},{2,0},{4,6},{6,4},{8,10},{10,8},{12,14},{14,12},{1,3},{3,1},... | collective-permute-start | bytes 626696 | tf_op jit(solution)/shard_map/ppermute | solution.py:451
  54.1 1.9 %own_part.5 = (f32[256,384]{1,0:T(8,128)S(1)}, f32[256,128]{1,0:T(8,128)S(1)}) custom-call(s32[8,8]{1,0:T(8,128)S(1)} %copy-done.3, bf16[256,1536]{1,0:T(8,128)(2,1)S(1)} %copy-done.2, bf16[256,1536]{1,0:T(8,128)(2,1)S(1)} %copy-done, bf16[256,1536]{1,0:T(8,128)(2,1)S(1)} %copy-done.1, bf16[256,1536]{1,0:T(8,128)(2,1)S(1)} %collective-permute-done.5.sib_keys, ...), custom_call_target="tpu_custom_call" | custom-call | flops 301989888 | bytes 1048576 | tf_op jit(solution)/shard_map/own_part/pallas_call | solution.py:297
  56.1 2.5 %partner_part.6.rest_4_ = bf16[272,384]{1,0:T(8,128)(2,1)S(1)} custom-call(s32[8,8]{1,0:T(8,128)S(1)} %copy-done.3, bf16[256,1536]{1,0:T(8,128)(2,1)S(1)} %collective-permute-done.3.refs_1_.query, bf16[256,1536]{1,0:T(8,128)(2,1)S(1)} %copy-done, bf16[256,1536]{1,0:T(8,128)(2,1)S(1)} %copy-done.1, bf16[256,1536]{1,0:T(8,128)(2,1)S(1)} %collective-permute-done.5.sib_keys, ...), custom_call_target="tpu_custom_call" | custom-call | flops 301989888 | bytes 1048576 | tf_op jit(solution)/shard_map/partner_part/pallas_call | solution.py:297
  58.6 2.4 %partner_part.7 = bf16[272,384]{1,0:T(8,128)(2,1)S(1)} custom-call(s32[8,8]{1,0:T(8,128)S(1)} %copy-done.3, bf16[256,1536]{1,0:T(8,128)(2,1)S(1)} %collective-permute-done.3.refs_1_.query, bf16[256,1536]{1,0:T(8,128)(2,1)S(1)} %copy-done, bf16[256,1536]{1,0:T(8,128)(2,1)S(1)} %copy-done.1, bf16[256,1536]{1,0:T(8,128)(2,1)S(1)} %collective-permute-done.5.sib_keys, ...), custom_call_target="tpu_custom_call" | custom-call | flops 301989888 | bytes 1048576 | tf_op jit(solution)/shard_map/partner_part/pallas_call | solution.py:297
  61.0 2.0 %collective-permute-start.17 = (bf16[272,384]{1,0:T(8,128)(2,1)S(1)}, bf16[272,384]{1,0:T(8,128)(2,1)S(1)}, u32[]{:S(2)}, u32[]{:S(2)}) collective-permute-start(bf16[272,384]{1,0:T(8,128)(2,1)S(1)} %partner_part.7), channel_id=1, source_target_pairs={{0,2},{2,0},{4,6},{6,4},{8,10},{10,8},{12,14},{14,12},{1,3},{3,1},... | collective-permute-start | bytes 626696 | tf_op jit(solution)/shard_map/ppermute | solution.py:453
  63.1 3.0 %own_part.3 = (f32[256,768]{1,0:T(8,128)S(1)}, f32[256,128]{1,0:T(8,128)S(1)}) custom-call(s32[8,8]{1,0:T(8,128)S(1)} %copy-done.3, bf16[256,1536]{1,0:T(8,128)(2,1)S(1)} %copy-done.2, bf16[256,1536]{1,0:T(8,128)(2,1)S(1)} %copy-done, bf16[256,1536]{1,0:T(8,128)(2,1)S(1)} %copy-done.1, bf16[256,1536]{1,0:T(8,128)(2,1)S(1)} %collective-permute-done.5.sib_keys, ...), custom_call_target="tpu_custom_call" | custom-call | flops 603979776 | bytes 1048576 | tf_op jit(solution)/shard_map/own_part/pallas_call | solution.py:297
  66.1 2.4 %partner_part.5 = bf16[272,384]{1,0:T(8,128)(2,1)S(1)} custom-call(s32[8,8]{1,0:T(8,128)S(1)} %copy-done.3, bf16[256,1536]{1,0:T(8,128)(2,1)S(1)} %collective-permute-done.3.refs_1_.query, bf16[256,1536]{1,0:T(8,128)(2,1)S(1)} %copy-done, bf16[256,1536]{1,0:T(8,128)(2,1)S(1)} %copy-done.1, bf16[256,1536]{1,0:T(8,128)(2,1)S(1)} %collective-permute-done.5.sib_keys, ...), custom_call_target="tpu_custom_call" | custom-call | flops 301989888 | bytes 1048576 | tf_op jit(solution)/shard_map/partner_part/pallas_call | solution.py:297
  68.6 0.1 collective-permute-start.14
  68.6 2.4 %own_part.4 = (f32[256,384]{1,0:T(8,128)S(1)}, f32[256,128]{1,0:T(8,128)S(1)}) custom-call(s32[8,8]{1,0:T(8,128)S(1)} %copy-done.3, bf16[256,1536]{1,0:T(8,128)(2,1)S(1)} %copy-done.2, bf16[256,1536]{1,0:T(8,128)(2,1)S(1)} %copy-done, bf16[256,1536]{1,0:T(8,128)(2,1)S(1)} %copy-done.1, bf16[256,1536]{1,0:T(8,128)(2,1)S(1)} %collective-permute-done.5.sib_keys, ...), custom_call_target="tpu_custom_call" | custom-call | flops 301989888 | bytes 1048576 | tf_op jit(solution)/shard_map/own_part/pallas_call | solution.py:297
  71.1 3.7 %merge_and_project.2.refs_5_ = f32[256,3072]{1,0:T(8,128)S(1)} custom-call(bf16[768,3072]{1,0:T(8,128)(2,1)S(1)} %bitcast.1, bf16[768,3072]{1,0:T(8,128)(2,1)S(1)} %collective-permute-done.refs_0_.rest_7_.refs_1_, f32[256,384]{1,0:T(8,128)S(1)} %get-tuple-element.21.refs_2_, f32[256,128]{1,0:T(8,128)S(1)} %get-tuple-element.22.refs_3_, ...), custom_call_target="tpu_custom_call" | custom-call | flops 1811939328 | bytes 4194304 | tf_op jit(solution)/shard_map/merge_and_project/pallas_call | solution.py:340
  74.7 2.7 %merge_and_project.3 = bf16[256,3072]{1,0:T(8,128)(2,1)} custom-call(bf16[768,3072]{1,0:T(8,128)(2,1)S(1)} %bitcast.1, bf16[768,3072]{1,0:T(8,128)(2,1)S(1)} %collective-permute-done.refs_0_.rest_7_.refs_1_, f32[256,768]{1,0:T(8,128)S(1)} %get-tuple-element.19.refs_6_.refs_2_, f32[256,128]{1,0:T(8,128)S(1)} %get-tuple-element.20.rest_4_.refs_7_.refs_3_, ...), custom_call_target="tpu_custom_call" | custom-call | flops 603979776 | bytes 4194304 | tf_op jit(solution)/shard_map/merge_and_project/pallas_call | solution.py:340
  (42 shorter events, 0.6 us)
Async XLA Ops:
  0.0 21.2 %collective-permute-start = (bf16[768,3072]{1,0:T(8,128)(2,1)}, bf16[768,3072]{1,0:T(8,128)(2,1)S(1)}, u32[]{:S(2)}, u32[]{:S(2)}) collective-permute-start(bf16[768,3072]{1,0:T(8,128)(2,1)} %refs_0_.3), channel_id=1, source_target_pairs={{0,1},{1,0},{2,3},{3,2},{4,5},{5,4},{6,7},{7,6},{8,9},{9,8},{10,11... | collective-permute-start | bytes 14155784 | tf_op jit(solution)/shard_map/ppermute | solution.py:388
  2.2 6.3 %copy-start = (bf16[256,1536]{1,0:T(8,128)(2,1)S(1)}, bf16[256,1536]{1,0:T(8,128)(2,1)}, u32[]{:S(2)}) copy-start(bf16[256,1536]{1,0:T(8,128)(2,1)} %keys.13) | copy-start | bytes 2359300
  2.2 6.3 %copy-start.1 = (bf16[256,1536]{1,0:T(8,128)(2,1)S(1)}, bf16[256,1536]{1,0:T(8,128)(2,1)}, u32[]{:S(2)}) copy-start(bf16[256,1536]{1,0:T(8,128)(2,1)} %values.13) | copy-start | bytes 2359300
  2.3 24.4 %collective-permute-start.7 = (bf16[512,768]{1,0:T(8,128)(2,1)S(1)}, bf16[512,768]{1,0:T(8,128)(2,1)S(1)}, u32[]{:S(2)}, u32[]{:S(2)}) collective-permute-start(bf16[512,768]{1,0:T(8,128)(2,1)S(1)} %pad_maximum_fusion), channel_id=1, source_target_pairs={{0,4},{4,8},{6,2},{8,12},{10,6},{14,10},{1,5},{5,9},{7,3},{9,13},{... | collective-permute-start | bytes 2359304 | tf_op jit(solution)/shard_map/ppermute | solution.py:385
  7.0 4.3 %copy-start.2 = (bf16[256,1536]{1,0:T(8,128)(2,1)S(1)}, bf16[256,1536]{1,0:T(8,128)(2,1)}, u32[]{:S(2)}) copy-start(bf16[256,1536]{1,0:T(8,128)(2,1)} %query.5) | copy-start | bytes 2359300
  7.0 24.3 %collective-permute-start.9 = (bf16[512,768]{1,0:T(8,128)(2,1)S(1)}, bf16[512,768]{1,0:T(8,128)(2,1)S(1)}, u32[]{:S(2)}, u32[]{:S(2)}) collective-permute-start(bf16[512,768]{1,0:T(8,128)(2,1)S(1)} %pad_maximum_fusion.2), channel_id=1, source_target_pairs={{2,6},{4,0},{6,10},{8,4},{10,14},{12,8},{3,7},{5,1},{7,11},{9,5},{... | collective-permute-start | bytes 2359304 | tf_op jit(solution)/shard_map/ppermute | solution.py:386
  8.6 12.6 %collective-permute-start.1 = (bf16[512,384]{1,0:T(8,128)(2,1)S(1)}, bf16[512,384]{1,0:T(8,128)(2,1)S(1)}, u32[]{:S(2)}, u32[]{:S(2)}) collective-permute-start(bf16[512,384]{1,0:T(8,128)(2,1)S(1)} %pad_maximum_fusion.3), channel_id=1, source_target_pairs={{0,2},{2,0},{4,6},{6,4},{8,10},{10,8},{12,14},{14,12},{1,3},{3,1},... | collective-permute-start | bytes 1179656 | tf_op jit(solution)/shard_map/ppermute | solution.py:389
  11.3 26.1 %collective-permute-start.3 = (bf16[256,1536]{1,0:T(8,128)(2,1)S(1)}, bf16[256,1536]{1,0:T(8,128)(2,1)S(1)}, u32[]{:S(2)}, u32[]{:S(2)}) collective-permute-start(bf16[256,1536]{1,0:T(8,128)(2,1)S(1)} %copy-done.2), channel_id=1, source_target_pairs={{0,2},{2,0},{4,6},{6,4},{8,10},{10,8},{12,14},{14,12},{1,3},{3,1},... | collective-permute-start | bytes 2359304 | tf_op jit(solution)/shard_map/ppermute | solution.py:392
  21.2 16.1 %collective-permute-start.2 = (bf16[512,384]{1,0:T(8,128)(2,1)S(1)}, bf16[512,384]{1,0:T(8,128)(2,1)S(1)}, u32[]{:S(2)}, u32[]{:S(2)}) collective-permute-start(bf16[512,384]{1,0:T(8,128)(2,1)S(1)} %get-tuple-element.15), channel_id=1, source_target_pairs={{0,4},{4,8},{6,2},{8,12},{10,6},{14,10},{1,5},{5,9},{7,3},{9,13},{... | collective-permute-start | bytes 1179656 | tf_op jit(solution)/shard_map/ppermute | solution.py:393
  25.3 13.9 %collective-permute-start.4 = (bf16[512,384]{1,0:T(8,128)(2,1)S(1)}, bf16[512,384]{1,0:T(8,128)(2,1)S(1)}, u32[]{:S(2)}, u32[]{:S(2)}) collective-permute-start(bf16[512,384]{1,0:T(8,128)(2,1)S(1)} %get-tuple-element.16), channel_id=1, source_target_pairs={{2,6},{4,0},{6,10},{8,4},{10,14},{12,8},{3,7},{5,1},{7,11},{9,5},{... | collective-permute-start | bytes 1179656 | tf_op jit(solution)/shard_map/ppermute | solution.py:391
  26.8 24.9 %collective-permute-start.8 = (bf16[512,768]{1,0:T(8,128)(2,1)S(1)}, bf16[512,768]{1,0:T(8,128)(2,1)S(1)}, u32[]{:S(2)}, u32[]{:S(2)}) collective-permute-start(bf16[512,768]{1,0:T(8,128)(2,1)S(1)} %tie.5), channel_id=1, source_target_pairs={{0,4},{4,8},{6,2},{8,12},{10,6},{14,10},{1,5},{5,9},{7,3},{9,13},{... | collective-permute-start | bytes 2359304 | tf_op jit(solution)/shard_map/ppermute | solution.py:396
  31.4 24.7 %collective-permute-start.15 = (bf16[512,768]{1,0:T(8,128)(2,1)S(1)}, bf16[512,768]{1,0:T(8,128)(2,1)S(1)}, u32[]{:S(2)}, u32[]{:S(2)}) collective-permute-start(bf16[512,768]{1,0:T(8,128)(2,1)S(1)} %collective-permute-done.9.rest_1_), channel_id=1, source_target_pairs={{2,6},{4,0},{6,10},{8,4},{10,14},{12,8},{3,7},{5,1},{7,11},{9,5},{... | collective-permute-start | bytes 2359304 | tf_op jit(solution)/shard_map/ppermute | solution.py:394
  39.2 8.3 %copy-start.3 = (s32[8,8]{1,0:T(8,128)S(1)}, s32[8,8]{1,0:T(8,128)}, u32[]{:S(2)}) copy-start(s32[8,8]{1,0:T(8,128)} %table_ref.13) | copy-start | bytes 772
  39.2 2.3 %collective-permute-start.5 = (bf16[256,1536]{1,0:T(8,128)(2,1)S(1)}, bf16[256,1536]{1,0:T(8,128)(2,1)S(1)}, u32[]{:S(2)}, u32[]{:S(2)}) collective-permute-start(bf16[256,1536]{1,0:T(8,128)(2,1)S(1)} %get-tuple-element.17), channel_id=1, source_target_pairs={{0,1},{1,0},{2,3},{3,2},{4,5},{5,4},{6,7},{7,6},{8,9},{9,8},{10,11... | collective-permute-start | bytes 2359304 | tf_op jit(solution)/shard_map/ppermute | solution.py:400
  39.2 3.6 %collective-permute-start.6 = (bf16[256,1536]{1,0:T(8,128)(2,1)S(1)}, bf16[256,1536]{1,0:T(8,128)(2,1)S(1)}, u32[]{:S(2)}, u32[]{:S(2)}) collective-permute-start(bf16[256,1536]{1,0:T(8,128)(2,1)S(1)} %get-tuple-element.18), channel_id=1, source_target_pairs={{0,1},{1,0},{2,3},{3,2},{4,5},{5,4},{6,7},{7,6},{8,9},{9,8},{10,11... | collective-permute-start | bytes 2359304 | tf_op jit(solution)/shard_map/ppermute | solution.py:401
  39.8 16.2 %collective-permute-start.11 = (bf16[256,1536]{1,0:T(8,128)(2,1)S(1)}, bf16[256,1536]{1,0:T(8,128)(2,1)S(1)}, u32[]{:S(2)}, u32[]{:S(2)}) collective-permute-start(bf16[256,1536]{1,0:T(8,128)(2,1)S(1)} %maximum_maximum_fusion), channel_id=1, source_target_pairs={{0,1},{1,0},{2,3},{3,2},{4,5},{5,4},{6,7},{7,6},{8,9},{9,8},{10,11... | collective-permute-start | bytes 2359304 | tf_op jit(solution)/shard_map/ppermute | solution.py:402
  41.5 24.6 %collective-permute-start.10 = (bf16[512,384]{1,0:T(8,128)(2,1)S(1)}, bf16[512,384]{1,0:T(8,128)(2,1)S(1)}, u32[]{:S(2)}, u32[]{:S(2)}) collective-permute-start(bf16[512,384]{1,0:T(8,128)(2,1)S(1)} %collective-permute-done.4.refs_2_.rest_2_.rest_1_), channel_id=1, source_target_pairs={{2,6},{4,0},{6,10},{8,4},{10,14},{12,8},{3,7},{5,1},{7,11},{9,5},{... | collective-permute-start | bytes 1179656 | tf_op jit(solution)/shard_map/ppermute | solution.py:398
  42.8 23.3 %collective-permute-start.12 = (bf16[512,384]{1,0:T(8,128)(2,1)S(1)}, bf16[512,384]{1,0:T(8,128)(2,1)S(1)}, u32[]{:S(2)}, u32[]{:S(2)}) collective-permute-start(bf16[512,384]{1,0:T(8,128)(2,1)S(1)} %collective-permute-done.2.refs_0_.rest_1_), channel_id=1, source_target_pairs={{0,4},{4,8},{6,2},{8,12},{10,6},{14,10},{1,5},{5,9},{7,3},{9,13},{... | collective-permute-start | bytes 1179656 | tf_op jit(solution)/shard_map/ppermute | solution.py:397
  51.6 14.4 %collective-permute-start.13 = (bf16[272,384]{1,0:T(8,128)(2,1)S(1)}, bf16[272,384]{1,0:T(8,128)(2,1)S(1)}, u32[]{:S(2)}, u32[]{:S(2)}) collective-permute-start(bf16[272,384]{1,0:T(8,128)(2,1)S(1)} %partner_part.4.rest_4_), channel_id=1, source_target_pairs={{0,2},{2,0},{4,6},{6,4},{8,10},{10,8},{12,14},{14,12},{1,3},{3,1},... | collective-permute-start | bytes 626696 | tf_op jit(solution)/shard_map/ppermute | solution.py:451
  58.5 12.5 %collective-permute-start.16 = (bf16[272,384]{1,0:T(8,128)(2,1)S(1)}, bf16[272,384]{1,0:T(8,128)(2,1)S(1)}, u32[]{:S(2)}, u32[]{:S(2)}) collective-permute-start(bf16[272,384]{1,0:T(8,128)(2,1)S(1)} %partner_part.6.rest_4_), channel_id=1, source_target_pairs={{0,2},{2,0},{4,6},{6,4},{8,10},{10,8},{12,14},{14,12},{1,3},{3,1},... | collective-permute-start | bytes 626696 | tf_op jit(solution)/shard_map/ppermute | solution.py:452
  61.0 10.0 %collective-permute-start.17 = (bf16[272,384]{1,0:T(8,128)(2,1)S(1)}, bf16[272,384]{1,0:T(8,128)(2,1)S(1)}, u32[]{:S(2)}, u32[]{:S(2)}) collective-permute-start(bf16[272,384]{1,0:T(8,128)(2,1)S(1)} %partner_part.7), channel_id=1, source_target_pairs={{0,2},{2,0},{4,6},{6,4},{8,10},{10,8},{12,14},{14,12},{1,3},{3,1},... | collective-permute-start | bytes 626696 | tf_op jit(solution)/shard_map/ppermute | solution.py:453
  66.1 5.0 %slice-start = ((s8[4718592]{0:T(1024)(128)(4,1)}), s8[4194304]{0:T(1024)(128)(4,1)S(1)}, s32[]{:S(2)}) async-start(s8[4718592]{0:T(1024)(128)(4,1)} %bitcast), calls=%async_computation | async-start | bytes 8388608
  66.1 5.0 %slice-start.1 = ((s8[4718592]{0:T(1024)(128)(4,1)}), s8[524288]{0:T(1024)(128)(4,1)S(1)}, s32[]{:S(2)}) async-start(s8[4718592]{0:T(1024)(128)(4,1)} %bitcast), calls=%async_computation.1 | async-start | bytes 1048576
  68.6 6.2 %collective-permute-start.14 = (bf16[272,384]{1,0:T(8,128)(2,1)S(1)}, bf16[272,384]{1,0:T(8,128)(2,1)S(1)}, u32[]{:S(2)}, u32[]{:S(2)}) collective-permute-start(bf16[272,384]{1,0:T(8,128)(2,1)S(1)} %partner_part.5), channel_id=1, source_target_pairs={{0,2},{2,0},{4,6},{6,4},{8,10},{10,8},{12,14},{14,12},{1,3},{3,1},... | collective-permute-start | bytes 626696 | tf_op jit(solution)/shard_map/ppermute | solution.py:460

commit v11 on v10

--- a/solution.py
+++ b/solution.py
@@ -11,7 +11,7 @@
 DH = 128
 BS = 128
 CROSS = 3
-BATCH = 4
+BATCH = 6
 TILE = 768
 NEG = -1e30
 LOG2_SCALE = math.log2(math.e) / math.sqrt(DH)
@@ -442,10 +442,10 @@
             after,
         )
 
-    part_low = partner_part((0, 3), ("major1", "major2"))
     own_early = own_part((3, 6), ("major1", "minor1"))
+    part_low = partner_part((0, 3), ("major1", "major2"), (own_early[1],))
     part_middle = partner_part(
-        (3, 6), ("major1", "minor1", "minor3", "nearest"), (part_low, own_early[1], major3)
+        (3, 6), ("major1", "minor1", "minor3", "nearest"), (part_low, major3)
     )
     part_late = partner_part((6, 9), ("major3", "minor1", "minor3", "nearest"), (part_middle,))
     part_low = lax.ppermute(part_low, "frame", partner_moves)

time: 77.8 us -> 77.6 us (level)
  waiting for transfers between devices: 20 us -> 21.9 us
  starting transfers between devices: 31.7 us -> 30.6 us
  Pallas kernels: 23.1 us -> 22.1 us
    ppermute x1, starting transfers between devices: 2.05 us -> 0.05 us  [per_device(): part_late = lax.ppermute(part_late, 'frame', partner_moves)]
    ppermute x1, starting transfers between devices: 0.05 us -> 2.01 us  [per_device(): part_middle = lax.ppermute(part_middle, 'frame', partner_moves)]
    ppermute x1, waiting for transfers between devices: 0.04 us -> 1.99 us  [per_device(): minor3 = lax.ppermute(minor1, 'frame', near_moves)]
    ppermute x1, starting transfers between devices: 4.75 us -> 3.43 us  [per_device(): major4 = lax.ppermute(major2, 'frame', away_moves)]
    pallas_call x7, Pallas kernels: 16.7 us -> 15.7 us  [run(): pl.pallas_call(body, grid=(1,), in_specs=[pl.BlockSpec(memory_space=pltpu...]
  transfers between devices with their start and end apart: 18 -> 18, of which waited for: 5 -> 7; matrix products, arithmetic and copies ran while one was open for 3% -> 3% of each run, Pallas kernels for 26% -> 25%
where the time goes in v11:
time: 77.6 us; the launch traced here: 77.3 us
  starting transfers between devices  30.6 us (39%)
  Pallas kernels  22.1 us (28%)
  waiting for transfers between devices  21.9 us (28%)
  local copies, waits for them, and re-layouts  2.05 us (3%)
    pallas_call x7, Pallas kernels, run(): pl.pallas_call(body, grid=(1,), in_specs=[pl.BlockSpec(memory_space=pltpu...  15.7 us
    ppermute x1, waiting for transfers between devices, per_device(): cross = lax.ppermute(pack(0, 3), 'frame', partner_moves)  9.8 us
    pallas_call x2, Pallas kernels, project(): pl.pallas_call(functools.partial(project_kernel, span, tuple((group for g...  6.39 us
    ppermute x1, starting transfers between devices, per_device(): major1 = lax.ppermute(pack(0, 6), 'frame', away_moves)  4.66 us
    ppermute x1, waiting for transfers between devices, per_device(): partner_query = lax.ppermute(queries, 'frame', partner_moves)  4.65 us
    ppermute x1, starting transfers between devices, per_device(): major3 = lax.ppermute(to_major3, 'frame', away_moves)  4.6 us
    ppermute x1, starting transfers between devices, per_device(): major2 = lax.ppermute(cross, 'frame', away_moves)  4.03 us
    ppermute x1, starting transfers between devices, per_device(): major4 = lax.ppermute(major2, 'frame', away_moves)  3.43 us
  transfers between devices with their start and end apart: 18, of which 7 were waited for; matrix products, arithmetic and copies ran while one was open for 3% of the time, Pallas kernels for 25%

profile of v11, /device:TPU:0, one launch (start us, length us, event | category | flops | bytes accessed | tf_op | source)
XLA Modules:
  0.0 77.3 jit_solution(1346255332153612283)
XLA Ops:
  0.0 0.5 collective-permute-start
  0.5 1.8 %fusion.1 = (bf16[256,768]{1,0:T(8,128)(2,1)S(1)}, bf16[256,768]{1,0:T(8,128)(2,1)S(1)}, bf16[256,768]{1,0:T(8,128)(2,1)S(1)}, bf16[256,768]{1,0:T(8,128)(2,1)S(...) fusion(bf16[256,1536]{1,0:T(8,128)(2,1)} %keys.13, bf16[256,1536]{1,0:T(8,128)(2,1)} %values.13), kind=kLoop, calls=%fused_computation.7 | loop fusion | bytes 4718592 | tf_op jit(solution)/shard_map/slice | solution.py:377
  2.3 4.7 %collective-permute-start.7 = (bf16[512,768]{1,0:T(8,128)(2,1)S(1)}, bf16[512,768]{1,0:T(8,128)(2,1)S(1)}, u32[]{:S(2)}, u32[]{:S(2)}) collective-permute-start(bf16[512,768]{1,0:T(8,128)(2,1)S(1)} %pad_maximum_fusion), channel_id=1, source_target_pairs={{0,4},{4,8},{6,2},{8,12},{10,6},{14,10},{1,5},{5,9},{7,3},{9,13},{... | collective-permute-start | bytes 2359304 | tf_op jit(solution)/shard_map/ppermute | solution.py:385
  7.0 1.4 %collective-permute-start.9 = (bf16[512,768]{1,0:T(8,128)(2,1)S(1)}, bf16[512,768]{1,0:T(8,128)(2,1)S(1)}, u32[]{:S(2)}, u32[]{:S(2)}) collective-permute-start(bf16[512,768]{1,0:T(8,128)(2,1)S(1)} %pad_maximum_fusion.2), channel_id=1, source_target_pairs={{2,6},{4,0},{6,10},{8,4},{10,14},{12,8},{3,7},{5,1},{7,11},{9,5},{... | collective-permute-start | bytes 2359304 | tf_op jit(solution)/shard_map/ppermute | solution.py:386
  8.6 2.7 %collective-permute-start.1 = (bf16[512,384]{1,0:T(8,128)(2,1)S(1)}, bf16[512,384]{1,0:T(8,128)(2,1)S(1)}, u32[]{:S(2)}, u32[]{:S(2)}) collective-permute-start(bf16[512,384]{1,0:T(8,128)(2,1)S(1)} %pad_maximum_fusion.3), channel_id=1, source_target_pairs={{0,2},{2,0},{4,6},{6,4},{8,10},{10,8},{12,14},{14,12},{1,3},{3,1},... | collective-permute-start | bytes 1179656 | tf_op jit(solution)/shard_map/ppermute | solution.py:389
  11.3 0.1 collective-permute-start.3
  11.4 9.8 %collective-permute-done.1.refs_1_ = bf16[512,384]{1,0:T(8,128)(2,1)S(1)} collective-permute-done((bf16[512,384]{1,0:T(8,128)(2,1)S(1)}, bf16[512,384]{1,0:T(8,128)(2,1)S(1)}, u32[]{:S(2)}, u32[]{:S(2)}) %collective-permute-start.1) | collective-permute-done | bytes 393248 | tf_op jit(solution)/shard_map/ppermute | solution.py:389
  21.2 4.0 %collective-permute-start.2 = (bf16[512,384]{1,0:T(8,128)(2,1)S(1)}, bf16[512,384]{1,0:T(8,128)(2,1)S(1)}, u32[]{:S(2)}, u32[]{:S(2)}) collective-permute-start(bf16[512,384]{1,0:T(8,128)(2,1)S(1)} %get-tuple-element.15), channel_id=1, source_target_pairs={{0,4},{4,8},{6,2},{8,12},{10,6},{14,10},{1,5},{5,9},{7,3},{9,13},{... | collective-permute-start | bytes 1179656 | tf_op jit(solution)/shard_map/ppermute | solution.py:393
  25.3 1.3 %collective-permute-start.4 = (bf16[512,384]{1,0:T(8,128)(2,1)S(1)}, bf16[512,384]{1,0:T(8,128)(2,1)S(1)}, u32[]{:S(2)}, u32[]{:S(2)}) collective-permute-start(bf16[512,384]{1,0:T(8,128)(2,1)S(1)} %get-tuple-element.16), channel_id=1, source_target_pairs={{2,6},{4,0},{6,10},{8,4},{10,14},{12,8},{3,7},{5,1},{7,11},{9,5},{... | collective-permute-start | bytes 1179656 | tf_op jit(solution)/shard_map/ppermute | solution.py:391
  26.8 4.6 %collective-permute-start.8 = (bf16[512,768]{1,0:T(8,128)(2,1)S(1)}, bf16[512,768]{1,0:T(8,128)(2,1)S(1)}, u32[]{:S(2)}, u32[]{:S(2)}) collective-permute-start(bf16[512,768]{1,0:T(8,128)(2,1)S(1)} %tie.5), channel_id=1, source_target_pairs={{0,4},{4,8},{6,2},{8,12},{10,6},{14,10},{1,5},{5,9},{7,3},{9,13},{... | collective-permute-start | bytes 2359304 | tf_op jit(solution)/shard_map/ppermute | solution.py:396
  31.4 1.3 %collective-permute-start.15 = (bf16[512,768]{1,0:T(8,128)(2,1)S(1)}, bf16[512,768]{1,0:T(8,128)(2,1)S(1)}, u32[]{:S(2)}, u32[]{:S(2)}) collective-permute-start(bf16[512,768]{1,0:T(8,128)(2,1)S(1)} %collective-permute-done.9.rest_1_), channel_id=1, source_target_pairs={{2,6},{4,0},{6,10},{8,4},{10,14},{12,8},{3,7},{5,1},{7,11},{9,5},{... | collective-permute-start | bytes 2359304 | tf_op jit(solution)/shard_map/ppermute | solution.py:394
  32.7 4.7 %collective-permute-done.3.refs_1_.query = bf16[256,1536]{1,0:T(8,128)(2,1)S(1)} collective-permute-done((bf16[256,1536]{1,0:T(8,128)(2,1)S(1)}, bf16[256,1536]{1,0:T(8,128)(2,1)S(1)}, u32[]{:S(2)}, u32[]{:S(2)}) %collective-permute-start.3) | collective-permute-done | bytes 786464 | tf_op jit(solution)/shard_map/ppermute | solution.py:392
  37.4 1.8 %collective-permute-done.4.refs_2_.rest_2_.rest_1_ = bf16[512,384]{1,0:T(8,128)(2,1)S(1)} collective-permute-done((bf16[512,384]{1,0:T(8,128)(2,1)S(1)}, bf16[512,384]{1,0:T(8,128)(2,1)S(1)}, u32[]{:S(2)}, u32[]{:S(2)}) %collective-permute-start.4) | collective-permute-done | bytes 393248 | tf_op jit(solution)/shard_map/ppermute | solution.py:391
  39.2 0.5 collective-permute-start.6
  39.9 1.6 %collective-permute-done.5.sib_keys = bf16[256,1536]{1,0:T(8,128)(2,1)S(1)} collective-permute-done((bf16[256,1536]{1,0:T(8,128)(2,1)S(1)}, bf16[256,1536]{1,0:T(8,128)(2,1)S(1)}, u32[]{:S(2)}, u32[]{:S(2)}) %collective-permute-start.5) | collective-permute-done | bytes 786464 | tf_op jit(solution)/shard_map/ppermute | solution.py:400
  41.5 3.4 %collective-permute-start.12 = (bf16[512,384]{1,0:T(8,128)(2,1)S(1)}, bf16[512,384]{1,0:T(8,128)(2,1)S(1)}, u32[]{:S(2)}, u32[]{:S(2)}) collective-permute-start(bf16[512,384]{1,0:T(8,128)(2,1)S(1)} %collective-permute-done.2.refs_0_.rest_1_), channel_id=1, source_target_pairs={{0,4},{4,8},{6,2},{8,12},{10,6},{14,10},{1,5},{5,9},{7,3},{9,13},{... | collective-permute-start | bytes 1179656 | tf_op jit(solution)/shard_map/ppermute | solution.py:397
  44.9 1.5 %collective-permute-start.10 = (bf16[512,384]{1,0:T(8,128)(2,1)S(1)}, bf16[512,384]{1,0:T(8,128)(2,1)S(1)}, u32[]{:S(2)}, u32[]{:S(2)}) collective-permute-start(bf16[512,384]{1,0:T(8,128)(2,1)S(1)} %collective-permute-done.4.refs_2_.rest_2_.rest_1_), channel_id=1, source_target_pairs={{2,6},{4,0},{6,10},{8,4},{10,14},{12,8},{3,7},{5,1},{7,11},{9,5},{... | collective-permute-start | bytes 1179656 | tf_op jit(solution)/shard_map/ppermute | solution.py:398
  46.4 1.9 %own_part.4 = (f32[256,384]{1,0:T(8,128)S(1)}, f32[256,128]{1,0:T(8,128)S(1)}) custom-call(s32[8,8]{1,0:T(8,128)S(1)} %copy-done.3, bf16[256,1536]{1,0:T(8,128)(2,1)S(1)} %copy-done.2, bf16[256,1536]{1,0:T(8,128)(2,1)S(1)} %copy-done, bf16[256,1536]{1,0:T(8,128)(2,1)S(1)} %copy-done.1, bf16[256,1536]{1,0:T(8,128)(2,1)S(1)} %collective-permute-done.5.sib_keys, ...), custom_call_target="tpu_custom_call" | custom-call | flops 301989888 | bytes 1048576 | tf_op jit(solution)/shard_map/own_part/pallas_call | solution.py:297
  48.3 1.8 %partner_part.4.rest_4_ = bf16[272,384]{1,0:T(8,128)(2,1)S(1)} custom-call(s32[8,8]{1,0:T(8,128)S(1)} %copy-done.3, bf16[256,1536]{1,0:T(8,128)(2,1)S(1)} %collective-permute-done.3.refs_1_.query, bf16[256,1536]{1,0:T(8,128)(2,1)S(1)} %copy-done, bf16[256,1536]{1,0:T(8,128)(2,1)S(1)} %copy-done.1, bf16[256,1536]{1,0:T(8,128)(2,1)S(1)} %collective-permute-done.5.sib_keys, ...), custom_call_target="tpu_custom_call" | custom-call | flops 301989888 | bytes 1048576 | tf_op jit(solution)/shard_map/partner_part/pallas_call | solution.py:297
  50.2 1.5 %collective-permute-done.8.rest_0_.rest_5_ = bf16[512,768]{1,0:T(8,128)(2,1)S(1)} collective-permute-done((bf16[512,768]{1,0:T(8,128)(2,1)S(1)}, bf16[512,768]{1,0:T(8,128)(2,1)S(1)}, u32[]{:S(2)}, u32[]{:S(2)}) %collective-permute-start.8) | collective-permute-done | bytes 786464 | tf_op jit(solution)/shard_map/ppermute | solution.py:396
  51.6 2.4 %collective-permute-start.13 = (bf16[272,384]{1,0:T(8,128)(2,1)S(1)}, bf16[272,384]{1,0:T(8,128)(2,1)S(1)}, u32[]{:S(2)}, u32[]{:S(2)}) collective-permute-start(bf16[272,384]{1,0:T(8,128)(2,1)S(1)} %partner_part.4.rest_4_), channel_id=1, source_target_pairs={{0,2},{2,0},{4,6},{6,4},{8,10},{10,8},{12,14},{14,12},{1,3},{3,1},... | collective-permute-start | bytes 626696 | tf_op jit(solution)/shard_map/ppermute | solution.py:451
  54.1 2.0 %collective-permute-done.15.rest_2_ = bf16[512,768]{1,0:T(8,128)(2,1)S(1)} collective-permute-done((bf16[512,768]{1,0:T(8,128)(2,1)S(1)}, bf16[512,768]{1,0:T(8,128)(2,1)S(1)}, u32[]{:S(2)}, u32[]{:S(2)}) %collective-permute-start.15) | collective-permute-done | bytes 786464 | tf_op jit(solution)/shard_map/ppermute | solution.py:394
  56.1 2.2 %partner_part.6.rest_4_ = bf16[272,384]{1,0:T(8,128)(2,1)S(1)} custom-call(s32[8,8]{1,0:T(8,128)S(1)} %copy-done.3, bf16[256,1536]{1,0:T(8,128)(2,1)S(1)} %collective-permute-done.3.refs_1_.query, bf16[256,1536]{1,0:T(8,128)(2,1)S(1)} %copy-done, bf16[256,1536]{1,0:T(8,128)(2,1)S(1)} %copy-done.1, bf16[256,1536]{1,0:T(8,128)(2,1)S(1)} %collective-permute-done.5.sib_keys, ...), custom_call_target="tpu_custom_call" | custom-call | flops 301989888 | bytes 1048576 | tf_op jit(solution)/shard_map/partner_part/pallas_call | solution.py:297
  58.3 2.3 %partner_part.7 = bf16[272,384]{1,0:T(8,128)(2,1)S(1)} custom-call(s32[8,8]{1,0:T(8,128)S(1)} %copy-done.3, bf16[256,1536]{1,0:T(8,128)(2,1)S(1)} %collective-permute-done.3.refs_1_.query, bf16[256,1536]{1,0:T(8,128)(2,1)S(1)} %copy-done, bf16[256,1536]{1,0:T(8,128)(2,1)S(1)} %copy-done.1, bf16[256,1536]{1,0:T(8,128)(2,1)S(1)} %collective-permute-done.5.sib_keys, ...), custom_call_target="tpu_custom_call" | custom-call | flops 301989888 | bytes 1048576 | tf_op jit(solution)/shard_map/partner_part/pallas_call | solution.py:297
  60.6 2.0 %collective-permute-start.16 = (bf16[272,384]{1,0:T(8,128)(2,1)S(1)}, bf16[272,384]{1,0:T(8,128)(2,1)S(1)}, u32[]{:S(2)}, u32[]{:S(2)}) collective-permute-start(bf16[272,384]{1,0:T(8,128)(2,1)S(1)} %partner_part.6.rest_4_), channel_id=1, source_target_pairs={{0,2},{2,0},{4,6},{6,4},{8,10},{10,8},{12,14},{14,12},{1,3},{3,1},... | collective-permute-start | bytes 626696 | tf_op jit(solution)/shard_map/ppermute | solution.py:452
  62.6 3.0 %own_part.3 = (f32[256,768]{1,0:T(8,128)S(1)}, f32[256,128]{1,0:T(8,128)S(1)}) custom-call(s32[8,8]{1,0:T(8,128)S(1)} %copy-done.3, bf16[256,1536]{1,0:T(8,128)(2,1)S(1)} %copy-done.2, bf16[256,1536]{1,0:T(8,128)(2,1)S(1)} %copy-done, bf16[256,1536]{1,0:T(8,128)(2,1)S(1)} %copy-done.1, bf16[256,1536]{1,0:T(8,128)(2,1)S(1)} %collective-permute-done.5.sib_keys, ...), custom_call_target="tpu_custom_call" | custom-call | flops 603979776 | bytes 1048576 | tf_op jit(solution)/shard_map/own_part/pallas_call | solution.py:297
  65.7 2.3 %partner_part.5 = bf16[272,384]{1,0:T(8,128)(2,1)S(1)} custom-call(s32[8,8]{1,0:T(8,128)S(1)} %copy-done.3, bf16[256,1536]{1,0:T(8,128)(2,1)S(1)} %collective-permute-done.3.refs_1_.query, bf16[256,1536]{1,0:T(8,128)(2,1)S(1)} %copy-done, bf16[256,1536]{1,0:T(8,128)(2,1)S(1)} %copy-done.1, bf16[256,1536]{1,0:T(8,128)(2,1)S(1)} %collective-permute-done.5.sib_keys, ...), custom_call_target="tpu_custom_call" | custom-call | flops 301989888 | bytes 1048576 | tf_op jit(solution)/shard_map/partner_part/pallas_call | solution.py:297
  68.0 0.1 collective-permute-start.14
  68.1 2.2 %own_part.5 = (f32[256,384]{1,0:T(8,128)S(1)}, f32[256,128]{1,0:T(8,128)S(1)}) custom-call(s32[8,8]{1,0:T(8,128)S(1)} %copy-done.3, bf16[256,1536]{1,0:T(8,128)(2,1)S(1)} %copy-done.2, bf16[256,1536]{1,0:T(8,128)(2,1)S(1)} %copy-done, bf16[256,1536]{1,0:T(8,128)(2,1)S(1)} %copy-done.1, bf16[256,1536]{1,0:T(8,128)(2,1)S(1)} %collective-permute-done.5.sib_keys, ...), custom_call_target="tpu_custom_call" | custom-call | flops 301989888 | bytes 1048576 | tf_op jit(solution)/shard_map/own_part/pallas_call | solution.py:297
  70.3 0.6 collective-permute-done.16.refs_9_
  70.9 3.7 %merge_and_project.2.refs_5_ = f32[256,3072]{1,0:T(8,128)S(1)} custom-call(bf16[768,3072]{1,0:T(8,128)(2,1)S(1)} %bitcast.1, bf16[768,3072]{1,0:T(8,128)(2,1)S(1)} %collective-permute-done.refs_0_.rest_7_.refs_1_, f32[256,384]{1,0:T(8,128)S(1)} %get-tuple-element.22.refs_2_, f32[256,128]{1,0:T(8,128)S(1)} %get-tuple-element.23.refs_3_, ...), custom_call_target="tpu_custom_call" | custom-call | flops 1811939328 | bytes 4194304 | tf_op jit(solution)/shard_map/merge_and_project/pallas_call | solution.py:340
  74.6 2.7 %merge_and_project.3 = bf16[256,3072]{1,0:T(8,128)(2,1)} custom-call(bf16[768,3072]{1,0:T(8,128)(2,1)S(1)} %bitcast.1, bf16[768,3072]{1,0:T(8,128)(2,1)S(1)} %collective-permute-done.refs_0_.rest_7_.refs_1_, f32[256,768]{1,0:T(8,128)S(1)} %get-tuple-element.19.refs_6_.refs_2_, f32[256,128]{1,0:T(8,128)S(1)} %get-tuple-element.20.rest_4_.refs_7_.refs_3_, ...), custom_call_target="tpu_custom_call" | custom-call | flops 603979776 | bytes 4194304 | tf_op jit(solution)/shard_map/merge_and_project/pallas_call | solution.py:340
  (42 shorter events, 0.7 us)
Async XLA Ops:
  0.0 21.2 %collective-permute-start = (bf16[768,3072]{1,0:T(8,128)(2,1)}, bf16[768,3072]{1,0:T(8,128)(2,1)S(1)}, u32[]{:S(2)}, u32[]{:S(2)}) collective-permute-start(bf16[768,3072]{1,0:T(8,128)(2,1)} %refs_0_.3), channel_id=1, source_target_pairs={{0,1},{1,0},{2,3},{3,2},{4,5},{5,4},{6,7},{7,6},{8,9},{9,8},{10,11... | collective-permute-start | bytes 14155784 | tf_op jit(solution)/shard_map/ppermute | solution.py:388
  2.2 6.3 %copy-start = (bf16[256,1536]{1,0:T(8,128)(2,1)S(1)}, bf16[256,1536]{1,0:T(8,128)(2,1)}, u32[]{:S(2)}) copy-start(bf16[256,1536]{1,0:T(8,128)(2,1)} %keys.13) | copy-start | bytes 2359300
  2.2 6.3 %copy-start.1 = (bf16[256,1536]{1,0:T(8,128)(2,1)S(1)}, bf16[256,1536]{1,0:T(8,128)(2,1)}, u32[]{:S(2)}) copy-start(bf16[256,1536]{1,0:T(8,128)(2,1)} %values.13) | copy-start | bytes 2359300
  2.3 24.4 %collective-permute-start.7 = (bf16[512,768]{1,0:T(8,128)(2,1)S(1)}, bf16[512,768]{1,0:T(8,128)(2,1)S(1)}, u32[]{:S(2)}, u32[]{:S(2)}) collective-permute-start(bf16[512,768]{1,0:T(8,128)(2,1)S(1)} %pad_maximum_fusion), channel_id=1, source_target_pairs={{0,4},{4,8},{6,2},{8,12},{10,6},{14,10},{1,5},{5,9},{7,3},{9,13},{... | collective-permute-start | bytes 2359304 | tf_op jit(solution)/shard_map/ppermute | solution.py:385
  7.0 4.3 %copy-start.2 = (bf16[256,1536]{1,0:T(8,128)(2,1)S(1)}, bf16[256,1536]{1,0:T(8,128)(2,1)}, u32[]{:S(2)}) copy-start(bf16[256,1536]{1,0:T(8,128)(2,1)} %query.5) | copy-start | bytes 2359300
  7.0 24.3 %collective-permute-start.9 = (bf16[512,768]{1,0:T(8,128)(2,1)S(1)}, bf16[512,768]{1,0:T(8,128)(2,1)S(1)}, u32[]{:S(2)}, u32[]{:S(2)}) collective-permute-start(bf16[512,768]{1,0:T(8,128)(2,1)S(1)} %pad_maximum_fusion.2), channel_id=1, source_target_pairs={{2,6},{4,0},{6,10},{8,4},{10,14},{12,8},{3,7},{5,1},{7,11},{9,5},{... | collective-permute-start | bytes 2359304 | tf_op jit(solution)/shard_map/ppermute | solution.py:386
  8.6 12.6 %collective-permute-start.1 = (bf16[512,384]{1,0:T(8,128)(2,1)S(1)}, bf16[512,384]{1,0:T(8,128)(2,1)S(1)}, u32[]{:S(2)}, u32[]{:S(2)}) collective-permute-start(bf16[512,384]{1,0:T(8,128)(2,1)S(1)} %pad_maximum_fusion.3), channel_id=1, source_target_pairs={{0,2},{2,0},{4,6},{6,4},{8,10},{10,8},{12,14},{14,12},{1,3},{3,1},... | collective-permute-start | bytes 1179656 | tf_op jit(solution)/shard_map/ppermute | solution.py:389
  11.3 26.1 %collective-permute-start.3 = (bf16[256,1536]{1,0:T(8,128)(2,1)S(1)}, bf16[256,1536]{1,0:T(8,128)(2,1)S(1)}, u32[]{:S(2)}, u32[]{:S(2)}) collective-permute-start(bf16[256,1536]{1,0:T(8,128)(2,1)S(1)} %copy-done.2), channel_id=1, source_target_pairs={{0,2},{2,0},{4,6},{6,4},{8,10},{10,8},{12,14},{14,12},{1,3},{3,1},... | collective-permute-start | bytes 2359304 | tf_op jit(solution)/shard_map/ppermute | solution.py:392
  21.2 16.1 %collective-permute-start.2 = (bf16[512,384]{1,0:T(8,128)(2,1)S(1)}, bf16[512,384]{1,0:T(8,128)(2,1)S(1)}, u32[]{:S(2)}, u32[]{:S(2)}) collective-permute-start(bf16[512,384]{1,0:T(8,128)(2,1)S(1)} %get-tuple-element.15), channel_id=1, source_target_pairs={{0,4},{4,8},{6,2},{8,12},{10,6},{14,10},{1,5},{5,9},{7,3},{9,13},{... | collective-permute-start | bytes 1179656 | tf_op jit(solution)/shard_map/ppermute | solution.py:393
  25.3 13.9 %collective-permute-start.4 = (bf16[512,384]{1,0:T(8,128)(2,1)S(1)}, bf16[512,384]{1,0:T(8,128)(2,1)S(1)}, u32[]{:S(2)}, u32[]{:S(2)}) collective-permute-start(bf16[512,384]{1,0:T(8,128)(2,1)S(1)} %get-tuple-element.16), channel_id=1, source_target_pairs={{2,6},{4,0},{6,10},{8,4},{10,14},{12,8},{3,7},{5,1},{7,11},{9,5},{... | collective-permute-start | bytes 1179656 | tf_op jit(solution)/shard_map/ppermute | solution.py:391
  26.8 24.9 %collective-permute-start.8 = (bf16[512,768]{1,0:T(8,128)(2,1)S(1)}, bf16[512,768]{1,0:T(8,128)(2,1)S(1)}, u32[]{:S(2)}, u32[]{:S(2)}) collective-permute-start(bf16[512,768]{1,0:T(8,128)(2,1)S(1)} %tie.5), channel_id=1, source_target_pairs={{0,4},{4,8},{6,2},{8,12},{10,6},{14,10},{1,5},{5,9},{7,3},{9,13},{... | collective-permute-start | bytes 2359304 | tf_op jit(solution)/shard_map/ppermute | solution.py:396
  31.4 24.7 %collective-permute-start.15 = (bf16[512,768]{1,0:T(8,128)(2,1)S(1)}, bf16[512,768]{1,0:T(8,128)(2,1)S(1)}, u32[]{:S(2)}, u32[]{:S(2)}) collective-permute-start(bf16[512,768]{1,0:T(8,128)(2,1)S(1)} %collective-permute-done.9.rest_1_), channel_id=1, source_target_pairs={{2,6},{4,0},{6,10},{8,4},{10,14},{12,8},{3,7},{5,1},{7,11},{9,5},{... | collective-permute-start | bytes 2359304 | tf_op jit(solution)/shard_map/ppermute | solution.py:394
  39.2 7.2 %copy-start.3 = (s32[8,8]{1,0:T(8,128)S(1)}, s32[8,8]{1,0:T(8,128)}, u32[]{:S(2)}) copy-start(s32[8,8]{1,0:T(8,128)} %table_ref.13) | copy-start | bytes 772
  39.2 2.3 %collective-permute-start.5 = (bf16[256,1536]{1,0:T(8,128)(2,1)S(1)}, bf16[256,1536]{1,0:T(8,128)(2,1)S(1)}, u32[]{:S(2)}, u32[]{:S(2)}) collective-permute-start(bf16[256,1536]{1,0:T(8,128)(2,1)S(1)} %get-tuple-element.17), channel_id=1, source_target_pairs={{0,1},{1,0},{2,3},{3,2},{4,5},{5,4},{6,7},{7,6},{8,9},{9,8},{10,11... | collective-permute-start | bytes 2359304 | tf_op jit(solution)/shard_map/ppermute | solution.py:400
  39.2 5.7 %collective-permute-start.6 = (bf16[256,1536]{1,0:T(8,128)(2,1)S(1)}, bf16[256,1536]{1,0:T(8,128)(2,1)S(1)}, u32[]{:S(2)}, u32[]{:S(2)}) collective-permute-start(bf16[256,1536]{1,0:T(8,128)(2,1)S(1)} %get-tuple-element.18), channel_id=1, source_target_pairs={{0,1},{1,0},{2,3},{3,2},{4,5},{5,4},{6,7},{7,6},{8,9},{9,8},{10,11... | collective-permute-start | bytes 2359304 | tf_op jit(solution)/shard_map/ppermute | solution.py:401
  39.8 16.2 %collective-permute-start.11 = (bf16[256,1536]{1,0:T(8,128)(2,1)S(1)}, bf16[256,1536]{1,0:T(8,128)(2,1)S(1)}, u32[]{:S(2)}, u32[]{:S(2)}) collective-permute-start(bf16[256,1536]{1,0:T(8,128)(2,1)S(1)} %maximum_maximum_fusion), channel_id=1, source_target_pairs={{0,1},{1,0},{2,3},{3,2},{4,5},{5,4},{6,7},{7,6},{8,9},{9,8},{10,11... | collective-permute-start | bytes 2359304 | tf_op jit(solution)/shard_map/ppermute | solution.py:402
  41.5 24.2 %collective-permute-start.12 = (bf16[512,384]{1,0:T(8,128)(2,1)S(1)}, bf16[512,384]{1,0:T(8,128)(2,1)S(1)}, u32[]{:S(2)}, u32[]{:S(2)}) collective-permute-start(bf16[512,384]{1,0:T(8,128)(2,1)S(1)} %collective-permute-done.2.refs_0_.rest_1_), channel_id=1, source_target_pairs={{0,4},{4,8},{6,2},{8,12},{10,6},{14,10},{1,5},{5,9},{7,3},{9,13},{... | collective-permute-start | bytes 1179656 | tf_op jit(solution)/shard_map/ppermute | solution.py:397
  44.9 20.7 %collective-permute-start.10 = (bf16[512,384]{1,0:T(8,128)(2,1)S(1)}, bf16[512,384]{1,0:T(8,128)(2,1)S(1)}, u32[]{:S(2)}, u32[]{:S(2)}) collective-permute-start(bf16[512,384]{1,0:T(8,128)(2,1)S(1)} %collective-permute-done.4.refs_2_.rest_2_.rest_1_), channel_id=1, source_target_pairs={{2,6},{4,0},{6,10},{8,4},{10,14},{12,8},{3,7},{5,1},{7,11},{9,5},{... | collective-permute-start | bytes 1179656 | tf_op jit(solution)/shard_map/ppermute | solution.py:398
  51.6 14.0 %collective-permute-start.13 = (bf16[272,384]{1,0:T(8,128)(2,1)S(1)}, bf16[272,384]{1,0:T(8,128)(2,1)S(1)}, u32[]{:S(2)}, u32[]{:S(2)}) collective-permute-start(bf16[272,384]{1,0:T(8,128)(2,1)S(1)} %partner_part.4.rest_4_), channel_id=1, source_target_pairs={{0,2},{2,0},{4,6},{6,4},{8,10},{10,8},{12,14},{14,12},{1,3},{3,1},... | collective-permute-start | bytes 626696 | tf_op jit(solution)/shard_map/ppermute | solution.py:451
  60.6 9.8 %collective-permute-start.17 = (bf16[272,384]{1,0:T(8,128)(2,1)S(1)}, bf16[272,384]{1,0:T(8,128)(2,1)S(1)}, u32[]{:S(2)}, u32[]{:S(2)}) collective-permute-start(bf16[272,384]{1,0:T(8,128)(2,1)S(1)} %partner_part.7), channel_id=1, source_target_pairs={{0,2},{2,0},{4,6},{6,4},{8,10},{10,8},{12,14},{14,12},{1,3},{3,1},... | collective-permute-start | bytes 626696 | tf_op jit(solution)/shard_map/ppermute | solution.py:453
  60.6 10.3 %collective-permute-start.16 = (bf16[272,384]{1,0:T(8,128)(2,1)S(1)}, bf16[272,384]{1,0:T(8,128)(2,1)S(1)}, u32[]{:S(2)}, u32[]{:S(2)}) collective-permute-start(bf16[272,384]{1,0:T(8,128)(2,1)S(1)} %partner_part.6.rest_4_), channel_id=1, source_target_pairs={{0,2},{2,0},{4,6},{6,4},{8,10},{10,8},{12,14},{14,12},{1,3},{3,1},... | collective-permute-start | bytes 626696 | tf_op jit(solution)/shard_map/ppermute | solution.py:452
  65.7 5.2 %slice-start = ((s8[4718592]{0:T(1024)(128)(4,1)}), s8[4194304]{0:T(1024)(128)(4,1)S(1)}, s32[]{:S(2)}) async-start(s8[4718592]{0:T(1024)(128)(4,1)} %bitcast), calls=%async_computation | async-start | bytes 8388608
  65.7 5.2 %slice-start.1 = ((s8[4718592]{0:T(1024)(128)(4,1)}), s8[524288]{0:T(1024)(128)(4,1)S(1)}, s32[]{:S(2)}) async-start(s8[4718592]{0:T(1024)(128)(4,1)} %bitcast), calls=%async_computation.1 | async-start | bytes 1048576
  68.0 6.6 %collective-permute-start.14 = (bf16[272,384]{1,0:T(8,128)(2,1)S(1)}, bf16[272,384]{1,0:T(8,128)(2,1)S(1)}, u32[]{:S(2)}, u32[]{:S(2)}) collective-permute-start(bf16[272,384]{1,0:T(8,128)(2,1)S(1)} %partner_part.5), channel_id=1, source_target_pairs={{0,2},{2,0},{4,6},{6,4},{8,10},{10,8},{12,14},{14,12},{1,3},{3,1},... | collective-permute-start | bytes 626696 | tf_op jit(solution)/shard_map/ppermute | solution.py:460

commit v12 on v11

--- a/solution.py
+++ b/solution.py
@@ -444,14 +444,14 @@
 
     own_early = own_part((3, 6), ("major1", "minor1"))
     part_low = partner_part((0, 3), ("major1", "major2"), (own_early[1],))
+    own_late = own_part((6, 12), ("major3", "minor1", "minor2"), (part_low,))
     part_middle = partner_part(
-        (3, 6), ("major1", "minor1", "minor3", "nearest"), (part_low, major3)
+        (3, 6), ("major1", "minor1", "minor3", "nearest"), (own_late[1],)
     )
     part_late = partner_part((6, 9), ("major3", "minor1", "minor3", "nearest"), (part_middle,))
     part_low = lax.ppermute(part_low, "frame", partner_moves)
     part_middle = lax.ppermute(part_middle, "frame", partner_moves)
     part_late = lax.ppermute(part_late, "frame", partner_moves)
-    own_late = own_part((6, 12), ("major3", "minor1", "minor2"))
     part_high = partner_part(
         (9, 12),
         ("major3", "minor2", "minor4", "nearest"),

time: 77.6 us -> 78.3 us (level)
  starting transfers between devices: 30.6 us -> 31.7 us
    ppermute x1, waiting for transfers between devices: 0.01 us -> 3.23 us  [per_device(): part_late = lax.ppermute(part_late, 'frame', partner_moves)]
    ppermute x1, starting transfers between devices: 0.05 us -> 2.05 us  [per_device(): part_late = lax.ppermute(part_late, 'frame', partner_moves)]
    ppermute x1, waiting for transfers between devices: 1.99 us -> 0.01 us  [per_device(): minor3 = lax.ppermute(minor1, 'frame', near_moves)]
    ppermute x1, starting transfers between devices: 2.01 us -> 0.05 us  [per_device(): part_middle = lax.ppermute(part_middle, 'frame', partner_moves)]
    ppermute x1, starting transfers between devices: 3.43 us -> 4.75 us  [per_device(): major4 = lax.ppermute(major2, 'frame', away_moves)]
    ppermute x1, waiting for transfers between devices: 1.48 us -> 0.34 us  [per_device(): major3 = lax.ppermute(to_major3, 'frame', away_moves)]
  transfers between devices with their start and end apart: 18 -> 18, of which waited for: 7 -> 6; matrix products, arithmetic and copies ran while one was open for 3% -> 3% of each run, Pallas kernels for 25% -> 25%
where the time goes in v12:
time: 78.3 us; the launch traced here: 78 us
  starting transfers between devices  31.7 us (40%)
  Pallas kernels  22.1 us (28%)
  waiting for transfers between devices  21.5 us (27%)
  local copies, waits for them, and re-layouts  2.05 us (3%)
    pallas_call x7, Pallas kernels, run(): pl.pallas_call(body, grid=(1,), in_specs=[pl.BlockSpec(memory_space=pltpu...  15.7 us
    ppermute x1, waiting for transfers between devices, per_device(): cross = lax.ppermute(pack(0, 3), 'frame', partner_moves)  9.8 us
    pallas_call x2, Pallas kernels, project(): pl.pallas_call(functools.partial(project_kernel, span, tuple((group for g...  6.38 us
    ppermute x1, starting transfers between devices, per_device(): major4 = lax.ppermute(major2, 'frame', away_moves)  4.75 us
    ppermute x1, starting transfers between devices, per_device(): major1 = lax.ppermute(pack(0, 6), 'frame', away_moves)  4.66 us
    ppermute x1, waiting for transfers between devices, per_device(): partner_query = lax.ppermute(queries, 'frame', partner_moves)  4.65 us
    ppermute x1, starting transfers between devices, per_device(): major3 = lax.ppermute(to_major3, 'frame', away_moves)  4.6 us
    ppermute x1, starting transfers between devices, per_device(): major2 = lax.ppermute(cross, 'frame', away_moves)  4.03 us
  transfers between devices with their start and end apart: 18, of which 6 were waited for; matrix products, arithmetic and copies ran while one was open for 3% of the time, Pallas kernels for 25%

profile of v12, /device:TPU:0, one launch (start us, length us, event | category | flops | bytes accessed | tf_op | source)
XLA Modules:
  0.0 78.0 jit_solution(8207650403630454555)
XLA Ops:
  0.0 0.5 collective-permute-start
  0.5 1.8 %fusion.1 = (bf16[256,768]{1,0:T(8,128)(2,1)S(1)}, bf16[256,768]{1,0:T(8,128)(2,1)S(1)}, bf16[256,768]{1,0:T(8,128)(2,1)S(1)}, bf16[256,768]{1,0:T(8,128)(2,1)S(...) fusion(bf16[256,1536]{1,0:T(8,128)(2,1)} %keys.13, bf16[256,1536]{1,0:T(8,128)(2,1)} %values.13), kind=kLoop, calls=%fused_computation.7 | loop fusion | bytes 4718592 | tf_op jit(solution)/shard_map/slice | solution.py:377
  2.3 4.7 %collective-permute-start.7 = (bf16[512,768]{1,0:T(8,128)(2,1)S(1)}, bf16[512,768]{1,0:T(8,128)(2,1)S(1)}, u32[]{:S(2)}, u32[]{:S(2)}) collective-permute-start(bf16[512,768]{1,0:T(8,128)(2,1)S(1)} %pad_maximum_fusion), channel_id=1, source_target_pairs={{0,4},{4,8},{6,2},{8,12},{10,6},{14,10},{1,5},{5,9},{7,3},{9,13},{... | collective-permute-start | bytes 2359304 | tf_op jit(solution)/shard_map/ppermute | solution.py:385
  7.0 1.4 %collective-permute-start.9 = (bf16[512,768]{1,0:T(8,128)(2,1)S(1)}, bf16[512,768]{1,0:T(8,128)(2,1)S(1)}, u32[]{:S(2)}, u32[]{:S(2)}) collective-permute-start(bf16[512,768]{1,0:T(8,128)(2,1)S(1)} %pad_maximum_fusion.2), channel_id=1, source_target_pairs={{2,6},{4,0},{6,10},{8,4},{10,14},{12,8},{3,7},{5,1},{7,11},{9,5},{... | collective-permute-start | bytes 2359304 | tf_op jit(solution)/shard_map/ppermute | solution.py:386
  8.5 0.1 fusion.3
  8.6 2.7 %collective-permute-start.1 = (bf16[512,384]{1,0:T(8,128)(2,1)S(1)}, bf16[512,384]{1,0:T(8,128)(2,1)S(1)}, u32[]{:S(2)}, u32[]{:S(2)}) collective-permute-start(bf16[512,384]{1,0:T(8,128)(2,1)S(1)} %pad_maximum_fusion.3), channel_id=1, source_target_pairs={{0,2},{2,0},{4,6},{6,4},{8,10},{10,8},{12,14},{14,12},{1,3},{3,1},... | collective-permute-start | bytes 1179656 | tf_op jit(solution)/shard_map/ppermute | solution.py:389
  11.3 0.1 collective-permute-start.3
  11.4 9.8 %collective-permute-done.1.refs_1_ = bf16[512,384]{1,0:T(8,128)(2,1)S(1)} collective-permute-done((bf16[512,384]{1,0:T(8,128)(2,1)S(1)}, bf16[512,384]{1,0:T(8,128)(2,1)S(1)}, u32[]{:S(2)}, u32[]{:S(2)}) %collective-permute-start.1) | collective-permute-done | bytes 393248 | tf_op jit(solution)/shard_map/ppermute | solution.py:389
  21.2 4.0 %collective-permute-start.2 = (bf16[512,384]{1,0:T(8,128)(2,1)S(1)}, bf16[512,384]{1,0:T(8,128)(2,1)S(1)}, u32[]{:S(2)}, u32[]{:S(2)}) collective-permute-start(bf16[512,384]{1,0:T(8,128)(2,1)S(1)} %get-tuple-element.15), channel_id=1, source_target_pairs={{0,4},{4,8},{6,2},{8,12},{10,6},{14,10},{1,5},{5,9},{7,3},{9,13},{... | collective-permute-start | bytes 1179656 | tf_op jit(solution)/shard_map/ppermute | solution.py:393
  25.3 1.3 %collective-permute-start.4 = (bf16[512,384]{1,0:T(8,128)(2,1)S(1)}, bf16[512,384]{1,0:T(8,128)(2,1)S(1)}, u32[]{:S(2)}, u32[]{:S(2)}) collective-permute-start(bf16[512,384]{1,0:T(8,128)(2,1)S(1)} %get-tuple-element.16), channel_id=1, source_target_pairs={{2,6},{4,0},{6,10},{8,4},{10,14},{12,8},{3,7},{5,1},{7,11},{9,5},{... | collective-permute-start | bytes 1179656 | tf_op jit(solution)/shard_map/ppermute | solution.py:391
  26.8 4.6 %collective-permute-start.8 = (bf16[512,768]{1,0:T(8,128)(2,1)S(1)}, bf16[512,768]{1,0:T(8,128)(2,1)S(1)}, u32[]{:S(2)}, u32[]{:S(2)}) collective-permute-start(bf16[512,768]{1,0:T(8,128)(2,1)S(1)} %tie.5), channel_id=1, source_target_pairs={{0,4},{4,8},{6,2},{8,12},{10,6},{14,10},{1,5},{5,9},{7,3},{9,13},{... | collective-permute-start | bytes 2359304 | tf_op jit(solution)/shard_map/ppermute | solution.py:396
  31.4 1.3 %collective-permute-start.15 = (bf16[512,768]{1,0:T(8,128)(2,1)S(1)}, bf16[512,768]{1,0:T(8,128)(2,1)S(1)}, u32[]{:S(2)}, u32[]{:S(2)}) collective-permute-start(bf16[512,768]{1,0:T(8,128)(2,1)S(1)} %collective-permute-done.9.rest_1_), channel_id=1, source_target_pairs={{2,6},{4,0},{6,10},{8,4},{10,14},{12,8},{3,7},{5,1},{7,11},{9,5},{... | collective-permute-start | bytes 2359304 | tf_op jit(solution)/shard_map/ppermute | solution.py:394
  32.7 4.7 %collective-permute-done.3.refs_1_.query = bf16[256,1536]{1,0:T(8,128)(2,1)S(1)} collective-permute-done((bf16[256,1536]{1,0:T(8,128)(2,1)S(1)}, bf16[256,1536]{1,0:T(8,128)(2,1)S(1)}, u32[]{:S(2)}, u32[]{:S(2)}) %collective-permute-start.3) | collective-permute-done | bytes 786464 | tf_op jit(solution)/shard_map/ppermute | solution.py:392
  37.4 1.8 %collective-permute-done.4.refs_2_.rest_2_.rest_1_ = bf16[512,384]{1,0:T(8,128)(2,1)S(1)} collective-permute-done((bf16[512,384]{1,0:T(8,128)(2,1)S(1)}, bf16[512,384]{1,0:T(8,128)(2,1)S(1)}, u32[]{:S(2)}, u32[]{:S(2)}) %collective-permute-start.4) | collective-permute-done | bytes 393248 | tf_op jit(solution)/shard_map/ppermute | solution.py:391
  39.2 0.5 collective-permute-start.6
  39.9 1.6 %collective-permute-done.5.sib_keys = bf16[256,1536]{1,0:T(8,128)(2,1)S(1)} collective-permute-done((bf16[256,1536]{1,0:T(8,128)(2,1)S(1)}, bf16[256,1536]{1,0:T(8,128)(2,1)S(1)}, u32[]{:S(2)}, u32[]{:S(2)}) %collective-permute-start.5) | collective-permute-done | bytes 786464 | tf_op jit(solution)/shard_map/ppermute | solution.py:400
  41.5 1.3 %collective-permute-start.10 = (bf16[512,384]{1,0:T(8,128)(2,1)S(1)}, bf16[512,384]{1,0:T(8,128)(2,1)S(1)}, u32[]{:S(2)}, u32[]{:S(2)}) collective-permute-start(bf16[512,384]{1,0:T(8,128)(2,1)S(1)} %collective-permute-done.4.refs_2_.rest_2_.rest_1_), channel_id=1, source_target_pairs={{2,6},{4,0},{6,10},{8,4},{10,14},{12,8},{3,7},{5,1},{7,11},{9,5},{... | collective-permute-start | bytes 1179656 | tf_op jit(solution)/shard_map/ppermute | solution.py:398
  42.8 4.8 %collective-permute-start.12 = (bf16[512,384]{1,0:T(8,128)(2,1)S(1)}, bf16[512,384]{1,0:T(8,128)(2,1)S(1)}, u32[]{:S(2)}, u32[]{:S(2)}) collective-permute-start(bf16[512,384]{1,0:T(8,128)(2,1)S(1)} %collective-permute-done.2.refs_0_.rest_1_), channel_id=1, source_target_pairs={{0,4},{4,8},{6,2},{8,12},{10,6},{14,10},{1,5},{5,9},{7,3},{9,13},{... | collective-permute-start | bytes 1179656 | tf_op jit(solution)/shard_map/ppermute | solution.py:397
  47.6 1.9 %own_part.3 = (f32[256,384]{1,0:T(8,128)S(1)}, f32[256,128]{1,0:T(8,128)S(1)}) custom-call(s32[8,8]{1,0:T(8,128)S(1)} %copy-done.3, bf16[256,1536]{1,0:T(8,128)(2,1)S(1)} %copy-done.2, bf16[256,1536]{1,0:T(8,128)(2,1)S(1)} %copy-done, bf16[256,1536]{1,0:T(8,128)(2,1)S(1)} %copy-done.1, bf16[256,1536]{1,0:T(8,128)(2,1)S(1)} %collective-permute-done.5.sib_keys, ...), custom_call_target="tpu_custom_call" | custom-call | flops 301989888 | bytes 1048576 | tf_op jit(solution)/shard_map/own_part/pallas_call | solution.py:297
  49.5 1.8 %partner_part.4.rest_3_ = bf16[272,384]{1,0:T(8,128)(2,1)S(1)} custom-call(s32[8,8]{1,0:T(8,128)S(1)} %copy-done.3, bf16[256,1536]{1,0:T(8,128)(2,1)S(1)} %collective-permute-done.3.refs_1_.query, bf16[256,1536]{1,0:T(8,128)(2,1)S(1)} %copy-done, bf16[256,1536]{1,0:T(8,128)(2,1)S(1)} %copy-done.1, bf16[256,1536]{1,0:T(8,128)(2,1)S(1)} %collective-permute-done.5.sib_keys, ...), custom_call_target="tpu_custom_call" | custom-call | flops 301989888 | bytes 1048576 | tf_op jit(solution)/shard_map/partner_part/pallas_call | solution.py:297
  51.3 0.3 collective-permute-done.8.rest_0_
  51.6 2.4 %collective-permute-start.13 = (bf16[272,384]{1,0:T(8,128)(2,1)S(1)}, bf16[272,384]{1,0:T(8,128)(2,1)S(1)}, u32[]{:S(2)}, u32[]{:S(2)}) collective-permute-start(bf16[272,384]{1,0:T(8,128)(2,1)S(1)} %partner_part.4.rest_3_), channel_id=1, source_target_pairs={{0,2},{2,0},{4,6},{6,4},{8,10},{10,8},{12,14},{14,12},{1,3},{3,1},... | collective-permute-start | bytes 626696 | tf_op jit(solution)/shard_map/ppermute | solution.py:452
  54.1 3.0 %own_part.4 = (f32[256,768]{1,0:T(8,128)S(1)}, f32[256,128]{1,0:T(8,128)S(1)}) custom-call(s32[8,8]{1,0:T(8,128)S(1)} %copy-done.3, bf16[256,1536]{1,0:T(8,128)(2,1)S(1)} %copy-done.2, bf16[256,1536]{1,0:T(8,128)(2,1)S(1)} %copy-done, bf16[256,1536]{1,0:T(8,128)(2,1)S(1)} %copy-done.1, bf16[256,1536]{1,0:T(8,128)(2,1)S(1)} %collective-permute-done.5.sib_keys, ...), custom_call_target="tpu_custom_call" | custom-call | flops 603979776 | bytes 1048576 | tf_op jit(solution)/shard_map/own_part/pallas_call | solution.py:297
  57.1 2.2 %partner_part.6.rest_4_ = bf16[272,384]{1,0:T(8,128)(2,1)S(1)} custom-call(s32[8,8]{1,0:T(8,128)S(1)} %copy-done.3, bf16[256,1536]{1,0:T(8,128)(2,1)S(1)} %collective-permute-done.3.refs_1_.query, bf16[256,1536]{1,0:T(8,128)(2,1)S(1)} %copy-done, bf16[256,1536]{1,0:T(8,128)(2,1)S(1)} %copy-done.1, bf16[256,1536]{1,0:T(8,128)(2,1)S(1)} %collective-permute-done.5.sib_keys, ...), custom_call_target="tpu_custom_call" | custom-call | flops 301989888 | bytes 1048576 | tf_op jit(solution)/shard_map/partner_part/pallas_call | solution.py:297
  59.4 2.2 %partner_part.7 = bf16[272,384]{1,0:T(8,128)(2,1)S(1)} custom-call(s32[8,8]{1,0:T(8,128)S(1)} %copy-done.3, bf16[256,1536]{1,0:T(8,128)(2,1)S(1)} %collective-permute-done.3.refs_1_.query, bf16[256,1536]{1,0:T(8,128)(2,1)S(1)} %copy-done, bf16[256,1536]{1,0:T(8,128)(2,1)S(1)} %copy-done.1, bf16[256,1536]{1,0:T(8,128)(2,1)S(1)} %collective-permute-done.5.sib_keys, ...), custom_call_target="tpu_custom_call" | custom-call | flops 301989888 | bytes 1048576 | tf_op jit(solution)/shard_map/partner_part/pallas_call | solution.py:297
  61.7 2.1 %collective-permute-start.17 = (bf16[272,384]{1,0:T(8,128)(2,1)S(1)}, bf16[272,384]{1,0:T(8,128)(2,1)S(1)}, u32[]{:S(2)}, u32[]{:S(2)}) collective-permute-start(bf16[272,384]{1,0:T(8,128)(2,1)S(1)} %partner_part.7), channel_id=1, source_target_pairs={{0,2},{2,0},{4,6},{6,4},{8,10},{10,8},{12,14},{14,12},{1,3},{3,1},... | collective-permute-start | bytes 626696 | tf_op jit(solution)/shard_map/ppermute | solution.py:454
  63.7 2.2 %partner_part.5 = bf16[272,384]{1,0:T(8,128)(2,1)S(1)} custom-call(s32[8,8]{1,0:T(8,128)S(1)} %copy-done.3, bf16[256,1536]{1,0:T(8,128)(2,1)S(1)} %collective-permute-done.3.refs_1_.query, bf16[256,1536]{1,0:T(8,128)(2,1)S(1)} %copy-done, bf16[256,1536]{1,0:T(8,128)(2,1)S(1)} %copy-done.1, bf16[256,1536]{1,0:T(8,128)(2,1)S(1)} %collective-permute-done.5.sib_keys, ...), custom_call_target="tpu_custom_call" | custom-call | flops 301989888 | bytes 1048576 | tf_op jit(solution)/shard_map/partner_part/pallas_call | solution.py:297
  66.0 0.1 collective-permute-start.14
  66.0 2.2 %own_part.5 = (f32[256,384]{1,0:T(8,128)S(1)}, f32[256,128]{1,0:T(8,128)S(1)}) custom-call(s32[8,8]{1,0:T(8,128)S(1)} %copy-done.3, bf16[256,1536]{1,0:T(8,128)(2,1)S(1)} %copy-done.2, bf16[256,1536]{1,0:T(8,128)(2,1)S(1)} %copy-done, bf16[256,1536]{1,0:T(8,128)(2,1)S(1)} %copy-done.1, bf16[256,1536]{1,0:T(8,128)(2,1)S(1)} %collective-permute-done.5.sib_keys, ...), custom_call_target="tpu_custom_call" | custom-call | flops 301989888 | bytes 1048576 | tf_op jit(solution)/shard_map/own_part/pallas_call | solution.py:297
  68.3 3.2 %collective-permute-done.17.refs_10_ = bf16[272,384]{1,0:T(8,128)(2,1)S(1)} collective-permute-done((bf16[272,384]{1,0:T(8,128)(2,1)S(1)}, bf16[272,384]{1,0:T(8,128)(2,1)S(1)}, u32[]{:S(2)}, u32[]{:S(2)}) %collective-permute-start.17) | collective-permute-done | bytes 208928 | tf_op jit(solution)/shard_map/ppermute | solution.py:454
  71.5 3.6 %merge_and_project.2.refs_5_ = f32[256,3072]{1,0:T(8,128)S(1)} custom-call(bf16[768,3072]{1,0:T(8,128)(2,1)S(1)} %bitcast.1, bf16[768,3072]{1,0:T(8,128)(2,1)S(1)} %collective-permute-done.refs_0_.rest_7_.refs_1_, f32[256,384]{1,0:T(8,128)S(1)} %get-tuple-element.22.refs_2_, f32[256,128]{1,0:T(8,128)S(1)} %get-tuple-element.23.refs_3_, ...), custom_call_target="tpu_custom_call" | custom-call | flops 1811939328 | bytes 4194304 | tf_op jit(solution)/shard_map/merge_and_project/pallas_call | solution.py:340
  75.2 2.7 %merge_and_project.3 = bf16[256,3072]{1,0:T(8,128)(2,1)} custom-call(bf16[768,3072]{1,0:T(8,128)(2,1)S(1)} %bitcast.1, bf16[768,3072]{1,0:T(8,128)(2,1)S(1)} %collective-permute-done.refs_0_.rest_7_.refs_1_, f32[256,768]{1,0:T(8,128)S(1)} %get-tuple-element.20.refs_6_.refs_2_, f32[256,128]{1,0:T(8,128)S(1)} %get-tuple-element.21.rest_4_.refs_7_.refs_3_, ...), custom_call_target="tpu_custom_call" | custom-call | flops 603979776 | bytes 4194304 | tf_op jit(solution)/shard_map/merge_and_project/pallas_call | solution.py:340
  (42 shorter events, 0.7 us)
Async XLA Ops:
  0.0 21.2 %collective-permute-start = (bf16[768,3072]{1,0:T(8,128)(2,1)}, bf16[768,3072]{1,0:T(8,128)(2,1)S(1)}, u32[]{:S(2)}, u32[]{:S(2)}) collective-permute-start(bf16[768,3072]{1,0:T(8,128)(2,1)} %refs_0_.3), channel_id=1, source_target_pairs={{0,1},{1,0},{2,3},{3,2},{4,5},{5,4},{6,7},{7,6},{8,9},{9,8},{10,11... | collective-permute-start | bytes 14155784 | tf_op jit(solution)/shard_map/ppermute | solution.py:388
  2.2 6.3 %copy-start = (bf16[256,1536]{1,0:T(8,128)(2,1)S(1)}, bf16[256,1536]{1,0:T(8,128)(2,1)}, u32[]{:S(2)}) copy-start(bf16[256,1536]{1,0:T(8,128)(2,1)} %keys.13) | copy-start | bytes 2359300
  2.2 6.3 %copy-start.1 = (bf16[256,1536]{1,0:T(8,128)(2,1)S(1)}, bf16[256,1536]{1,0:T(8,128)(2,1)}, u32[]{:S(2)}) copy-start(bf16[256,1536]{1,0:T(8,128)(2,1)} %values.13) | copy-start | bytes 2359300
  2.3 24.4 %collective-permute-start.7 = (bf16[512,768]{1,0:T(8,128)(2,1)S(1)}, bf16[512,768]{1,0:T(8,128)(2,1)S(1)}, u32[]{:S(2)}, u32[]{:S(2)}) collective-permute-start(bf16[512,768]{1,0:T(8,128)(2,1)S(1)} %pad_maximum_fusion), channel_id=1, source_target_pairs={{0,4},{4,8},{6,2},{8,12},{10,6},{14,10},{1,5},{5,9},{7,3},{9,13},{... | collective-permute-start | bytes 2359304 | tf_op jit(solution)/shard_map/ppermute | solution.py:385
  7.0 4.3 %copy-start.2 = (bf16[256,1536]{1,0:T(8,128)(2,1)S(1)}, bf16[256,1536]{1,0:T(8,128)(2,1)}, u32[]{:S(2)}) copy-start(bf16[256,1536]{1,0:T(8,128)(2,1)} %query.5) | copy-start | bytes 2359300
  7.0 24.3 %collective-permute-start.9 = (bf16[512,768]{1,0:T(8,128)(2,1)S(1)}, bf16[512,768]{1,0:T(8,128)(2,1)S(1)}, u32[]{:S(2)}, u32[]{:S(2)}) collective-permute-start(bf16[512,768]{1,0:T(8,128)(2,1)S(1)} %pad_maximum_fusion.2), channel_id=1, source_target_pairs={{2,6},{4,0},{6,10},{8,4},{10,14},{12,8},{3,7},{5,1},{7,11},{9,5},{... | collective-permute-start | bytes 2359304 | tf_op jit(solution)/shard_map/ppermute | solution.py:386
  8.6 12.6 %collective-permute-start.1 = (bf16[512,384]{1,0:T(8,128)(2,1)S(1)}, bf16[512,384]{1,0:T(8,128)(2,1)S(1)}, u32[]{:S(2)}, u32[]{:S(2)}) collective-permute-start(bf16[512,384]{1,0:T(8,128)(2,1)S(1)} %pad_maximum_fusion.3), channel_id=1, source_target_pairs={{0,2},{2,0},{4,6},{6,4},{8,10},{10,8},{12,14},{14,12},{1,3},{3,1},... | collective-permute-start | bytes 1179656 | tf_op jit(solution)/shard_map/ppermute | solution.py:389
  11.3 26.1 %collective-permute-start.3 = (bf16[256,1536]{1,0:T(8,128)(2,1)S(1)}, bf16[256,1536]{1,0:T(8,128)(2,1)S(1)}, u32[]{:S(2)}, u32[]{:S(2)}) collective-permute-start(bf16[256,1536]{1,0:T(8,128)(2,1)S(1)} %copy-done.2), channel_id=1, source_target_pairs={{0,2},{2,0},{4,6},{6,4},{8,10},{10,8},{12,14},{14,12},{1,3},{3,1},... | collective-permute-start | bytes 2359304 | tf_op jit(solution)/shard_map/ppermute | solution.py:392
  21.2 16.1 %collective-permute-start.2 = (bf16[512,384]{1,0:T(8,128)(2,1)S(1)}, bf16[512,384]{1,0:T(8,128)(2,1)S(1)}, u32[]{:S(2)}, u32[]{:S(2)}) collective-permute-start(bf16[512,384]{1,0:T(8,128)(2,1)S(1)} %get-tuple-element.15), channel_id=1, source_target_pairs={{0,4},{4,8},{6,2},{8,12},{10,6},{14,10},{1,5},{5,9},{7,3},{9,13},{... | collective-permute-start | bytes 1179656 | tf_op jit(solution)/shard_map/ppermute | solution.py:393
  25.3 13.9 %collective-permute-start.4 = (bf16[512,384]{1,0:T(8,128)(2,1)S(1)}, bf16[512,384]{1,0:T(8,128)(2,1)S(1)}, u32[]{:S(2)}, u32[]{:S(2)}) collective-permute-start(bf16[512,384]{1,0:T(8,128)(2,1)S(1)} %get-tuple-element.16), channel_id=1, source_target_pairs={{2,6},{4,0},{6,10},{8,4},{10,14},{12,8},{3,7},{5,1},{7,11},{9,5},{... | collective-permute-start | bytes 1179656 | tf_op jit(solution)/shard_map/ppermute | solution.py:391
  26.8 24.9 %collective-permute-start.8 = (bf16[512,768]{1,0:T(8,128)(2,1)S(1)}, bf16[512,768]{1,0:T(8,128)(2,1)S(1)}, u32[]{:S(2)}, u32[]{:S(2)}) collective-permute-start(bf16[512,768]{1,0:T(8,128)(2,1)S(1)} %tie.5), channel_id=1, source_target_pairs={{0,4},{4,8},{6,2},{8,12},{10,6},{14,10},{1,5},{5,9},{7,3},{9,13},{... | collective-permute-start | bytes 2359304 | tf_op jit(solution)/shard_map/ppermute | solution.py:396
  31.4 25.7 %collective-permute-start.15 = (bf16[512,768]{1,0:T(8,128)(2,1)S(1)}, bf16[512,768]{1,0:T(8,128)(2,1)S(1)}, u32[]{:S(2)}, u32[]{:S(2)}) collective-permute-start(bf16[512,768]{1,0:T(8,128)(2,1)S(1)} %collective-permute-done.9.rest_1_), channel_id=1, source_target_pairs={{2,6},{4,0},{6,10},{8,4},{10,14},{12,8},{3,7},{5,1},{7,11},{9,5},{... | collective-permute-start | bytes 2359304 | tf_op jit(solution)/shard_map/ppermute | solution.py:394
  39.2 8.3 %copy-start.3 = (s32[8,8]{1,0:T(8,128)S(1)}, s32[8,8]{1,0:T(8,128)}, u32[]{:S(2)}) copy-start(s32[8,8]{1,0:T(8,128)} %table_ref.13) | copy-start | bytes 772
  39.2 2.3 %collective-permute-start.5 = (bf16[256,1536]{1,0:T(8,128)(2,1)S(1)}, bf16[256,1536]{1,0:T(8,128)(2,1)S(1)}, u32[]{:S(2)}, u32[]{:S(2)}) collective-permute-start(bf16[256,1536]{1,0:T(8,128)(2,1)S(1)} %get-tuple-element.17), channel_id=1, source_target_pairs={{0,1},{1,0},{2,3},{3,2},{4,5},{5,4},{6,7},{7,6},{8,9},{9,8},{10,11... | collective-permute-start | bytes 2359304 | tf_op jit(solution)/shard_map/ppermute | solution.py:400
  39.2 3.6 %collective-permute-start.6 = (bf16[256,1536]{1,0:T(8,128)(2,1)S(1)}, bf16[256,1536]{1,0:T(8,128)(2,1)S(1)}, u32[]{:S(2)}, u32[]{:S(2)}) collective-permute-start(bf16[256,1536]{1,0:T(8,128)(2,1)S(1)} %get-tuple-element.18), channel_id=1, source_target_pairs={{0,1},{1,0},{2,3},{3,2},{4,5},{5,4},{6,7},{7,6},{8,9},{9,8},{10,11... | collective-permute-start | bytes 2359304 | tf_op jit(solution)/shard_map/ppermute | solution.py:401
  39.8 17.2 %collective-permute-start.11 = (bf16[256,1536]{1,0:T(8,128)(2,1)S(1)}, bf16[256,1536]{1,0:T(8,128)(2,1)S(1)}, u32[]{:S(2)}, u32[]{:S(2)}) collective-permute-start(bf16[256,1536]{1,0:T(8,128)(2,1)S(1)} %maximum_maximum_fusion), channel_id=1, source_target_pairs={{0,1},{1,0},{2,3},{3,2},{4,5},{5,4},{6,7},{7,6},{8,9},{9,8},{10,11... | collective-permute-start | bytes 2359304 | tf_op jit(solution)/shard_map/ppermute | solution.py:402
  41.5 22.2 %collective-permute-start.10 = (bf16[512,384]{1,0:T(8,128)(2,1)S(1)}, bf16[512,384]{1,0:T(8,128)(2,1)S(1)}, u32[]{:S(2)}, u32[]{:S(2)}) collective-permute-start(bf16[512,384]{1,0:T(8,128)(2,1)S(1)} %collective-permute-done.4.refs_2_.rest_2_.rest_1_), channel_id=1, source_target_pairs={{2,6},{4,0},{6,10},{8,4},{10,14},{12,8},{3,7},{5,1},{7,11},{9,5},{... | collective-permute-start | bytes 1179656 | tf_op jit(solution)/shard_map/ppermute | solution.py:398
  42.8 20.9 %collective-permute-start.12 = (bf16[512,384]{1,0:T(8,128)(2,1)S(1)}, bf16[512,384]{1,0:T(8,128)(2,1)S(1)}, u32[]{:S(2)}, u32[]{:S(2)}) collective-permute-start(bf16[512,384]{1,0:T(8,128)(2,1)S(1)} %collective-permute-done.2.refs_0_.rest_1_), channel_id=1, source_target_pairs={{0,4},{4,8},{6,2},{8,12},{10,6},{14,10},{1,5},{5,9},{7,3},{9,13},{... | collective-permute-start | bytes 1179656 | tf_op jit(solution)/shard_map/ppermute | solution.py:397
  51.6 12.1 %collective-permute-start.13 = (bf16[272,384]{1,0:T(8,128)(2,1)S(1)}, bf16[272,384]{1,0:T(8,128)(2,1)S(1)}, u32[]{:S(2)}, u32[]{:S(2)}) collective-permute-start(bf16[272,384]{1,0:T(8,128)(2,1)S(1)} %partner_part.4.rest_3_), channel_id=1, source_target_pairs={{0,2},{2,0},{4,6},{6,4},{8,10},{10,8},{12,14},{14,12},{1,3},{3,1},... | collective-permute-start | bytes 626696 | tf_op jit(solution)/shard_map/ppermute | solution.py:452
  59.3 9.0 %collective-permute-start.16 = (bf16[272,384]{1,0:T(8,128)(2,1)S(1)}, bf16[272,384]{1,0:T(8,128)(2,1)S(1)}, u32[]{:S(2)}, u32[]{:S(2)}) collective-permute-start(bf16[272,384]{1,0:T(8,128)(2,1)S(1)} %partner_part.6.rest_4_), channel_id=1, source_target_pairs={{0,2},{2,0},{4,6},{6,4},{8,10},{10,8},{12,14},{14,12},{1,3},{3,1},... | collective-permute-start | bytes 626696 | tf_op jit(solution)/shard_map/ppermute | solution.py:453
  59.4 12.2 %slice-start = ((s8[4718592]{0:T(1024)(128)(4,1)}), s8[4194304]{0:T(1024)(128)(4,1)S(1)}, s32[]{:S(2)}) async-start(s8[4718592]{0:T(1024)(128)(4,1)} %bitcast), calls=%async_computation | async-start | bytes 8388608
  61.6 9.9 %slice-start.1 = ((s8[4718592]{0:T(1024)(128)(4,1)}), s8[524288]{0:T(1024)(128)(4,1)S(1)}, s32[]{:S(2)}) async-start(s8[4718592]{0:T(1024)(128)(4,1)} %bitcast), calls=%async_computation.1 | async-start | bytes 1048576
  61.7 9.9 %collective-permute-start.17 = (bf16[272,384]{1,0:T(8,128)(2,1)S(1)}, bf16[272,384]{1,0:T(8,128)(2,1)S(1)}, u32[]{:S(2)}, u32[]{:S(2)}) collective-permute-start(bf16[272,384]{1,0:T(8,128)(2,1)S(1)} %partner_part.7), channel_id=1, source_target_pairs={{0,2},{2,0},{4,6},{6,4},{8,10},{10,8},{12,14},{14,12},{1,3},{3,1},... | collective-permute-start | bytes 626696 | tf_op jit(solution)/shard_map/ppermute | solution.py:454
  66.0 9.2 %collective-permute-start.14 = (bf16[272,384]{1,0:T(8,128)(2,1)S(1)}, bf16[272,384]{1,0:T(8,128)(2,1)S(1)}, u32[]{:S(2)}, u32[]{:S(2)}) collective-permute-start(bf16[272,384]{1,0:T(8,128)(2,1)S(1)} %partner_part.5), channel_id=1, source_target_pairs={{0,2},{2,0},{4,6},{6,4},{8,10},{10,8},{12,14},{14,12},{1,3},{3,1},... | collective-permute-start | bytes 626696 | tf_op jit(solution)/shard_map/ppermute | solution.py:460

commit v13 on v12

--- a/solution.py
+++ b/solution.py
@@ -396,7 +396,7 @@
     major3 = lax.ppermute(to_major3, "frame", away_moves)
     major4 = lax.ppermute(major2, "frame", away_moves)
     minor4 = lax.ppermute(minor2, "frame", near_moves)
-    to_sib_keys, to_sib_values = tie((major2, partner_query, minor2), key_tokens, value_tokens)
+    to_sib_keys, to_sib_values = tie((major2, partner_query, minor2, major1), key_tokens, value_tokens)
     sib_keys = lax.ppermute(to_sib_keys, "head", core_moves)
     sib_values = lax.ppermute(to_sib_values, "head", core_moves)
     nearest = lax.ppermute(firsts(minor1, minor2, major2), "head", core_moves)
@@ -444,13 +444,13 @@
 
     own_early = own_part((3, 6), ("major1", "minor1"))
     part_low = partner_part((0, 3), ("major1", "major2"), (own_early[1],))
-    own_late = own_part((6, 12), ("major3", "minor1", "minor2"), (part_low,))
     part_middle = partner_part(
-        (3, 6), ("major1", "minor1", "minor3", "nearest"), (own_late[1],)
+        (3, 6), ("major1", "minor1", "minor3", "nearest"), (part_low,)
     )
     part_late = partner_part((6, 9), ("major3", "minor1", "minor3", "nearest"), (part_middle,))
     part_low = lax.ppermute(part_low, "frame", partner_moves)
     part_middle = lax.ppermute(part_middle, "frame", partner_moves)
+    own_late = own_part((6, 12), ("major3", "minor1", "minor2"), (part_late,))
     part_late = lax.ppermute(part_late, "frame", partner_moves)
     part_high = partner_part(
         (9, 12),

time: 78.3 us -> 82.7 us (1.056)
  starting transfers between devices: 31.7 us -> 34.7 us
  waiting for transfers between devices: 21.5 us -> 22.8 us
    ppermute x1, waiting for transfers between devices: 4.65 us -> 8.63 us  [per_device(): partner_query = lax.ppermute(queries, 'frame', partner_moves)]
    ppermute x1, waiting for transfers between devices: 9.8 us -> 6.2 us  [per_device(): cross = lax.ppermute(pack(0, 3), 'frame', partner_moves)]
    ppermute x1, waiting for transfers between devices: 3.23 us -> 0.01 us  [per_device(): part_late = lax.ppermute(part_late, 'frame', partner_moves)]
    ppermute x1, waiting for transfers between devices: 0.34 us -> 3.51 us  [per_device(): major3 = lax.ppermute(to_major3, 'frame', away_moves)]
    ppermute x1, starting transfers between devices: 0.08 us -> 2.66 us  [per_device(): part_high = lax.ppermute(part_high, 'frame', partner_moves)]
    ppermute x1, waiting for transfers between devices: 0.01 us -> 2.54 us  [per_device(): major2 = lax.ppermute(cross, 'frame', away_moves)]
    ppermute x1, starting transfers between devices: 2.42 us -> 0.05 us  [per_device(): part_low = lax.ppermute(part_low, 'frame', partner_moves)]
    ppermute x1, starting transfers between devices: 2.65 us -> 4.82 us  [per_device(): cross = lax.ppermute(pack(0, 3), 'frame', partner_moves)]
  transfers between devices with their start and end apart: 18 -> 18, of which waited for: 6 -> 7; matrix products, arithmetic and copies ran while one was open for 3% -> 3% of each run, Pallas kernels for 25% -> 24%
where the time goes in v13:
time: 82.7 us; the launch traced here: 82.3 us
  starting transfers between devices  34.7 us (42%)
  waiting for transfers between devices  22.8 us (28%)
  Pallas kernels  22.1 us (27%)
  local copies, waits for them, and re-layouts  2.05 us (2%)
    pallas_call x7, Pallas kernels, run(): pl.pallas_call(body, grid=(1,), in_specs=[pl.BlockSpec(memory_space=pltpu...  15.7 us
    ppermute x1, waiting for transfers between devices, per_device(): partner_query = lax.ppermute(queries, 'frame', partner_moves)  8.63 us
    pallas_call x2, Pallas kernels, project(): pl.pallas_call(functools.partial(project_kernel, span, tuple((group for g...  6.39 us
    ppermute x1, waiting for transfers between devices, per_device(): cross = lax.ppermute(pack(0, 3), 'frame', partner_moves)  6.2 us
    ppermute x1, starting transfers between devices, per_device(): cross = lax.ppermute(pack(0, 3), 'frame', partner_moves)  4.82 us
    ppermute x1, starting transfers between devices, per_device(): major4 = lax.ppermute(major2, 'frame', away_moves)  4.75 us
    ppermute x1, starting transfers between devices, per_device(): major3 = lax.ppermute(to_major3, 'frame', away_moves)  4.47 us
    ppermute x1, waiting for transfers between devices, per_device(): major3 = lax.ppermute(to_major3, 'frame', away_moves)  3.51 us
  transfers between devices with their start and end apart: 18, of which 7 were waited for; matrix products, arithmetic and copies ran while one was open for 3% of the time, Pallas kernels for 24%

profile of v13, /device:TPU:0, one launch (start us, length us, event | category | flops | bytes accessed | tf_op | source)
XLA Modules:
  0.0 82.3 jit_solution(2537890336256172791)
XLA Ops:
  0.0 0.5 collective-permute-start
  0.5 1.8 %fusion.1 = (bf16[256,768]{1,0:T(8,128)(2,1)S(1)}, bf16[256,768]{1,0:T(8,128)(2,1)S(1)}, bf16[256,768]{1,0:T(8,128)(2,1)S(1)}, bf16[256,768]{1,0:T(8,128)(2,1)S(...) fusion(bf16[256,1536]{1,0:T(8,128)(2,1)} %keys.13, bf16[256,1536]{1,0:T(8,128)(2,1)} %values.13), kind=kLoop, calls=%fused_computation.7 | loop fusion | bytes 4718592 | tf_op jit(solution)/shard_map/slice | solution.py:377
  2.3 1.4 %collective-permute-start.9 = (bf16[512,768]{1,0:T(8,128)(2,1)S(1)}, bf16[512,768]{1,0:T(8,128)(2,1)S(1)}, u32[]{:S(2)}, u32[]{:S(2)}) collective-permute-start(bf16[512,768]{1,0:T(8,128)(2,1)S(1)} %pad_maximum_fusion.2), channel_id=1, source_target_pairs={{2,6},{4,0},{6,10},{8,4},{10,14},{12,8},{3,7},{5,1},{7,11},{9,5},{... | collective-permute-start | bytes 2359304 | tf_op jit(solution)/shard_map/ppermute | solution.py:386
  3.8 0.1 fusion.3
  3.9 4.8 %collective-permute-start.1 = (bf16[512,384]{1,0:T(8,128)(2,1)S(1)}, bf16[512,384]{1,0:T(8,128)(2,1)S(1)}, u32[]{:S(2)}, u32[]{:S(2)}) collective-permute-start(bf16[512,384]{1,0:T(8,128)(2,1)S(1)} %pad_maximum_fusion.3), channel_id=1, source_target_pairs={{0,2},{2,0},{4,6},{6,4},{8,10},{10,8},{12,14},{14,12},{1,3},{3,1},... | collective-permute-start | bytes 1179656 | tf_op jit(solution)/shard_map/ppermute | solution.py:389
  8.7 0.1 collective-permute-start.3
  8.9 3.5 %collective-permute-start.5 = (bf16[512,768]{1,0:T(8,128)(2,1)S(1)}, bf16[512,768]{1,0:T(8,128)(2,1)S(1)}, u32[]{:S(2)}, u32[]{:S(2)}) collective-permute-start(bf16[512,768]{1,0:T(8,128)(2,1)S(1)} %pad_maximum_fusion), channel_id=1, source_target_pairs={{0,4},{4,8},{6,2},{8,12},{10,6},{14,10},{1,5},{5,9},{7,3},{9,13},{... | collective-permute-start | bytes 2359304 | tf_op jit(solution)/shard_map/ppermute | solution.py:385
  12.4 6.2 %collective-permute-done.1.refs_1_ = bf16[512,384]{1,0:T(8,128)(2,1)S(1)} collective-permute-done((bf16[512,384]{1,0:T(8,128)(2,1)S(1)}, bf16[512,384]{1,0:T(8,128)(2,1)S(1)}, u32[]{:S(2)}, u32[]{:S(2)}) %collective-permute-start.1) | collective-permute-done | bytes 393248 | tf_op jit(solution)/shard_map/ppermute | solution.py:389
  18.6 3.4 %collective-permute-start.2 = (bf16[512,384]{1,0:T(8,128)(2,1)S(1)}, bf16[512,384]{1,0:T(8,128)(2,1)S(1)}, u32[]{:S(2)}, u32[]{:S(2)}) collective-permute-start(bf16[512,384]{1,0:T(8,128)(2,1)S(1)} %get-tuple-element.15), channel_id=1, source_target_pairs={{0,4},{4,8},{6,2},{8,12},{10,6},{14,10},{1,5},{5,9},{7,3},{9,13},{... | collective-permute-start | bytes 1179656 | tf_op jit(solution)/shard_map/ppermute | solution.py:393
  22.1 1.3 %collective-permute-start.4 = (bf16[512,384]{1,0:T(8,128)(2,1)S(1)}, bf16[512,384]{1,0:T(8,128)(2,1)S(1)}, u32[]{:S(2)}, u32[]{:S(2)}) collective-permute-start(bf16[512,384]{1,0:T(8,128)(2,1)S(1)} %get-tuple-element.16), channel_id=1, source_target_pairs={{2,6},{4,0},{6,10},{8,4},{10,14},{12,8},{3,7},{5,1},{7,11},{9,5},{... | collective-permute-start | bytes 1179656 | tf_op jit(solution)/shard_map/ppermute | solution.py:391
  23.5 1.6 %collective-permute-done.9.rest_1_ = bf16[512,768]{1,0:T(8,128)(2,1)S(1)} collective-permute-done((bf16[512,768]{1,0:T(8,128)(2,1)S(1)}, bf16[512,768]{1,0:T(8,128)(2,1)S(1)}, u32[]{:S(2)}, u32[]{:S(2)}) %collective-permute-start.9) | collective-permute-done | bytes 786464 | tf_op jit(solution)/shard_map/ppermute | solution.py:386
  25.1 1.3 %collective-permute-start.10 = (bf16[512,768]{1,0:T(8,128)(2,1)S(1)}, bf16[512,768]{1,0:T(8,128)(2,1)S(1)}, u32[]{:S(2)}, u32[]{:S(2)}) collective-permute-start(bf16[512,768]{1,0:T(8,128)(2,1)S(1)} %collective-permute-done.9.rest_1_), channel_id=1, source_target_pairs={{2,6},{4,0},{6,10},{8,4},{10,14},{12,8},{3,7},{5,1},{7,11},{9,5},{... | collective-permute-start | bytes 2359304 | tf_op jit(solution)/shard_map/ppermute | solution.py:394
  26.5 8.6 %collective-permute-done.3.refs_1_.query = bf16[256,1536]{1,0:T(8,128)(2,1)S(1)} collective-permute-done((bf16[256,1536]{1,0:T(8,128)(2,1)S(1)}, bf16[256,1536]{1,0:T(8,128)(2,1)S(1)}, u32[]{:S(2)}, u32[]{:S(2)}) %collective-permute-start.3) | collective-permute-done | bytes 786464 | tf_op jit(solution)/shard_map/ppermute | solution.py:392
  35.1 2.5 %collective-permute-done.2.refs_0_.rest_1_ = bf16[512,384]{1,0:T(8,128)(2,1)S(1)} collective-permute-done((bf16[512,384]{1,0:T(8,128)(2,1)S(1)}, bf16[512,384]{1,0:T(8,128)(2,1)S(1)}, u32[]{:S(2)}, u32[]{:S(2)}) %collective-permute-start.2) | collective-permute-done | bytes 393248 | tf_op jit(solution)/shard_map/ppermute | solution.py:393
  37.6 0.5 collective-permute-start.7
  38.4 4.5 %collective-permute-start.8 = (bf16[512,768]{1,0:T(8,128)(2,1)S(1)}, bf16[512,768]{1,0:T(8,128)(2,1)S(1)}, u32[]{:S(2)}, u32[]{:S(2)}) collective-permute-start(bf16[512,768]{1,0:T(8,128)(2,1)S(1)} %tie.5), channel_id=1, source_target_pairs={{0,4},{4,8},{6,2},{8,12},{10,6},{14,10},{1,5},{5,9},{7,3},{9,13},{... | collective-permute-start | bytes 2359304 | tf_op jit(solution)/shard_map/ppermute | solution.py:396
  42.9 1.3 %collective-permute-start.12 = (bf16[512,384]{1,0:T(8,128)(2,1)S(1)}, bf16[512,384]{1,0:T(8,128)(2,1)S(1)}, u32[]{:S(2)}, u32[]{:S(2)}) collective-permute-start(bf16[512,384]{1,0:T(8,128)(2,1)S(1)} %collective-permute-done.4.refs_2_.rest_2_.rest_1_), channel_id=1, source_target_pairs={{2,6},{4,0},{6,10},{8,4},{10,14},{12,8},{3,7},{5,1},{7,11},{9,5},{... | collective-permute-start | bytes 1179656 | tf_op jit(solution)/shard_map/ppermute | solution.py:398
  44.2 4.8 %collective-permute-start.13 = (bf16[512,384]{1,0:T(8,128)(2,1)S(1)}, bf16[512,384]{1,0:T(8,128)(2,1)S(1)}, u32[]{:S(2)}, u32[]{:S(2)}) collective-permute-start(bf16[512,384]{1,0:T(8,128)(2,1)S(1)} %collective-permute-done.2.refs_0_.rest_1_), channel_id=1, source_target_pairs={{0,4},{4,8},{6,2},{8,12},{10,6},{14,10},{1,5},{5,9},{7,3},{9,13},{... | collective-permute-start | bytes 1179656 | tf_op jit(solution)/shard_map/ppermute | solution.py:397
  49.0 1.9 %own_part.3 = (f32[256,384]{1,0:T(8,128)S(1)}, f32[256,128]{1,0:T(8,128)S(1)}) custom-call(s32[8,8]{1,0:T(8,128)S(1)} %copy-done.3, bf16[256,1536]{1,0:T(8,128)(2,1)S(1)} %copy-done.2, bf16[256,1536]{1,0:T(8,128)(2,1)S(1)} %copy-done, bf16[256,1536]{1,0:T(8,128)(2,1)S(1)} %copy-done.1, bf16[256,1536]{1,0:T(8,128)(2,1)S(1)} %collective-permute-done.6.sib_keys, ...), custom_call_target="tpu_custom_call" | custom-call | flops 301989888 | bytes 1048576 | tf_op jit(solution)/shard_map/own_part/pallas_call | solution.py:297
  50.9 1.8 %partner_part.4.rest_4_ = bf16[272,384]{1,0:T(8,128)(2,1)S(1)} custom-call(s32[8,8]{1,0:T(8,128)S(1)} %copy-done.3, bf16[256,1536]{1,0:T(8,128)(2,1)S(1)} %collective-permute-done.3.refs_1_.query, bf16[256,1536]{1,0:T(8,128)(2,1)S(1)} %copy-done, bf16[256,1536]{1,0:T(8,128)(2,1)S(1)} %copy-done.1, bf16[256,1536]{1,0:T(8,128)(2,1)S(1)} %collective-permute-done.6.sib_keys, ...), custom_call_target="tpu_custom_call" | custom-call | flops 301989888 | bytes 1048576 | tf_op jit(solution)/shard_map/partner_part/pallas_call | solution.py:297
  52.7 0.1 collective-permute-done.10.rest_2_
  52.9 2.3 %partner_part.5.rest_4_ = bf16[272,384]{1,0:T(8,128)(2,1)S(1)} custom-call(s32[8,8]{1,0:T(8,128)S(1)} %copy-done.3, bf16[256,1536]{1,0:T(8,128)(2,1)S(1)} %collective-permute-done.3.refs_1_.query, bf16[256,1536]{1,0:T(8,128)(2,1)S(1)} %copy-done, bf16[256,1536]{1,0:T(8,128)(2,1)S(1)} %copy-done.1, bf16[256,1536]{1,0:T(8,128)(2,1)S(1)} %collective-permute-done.6.sib_keys, ...), custom_call_target="tpu_custom_call" | custom-call | flops 301989888 | bytes 1048576 | tf_op jit(solution)/shard_map/partner_part/pallas_call | solution.py:297
  55.2 2.0 %collective-permute-start.16 = (bf16[272,384]{1,0:T(8,128)(2,1)S(1)}, bf16[272,384]{1,0:T(8,128)(2,1)S(1)}, u32[]{:S(2)}, u32[]{:S(2)}) collective-permute-start(bf16[272,384]{1,0:T(8,128)(2,1)S(1)} %partner_part.5.rest_4_), channel_id=1, source_target_pairs={{0,2},{2,0},{4,6},{6,4},{8,10},{10,8},{12,14},{14,12},{1,3},{3,1},... | collective-permute-start | bytes 626696 | tf_op jit(solution)/shard_map/ppermute | solution.py:452
  57.2 3.5 %collective-permute-done.8.rest_0_ = bf16[512,768]{1,0:T(8,128)(2,1)S(1)} collective-permute-done((bf16[512,768]{1,0:T(8,128)(2,1)S(1)}, bf16[512,768]{1,0:T(8,128)(2,1)S(1)}, u32[]{:S(2)}, u32[]{:S(2)}) %collective-permute-start.8) | collective-permute-done | bytes 786464 | tf_op jit(solution)/shard_map/ppermute | solution.py:396
  60.7 2.3 %partner_part.6.rest_3_ = bf16[272,384]{1,0:T(8,128)(2,1)S(1)} custom-call(s32[8,8]{1,0:T(8,128)S(1)} %copy-done.3, bf16[256,1536]{1,0:T(8,128)(2,1)S(1)} %collective-permute-done.3.refs_1_.query, bf16[256,1536]{1,0:T(8,128)(2,1)S(1)} %copy-done, bf16[256,1536]{1,0:T(8,128)(2,1)S(1)} %copy-done.1, bf16[256,1536]{1,0:T(8,128)(2,1)S(1)} %collective-permute-done.6.sib_keys, ...), custom_call_target="tpu_custom_call" | custom-call | flops 301989888 | bytes 1048576 | tf_op jit(solution)/shard_map/partner_part/pallas_call | solution.py:297
  63.0 2.6 %collective-permute-start.17 = (bf16[272,384]{1,0:T(8,128)(2,1)S(1)}, bf16[272,384]{1,0:T(8,128)(2,1)S(1)}, u32[]{:S(2)}, u32[]{:S(2)}) collective-permute-start(bf16[272,384]{1,0:T(8,128)(2,1)S(1)} %partner_part.6.rest_3_), channel_id=1, source_target_pairs={{0,2},{2,0},{4,6},{6,4},{8,10},{10,8},{12,14},{14,12},{1,3},{3,1},... | collective-permute-start | bytes 626696 | tf_op jit(solution)/shard_map/ppermute | solution.py:454
  65.6 3.0 %own_part.4 = (f32[256,768]{1,0:T(8,128)S(1)}, f32[256,128]{1,0:T(8,128)S(1)}) custom-call(s32[8,8]{1,0:T(8,128)S(1)} %copy-done.3, bf16[256,1536]{1,0:T(8,128)(2,1)S(1)} %copy-done.2, bf16[256,1536]{1,0:T(8,128)(2,1)S(1)} %copy-done, bf16[256,1536]{1,0:T(8,128)(2,1)S(1)} %copy-done.1, bf16[256,1536]{1,0:T(8,128)(2,1)S(1)} %collective-permute-done.6.sib_keys, ...), custom_call_target="tpu_custom_call" | custom-call | flops 603979776 | bytes 1048576 | tf_op jit(solution)/shard_map/own_part/pallas_call | solution.py:297
  68.7 2.3 %partner_part.7 = bf16[272,384]{1,0:T(8,128)(2,1)S(1)} custom-call(s32[8,8]{1,0:T(8,128)S(1)} %copy-done.3, bf16[256,1536]{1,0:T(8,128)(2,1)S(1)} %collective-permute-done.3.refs_1_.query, bf16[256,1536]{1,0:T(8,128)(2,1)S(1)} %copy-done, bf16[256,1536]{1,0:T(8,128)(2,1)S(1)} %copy-done.1, bf16[256,1536]{1,0:T(8,128)(2,1)S(1)} %collective-permute-done.6.sib_keys, ...), custom_call_target="tpu_custom_call" | custom-call | flops 301989888 | bytes 1048576 | tf_op jit(solution)/shard_map/partner_part/pallas_call | solution.py:297
  70.9 2.7 %collective-permute-start.15 = (bf16[272,384]{1,0:T(8,128)(2,1)S(1)}, bf16[272,384]{1,0:T(8,128)(2,1)S(1)}, u32[]{:S(2)}, u32[]{:S(2)}) collective-permute-start(bf16[272,384]{1,0:T(8,128)(2,1)S(1)} %partner_part.7), channel_id=1, source_target_pairs={{0,2},{2,0},{4,6},{6,4},{8,10},{10,8},{12,14},{14,12},{1,3},{3,1},... | collective-permute-start | bytes 626696 | tf_op jit(solution)/shard_map/ppermute | solution.py:460
  73.6 2.2 %own_part.5 = (f32[256,384]{1,0:T(8,128)S(1)}, f32[256,128]{1,0:T(8,128)S(1)}) custom-call(s32[8,8]{1,0:T(8,128)S(1)} %copy-done.3, bf16[256,1536]{1,0:T(8,128)(2,1)S(1)} %copy-done.2, bf16[256,1536]{1,0:T(8,128)(2,1)S(1)} %copy-done, bf16[256,1536]{1,0:T(8,128)(2,1)S(1)} %copy-done.1, bf16[256,1536]{1,0:T(8,128)(2,1)S(1)} %collective-permute-done.6.sib_keys, ...), custom_call_target="tpu_custom_call" | custom-call | flops 301989888 | bytes 1048576 | tf_op jit(solution)/shard_map/own_part/pallas_call | solution.py:297
  75.9 3.7 %merge_and_project.2.refs_5_ = f32[256,3072]{1,0:T(8,128)S(1)} custom-call(bf16[768,3072]{1,0:T(8,128)(2,1)S(1)} %bitcast.1, bf16[768,3072]{1,0:T(8,128)(2,1)S(1)} %collective-permute-done.refs_0_.rest_7_.refs_1_, f32[256,384]{1,0:T(8,128)S(1)} %get-tuple-element.22.refs_2_, f32[256,128]{1,0:T(8,128)S(1)} %get-tuple-element.23.refs_3_, ...), custom_call_target="tpu_custom_call" | custom-call | flops 1811939328 | bytes 4194304 | tf_op jit(solution)/shard_map/merge_and_project/pallas_call | solution.py:340
  79.6 2.7 %merge_and_project.3 = bf16[256,3072]{1,0:T(8,128)(2,1)} custom-call(bf16[768,3072]{1,0:T(8,128)(2,1)S(1)} %bitcast.1, bf16[768,3072]{1,0:T(8,128)(2,1)S(1)} %collective-permute-done.refs_0_.rest_7_.refs_1_, f32[256,768]{1,0:T(8,128)S(1)} %get-tuple-element.20.refs_6_.refs_2_, f32[256,128]{1,0:T(8,128)S(1)} %get-tuple-element.21.rest_4_.refs_7_.refs_3_, ...), custom_call_target="tpu_custom_call" | custom-call | flops 603979776 | bytes 4194304 | tf_op jit(solution)/shard_map/merge_and_project/pallas_call | solution.py:340
  (42 shorter events, 0.7 us)
Async XLA Ops:
  0.0 18.6 %collective-permute-start = (bf16[768,3072]{1,0:T(8,128)(2,1)}, bf16[768,3072]{1,0:T(8,128)(2,1)S(1)}, u32[]{:S(2)}, u32[]{:S(2)}) collective-permute-start(bf16[768,3072]{1,0:T(8,128)(2,1)} %refs_0_.3), channel_id=1, source_target_pairs={{0,1},{1,0},{2,3},{3,2},{4,5},{5,4},{6,7},{7,6},{8,9},{9,8},{10,11... | collective-permute-start | bytes 14155784 | tf_op jit(solution)/shard_map/ppermute | solution.py:388
  2.2 1.5 %copy-start = (bf16[256,1536]{1,0:T(8,128)(2,1)S(1)}, bf16[256,1536]{1,0:T(8,128)(2,1)}, u32[]{:S(2)}) copy-start(bf16[256,1536]{1,0:T(8,128)(2,1)} %keys.13) | copy-start | bytes 2359300
  2.2 1.5 %copy-start.1 = (bf16[256,1536]{1,0:T(8,128)(2,1)S(1)}, bf16[256,1536]{1,0:T(8,128)(2,1)}, u32[]{:S(2)}) copy-start(bf16[256,1536]{1,0:T(8,128)(2,1)} %values.13) | copy-start | bytes 2359300
  2.3 6.4 %copy-start.2 = (bf16[256,1536]{1,0:T(8,128)(2,1)S(1)}, bf16[256,1536]{1,0:T(8,128)(2,1)}, u32[]{:S(2)}) copy-start(bf16[256,1536]{1,0:T(8,128)(2,1)} %query.5) | copy-start | bytes 2359300
  2.3 22.8 %collective-permute-start.9 = (bf16[512,768]{1,0:T(8,128)(2,1)S(1)}, bf16[512,768]{1,0:T(8,128)(2,1)S(1)}, u32[]{:S(2)}, u32[]{:S(2)}) collective-permute-start(bf16[512,768]{1,0:T(8,128)(2,1)S(1)} %pad_maximum_fusion.2), channel_id=1, source_target_pairs={{2,6},{4,0},{6,10},{8,4},{10,14},{12,8},{3,7},{5,1},{7,11},{9,5},{... | collective-permute-start | bytes 2359304 | tf_op jit(solution)/shard_map/ppermute | solution.py:386
  3.9 14.7 %collective-permute-start.1 = (bf16[512,384]{1,0:T(8,128)(2,1)S(1)}, bf16[512,384]{1,0:T(8,128)(2,1)S(1)}, u32[]{:S(2)}, u32[]{:S(2)}) collective-permute-start(bf16[512,384]{1,0:T(8,128)(2,1)S(1)} %pad_maximum_fusion.3), channel_id=1, source_target_pairs={{0,2},{2,0},{4,6},{6,4},{8,10},{10,8},{12,14},{14,12},{1,3},{3,1},... | collective-permute-start | bytes 1179656 | tf_op jit(solution)/shard_map/ppermute | solution.py:389
  8.7 26.4 %collective-permute-start.3 = (bf16[256,1536]{1,0:T(8,128)(2,1)S(1)}, bf16[256,1536]{1,0:T(8,128)(2,1)S(1)}, u32[]{:S(2)}, u32[]{:S(2)}) collective-permute-start(bf16[256,1536]{1,0:T(8,128)(2,1)S(1)} %copy-done.2), channel_id=1, source_target_pairs={{0,2},{2,0},{4,6},{6,4},{8,10},{10,8},{12,14},{14,12},{1,3},{3,1},... | collective-permute-start | bytes 2359304 | tf_op jit(solution)/shard_map/ppermute | solution.py:392
  8.9 26.2 %collective-permute-start.5 = (bf16[512,768]{1,0:T(8,128)(2,1)S(1)}, bf16[512,768]{1,0:T(8,128)(2,1)S(1)}, u32[]{:S(2)}, u32[]{:S(2)}) collective-permute-start(bf16[512,768]{1,0:T(8,128)(2,1)S(1)} %pad_maximum_fusion), channel_id=1, source_target_pairs={{0,4},{4,8},{6,2},{8,12},{10,6},{14,10},{1,5},{5,9},{7,3},{9,13},{... | collective-permute-start | bytes 2359304 | tf_op jit(solution)/shard_map/ppermute | solution.py:385
  18.6 19.0 %collective-permute-start.2 = (bf16[512,384]{1,0:T(8,128)(2,1)S(1)}, bf16[512,384]{1,0:T(8,128)(2,1)S(1)}, u32[]{:S(2)}, u32[]{:S(2)}) collective-permute-start(bf16[512,384]{1,0:T(8,128)(2,1)S(1)} %get-tuple-element.15), channel_id=1, source_target_pairs={{0,4},{4,8},{6,2},{8,12},{10,6},{14,10},{1,5},{5,9},{7,3},{9,13},{... | collective-permute-start | bytes 1179656 | tf_op jit(solution)/shard_map/ppermute | solution.py:393
  22.1 15.6 %collective-permute-start.4 = (bf16[512,384]{1,0:T(8,128)(2,1)S(1)}, bf16[512,384]{1,0:T(8,128)(2,1)S(1)}, u32[]{:S(2)}, u32[]{:S(2)}) collective-permute-start(bf16[512,384]{1,0:T(8,128)(2,1)S(1)} %get-tuple-element.16), channel_id=1, source_target_pairs={{2,6},{4,0},{6,10},{8,4},{10,14},{12,8},{3,7},{5,1},{7,11},{9,5},{... | collective-permute-start | bytes 1179656 | tf_op jit(solution)/shard_map/ppermute | solution.py:391
  25.1 27.7 %collective-permute-start.10 = (bf16[512,768]{1,0:T(8,128)(2,1)S(1)}, bf16[512,768]{1,0:T(8,128)(2,1)S(1)}, u32[]{:S(2)}, u32[]{:S(2)}) collective-permute-start(bf16[512,768]{1,0:T(8,128)(2,1)S(1)} %collective-permute-done.9.rest_1_), channel_id=1, source_target_pairs={{2,6},{4,0},{6,10},{8,4},{10,14},{12,8},{3,7},{5,1},{7,11},{9,5},{... | collective-permute-start | bytes 2359304 | tf_op jit(solution)/shard_map/ppermute | solution.py:394
  37.6 5.3 %collective-permute-start.6 = (bf16[256,1536]{1,0:T(8,128)(2,1)S(1)}, bf16[256,1536]{1,0:T(8,128)(2,1)S(1)}, u32[]{:S(2)}, u32[]{:S(2)}) collective-permute-start(bf16[256,1536]{1,0:T(8,128)(2,1)S(1)} %get-tuple-element.17), channel_id=1, source_target_pairs={{0,1},{1,0},{2,3},{3,2},{4,5},{5,4},{6,7},{7,6},{8,9},{9,8},{10,11... | collective-permute-start | bytes 2359304 | tf_op jit(solution)/shard_map/ppermute | solution.py:400
  37.6 6.6 %collective-permute-start.7 = (bf16[256,1536]{1,0:T(8,128)(2,1)S(1)}, bf16[256,1536]{1,0:T(8,128)(2,1)S(1)}, u32[]{:S(2)}, u32[]{:S(2)}) collective-permute-start(bf16[256,1536]{1,0:T(8,128)(2,1)S(1)} %get-tuple-element.18), channel_id=1, source_target_pairs={{0,1},{1,0},{2,3},{3,2},{4,5},{5,4},{6,7},{7,6},{8,9},{9,8},{10,11... | collective-permute-start | bytes 2359304 | tf_op jit(solution)/shard_map/ppermute | solution.py:401
  38.3 14.7 %collective-permute-start.11 = (bf16[256,1536]{1,0:T(8,128)(2,1)S(1)}, bf16[256,1536]{1,0:T(8,128)(2,1)S(1)}, u32[]{:S(2)}, u32[]{:S(2)}) collective-permute-start(bf16[256,1536]{1,0:T(8,128)(2,1)S(1)} %maximum_maximum_fusion), channel_id=1, source_target_pairs={{0,1},{1,0},{2,3},{3,2},{4,5},{5,4},{6,7},{7,6},{8,9},{9,8},{10,11... | collective-permute-start | bytes 2359304 | tf_op jit(solution)/shard_map/ppermute | solution.py:402
  38.3 10.6 %copy-start.3 = (s32[8,8]{1,0:T(8,128)S(1)}, s32[8,8]{1,0:T(8,128)}, u32[]{:S(2)}) copy-start(s32[8,8]{1,0:T(8,128)} %table_ref.13) | copy-start | bytes 772
  38.4 22.3 %collective-permute-start.8 = (bf16[512,768]{1,0:T(8,128)(2,1)S(1)}, bf16[512,768]{1,0:T(8,128)(2,1)S(1)}, u32[]{:S(2)}, u32[]{:S(2)}) collective-permute-start(bf16[512,768]{1,0:T(8,128)(2,1)S(1)} %tie.5), channel_id=1, source_target_pairs={{0,4},{4,8},{6,2},{8,12},{10,6},{14,10},{1,5},{5,9},{7,3},{9,13},{... | collective-permute-start | bytes 2359304 | tf_op jit(solution)/shard_map/ppermute | solution.py:396
  42.9 25.7 %collective-permute-start.12 = (bf16[512,384]{1,0:T(8,128)(2,1)S(1)}, bf16[512,384]{1,0:T(8,128)(2,1)S(1)}, u32[]{:S(2)}, u32[]{:S(2)}) collective-permute-start(bf16[512,384]{1,0:T(8,128)(2,1)S(1)} %collective-permute-done.4.refs_2_.rest_2_.rest_1_), channel_id=1, source_target_pairs={{2,6},{4,0},{6,10},{8,4},{10,14},{12,8},{3,7},{5,1},{7,11},{9,5},{... | collective-permute-start | bytes 1179656 | tf_op jit(solution)/shard_map/ppermute | solution.py:398
  44.2 24.5 %collective-permute-start.13 = (bf16[512,384]{1,0:T(8,128)(2,1)S(1)}, bf16[512,384]{1,0:T(8,128)(2,1)S(1)}, u32[]{:S(2)}, u32[]{:S(2)}) collective-permute-start(bf16[512,384]{1,0:T(8,128)(2,1)S(1)} %collective-permute-done.2.refs_0_.rest_1_), channel_id=1, source_target_pairs={{0,4},{4,8},{6,2},{8,12},{10,6},{14,10},{1,5},{5,9},{7,3},{9,13},{... | collective-permute-start | bytes 1179656 | tf_op jit(solution)/shard_map/ppermute | solution.py:397
  52.9 15.8 %collective-permute-start.14 = (bf16[272,384]{1,0:T(8,128)(2,1)S(1)}, bf16[272,384]{1,0:T(8,128)(2,1)S(1)}, u32[]{:S(2)}, u32[]{:S(2)}) collective-permute-start(bf16[272,384]{1,0:T(8,128)(2,1)S(1)} %partner_part.4.rest_4_), channel_id=1, source_target_pairs={{0,2},{2,0},{4,6},{6,4},{8,10},{10,8},{12,14},{14,12},{1,3},{3,1},... | collective-permute-start | bytes 626696 | tf_op jit(solution)/shard_map/ppermute | solution.py:451
  55.2 20.7 %collective-permute-start.16 = (bf16[272,384]{1,0:T(8,128)(2,1)S(1)}, bf16[272,384]{1,0:T(8,128)(2,1)S(1)}, u32[]{:S(2)}, u32[]{:S(2)}) collective-permute-start(bf16[272,384]{1,0:T(8,128)(2,1)S(1)} %partner_part.5.rest_4_), channel_id=1, source_target_pairs={{0,2},{2,0},{4,6},{6,4},{8,10},{10,8},{12,14},{14,12},{1,3},{3,1},... | collective-permute-start | bytes 626696 | tf_op jit(solution)/shard_map/ppermute | solution.py:452
  63.0 12.9 %collective-permute-start.17 = (bf16[272,384]{1,0:T(8,128)(2,1)S(1)}, bf16[272,384]{1,0:T(8,128)(2,1)S(1)}, u32[]{:S(2)}, u32[]{:S(2)}) collective-permute-start(bf16[272,384]{1,0:T(8,128)(2,1)S(1)} %partner_part.6.rest_3_), channel_id=1, source_target_pairs={{0,2},{2,0},{4,6},{6,4},{8,10},{10,8},{12,14},{14,12},{1,3},{3,1},... | collective-permute-start | bytes 626696 | tf_op jit(solution)/shard_map/ppermute | solution.py:454
  68.7 7.2 %slice-start = ((s8[4718592]{0:T(1024)(128)(4,1)}), s8[4194304]{0:T(1024)(128)(4,1)S(1)}, s32[]{:S(2)}) async-start(s8[4718592]{0:T(1024)(128)(4,1)} %bitcast), calls=%async_computation | async-start | bytes 8388608
  68.7 7.2 %slice-start.1 = ((s8[4718592]{0:T(1024)(128)(4,1)}), s8[524288]{0:T(1024)(128)(4,1)S(1)}, s32[]{:S(2)}) async-start(s8[4718592]{0:T(1024)(128)(4,1)} %bitcast), calls=%async_computation.1 | async-start | bytes 1048576
  70.9 8.6 %collective-permute-start.15 = (bf16[272,384]{1,0:T(8,128)(2,1)S(1)}, bf16[272,384]{1,0:T(8,128)(2,1)S(1)}, u32[]{:S(2)}, u32[]{:S(2)}) collective-permute-start(bf16[272,384]{1,0:T(8,128)(2,1)S(1)} %partner_part.7), channel_id=1, source_target_pairs={{0,2},{2,0},{4,6},{6,4},{8,10},{10,8},{12,14},{14,12},{1,3},{3,1},... | collective-permute-start | bytes 626696 | tf_op jit(solution)/shard_map/ppermute | solution.py:460

commit v14 on v10

--- a/solution.py
+++ b/solution.py
@@ -11,7 +11,7 @@
 DH = 128
 BS = 128
 CROSS = 3
-BATCH = 4
+BATCH = 6
 TILE = 768
 NEG = -1e30
 LOG2_SCALE = math.log2(math.e) / math.sqrt(DH)

time: 77.8 us -> 77.1 us (level)
  Pallas kernels: 23.1 us -> 22.1 us
    pallas_call x7, Pallas kernels: 16.7 us -> 15.7 us  [run(): pl.pallas_call(body, grid=(1,), in_specs=[pl.BlockSpec(memory_space=pltpu...]
  transfers between devices with their start and end apart: 18 -> 18, of which waited for: 5 -> 6; matrix products, arithmetic and copies ran while one was open for 3% -> 3% of each run, Pallas kernels for 26% -> 25%
where the time goes in v14:
time: 77.1 us; the launch traced here: 76.8 us
  starting transfers between devices  31.7 us (41%)
  Pallas kernels  22.1 us (29%)
  waiting for transfers between devices  20.2 us (26%)
  local copies, waits for them, and re-layouts  2.05 us (3%)
    pallas_call x7, Pallas kernels, run(): pl.pallas_call(body, grid=(1,), in_specs=[pl.BlockSpec(memory_space=pltpu...  15.7 us
    ppermute x1, waiting for transfers between devices, per_device(): cross = lax.ppermute(pack(0, 3), 'frame', partner_moves)  9.8 us
    pallas_call x2, Pallas kernels, project(): pl.pallas_call(functools.partial(project_kernel, span, tuple((group for g...  6.4 us
    ppermute x1, starting transfers between devices, per_device(): major4 = lax.ppermute(major2, 'frame', away_moves)  4.75 us
    ppermute x1, starting transfers between devices, per_device(): major1 = lax.ppermute(pack(0, 6), 'frame', away_moves)  4.66 us
    ppermute x1, waiting for transfers between devices, per_device(): partner_query = lax.ppermute(queries, 'frame', partner_moves)  4.65 us
    ppermute x1, starting transfers between devices, per_device(): major3 = lax.ppermute(to_major3, 'frame', away_moves)  4.6 us
    ppermute x1, starting transfers between devices, per_device(): major2 = lax.ppermute(cross, 'frame', away_moves)  4.03 us
  transfers between devices with their start and end apart: 18, of which 6 were waited for; matrix products, arithmetic and copies ran while one was open for 3% of the time, Pallas kernels for 25%

profile of v14, /device:TPU:0, one launch (start us, length us, event | category | flops | bytes accessed | tf_op | source)
XLA Modules:
  0.0 76.8 jit_solution(1120408970125684832)
XLA Ops:
  0.0 0.5 collective-permute-start
  0.5 1.8 %fusion.1 = (bf16[256,768]{1,0:T(8,128)(2,1)S(1)}, bf16[256,768]{1,0:T(8,128)(2,1)S(1)}, bf16[256,768]{1,0:T(8,128)(2,1)S(1)}, bf16[256,768]{1,0:T(8,128)(2,1)S(...) fusion(bf16[256,1536]{1,0:T(8,128)(2,1)} %keys.13, bf16[256,1536]{1,0:T(8,128)(2,1)} %values.13), kind=kLoop, calls=%fused_computation.7 | loop fusion | bytes 4718592 | tf_op jit(solution)/shard_map/slice | solution.py:377
  2.3 4.7 %collective-permute-start.7 = (bf16[512,768]{1,0:T(8,128)(2,1)S(1)}, bf16[512,768]{1,0:T(8,128)(2,1)S(1)}, u32[]{:S(2)}, u32[]{:S(2)}) collective-permute-start(bf16[512,768]{1,0:T(8,128)(2,1)S(1)} %pad_maximum_fusion), channel_id=1, source_target_pairs={{0,4},{4,8},{6,2},{8,12},{10,6},{14,10},{1,5},{5,9},{7,3},{9,13},{... | collective-permute-start | bytes 2359304 | tf_op jit(solution)/shard_map/ppermute | solution.py:385
  7.0 1.4 %collective-permute-start.9 = (bf16[512,768]{1,0:T(8,128)(2,1)S(1)}, bf16[512,768]{1,0:T(8,128)(2,1)S(1)}, u32[]{:S(2)}, u32[]{:S(2)}) collective-permute-start(bf16[512,768]{1,0:T(8,128)(2,1)S(1)} %pad_maximum_fusion.2), channel_id=1, source_target_pairs={{2,6},{4,0},{6,10},{8,4},{10,14},{12,8},{3,7},{5,1},{7,11},{9,5},{... | collective-permute-start | bytes 2359304 | tf_op jit(solution)/shard_map/ppermute | solution.py:386
  8.5 0.1 fusion.3
  8.6 2.7 %collective-permute-start.1 = (bf16[512,384]{1,0:T(8,128)(2,1)S(1)}, bf16[512,384]{1,0:T(8,128)(2,1)S(1)}, u32[]{:S(2)}, u32[]{:S(2)}) collective-permute-start(bf16[512,384]{1,0:T(8,128)(2,1)S(1)} %pad_maximum_fusion.3), channel_id=1, source_target_pairs={{0,2},{2,0},{4,6},{6,4},{8,10},{10,8},{12,14},{14,12},{1,3},{3,1},... | collective-permute-start | bytes 1179656 | tf_op jit(solution)/shard_map/ppermute | solution.py:389
  11.3 0.1 collective-permute-start.3
  11.4 9.8 %collective-permute-done.1.refs_1_ = bf16[512,384]{1,0:T(8,128)(2,1)S(1)} collective-permute-done((bf16[512,384]{1,0:T(8,128)(2,1)S(1)}, bf16[512,384]{1,0:T(8,128)(2,1)S(1)}, u32[]{:S(2)}, u32[]{:S(2)}) %collective-permute-start.1) | collective-permute-done | bytes 393248 | tf_op jit(solution)/shard_map/ppermute | solution.py:389
  21.2 4.0 %collective-permute-start.2 = (bf16[512,384]{1,0:T(8,128)(2,1)S(1)}, bf16[512,384]{1,0:T(8,128)(2,1)S(1)}, u32[]{:S(2)}, u32[]{:S(2)}) collective-permute-start(bf16[512,384]{1,0:T(8,128)(2,1)S(1)} %get-tuple-element.15), channel_id=1, source_target_pairs={{0,4},{4,8},{6,2},{8,12},{10,6},{14,10},{1,5},{5,9},{7,3},{9,13},{... | collective-permute-start | bytes 1179656 | tf_op jit(solution)/shard_map/ppermute | solution.py:393
  25.3 1.3 %collective-permute-start.4 = (bf16[512,384]{1,0:T(8,128)(2,1)S(1)}, bf16[512,384]{1,0:T(8,128)(2,1)S(1)}, u32[]{:S(2)}, u32[]{:S(2)}) collective-permute-start(bf16[512,384]{1,0:T(8,128)(2,1)S(1)} %get-tuple-element.16), channel_id=1, source_target_pairs={{2,6},{4,0},{6,10},{8,4},{10,14},{12,8},{3,7},{5,1},{7,11},{9,5},{... | collective-permute-start | bytes 1179656 | tf_op jit(solution)/shard_map/ppermute | solution.py:391
  26.8 4.6 %collective-permute-start.8 = (bf16[512,768]{1,0:T(8,128)(2,1)S(1)}, bf16[512,768]{1,0:T(8,128)(2,1)S(1)}, u32[]{:S(2)}, u32[]{:S(2)}) collective-permute-start(bf16[512,768]{1,0:T(8,128)(2,1)S(1)} %tie.5), channel_id=1, source_target_pairs={{0,4},{4,8},{6,2},{8,12},{10,6},{14,10},{1,5},{5,9},{7,3},{9,13},{... | collective-permute-start | bytes 2359304 | tf_op jit(solution)/shard_map/ppermute | solution.py:396
  31.4 1.3 %collective-permute-start.15 = (bf16[512,768]{1,0:T(8,128)(2,1)S(1)}, bf16[512,768]{1,0:T(8,128)(2,1)S(1)}, u32[]{:S(2)}, u32[]{:S(2)}) collective-permute-start(bf16[512,768]{1,0:T(8,128)(2,1)S(1)} %collective-permute-done.9.rest_1_), channel_id=1, source_target_pairs={{2,6},{4,0},{6,10},{8,4},{10,14},{12,8},{3,7},{5,1},{7,11},{9,5},{... | collective-permute-start | bytes 2359304 | tf_op jit(solution)/shard_map/ppermute | solution.py:394
  32.7 4.7 %collective-permute-done.3.refs_1_.query = bf16[256,1536]{1,0:T(8,128)(2,1)S(1)} collective-permute-done((bf16[256,1536]{1,0:T(8,128)(2,1)S(1)}, bf16[256,1536]{1,0:T(8,128)(2,1)S(1)}, u32[]{:S(2)}, u32[]{:S(2)}) %collective-permute-start.3) | collective-permute-done | bytes 786464 | tf_op jit(solution)/shard_map/ppermute | solution.py:392
  37.4 1.8 %collective-permute-done.4.refs_2_.rest_2_.rest_1_ = bf16[512,384]{1,0:T(8,128)(2,1)S(1)} collective-permute-done((bf16[512,384]{1,0:T(8,128)(2,1)S(1)}, bf16[512,384]{1,0:T(8,128)(2,1)S(1)}, u32[]{:S(2)}, u32[]{:S(2)}) %collective-permute-start.4) | collective-permute-done | bytes 393248 | tf_op jit(solution)/shard_map/ppermute | solution.py:391
  39.2 0.5 collective-permute-start.6
  39.8 0.1 collective-permute-start.11
  39.9 1.6 %collective-permute-done.5.sib_keys = bf16[256,1536]{1,0:T(8,128)(2,1)S(1)} collective-permute-done((bf16[256,1536]{1,0:T(8,128)(2,1)S(1)}, bf16[256,1536]{1,0:T(8,128)(2,1)S(1)}, u32[]{:S(2)}, u32[]{:S(2)}) %collective-permute-start.5) | collective-permute-done | bytes 786464 | tf_op jit(solution)/shard_map/ppermute | solution.py:400
  41.5 1.3 %collective-permute-start.10 = (bf16[512,384]{1,0:T(8,128)(2,1)S(1)}, bf16[512,384]{1,0:T(8,128)(2,1)S(1)}, u32[]{:S(2)}, u32[]{:S(2)}) collective-permute-start(bf16[512,384]{1,0:T(8,128)(2,1)S(1)} %collective-permute-done.4.refs_2_.rest_2_.rest_1_), channel_id=1, source_target_pairs={{2,6},{4,0},{6,10},{8,4},{10,14},{12,8},{3,7},{5,1},{7,11},{9,5},{... | collective-permute-start | bytes 1179656 | tf_op jit(solution)/shard_map/ppermute | solution.py:398
  42.8 4.8 %collective-permute-start.12 = (bf16[512,384]{1,0:T(8,128)(2,1)S(1)}, bf16[512,384]{1,0:T(8,128)(2,1)S(1)}, u32[]{:S(2)}, u32[]{:S(2)}) collective-permute-start(bf16[512,384]{1,0:T(8,128)(2,1)S(1)} %collective-permute-done.2.refs_0_.rest_1_), channel_id=1, source_target_pairs={{0,4},{4,8},{6,2},{8,12},{10,6},{14,10},{1,5},{5,9},{7,3},{9,13},{... | collective-permute-start | bytes 1179656 | tf_op jit(solution)/shard_map/ppermute | solution.py:397
  47.6 1.8 %partner_part.4.rest_4_ = bf16[272,384]{1,0:T(8,128)(2,1)S(1)} custom-call(s32[8,8]{1,0:T(8,128)S(1)} %copy-done.3, bf16[256,1536]{1,0:T(8,128)(2,1)S(1)} %collective-permute-done.3.refs_1_.query, bf16[256,1536]{1,0:T(8,128)(2,1)S(1)} %copy-done, bf16[256,1536]{1,0:T(8,128)(2,1)S(1)} %copy-done.1, bf16[256,1536]{1,0:T(8,128)(2,1)S(1)} %collective-permute-done.5.sib_keys, ...), custom_call_target="tpu_custom_call" | custom-call | flops 301989888 | bytes 1048576 | tf_op jit(solution)/shard_map/partner_part/pallas_call | solution.py:297
  49.4 2.2 %collective-permute-done.8.rest_0_.rest_6_ = bf16[512,768]{1,0:T(8,128)(2,1)S(1)} collective-permute-done((bf16[512,768]{1,0:T(8,128)(2,1)S(1)}, bf16[512,768]{1,0:T(8,128)(2,1)S(1)}, u32[]{:S(2)}, u32[]{:S(2)}) %collective-permute-start.8) | collective-permute-done | bytes 786464 | tf_op jit(solution)/shard_map/ppermute | solution.py:396
  51.6 2.4 %collective-permute-start.13 = (bf16[272,384]{1,0:T(8,128)(2,1)S(1)}, bf16[272,384]{1,0:T(8,128)(2,1)S(1)}, u32[]{:S(2)}, u32[]{:S(2)}) collective-permute-start(bf16[272,384]{1,0:T(8,128)(2,1)S(1)} %partner_part.4.rest_4_), channel_id=1, source_target_pairs={{0,2},{2,0},{4,6},{6,4},{8,10},{10,8},{12,14},{14,12},{1,3},{3,1},... | collective-permute-start | bytes 626696 | tf_op jit(solution)/shard_map/ppermute | solution.py:451
  54.1 1.9 %own_part.5 = (f32[256,384]{1,0:T(8,128)S(1)}, f32[256,128]{1,0:T(8,128)S(1)}) custom-call(s32[8,8]{1,0:T(8,128)S(1)} %copy-done.3, bf16[256,1536]{1,0:T(8,128)(2,1)S(1)} %copy-done.2, bf16[256,1536]{1,0:T(8,128)(2,1)S(1)} %copy-done, bf16[256,1536]{1,0:T(8,128)(2,1)S(1)} %copy-done.1, bf16[256,1536]{1,0:T(8,128)(2,1)S(1)} %collective-permute-done.5.sib_keys, ...), custom_call_target="tpu_custom_call" | custom-call | flops 301989888 | bytes 1048576 | tf_op jit(solution)/shard_map/own_part/pallas_call | solution.py:297
  56.0 0.1 collective-permute-done.15.rest_2_
  56.1 2.2 %partner_part.6.rest_4_ = bf16[272,384]{1,0:T(8,128)(2,1)S(1)} custom-call(s32[8,8]{1,0:T(8,128)S(1)} %copy-done.3, bf16[256,1536]{1,0:T(8,128)(2,1)S(1)} %collective-permute-done.3.refs_1_.query, bf16[256,1536]{1,0:T(8,128)(2,1)S(1)} %copy-done, bf16[256,1536]{1,0:T(8,128)(2,1)S(1)} %copy-done.1, bf16[256,1536]{1,0:T(8,128)(2,1)S(1)} %collective-permute-done.5.sib_keys, ...), custom_call_target="tpu_custom_call" | custom-call | flops 301989888 | bytes 1048576 | tf_op jit(solution)/shard_map/partner_part/pallas_call | solution.py:297
  58.4 2.3 %partner_part.7 = bf16[272,384]{1,0:T(8,128)(2,1)S(1)} custom-call(s32[8,8]{1,0:T(8,128)S(1)} %copy-done.3, bf16[256,1536]{1,0:T(8,128)(2,1)S(1)} %collective-permute-done.3.refs_1_.query, bf16[256,1536]{1,0:T(8,128)(2,1)S(1)} %copy-done, bf16[256,1536]{1,0:T(8,128)(2,1)S(1)} %copy-done.1, bf16[256,1536]{1,0:T(8,128)(2,1)S(1)} %collective-permute-done.5.sib_keys, ...), custom_call_target="tpu_custom_call" | custom-call | flops 301989888 | bytes 1048576 | tf_op jit(solution)/shard_map/partner_part/pallas_call | solution.py:297
  60.6 2.1 %collective-permute-start.17 = (bf16[272,384]{1,0:T(8,128)(2,1)S(1)}, bf16[272,384]{1,0:T(8,128)(2,1)S(1)}, u32[]{:S(2)}, u32[]{:S(2)}) collective-permute-start(bf16[272,384]{1,0:T(8,128)(2,1)S(1)} %partner_part.7), channel_id=1, source_target_pairs={{0,2},{2,0},{4,6},{6,4},{8,10},{10,8},{12,14},{14,12},{1,3},{3,1},... | collective-permute-start | bytes 626696 | tf_op jit(solution)/shard_map/ppermute | solution.py:453
  62.7 3.0 %own_part.3 = (f32[256,768]{1,0:T(8,128)S(1)}, f32[256,128]{1,0:T(8,128)S(1)}) custom-call(s32[8,8]{1,0:T(8,128)S(1)} %copy-done.3, bf16[256,1536]{1,0:T(8,128)(2,1)S(1)} %copy-done.2, bf16[256,1536]{1,0:T(8,128)(2,1)S(1)} %copy-done, bf16[256,1536]{1,0:T(8,128)(2,1)S(1)} %copy-done.1, bf16[256,1536]{1,0:T(8,128)(2,1)S(1)} %collective-permute-done.5.sib_keys, ...), custom_call_target="tpu_custom_call" | custom-call | flops 603979776 | bytes 1048576 | tf_op jit(solution)/shard_map/own_part/pallas_call | solution.py:297
  65.7 2.3 %partner_part.5 = bf16[272,384]{1,0:T(8,128)(2,1)S(1)} custom-call(s32[8,8]{1,0:T(8,128)S(1)} %copy-done.3, bf16[256,1536]{1,0:T(8,128)(2,1)S(1)} %collective-permute-done.3.refs_1_.query, bf16[256,1536]{1,0:T(8,128)(2,1)S(1)} %copy-done, bf16[256,1536]{1,0:T(8,128)(2,1)S(1)} %copy-done.1, bf16[256,1536]{1,0:T(8,128)(2,1)S(1)} %collective-permute-done.5.sib_keys, ...), custom_call_target="tpu_custom_call" | custom-call | flops 301989888 | bytes 1048576 | tf_op jit(solution)/shard_map/partner_part/pallas_call | solution.py:297
  68.0 2.2 %own_part.4 = (f32[256,384]{1,0:T(8,128)S(1)}, f32[256,128]{1,0:T(8,128)S(1)}) custom-call(s32[8,8]{1,0:T(8,128)S(1)} %copy-done.3, bf16[256,1536]{1,0:T(8,128)(2,1)S(1)} %copy-done.2, bf16[256,1536]{1,0:T(8,128)(2,1)S(1)} %copy-done, bf16[256,1536]{1,0:T(8,128)(2,1)S(1)} %copy-done.1, bf16[256,1536]{1,0:T(8,128)(2,1)S(1)} %collective-permute-done.5.sib_keys, ...), custom_call_target="tpu_custom_call" | custom-call | flops 301989888 | bytes 1048576 | tf_op jit(solution)/shard_map/own_part/pallas_call | solution.py:297
  70.3 3.7 %merge_and_project.2.refs_5_ = f32[256,3072]{1,0:T(8,128)S(1)} custom-call(bf16[768,3072]{1,0:T(8,128)(2,1)S(1)} %bitcast.1, bf16[768,3072]{1,0:T(8,128)(2,1)S(1)} %collective-permute-done.refs_0_.rest_7_.refs_1_, f32[256,384]{1,0:T(8,128)S(1)} %get-tuple-element.21.refs_2_, f32[256,128]{1,0:T(8,128)S(1)} %get-tuple-element.22.refs_3_, ...), custom_call_target="tpu_custom_call" | custom-call | flops 1811939328 | bytes 4194304 | tf_op jit(solution)/shard_map/merge_and_project/pallas_call | solution.py:340
  74.0 2.7 %merge_and_project.3 = bf16[256,3072]{1,0:T(8,128)(2,1)} custom-call(bf16[768,3072]{1,0:T(8,128)(2,1)S(1)} %bitcast.1, bf16[768,3072]{1,0:T(8,128)(2,1)S(1)} %collective-permute-done.refs_0_.rest_7_.refs_1_, f32[256,768]{1,0:T(8,128)S(1)} %get-tuple-element.19.refs_6_.refs_2_, f32[256,128]{1,0:T(8,128)S(1)} %get-tuple-element.20.rest_4_.refs_7_.refs_3_, ...), custom_call_target="tpu_custom_call" | custom-call | flops 603979776 | bytes 4194304 | tf_op jit(solution)/shard_map/merge_and_project/pallas_call | solution.py:340
  (42 shorter events, 0.7 us)
Async XLA Ops:
  0.0 21.2 %collective-permute-start = (bf16[768,3072]{1,0:T(8,128)(2,1)}, bf16[768,3072]{1,0:T(8,128)(2,1)S(1)}, u32[]{:S(2)}, u32[]{:S(2)}) collective-permute-start(bf16[768,3072]{1,0:T(8,128)(2,1)} %refs_0_.3), channel_id=1, source_target_pairs={{0,1},{1,0},{2,3},{3,2},{4,5},{5,4},{6,7},{7,6},{8,9},{9,8},{10,11... | collective-permute-start | bytes 14155784 | tf_op jit(solution)/shard_map/ppermute | solution.py:388
  2.2 6.3 %copy-start = (bf16[256,1536]{1,0:T(8,128)(2,1)S(1)}, bf16[256,1536]{1,0:T(8,128)(2,1)}, u32[]{:S(2)}) copy-start(bf16[256,1536]{1,0:T(8,128)(2,1)} %keys.13) | copy-start | bytes 2359300
  2.2 6.3 %copy-start.1 = (bf16[256,1536]{1,0:T(8,128)(2,1)S(1)}, bf16[256,1536]{1,0:T(8,128)(2,1)}, u32[]{:S(2)}) copy-start(bf16[256,1536]{1,0:T(8,128)(2,1)} %values.13) | copy-start | bytes 2359300
  2.3 24.4 %collective-permute-start.7 = (bf16[512,768]{1,0:T(8,128)(2,1)S(1)}, bf16[512,768]{1,0:T(8,128)(2,1)S(1)}, u32[]{:S(2)}, u32[]{:S(2)}) collective-permute-start(bf16[512,768]{1,0:T(8,128)(2,1)S(1)} %pad_maximum_fusion), channel_id=1, source_target_pairs={{0,4},{4,8},{6,2},{8,12},{10,6},{14,10},{1,5},{5,9},{7,3},{9,13},{... | collective-permute-start | bytes 2359304 | tf_op jit(solution)/shard_map/ppermute | solution.py:385
  7.0 4.3 %copy-start.2 = (bf16[256,1536]{1,0:T(8,128)(2,1)S(1)}, bf16[256,1536]{1,0:T(8,128)(2,1)}, u32[]{:S(2)}) copy-start(bf16[256,1536]{1,0:T(8,128)(2,1)} %query.5) | copy-start | bytes 2359300
  7.0 24.3 %collective-permute-start.9 = (bf16[512,768]{1,0:T(8,128)(2,1)S(1)}, bf16[512,768]{1,0:T(8,128)(2,1)S(1)}, u32[]{:S(2)}, u32[]{:S(2)}) collective-permute-start(bf16[512,768]{1,0:T(8,128)(2,1)S(1)} %pad_maximum_fusion.2), channel_id=1, source_target_pairs={{2,6},{4,0},{6,10},{8,4},{10,14},{12,8},{3,7},{5,1},{7,11},{9,5},{... | collective-permute-start | bytes 2359304 | tf_op jit(solution)/shard_map/ppermute | solution.py:386
  8.6 12.6 %collective-permute-start.1 = (bf16[512,384]{1,0:T(8,128)(2,1)S(1)}, bf16[512,384]{1,0:T(8,128)(2,1)S(1)}, u32[]{:S(2)}, u32[]{:S(2)}) collective-permute-start(bf16[512,384]{1,0:T(8,128)(2,1)S(1)} %pad_maximum_fusion.3), channel_id=1, source_target_pairs={{0,2},{2,0},{4,6},{6,4},{8,10},{10,8},{12,14},{14,12},{1,3},{3,1},... | collective-permute-start | bytes 1179656 | tf_op jit(solution)/shard_map/ppermute | solution.py:389
  11.3 26.1 %collective-permute-start.3 = (bf16[256,1536]{1,0:T(8,128)(2,1)S(1)}, bf16[256,1536]{1,0:T(8,128)(2,1)S(1)}, u32[]{:S(2)}, u32[]{:S(2)}) collective-permute-start(bf16[256,1536]{1,0:T(8,128)(2,1)S(1)} %copy-done.2), channel_id=1, source_target_pairs={{0,2},{2,0},{4,6},{6,4},{8,10},{10,8},{12,14},{14,12},{1,3},{3,1},... | collective-permute-start | bytes 2359304 | tf_op jit(solution)/shard_map/ppermute | solution.py:392
  21.2 16.1 %collective-permute-start.2 = (bf16[512,384]{1,0:T(8,128)(2,1)S(1)}, bf16[512,384]{1,0:T(8,128)(2,1)S(1)}, u32[]{:S(2)}, u32[]{:S(2)}) collective-permute-start(bf16[512,384]{1,0:T(8,128)(2,1)S(1)} %get-tuple-element.15), channel_id=1, source_target_pairs={{0,4},{4,8},{6,2},{8,12},{10,6},{14,10},{1,5},{5,9},{7,3},{9,13},{... | collective-permute-start | bytes 1179656 | tf_op jit(solution)/shard_map/ppermute | solution.py:393
  25.3 13.9 %collective-permute-start.4 = (bf16[512,384]{1,0:T(8,128)(2,1)S(1)}, bf16[512,384]{1,0:T(8,128)(2,1)S(1)}, u32[]{:S(2)}, u32[]{:S(2)}) collective-permute-start(bf16[512,384]{1,0:T(8,128)(2,1)S(1)} %get-tuple-element.16), channel_id=1, source_target_pairs={{2,6},{4,0},{6,10},{8,4},{10,14},{12,8},{3,7},{5,1},{7,11},{9,5},{... | collective-permute-start | bytes 1179656 | tf_op jit(solution)/shard_map/ppermute | solution.py:391
  26.8 24.9 %collective-permute-start.8 = (bf16[512,768]{1,0:T(8,128)(2,1)S(1)}, bf16[512,768]{1,0:T(8,128)(2,1)S(1)}, u32[]{:S(2)}, u32[]{:S(2)}) collective-permute-start(bf16[512,768]{1,0:T(8,128)(2,1)S(1)} %tie.5), channel_id=1, source_target_pairs={{0,4},{4,8},{6,2},{8,12},{10,6},{14,10},{1,5},{5,9},{7,3},{9,13},{... | collective-permute-start | bytes 2359304 | tf_op jit(solution)/shard_map/ppermute | solution.py:396
  31.4 24.7 %collective-permute-start.15 = (bf16[512,768]{1,0:T(8,128)(2,1)S(1)}, bf16[512,768]{1,0:T(8,128)(2,1)S(1)}, u32[]{:S(2)}, u32[]{:S(2)}) collective-permute-start(bf16[512,768]{1,0:T(8,128)(2,1)S(1)} %collective-permute-done.9.rest_1_), channel_id=1, source_target_pairs={{2,6},{4,0},{6,10},{8,4},{10,14},{12,8},{3,7},{5,1},{7,11},{9,5},{... | collective-permute-start | bytes 2359304 | tf_op jit(solution)/shard_map/ppermute | solution.py:394
  39.2 8.3 %copy-start.3 = (s32[8,8]{1,0:T(8,128)S(1)}, s32[8,8]{1,0:T(8,128)}, u32[]{:S(2)}) copy-start(s32[8,8]{1,0:T(8,128)} %table_ref.13) | copy-start | bytes 772
  39.2 2.3 %collective-permute-start.5 = (bf16[256,1536]{1,0:T(8,128)(2,1)S(1)}, bf16[256,1536]{1,0:T(8,128)(2,1)S(1)}, u32[]{:S(2)}, u32[]{:S(2)}) collective-permute-start(bf16[256,1536]{1,0:T(8,128)(2,1)S(1)} %get-tuple-element.17), channel_id=1, source_target_pairs={{0,1},{1,0},{2,3},{3,2},{4,5},{5,4},{6,7},{7,6},{8,9},{9,8},{10,11... | collective-permute-start | bytes 2359304 | tf_op jit(solution)/shard_map/ppermute | solution.py:400
  39.2 3.6 %collective-permute-start.6 = (bf16[256,1536]{1,0:T(8,128)(2,1)S(1)}, bf16[256,1536]{1,0:T(8,128)(2,1)S(1)}, u32[]{:S(2)}, u32[]{:S(2)}) collective-permute-start(bf16[256,1536]{1,0:T(8,128)(2,1)S(1)} %get-tuple-element.18), channel_id=1, source_target_pairs={{0,1},{1,0},{2,3},{3,2},{4,5},{5,4},{6,7},{7,6},{8,9},{9,8},{10,11... | collective-permute-start | bytes 2359304 | tf_op jit(solution)/shard_map/ppermute | solution.py:401
  39.8 16.2 %collective-permute-start.11 = (bf16[256,1536]{1,0:T(8,128)(2,1)S(1)}, bf16[256,1536]{1,0:T(8,128)(2,1)S(1)}, u32[]{:S(2)}, u32[]{:S(2)}) collective-permute-start(bf16[256,1536]{1,0:T(8,128)(2,1)S(1)} %maximum_maximum_fusion), channel_id=1, source_target_pairs={{0,1},{1,0},{2,3},{3,2},{4,5},{5,4},{6,7},{7,6},{8,9},{9,8},{10,11... | collective-permute-start | bytes 2359304 | tf_op jit(solution)/shard_map/ppermute | solution.py:402
  41.5 24.2 %collective-permute-start.10 = (bf16[512,384]{1,0:T(8,128)(2,1)S(1)}, bf16[512,384]{1,0:T(8,128)(2,1)S(1)}, u32[]{:S(2)}, u32[]{:S(2)}) collective-permute-start(bf16[512,384]{1,0:T(8,128)(2,1)S(1)} %collective-permute-done.4.refs_2_.rest_2_.rest_1_), channel_id=1, source_target_pairs={{2,6},{4,0},{6,10},{8,4},{10,14},{12,8},{3,7},{5,1},{7,11},{9,5},{... | collective-permute-start | bytes 1179656 | tf_op jit(solution)/shard_map/ppermute | solution.py:398
  42.8 22.9 %collective-permute-start.12 = (bf16[512,384]{1,0:T(8,128)(2,1)S(1)}, bf16[512,384]{1,0:T(8,128)(2,1)S(1)}, u32[]{:S(2)}, u32[]{:S(2)}) collective-permute-start(bf16[512,384]{1,0:T(8,128)(2,1)S(1)} %collective-permute-done.2.refs_0_.rest_1_), channel_id=1, source_target_pairs={{0,4},{4,8},{6,2},{8,12},{10,6},{14,10},{1,5},{5,9},{7,3},{9,13},{... | collective-permute-start | bytes 1179656 | tf_op jit(solution)/shard_map/ppermute | solution.py:397
  51.6 14.1 %collective-permute-start.13 = (bf16[272,384]{1,0:T(8,128)(2,1)S(1)}, bf16[272,384]{1,0:T(8,128)(2,1)S(1)}, u32[]{:S(2)}, u32[]{:S(2)}) collective-permute-start(bf16[272,384]{1,0:T(8,128)(2,1)S(1)} %partner_part.4.rest_4_), channel_id=1, source_target_pairs={{0,2},{2,0},{4,6},{6,4},{8,10},{10,8},{12,14},{14,12},{1,3},{3,1},... | collective-permute-start | bytes 626696 | tf_op jit(solution)/shard_map/ppermute | solution.py:451
  58.3 12.0 %collective-permute-start.16 = (bf16[272,384]{1,0:T(8,128)(2,1)S(1)}, bf16[272,384]{1,0:T(8,128)(2,1)S(1)}, u32[]{:S(2)}, u32[]{:S(2)}) collective-permute-start(bf16[272,384]{1,0:T(8,128)(2,1)S(1)} %partner_part.6.rest_4_), channel_id=1, source_target_pairs={{0,2},{2,0},{4,6},{6,4},{8,10},{10,8},{12,14},{14,12},{1,3},{3,1},... | collective-permute-start | bytes 626696 | tf_op jit(solution)/shard_map/ppermute | solution.py:452
  60.6 9.7 %collective-permute-start.17 = (bf16[272,384]{1,0:T(8,128)(2,1)S(1)}, bf16[272,384]{1,0:T(8,128)(2,1)S(1)}, u32[]{:S(2)}, u32[]{:S(2)}) collective-permute-start(bf16[272,384]{1,0:T(8,128)(2,1)S(1)} %partner_part.7), channel_id=1, source_target_pairs={{0,2},{2,0},{4,6},{6,4},{8,10},{10,8},{12,14},{14,12},{1,3},{3,1},... | collective-permute-start | bytes 626696 | tf_op jit(solution)/shard_map/ppermute | solution.py:453
  65.7 4.6 %slice-start = ((s8[4718592]{0:T(1024)(128)(4,1)}), s8[4194304]{0:T(1024)(128)(4,1)S(1)}, s32[]{:S(2)}) async-start(s8[4718592]{0:T(1024)(128)(4,1)} %bitcast), calls=%async_computation | async-start | bytes 8388608
  65.7 4.6 %slice-start.1 = ((s8[4718592]{0:T(1024)(128)(4,1)}), s8[524288]{0:T(1024)(128)(4,1)S(1)}, s32[]{:S(2)}) async-start(s8[4718592]{0:T(1024)(128)(4,1)} %bitcast), calls=%async_computation.1 | async-start | bytes 1048576
  68.0 6.0 %collective-permute-start.14 = (bf16[272,384]{1,0:T(8,128)(2,1)S(1)}, bf16[272,384]{1,0:T(8,128)(2,1)S(1)}, u32[]{:S(2)}, u32[]{:S(2)}) collective-permute-start(bf16[272,384]{1,0:T(8,128)(2,1)S(1)} %partner_part.5), channel_id=1, source_target_pairs={{0,2},{2,0},{4,6},{6,4},{8,10},{10,8},{12,14},{14,12},{1,3},{3,1},... | collective-permute-start | bytes 626696 | tf_op jit(solution)/shard_map/ppermute | solution.py:460

commit v15 on v14

--- a/solution.py
+++ b/solution.py
@@ -38,34 +38,39 @@
             raw = lax.dot_general(
                 query, keys, (((1,), (1,)), ((), ())), preferred_element_type=jnp.float32
             )
-            row.append(raw if valid is None else jnp.where(valid, raw, NEG))
+            count = keys.shape[0] // BS
+            valid = valid if isinstance(valid, tuple) else (valid,) * count
+            pieces = [raw[:, index * BS : (index + 1) * BS] for index in range(count)]
+            row.append(
+                [
+                    piece if allowed is None else jnp.where(allowed, piece, NEG)
+                    for piece, allowed in zip(pieces, valid)
+                ]
+            )
         scores.append(row)
     tops = []
     for row in scores:
         best = None
-        for raw in row:
-            for at in range(0, raw.shape[1], BS):
-                piece = raw[:, at : at + BS]
-                best = piece if best is None else jnp.maximum(best, piece)
+        for piece in sum(row, []):
+            best = piece if best is None else jnp.maximum(best, piece)
         tops.append(best.max(axis=1, keepdims=True))
     weights = [
-        [jnp.exp2((raw - top) * LOG2_SCALE) for raw in row] for row, top in zip(scores, tops)
+        [[jnp.exp2((piece - top) * LOG2_SCALE) for piece in pieces] for pieces in row]
+        for row, top in zip(scores, tops)
     ]
     totals = []
     for row in weights:
         total = None
-        for weight in row:
-            for at in range(0, weight.shape[1], BS):
-                piece = weight[:, at : at + BS]
-                total = piece if total is None else total + piece
+        for piece in sum(row, []):
+            total = piece if total is None else total + piece
         totals.append(total.sum(axis=1, keepdims=True))
     results = []
     for (_, parts), row, top, total in zip(problems, weights, tops, totals):
         blended = 0.0
-        for (_, values, _), weight in zip(parts, row):
-            blended = blended + jnp.dot(
-                weight.astype(jnp.bfloat16), values, preferred_element_type=jnp.float32
-            )
+        for (_, values, _), pieces in zip(parts, row):
+            weight = [piece.astype(jnp.bfloat16) for piece in pieces]
+            weight = weight[0] if len(weight) == 1 else jnp.concatenate(weight, axis=1)
+            blended = blended + jnp.dot(weight, values, preferred_element_type=jnp.float32)
         results.append((blended / total, top * LOG2_SCALE + jnp.log2(total)))
     return results
 
@@ -118,12 +123,12 @@
     return packed + pltpu.roll(packed, DH - pad, 1) + pltpu.roll(packed, DH - 2 * pad, 1)
 
 
-def pair(ref, col, block):
+def pair(ref, col, block, count=1):
     rows = ref.shape[0] // 2
     cols = head_cols(col)
     return (
-        ref[block * BS : (block + 1) * BS, cols],
-        ref[rows + block * BS : rows + (block + 1) * BS, cols],
+        ref[block * BS : (block + count) * BS, cols],
+        ref[rows + block * BS : rows + (block + count) * BS, cols],
     )
 
 
@@ -131,8 +136,8 @@
     def __init__(self, refs):
         self.refs = refs
 
-    def cross(self, head, block):
-        return pair(self.refs["major2"], head, block)
+    def cross(self, head, block, count=1):
+        return pair(self.refs["major2"], head, block, count)
 
     def far(self, head, block):
         return pair(self.refs["major4"], head, block)
@@ -142,10 +147,10 @@
             return pair(self.refs["major1"], head, block)
         return pair(self.refs["major3"], head - 6, block)
 
-    def near(self, head, block):
+    def near(self, head, block, count=1):
         if head < 9:
-            return pair(self.refs["minor1"], head - 3, block)
-        return pair(self.refs["minor2"], head - 9, block)
+            return pair(self.refs["minor1"], head - 3, block, count)
+        return pair(self.refs["minor2"], head - 9, block, count)
 
     def near_first(self, head):
         return pair(self.refs["nearest"], head - 3, 0)
@@ -176,19 +181,22 @@
         mine = slice(block * BS, (block + 1) * BS)
         cols = head_cols(head)
         last = block + 1 == blocks
-        parts = [(keys[mine, cols], values[mine, cols], None)]
         if last:
+            parts = [(keys[mine, cols], values[mine, cols], None)]
             parts.append((sib_keys[:BS, cols], sib_values[:BS, cols], own_count > 1))
         else:
-            after = slice((block + 1) * BS, (block + 2) * BS)
-            parts.append((keys[after, cols], values[after, cols], own_count > 1))
+            both = slice(block * BS, (block + 2) * BS)
+            parts = [(keys[both, cols], values[both, cols], (None, own_count > 1))]
         parts.append((*buffers.away(head, block), away_valid))
         if head < CROSS:
             parts.append((*buffers.cross(head, block), cross_valid))
         else:
-            parts.append((*buffers.near(head, block), near_count > 0))
-            after = buffers.near_first(head) if last else buffers.near(head, block + 1)
-            parts.append((*after, near_count > 1))
+            if last:
+                parts.append((*buffers.near(head, block), near_count > 0))
+                parts.append((*buffers.near_first(head), near_count > 1))
+            else:
+                allowed = (near_count > 0, near_count > 1)
+                parts.append((*buffers.near(head, block, 2), allowed))
             parts.append((*buffers.relay(head, block), relay_valid))
         return query[mine, cols], parts
 
@@ -217,9 +225,12 @@
         ]
         if head < CROSS:
             last = block + 1 == blocks
-            parts.append((*buffers.cross(head, block), cross_count > 0))
-            after = buffers.cross_first(head) if last else buffers.cross(head, block + 1)
-            parts.append((*after, cross_count > 1))
+            if last:
+                parts.append((*buffers.cross(head, block), cross_count > 0))
+                parts.append((*buffers.cross_first(head), cross_count > 1))
+            else:
+                allowed = (cross_count > 0, cross_count > 1)
+                parts.append((*buffers.cross(head, block, 2), allowed))
             parts.append((*buffers.far(head, block), far_valid))
         else:
             parts.append((*buffers.near(head, block), near_valid))
@@ -234,7 +245,10 @@
     owns = [(group, refs.pop(0), refs.pop(0)) for group in own_groups]
     parts = [(group, refs.pop(0)) for group in part_groups]
     base = refs.pop(0) if has_base else None
-    out, attended = refs
+    if has_base:
+        target, attended, out, sems = refs
+    else:
+        out, attended = refs
     rows = out.shape[0]
     lanes = lax.broadcasted_iota(jnp.int32, (rows, DH), 1)
     own_at, part_at = {}, {}
@@ -277,6 +291,12 @@
                         preferred_element_type=jnp.float32,
                     )
             out[:, at : at + TILE] = product.astype(out.dtype)
+            if has_base:
+                copy_out(at).start()
+
+    def copy_out(at):
+        cols = slice(at, at + TILE)
+        return pltpu.make_async_copy(out.at[:, cols], target.at[:, cols], sems.at[at // TILE])
 
     core = lax.axis_index("head")
 
@@ -287,6 +307,10 @@
     @pl.when(core != 0)
     def _():
         multiply((sib_weight, weight))
+
+    if has_base:
+        for at in range(0, out.shape[1], TILE):
+            copy_out(at).wait()
 
 
 def whole(shape):
@@ -335,8 +359,13 @@
     for _, own in owns:
         operands += own
     operands += [part for _, part in parts]
+    streams = []
     if base is not None:
         operands.append(base)
+        streams = [
+            pltpu.VMEM((rows, columns), dtype),
+            pltpu.SemaphoreType.DMA((columns // TILE,)),
+        ]
     return pl.pallas_call(
         functools.partial(
             project_kernel,
@@ -347,9 +376,9 @@
         ),
         grid=(1,),
         in_specs=[whole(x.shape) for x in operands],
-        out_specs=whole((rows, columns)),
+        out_specs=whole((rows, columns)) if base is None else pl.BlockSpec(memory_space=pl.ANY),
         out_shape=jax.ShapeDtypeStruct((rows, columns), dtype),
-        scratch_shapes=[pltpu.VMEM((rows, depth), jnp.bfloat16)],
+        scratch_shapes=[pltpu.VMEM((rows, depth), jnp.bfloat16), *streams],
         compiler_params=pltpu.CompilerParams(vmem_limit_bytes=8 * MIB),
         cost_estimate=pl.CostEstimate(
             flops=2 * rows * depth * columns, bytes_accessed=4 * MIB, transcendentals=0

time: 77.1 us -> 77.1 us (level)
  transfers between devices with their start and end apart: 18 -> 18, of which waited for: 6 -> 6; matrix products, arithmetic and copies ran while one was open for 3% -> 3% of each run, Pallas kernels for 25% -> 26%
where the time goes in v15:
time: 77.1 us; the launch traced here: 76.7 us
  starting transfers between devices  31.7 us (41%)
  Pallas kernels  22 us (29%)
  waiting for transfers between devices  20.1 us (26%)
  local copies, waits for them, and re-layouts  2.05 us (3%)
    pallas_call x7, Pallas kernels, run(): pl.pallas_call(body, grid=(1,), in_specs=[pl.BlockSpec(memory_space=pltpu...  15.9 us
    ppermute x1, waiting for transfers between devices, per_device(): cross = lax.ppermute(pack(0, 3), 'frame', partner_moves)  9.8 us
    pallas_call x2, Pallas kernels, project(): pl.pallas_call(functools.partial(project_kernel, span, tuple((group for g...  6.06 us
    ppermute x1, starting transfers between devices, per_device(): major4 = lax.ppermute(major2, 'frame', away_moves)  4.75 us
    ppermute x1, starting transfers between devices, per_device(): major1 = lax.ppermute(pack(0, 6), 'frame', away_moves)  4.66 us
    ppermute x1, waiting for transfers between devices, per_device(): partner_query = lax.ppermute(queries, 'frame', partner_moves)  4.65 us
    ppermute x1, starting transfers between devices, per_device(): major3 = lax.ppermute(to_major3, 'frame', away_moves)  4.6 us
    ppermute x1, starting transfers between devices, per_device(): major2 = lax.ppermute(cross, 'frame', away_moves)  4.03 us
  transfers between devices with their start and end apart: 18, of which 6 were waited for; matrix products, arithmetic and copies ran while one was open for 3% of the time, Pallas kernels for 26%

profile of v15, /device:TPU:0, one launch (start us, length us, event | category | flops | bytes accessed | tf_op | source)
XLA Modules:
  0.0 76.7 jit_solution(7747385614854783248)
XLA Ops:
  0.0 0.5 collective-permute-start
  0.5 1.8 %fusion.1 = (bf16[256,768]{1,0:T(8,128)(2,1)S(1)}, bf16[256,768]{1,0:T(8,128)(2,1)S(1)}, bf16[256,768]{1,0:T(8,128)(2,1)S(1)}, bf16[256,768]{1,0:T(8,128)(2,1)S(...) fusion(bf16[256,1536]{1,0:T(8,128)(2,1)} %keys.13, bf16[256,1536]{1,0:T(8,128)(2,1)} %values.13), kind=kLoop, calls=%fused_computation.7 | loop fusion | bytes 4718592 | tf_op jit(solution)/shard_map/slice | solution.py:406
  2.3 4.7 %collective-permute-start.7 = (bf16[512,768]{1,0:T(8,128)(2,1)S(1)}, bf16[512,768]{1,0:T(8,128)(2,1)S(1)}, u32[]{:S(2)}, u32[]{:S(2)}) collective-permute-start(bf16[512,768]{1,0:T(8,128)(2,1)S(1)} %pad_maximum_fusion), channel_id=1, source_target_pairs={{0,4},{4,8},{6,2},{8,12},{10,6},{14,10},{1,5},{5,9},{7,3},{9,13},{... | collective-permute-start | bytes 2359304 | tf_op jit(solution)/shard_map/ppermute | solution.py:414
  7.0 1.4 %collective-permute-start.9 = (bf16[512,768]{1,0:T(8,128)(2,1)S(1)}, bf16[512,768]{1,0:T(8,128)(2,1)S(1)}, u32[]{:S(2)}, u32[]{:S(2)}) collective-permute-start(bf16[512,768]{1,0:T(8,128)(2,1)S(1)} %pad_maximum_fusion.2), channel_id=1, source_target_pairs={{2,6},{4,0},{6,10},{8,4},{10,14},{12,8},{3,7},{5,1},{7,11},{9,5},{... | collective-permute-start | bytes 2359304 | tf_op jit(solution)/shard_map/ppermute | solution.py:415
  8.5 0.1 fusion.3
  8.6 2.7 %collective-permute-start.1 = (bf16[512,384]{1,0:T(8,128)(2,1)S(1)}, bf16[512,384]{1,0:T(8,128)(2,1)S(1)}, u32[]{:S(2)}, u32[]{:S(2)}) collective-permute-start(bf16[512,384]{1,0:T(8,128)(2,1)S(1)} %pad_maximum_fusion.3), channel_id=1, source_target_pairs={{0,2},{2,0},{4,6},{6,4},{8,10},{10,8},{12,14},{14,12},{1,3},{3,1},... | collective-permute-start | bytes 1179656 | tf_op jit(solution)/shard_map/ppermute | solution.py:418
  11.3 0.1 collective-permute-start.3
  11.4 9.8 %collective-permute-done.1.refs_1_ = bf16[512,384]{1,0:T(8,128)(2,1)S(1)} collective-permute-done((bf16[512,384]{1,0:T(8,128)(2,1)S(1)}, bf16[512,384]{1,0:T(8,128)(2,1)S(1)}, u32[]{:S(2)}, u32[]{:S(2)}) %collective-permute-start.1) | collective-permute-done | bytes 393248 | tf_op jit(solution)/shard_map/ppermute | solution.py:418
  21.2 4.0 %collective-permute-start.2 = (bf16[512,384]{1,0:T(8,128)(2,1)S(1)}, bf16[512,384]{1,0:T(8,128)(2,1)S(1)}, u32[]{:S(2)}, u32[]{:S(2)}) collective-permute-start(bf16[512,384]{1,0:T(8,128)(2,1)S(1)} %get-tuple-element.15), channel_id=1, source_target_pairs={{0,4},{4,8},{6,2},{8,12},{10,6},{14,10},{1,5},{5,9},{7,3},{9,13},{... | collective-permute-start | bytes 1179656 | tf_op jit(solution)/shard_map/ppermute | solution.py:422
  25.3 1.3 %collective-permute-start.4 = (bf16[512,384]{1,0:T(8,128)(2,1)S(1)}, bf16[512,384]{1,0:T(8,128)(2,1)S(1)}, u32[]{:S(2)}, u32[]{:S(2)}) collective-permute-start(bf16[512,384]{1,0:T(8,128)(2,1)S(1)} %get-tuple-element.16), channel_id=1, source_target_pairs={{2,6},{4,0},{6,10},{8,4},{10,14},{12,8},{3,7},{5,1},{7,11},{9,5},{... | collective-permute-start | bytes 1179656 | tf_op jit(solution)/shard_map/ppermute | solution.py:420
  26.8 4.6 %collective-permute-start.8 = (bf16[512,768]{1,0:T(8,128)(2,1)S(1)}, bf16[512,768]{1,0:T(8,128)(2,1)S(1)}, u32[]{:S(2)}, u32[]{:S(2)}) collective-permute-start(bf16[512,768]{1,0:T(8,128)(2,1)S(1)} %tie.5), channel_id=1, source_target_pairs={{0,4},{4,8},{6,2},{8,12},{10,6},{14,10},{1,5},{5,9},{7,3},{9,13},{... | collective-permute-start | bytes 2359304 | tf_op jit(solution)/shard_map/ppermute | solution.py:425
  31.4 1.3 %collective-permute-start.15 = (bf16[512,768]{1,0:T(8,128)(2,1)S(1)}, bf16[512,768]{1,0:T(8,128)(2,1)S(1)}, u32[]{:S(2)}, u32[]{:S(2)}) collective-permute-start(bf16[512,768]{1,0:T(8,128)(2,1)S(1)} %collective-permute-done.9.rest_1_), channel_id=1, source_target_pairs={{2,6},{4,0},{6,10},{8,4},{10,14},{12,8},{3,7},{5,1},{7,11},{9,5},{... | collective-permute-start | bytes 2359304 | tf_op jit(solution)/shard_map/ppermute | solution.py:423
  32.7 4.7 %collective-permute-done.3.refs_1_.query = bf16[256,1536]{1,0:T(8,128)(2,1)S(1)} collective-permute-done((bf16[256,1536]{1,0:T(8,128)(2,1)S(1)}, bf16[256,1536]{1,0:T(8,128)(2,1)S(1)}, u32[]{:S(2)}, u32[]{:S(2)}) %collective-permute-start.3) | collective-permute-done | bytes 786464 | tf_op jit(solution)/shard_map/ppermute | solution.py:421
  37.4 1.8 %collective-permute-done.4.refs_2_.rest_2_.rest_1_ = bf16[512,384]{1,0:T(8,128)(2,1)S(1)} collective-permute-done((bf16[512,384]{1,0:T(8,128)(2,1)S(1)}, bf16[512,384]{1,0:T(8,128)(2,1)S(1)}, u32[]{:S(2)}, u32[]{:S(2)}) %collective-permute-start.4) | collective-permute-done | bytes 393248 | tf_op jit(solution)/shard_map/ppermute | solution.py:420
  39.2 0.5 collective-permute-start.6
  39.8 0.1 collective-permute-start.11
  39.9 1.6 %collective-permute-done.5.sib_keys = bf16[256,1536]{1,0:T(8,128)(2,1)S(1)} collective-permute-done((bf16[256,1536]{1,0:T(8,128)(2,1)S(1)}, bf16[256,1536]{1,0:T(8,128)(2,1)S(1)}, u32[]{:S(2)}, u32[]{:S(2)}) %collective-permute-start.5) | collective-permute-done | bytes 786464 | tf_op jit(solution)/shard_map/ppermute | solution.py:429
  41.5 1.3 %collective-permute-start.10 = (bf16[512,384]{1,0:T(8,128)(2,1)S(1)}, bf16[512,384]{1,0:T(8,128)(2,1)S(1)}, u32[]{:S(2)}, u32[]{:S(2)}) collective-permute-start(bf16[512,384]{1,0:T(8,128)(2,1)S(1)} %collective-permute-done.4.refs_2_.rest_2_.rest_1_), channel_id=1, source_target_pairs={{2,6},{4,0},{6,10},{8,4},{10,14},{12,8},{3,7},{5,1},{7,11},{9,5},{... | collective-permute-start | bytes 1179656 | tf_op jit(solution)/shard_map/ppermute | solution.py:427
  42.8 4.8 %collective-permute-start.12 = (bf16[512,384]{1,0:T(8,128)(2,1)S(1)}, bf16[512,384]{1,0:T(8,128)(2,1)S(1)}, u32[]{:S(2)}, u32[]{:S(2)}) collective-permute-start(bf16[512,384]{1,0:T(8,128)(2,1)S(1)} %collective-permute-done.2.refs_0_.rest_1_), channel_id=1, source_target_pairs={{0,4},{4,8},{6,2},{8,12},{10,6},{14,10},{1,5},{5,9},{7,3},{9,13},{... | collective-permute-start | bytes 1179656 | tf_op jit(solution)/shard_map/ppermute | solution.py:426
  47.6 1.9 %partner_part.4.rest_4_ = bf16[272,384]{1,0:T(8,128)(2,1)S(1)} custom-call(s32[8,8]{1,0:T(8,128)S(1)} %copy-done.3, bf16[256,1536]{1,0:T(8,128)(2,1)S(1)} %collective-permute-done.3.refs_1_.query, bf16[256,1536]{1,0:T(8,128)(2,1)S(1)} %copy-done, bf16[256,1536]{1,0:T(8,128)(2,1)S(1)} %copy-done.1, bf16[256,1536]{1,0:T(8,128)(2,1)S(1)} %collective-permute-done.5.sib_keys, ...), custom_call_target="tpu_custom_call" | custom-call | flops 301989888 | bytes 1048576 | tf_op jit(solution)/shard_map/partner_part/pallas_call | solution.py:321
  49.5 2.1 %collective-permute-done.8.rest_0_.rest_6_ = bf16[512,768]{1,0:T(8,128)(2,1)S(1)} collective-permute-done((bf16[512,768]{1,0:T(8,128)(2,1)S(1)}, bf16[512,768]{1,0:T(8,128)(2,1)S(1)}, u32[]{:S(2)}, u32[]{:S(2)}) %collective-permute-start.8) | collective-permute-done | bytes 786464 | tf_op jit(solution)/shard_map/ppermute | solution.py:425
  51.6 2.4 %collective-permute-start.13 = (bf16[272,384]{1,0:T(8,128)(2,1)S(1)}, bf16[272,384]{1,0:T(8,128)(2,1)S(1)}, u32[]{:S(2)}, u32[]{:S(2)}) collective-permute-start(bf16[272,384]{1,0:T(8,128)(2,1)S(1)} %partner_part.4.rest_4_), channel_id=1, source_target_pairs={{0,2},{2,0},{4,6},{6,4},{8,10},{10,8},{12,14},{14,12},{1,3},{3,1},... | collective-permute-start | bytes 626696 | tf_op jit(solution)/shard_map/ppermute | solution.py:480
  54.1 1.9 %own_part.5 = (f32[256,384]{1,0:T(8,128)S(1)}, f32[256,128]{1,0:T(8,128)S(1)}) custom-call(s32[8,8]{1,0:T(8,128)S(1)} %copy-done.3, bf16[256,1536]{1,0:T(8,128)(2,1)S(1)} %copy-done.2, bf16[256,1536]{1,0:T(8,128)(2,1)S(1)} %copy-done, bf16[256,1536]{1,0:T(8,128)(2,1)S(1)} %copy-done.1, bf16[256,1536]{1,0:T(8,128)(2,1)S(1)} %collective-permute-done.5.sib_keys, ...), custom_call_target="tpu_custom_call" | custom-call | flops 301989888 | bytes 1048576 | tf_op jit(solution)/shard_map/own_part/pallas_call | solution.py:321
  56.0 0.1 collective-permute-done.15.rest_2_
  56.1 2.3 %partner_part.6.rest_4_ = bf16[272,384]{1,0:T(8,128)(2,1)S(1)} custom-call(s32[8,8]{1,0:T(8,128)S(1)} %copy-done.3, bf16[256,1536]{1,0:T(8,128)(2,1)S(1)} %collective-permute-done.3.refs_1_.query, bf16[256,1536]{1,0:T(8,128)(2,1)S(1)} %copy-done, bf16[256,1536]{1,0:T(8,128)(2,1)S(1)} %copy-done.1, bf16[256,1536]{1,0:T(8,128)(2,1)S(1)} %collective-permute-done.5.sib_keys, ...), custom_call_target="tpu_custom_call" | custom-call | flops 301989888 | bytes 1048576 | tf_op jit(solution)/shard_map/partner_part/pallas_call | solution.py:321
  58.4 2.3 %partner_part.7 = bf16[272,384]{1,0:T(8,128)(2,1)S(1)} custom-call(s32[8,8]{1,0:T(8,128)S(1)} %copy-done.3, bf16[256,1536]{1,0:T(8,128)(2,1)S(1)} %collective-permute-done.3.refs_1_.query, bf16[256,1536]{1,0:T(8,128)(2,1)S(1)} %copy-done, bf16[256,1536]{1,0:T(8,128)(2,1)S(1)} %copy-done.1, bf16[256,1536]{1,0:T(8,128)(2,1)S(1)} %collective-permute-done.5.sib_keys, ...), custom_call_target="tpu_custom_call" | custom-call | flops 301989888 | bytes 1048576 | tf_op jit(solution)/shard_map/partner_part/pallas_call | solution.py:321
  60.7 2.1 %collective-permute-start.17 = (bf16[272,384]{1,0:T(8,128)(2,1)S(1)}, bf16[272,384]{1,0:T(8,128)(2,1)S(1)}, u32[]{:S(2)}, u32[]{:S(2)}) collective-permute-start(bf16[272,384]{1,0:T(8,128)(2,1)S(1)} %partner_part.7), channel_id=1, source_target_pairs={{0,2},{2,0},{4,6},{6,4},{8,10},{10,8},{12,14},{14,12},{1,3},{3,1},... | collective-permute-start | bytes 626696 | tf_op jit(solution)/shard_map/ppermute | solution.py:482
  62.8 3.0 %own_part.3 = (f32[256,768]{1,0:T(8,128)S(1)}, f32[256,128]{1,0:T(8,128)S(1)}) custom-call(s32[8,8]{1,0:T(8,128)S(1)} %copy-done.3, bf16[256,1536]{1,0:T(8,128)(2,1)S(1)} %copy-done.2, bf16[256,1536]{1,0:T(8,128)(2,1)S(1)} %copy-done, bf16[256,1536]{1,0:T(8,128)(2,1)S(1)} %copy-done.1, bf16[256,1536]{1,0:T(8,128)(2,1)S(1)} %collective-permute-done.5.sib_keys, ...), custom_call_target="tpu_custom_call" | custom-call | flops 603979776 | bytes 1048576 | tf_op jit(solution)/shard_map/own_part/pallas_call | solution.py:321
  65.8 2.3 %partner_part.5 = bf16[272,384]{1,0:T(8,128)(2,1)S(1)} custom-call(s32[8,8]{1,0:T(8,128)S(1)} %copy-done.3, bf16[256,1536]{1,0:T(8,128)(2,1)S(1)} %collective-permute-done.3.refs_1_.query, bf16[256,1536]{1,0:T(8,128)(2,1)S(1)} %copy-done, bf16[256,1536]{1,0:T(8,128)(2,1)S(1)} %copy-done.1, bf16[256,1536]{1,0:T(8,128)(2,1)S(1)} %collective-permute-done.5.sib_keys, ...), custom_call_target="tpu_custom_call" | custom-call | flops 301989888 | bytes 1048576 | tf_op jit(solution)/shard_map/partner_part/pallas_call | solution.py:321
  68.2 2.2 %own_part.4 = (f32[256,384]{1,0:T(8,128)S(1)}, f32[256,128]{1,0:T(8,128)S(1)}) custom-call(s32[8,8]{1,0:T(8,128)S(1)} %copy-done.3, bf16[256,1536]{1,0:T(8,128)(2,1)S(1)} %copy-done.2, bf16[256,1536]{1,0:T(8,128)(2,1)S(1)} %copy-done, bf16[256,1536]{1,0:T(8,128)(2,1)S(1)} %copy-done.1, bf16[256,1536]{1,0:T(8,128)(2,1)S(1)} %collective-permute-done.5.sib_keys, ...), custom_call_target="tpu_custom_call" | custom-call | flops 301989888 | bytes 1048576 | tf_op jit(solution)/shard_map/own_part/pallas_call | solution.py:321
  70.5 3.7 %merge_and_project.2.refs_5_ = f32[256,3072]{1,0:T(8,128)S(1)} custom-call(bf16[768,3072]{1,0:T(8,128)(2,1)S(1)} %bitcast.1, bf16[768,3072]{1,0:T(8,128)(2,1)S(1)} %collective-permute-done.refs_0_.rest_7_.refs_1_, f32[256,384]{1,0:T(8,128)S(1)} %get-tuple-element.21.refs_2_, f32[256,128]{1,0:T(8,128)S(1)} %get-tuple-element.22.refs_3_, ...), custom_call_target="tpu_custom_call" | custom-call | flops 1811939328 | bytes 4194304 | tf_op jit(solution)/shard_map/merge_and_project/pallas_call | solution.py:369
  74.1 2.4 %merge_and_project.3 = bf16[256,3072]{1,0:T(8,128)(2,1)} custom-call(bf16[768,3072]{1,0:T(8,128)(2,1)S(1)} %bitcast.1, bf16[768,3072]{1,0:T(8,128)(2,1)S(1)} %collective-permute-done.refs_0_.rest_7_.refs_1_, f32[256,768]{1,0:T(8,128)S(1)} %get-tuple-element.19.refs_6_.refs_2_, f32[256,128]{1,0:T(8,128)S(1)} %get-tuple-element.20.rest_4_.refs_7_.refs_3_, ...), custom_call_target="tpu_custom_call" | custom-call | flops 603979776 | bytes 4194304 | tf_op jit(solution)/shard_map/merge_and_project/pallas_call | solution.py:369
  (42 shorter events, 0.7 us)
Async XLA Ops:
  0.0 21.2 %collective-permute-start = (bf16[768,3072]{1,0:T(8,128)(2,1)}, bf16[768,3072]{1,0:T(8,128)(2,1)S(1)}, u32[]{:S(2)}, u32[]{:S(2)}) collective-permute-start(bf16[768,3072]{1,0:T(8,128)(2,1)} %refs_0_.3), channel_id=1, source_target_pairs={{0,1},{1,0},{2,3},{3,2},{4,5},{5,4},{6,7},{7,6},{8,9},{9,8},{10,11... | collective-permute-start | bytes 14155784 | tf_op jit(solution)/shard_map/ppermute | solution.py:417
  2.2 6.3 %copy-start = (bf16[256,1536]{1,0:T(8,128)(2,1)S(1)}, bf16[256,1536]{1,0:T(8,128)(2,1)}, u32[]{:S(2)}) copy-start(bf16[256,1536]{1,0:T(8,128)(2,1)} %keys.13) | copy-start | bytes 2359300
  2.2 6.3 %copy-start.1 = (bf16[256,1536]{1,0:T(8,128)(2,1)S(1)}, bf16[256,1536]{1,0:T(8,128)(2,1)}, u32[]{:S(2)}) copy-start(bf16[256,1536]{1,0:T(8,128)(2,1)} %values.13) | copy-start | bytes 2359300
  2.3 24.4 %collective-permute-start.7 = (bf16[512,768]{1,0:T(8,128)(2,1)S(1)}, bf16[512,768]{1,0:T(8,128)(2,1)S(1)}, u32[]{:S(2)}, u32[]{:S(2)}) collective-permute-start(bf16[512,768]{1,0:T(8,128)(2,1)S(1)} %pad_maximum_fusion), channel_id=1, source_target_pairs={{0,4},{4,8},{6,2},{8,12},{10,6},{14,10},{1,5},{5,9},{7,3},{9,13},{... | collective-permute-start | bytes 2359304 | tf_op jit(solution)/shard_map/ppermute | solution.py:414
  7.0 4.3 %copy-start.2 = (bf16[256,1536]{1,0:T(8,128)(2,1)S(1)}, bf16[256,1536]{1,0:T(8,128)(2,1)}, u32[]{:S(2)}) copy-start(bf16[256,1536]{1,0:T(8,128)(2,1)} %query.5) | copy-start | bytes 2359300
  7.0 24.3 %collective-permute-start.9 = (bf16[512,768]{1,0:T(8,128)(2,1)S(1)}, bf16[512,768]{1,0:T(8,128)(2,1)S(1)}, u32[]{:S(2)}, u32[]{:S(2)}) collective-permute-start(bf16[512,768]{1,0:T(8,128)(2,1)S(1)} %pad_maximum_fusion.2), channel_id=1, source_target_pairs={{2,6},{4,0},{6,10},{8,4},{10,14},{12,8},{3,7},{5,1},{7,11},{9,5},{... | collective-permute-start | bytes 2359304 | tf_op jit(solution)/shard_map/ppermute | solution.py:415
  8.6 12.6 %collective-permute-start.1 = (bf16[512,384]{1,0:T(8,128)(2,1)S(1)}, bf16[512,384]{1,0:T(8,128)(2,1)S(1)}, u32[]{:S(2)}, u32[]{:S(2)}) collective-permute-start(bf16[512,384]{1,0:T(8,128)(2,1)S(1)} %pad_maximum_fusion.3), channel_id=1, source_target_pairs={{0,2},{2,0},{4,6},{6,4},{8,10},{10,8},{12,14},{14,12},{1,3},{3,1},... | collective-permute-start | bytes 1179656 | tf_op jit(solution)/shard_map/ppermute | solution.py:418
  11.3 26.1 %collective-permute-start.3 = (bf16[256,1536]{1,0:T(8,128)(2,1)S(1)}, bf16[256,1536]{1,0:T(8,128)(2,1)S(1)}, u32[]{:S(2)}, u32[]{:S(2)}) collective-permute-start(bf16[256,1536]{1,0:T(8,128)(2,1)S(1)} %copy-done.2), channel_id=1, source_target_pairs={{0,2},{2,0},{4,6},{6,4},{8,10},{10,8},{12,14},{14,12},{1,3},{3,1},... | collective-permute-start | bytes 2359304 | tf_op jit(solution)/shard_map/ppermute | solution.py:421
  21.2 16.1 %collective-permute-start.2 = (bf16[512,384]{1,0:T(8,128)(2,1)S(1)}, bf16[512,384]{1,0:T(8,128)(2,1)S(1)}, u32[]{:S(2)}, u32[]{:S(2)}) collective-permute-start(bf16[512,384]{1,0:T(8,128)(2,1)S(1)} %get-tuple-element.15), channel_id=1, source_target_pairs={{0,4},{4,8},{6,2},{8,12},{10,6},{14,10},{1,5},{5,9},{7,3},{9,13},{... | collective-permute-start | bytes 1179656 | tf_op jit(solution)/shard_map/ppermute | solution.py:422
  25.3 13.9 %collective-permute-start.4 = (bf16[512,384]{1,0:T(8,128)(2,1)S(1)}, bf16[512,384]{1,0:T(8,128)(2,1)S(1)}, u32[]{:S(2)}, u32[]{:S(2)}) collective-permute-start(bf16[512,384]{1,0:T(8,128)(2,1)S(1)} %get-tuple-element.16), channel_id=1, source_target_pairs={{2,6},{4,0},{6,10},{8,4},{10,14},{12,8},{3,7},{5,1},{7,11},{9,5},{... | collective-permute-start | bytes 1179656 | tf_op jit(solution)/shard_map/ppermute | solution.py:420
  26.8 24.9 %collective-permute-start.8 = (bf16[512,768]{1,0:T(8,128)(2,1)S(1)}, bf16[512,768]{1,0:T(8,128)(2,1)S(1)}, u32[]{:S(2)}, u32[]{:S(2)}) collective-permute-start(bf16[512,768]{1,0:T(8,128)(2,1)S(1)} %tie.5), channel_id=1, source_target_pairs={{0,4},{4,8},{6,2},{8,12},{10,6},{14,10},{1,5},{5,9},{7,3},{9,13},{... | collective-permute-start | bytes 2359304 | tf_op jit(solution)/shard_map/ppermute | solution.py:425
  31.4 24.7 %collective-permute-start.15 = (bf16[512,768]{1,0:T(8,128)(2,1)S(1)}, bf16[512,768]{1,0:T(8,128)(2,1)S(1)}, u32[]{:S(2)}, u32[]{:S(2)}) collective-permute-start(bf16[512,768]{1,0:T(8,128)(2,1)S(1)} %collective-permute-done.9.rest_1_), channel_id=1, source_target_pairs={{2,6},{4,0},{6,10},{8,4},{10,14},{12,8},{3,7},{5,1},{7,11},{9,5},{... | collective-permute-start | bytes 2359304 | tf_op jit(solution)/shard_map/ppermute | solution.py:423
  39.2 8.3 %copy-start.3 = (s32[8,8]{1,0:T(8,128)S(1)}, s32[8,8]{1,0:T(8,128)}, u32[]{:S(2)}) copy-start(s32[8,8]{1,0:T(8,128)} %table_ref.13) | copy-start | bytes 772
  39.2 2.3 %collective-permute-start.5 = (bf16[256,1536]{1,0:T(8,128)(2,1)S(1)}, bf16[256,1536]{1,0:T(8,128)(2,1)S(1)}, u32[]{:S(2)}, u32[]{:S(2)}) collective-permute-start(bf16[256,1536]{1,0:T(8,128)(2,1)S(1)} %get-tuple-element.17), channel_id=1, source_target_pairs={{0,1},{1,0},{2,3},{3,2},{4,5},{5,4},{6,7},{7,6},{8,9},{9,8},{10,11... | collective-permute-start | bytes 2359304 | tf_op jit(solution)/shard_map/ppermute | solution.py:429
  39.2 3.6 %collective-permute-start.6 = (bf16[256,1536]{1,0:T(8,128)(2,1)S(1)}, bf16[256,1536]{1,0:T(8,128)(2,1)S(1)}, u32[]{:S(2)}, u32[]{:S(2)}) collective-permute-start(bf16[256,1536]{1,0:T(8,128)(2,1)S(1)} %get-tuple-element.18), channel_id=1, source_target_pairs={{0,1},{1,0},{2,3},{3,2},{4,5},{5,4},{6,7},{7,6},{8,9},{9,8},{10,11... | collective-permute-start | bytes 2359304 | tf_op jit(solution)/shard_map/ppermute | solution.py:430
  39.8 16.2 %collective-permute-start.11 = (bf16[256,1536]{1,0:T(8,128)(2,1)S(1)}, bf16[256,1536]{1,0:T(8,128)(2,1)S(1)}, u32[]{:S(2)}, u32[]{:S(2)}) collective-permute-start(bf16[256,1536]{1,0:T(8,128)(2,1)S(1)} %maximum_maximum_fusion), channel_id=1, source_target_pairs={{0,1},{1,0},{2,3},{3,2},{4,5},{5,4},{6,7},{7,6},{8,9},{9,8},{10,11... | collective-permute-start | bytes 2359304 | tf_op jit(solution)/shard_map/ppermute | solution.py:431
  41.5 24.3 %collective-permute-start.10 = (bf16[512,384]{1,0:T(8,128)(2,1)S(1)}, bf16[512,384]{1,0:T(8,128)(2,1)S(1)}, u32[]{:S(2)}, u32[]{:S(2)}) collective-permute-start(bf16[512,384]{1,0:T(8,128)(2,1)S(1)} %collective-permute-done.4.refs_2_.rest_2_.rest_1_), channel_id=1, source_target_pairs={{2,6},{4,0},{6,10},{8,4},{10,14},{12,8},{3,7},{5,1},{7,11},{9,5},{... | collective-permute-start | bytes 1179656 | tf_op jit(solution)/shard_map/ppermute | solution.py:427
  42.8 23.0 %collective-permute-start.12 = (bf16[512,384]{1,0:T(8,128)(2,1)S(1)}, bf16[512,384]{1,0:T(8,128)(2,1)S(1)}, u32[]{:S(2)}, u32[]{:S(2)}) collective-permute-start(bf16[512,384]{1,0:T(8,128)(2,1)S(1)} %collective-permute-done.2.refs_0_.rest_1_), channel_id=1, source_target_pairs={{0,4},{4,8},{6,2},{8,12},{10,6},{14,10},{1,5},{5,9},{7,3},{9,13},{... | collective-permute-start | bytes 1179656 | tf_op jit(solution)/shard_map/ppermute | solution.py:426
  51.6 14.2 %collective-permute-start.13 = (bf16[272,384]{1,0:T(8,128)(2,1)S(1)}, bf16[272,384]{1,0:T(8,128)(2,1)S(1)}, u32[]{:S(2)}, u32[]{:S(2)}) collective-permute-start(bf16[272,384]{1,0:T(8,128)(2,1)S(1)} %partner_part.4.rest_4_), channel_id=1, source_target_pairs={{0,2},{2,0},{4,6},{6,4},{8,10},{10,8},{12,14},{14,12},{1,3},{3,1},... | collective-permute-start | bytes 626696 | tf_op jit(solution)/shard_map/ppermute | solution.py:480
  58.4 12.1 %collective-permute-start.16 = (bf16[272,384]{1,0:T(8,128)(2,1)S(1)}, bf16[272,384]{1,0:T(8,128)(2,1)S(1)}, u32[]{:S(2)}, u32[]{:S(2)}) collective-permute-start(bf16[272,384]{1,0:T(8,128)(2,1)S(1)} %partner_part.6.rest_4_), channel_id=1, source_target_pairs={{0,2},{2,0},{4,6},{6,4},{8,10},{10,8},{12,14},{14,12},{1,3},{3,1},... | collective-permute-start | bytes 626696 | tf_op jit(solution)/shard_map/ppermute | solution.py:481
  60.7 9.7 %collective-permute-start.17 = (bf16[272,384]{1,0:T(8,128)(2,1)S(1)}, bf16[272,384]{1,0:T(8,128)(2,1)S(1)}, u32[]{:S(2)}, u32[]{:S(2)}) collective-permute-start(bf16[272,384]{1,0:T(8,128)(2,1)S(1)} %partner_part.7), channel_id=1, source_target_pairs={{0,2},{2,0},{4,6},{6,4},{8,10},{10,8},{12,14},{14,12},{1,3},{3,1},... | collective-permute-start | bytes 626696 | tf_op jit(solution)/shard_map/ppermute | solution.py:482
  65.8 4.6 %slice-start = ((s8[4718592]{0:T(1024)(128)(4,1)}), s8[4194304]{0:T(1024)(128)(4,1)S(1)}, s32[]{:S(2)}) async-start(s8[4718592]{0:T(1024)(128)(4,1)} %bitcast), calls=%async_computation | async-start | bytes 8388608
  65.8 4.6 %slice-start.1 = ((s8[4718592]{0:T(1024)(128)(4,1)}), s8[524288]{0:T(1024)(128)(4,1)S(1)}, s32[]{:S(2)}) async-start(s8[4718592]{0:T(1024)(128)(4,1)} %bitcast), calls=%async_computation.1 | async-start | bytes 1048576
  68.1 6.0 %collective-permute-start.14 = (bf16[272,384]{1,0:T(8,128)(2,1)S(1)}, bf16[272,384]{1,0:T(8,128)(2,1)S(1)}, u32[]{:S(2)}, u32[]{:S(2)}) collective-permute-start(bf16[272,384]{1,0:T(8,128)(2,1)S(1)} %partner_part.5), channel_id=1, source_target_pairs={{0,2},{2,0},{4,6},{6,4},{8,10},{10,8},{12,14},{14,12},{1,3},{3,1},... | collective-permute-start | bytes 626696 | tf_op jit(solution)/shard_map/ppermute | solution.py:489

commit v16 on v15

--- a/solution.py
+++ b/solution.py
@@ -471,16 +471,17 @@
             after,
         )
 
-    part_low = partner_part((0, 3), ("major1", "major2"))
     own_early = own_part((3, 6), ("major1", "minor1"))
+    part_low = partner_part((0, 3), ("major1", "major2"), (own_early[1],))
+    own_middle = own_part((6, 9), ("major3", "minor1"), (part_low,))
     part_middle = partner_part(
-        (3, 6), ("major1", "minor1", "minor3", "nearest"), (part_low, own_early[1], major3)
+        (3, 6), ("major1", "minor1", "minor3", "nearest"), (own_middle[1],)
     )
     part_late = partner_part((6, 9), ("major3", "minor1", "minor3", "nearest"), (part_middle,))
     part_low = lax.ppermute(part_low, "frame", partner_moves)
     part_middle = lax.ppermute(part_middle, "frame", partner_moves)
+    own_late = own_part((9, 12), ("major3", "minor2"), (part_late,))
     part_late = lax.ppermute(part_late, "frame", partner_moves)
-    own_late = own_part((6, 12), ("major3", "minor1", "minor2"))
     part_high = partner_part(
         (9, 12),
         ("major3", "minor2", "minor4", "nearest"),
@@ -489,7 +490,7 @@
     part_high = lax.ppermute(part_high, "frame", partner_moves)
     own_low = own_part((0, 3), ("major1", "major2", "major4", "nearest"))
     weights = (*own_weight, *sib_weight)
-    owns = (((0, 3), own_low), ((3, 6), own_early), ((6, 12), own_late))
+    owns = (((0, 3), own_low), ((3, 6), own_early), ((6, 9), own_middle))
     base = project(
         (0, 9),
         owns,
@@ -499,7 +500,7 @@
         jnp.float32,
     )
     return project(
-        (9, 12), (((6, 12), own_late),), (((9, 12), part_high),), weights, base, jnp.bfloat16
+        (9, 12), (((9, 12), own_late),), (((9, 12), part_high),), weights, base, jnp.bfloat16
     )
 
 

time: 77.1 us -> 77.2 us (level)
  Pallas kernels: 22 us -> 22.8 us
    ppermute x1, waiting for transfers between devices: 2.15 us -> 0.25 us  [per_device(): major3 = lax.ppermute(to_major3, 'frame', away_moves)]
    ppermute x1, waiting for transfers between devices: 0.01 us -> 1.28 us  [per_device(): part_late = lax.ppermute(part_late, 'frame', partner_moves)]
    pallas_call x7 -> x8, Pallas kernels: 15.9 us -> 16.7 us  [run(): pl.pallas_call(body, grid=(1,), in_specs=[pl.BlockSpec(memory_space=pltpu...]
  transfers between devices with their start and end apart: 18 -> 18, of which waited for: 6 -> 7; matrix products, arithmetic and copies ran while one was open for 3% -> 3% of each run, Pallas kernels for 26% -> 27%
where the time goes in v16:
time: 77.2 us; the launch traced here: 76.9 us
  starting transfers between devices  31.7 us (41%)
  Pallas kernels  22.8 us (30%)
  waiting for transfers between devices  19.5 us (25%)
  local copies, waits for them, and re-layouts  2.05 us (3%)
    pallas_call x8, Pallas kernels, run(): pl.pallas_call(body, grid=(1,), in_specs=[pl.BlockSpec(memory_space=pltpu...  16.7 us
    ppermute x1, waiting for transfers between devices, per_device(): cross = lax.ppermute(pack(0, 3), 'frame', partner_moves)  9.8 us
    pallas_call x2, Pallas kernels, project(): pl.pallas_call(functools.partial(project_kernel, span, tuple((group for g...  6.06 us
    ppermute x1, starting transfers between devices, per_device(): major4 = lax.ppermute(major2, 'frame', away_moves)  4.75 us
    ppermute x1, starting transfers between devices, per_device(): major1 = lax.ppermute(pack(0, 6), 'frame', away_moves)  4.66 us
    ppermute x1, waiting for transfers between devices, per_device(): partner_query = lax.ppermute(queries, 'frame', partner_moves)  4.65 us
    ppermute x1, starting transfers between devices, per_device(): major3 = lax.ppermute(to_major3, 'frame', away_moves)  4.6 us
    ppermute x1, starting transfers between devices, per_device(): major2 = lax.ppermute(cross, 'frame', away_moves)  4.03 us
  transfers between devices with their start and end apart: 18, of which 7 were waited for; matrix products, arithmetic and copies ran while one was open for 3% of the time, Pallas kernels for 27%

profile of v16, /device:TPU:0, one launch (start us, length us, event | category | flops | bytes accessed | tf_op | source)
XLA Modules:
  0.0 76.9 jit_solution(1032568311601007318)
XLA Ops:
  0.0 0.5 collective-permute-start
  0.5 1.8 %fusion.1 = (bf16[256,768]{1,0:T(8,128)(2,1)S(1)}, bf16[256,768]{1,0:T(8,128)(2,1)S(1)}, bf16[256,768]{1,0:T(8,128)(2,1)S(1)}, bf16[256,768]{1,0:T(8,128)(2,1)S(...) fusion(bf16[256,1536]{1,0:T(8,128)(2,1)} %keys.15, bf16[256,1536]{1,0:T(8,128)(2,1)} %values.15), kind=kLoop, calls=%fused_computation.7 | loop fusion | bytes 4718592 | tf_op jit(solution)/shard_map/slice | solution.py:406
  2.3 4.7 %collective-permute-start.7 = (bf16[512,768]{1,0:T(8,128)(2,1)S(1)}, bf16[512,768]{1,0:T(8,128)(2,1)S(1)}, u32[]{:S(2)}, u32[]{:S(2)}) collective-permute-start(bf16[512,768]{1,0:T(8,128)(2,1)S(1)} %pad_maximum_fusion), channel_id=1, source_target_pairs={{0,4},{4,8},{6,2},{8,12},{10,6},{14,10},{1,5},{5,9},{7,3},{9,13},{... | collective-permute-start | bytes 2359304 | tf_op jit(solution)/shard_map/ppermute | solution.py:414
  7.0 1.4 %collective-permute-start.9 = (bf16[512,768]{1,0:T(8,128)(2,1)S(1)}, bf16[512,768]{1,0:T(8,128)(2,1)S(1)}, u32[]{:S(2)}, u32[]{:S(2)}) collective-permute-start(bf16[512,768]{1,0:T(8,128)(2,1)S(1)} %pad_maximum_fusion.2), channel_id=1, source_target_pairs={{2,6},{4,0},{6,10},{8,4},{10,14},{12,8},{3,7},{5,1},{7,11},{9,5},{... | collective-permute-start | bytes 2359304 | tf_op jit(solution)/shard_map/ppermute | solution.py:415
  8.6 2.7 %collective-permute-start.1 = (bf16[512,384]{1,0:T(8,128)(2,1)S(1)}, bf16[512,384]{1,0:T(8,128)(2,1)S(1)}, u32[]{:S(2)}, u32[]{:S(2)}) collective-permute-start(bf16[512,384]{1,0:T(8,128)(2,1)S(1)} %pad_maximum_fusion.3), channel_id=1, source_target_pairs={{0,2},{2,0},{4,6},{6,4},{8,10},{10,8},{12,14},{14,12},{1,3},{3,1},... | collective-permute-start | bytes 1179656 | tf_op jit(solution)/shard_map/ppermute | solution.py:418
  11.3 0.1 collective-permute-start.3
  11.4 9.8 %collective-permute-done.1.refs_1_ = bf16[512,384]{1,0:T(8,128)(2,1)S(1)} collective-permute-done((bf16[512,384]{1,0:T(8,128)(2,1)S(1)}, bf16[512,384]{1,0:T(8,128)(2,1)S(1)}, u32[]{:S(2)}, u32[]{:S(2)}) %collective-permute-start.1) | collective-permute-done | bytes 393248 | tf_op jit(solution)/shard_map/ppermute | solution.py:418
  21.2 4.0 %collective-permute-start.2 = (bf16[512,384]{1,0:T(8,128)(2,1)S(1)}, bf16[512,384]{1,0:T(8,128)(2,1)S(1)}, u32[]{:S(2)}, u32[]{:S(2)}) collective-permute-start(bf16[512,384]{1,0:T(8,128)(2,1)S(1)} %get-tuple-element.17), channel_id=1, source_target_pairs={{0,4},{4,8},{6,2},{8,12},{10,6},{14,10},{1,5},{5,9},{7,3},{9,13},{... | collective-permute-start | bytes 1179656 | tf_op jit(solution)/shard_map/ppermute | solution.py:422
  25.3 1.3 %collective-permute-start.4 = (bf16[512,384]{1,0:T(8,128)(2,1)S(1)}, bf16[512,384]{1,0:T(8,128)(2,1)S(1)}, u32[]{:S(2)}, u32[]{:S(2)}) collective-permute-start(bf16[512,384]{1,0:T(8,128)(2,1)S(1)} %get-tuple-element.18), channel_id=1, source_target_pairs={{2,6},{4,0},{6,10},{8,4},{10,14},{12,8},{3,7},{5,1},{7,11},{9,5},{... | collective-permute-start | bytes 1179656 | tf_op jit(solution)/shard_map/ppermute | solution.py:420
  26.8 4.6 %collective-permute-start.8 = (bf16[512,768]{1,0:T(8,128)(2,1)S(1)}, bf16[512,768]{1,0:T(8,128)(2,1)S(1)}, u32[]{:S(2)}, u32[]{:S(2)}) collective-permute-start(bf16[512,768]{1,0:T(8,128)(2,1)S(1)} %tie.5), channel_id=1, source_target_pairs={{0,4},{4,8},{6,2},{8,12},{10,6},{14,10},{1,5},{5,9},{7,3},{9,13},{... | collective-permute-start | bytes 2359304 | tf_op jit(solution)/shard_map/ppermute | solution.py:425
  31.4 1.3 %collective-permute-start.10 = (bf16[512,768]{1,0:T(8,128)(2,1)S(1)}, bf16[512,768]{1,0:T(8,128)(2,1)S(1)}, u32[]{:S(2)}, u32[]{:S(2)}) collective-permute-start(bf16[512,768]{1,0:T(8,128)(2,1)S(1)} %collective-permute-done.9.rest_1_), channel_id=1, source_target_pairs={{2,6},{4,0},{6,10},{8,4},{10,14},{12,8},{3,7},{5,1},{7,11},{9,5},{... | collective-permute-start | bytes 2359304 | tf_op jit(solution)/shard_map/ppermute | solution.py:423
  32.7 4.7 %collective-permute-done.3.refs_1_.query = bf16[256,1536]{1,0:T(8,128)(2,1)S(1)} collective-permute-done((bf16[256,1536]{1,0:T(8,128)(2,1)S(1)}, bf16[256,1536]{1,0:T(8,128)(2,1)S(1)}, u32[]{:S(2)}, u32[]{:S(2)}) %collective-permute-start.3) | collective-permute-done | bytes 786464 | tf_op jit(solution)/shard_map/ppermute | solution.py:421
  37.4 1.8 %collective-permute-done.4.refs_2_.rest_1_ = bf16[512,384]{1,0:T(8,128)(2,1)S(1)} collective-permute-done((bf16[512,384]{1,0:T(8,128)(2,1)S(1)}, bf16[512,384]{1,0:T(8,128)(2,1)S(1)}, u32[]{:S(2)}, u32[]{:S(2)}) %collective-permute-start.4) | collective-permute-done | bytes 393248 | tf_op jit(solution)/shard_map/ppermute | solution.py:420
  39.2 0.5 collective-permute-start.6
  39.9 1.6 %collective-permute-done.5.sib_keys = bf16[256,1536]{1,0:T(8,128)(2,1)S(1)} collective-permute-done((bf16[256,1536]{1,0:T(8,128)(2,1)S(1)}, bf16[256,1536]{1,0:T(8,128)(2,1)S(1)}, u32[]{:S(2)}, u32[]{:S(2)}) %collective-permute-start.5) | collective-permute-done | bytes 786464 | tf_op jit(solution)/shard_map/ppermute | solution.py:429
  41.5 1.3 %collective-permute-start.12 = (bf16[512,384]{1,0:T(8,128)(2,1)S(1)}, bf16[512,384]{1,0:T(8,128)(2,1)S(1)}, u32[]{:S(2)}, u32[]{:S(2)}) collective-permute-start(bf16[512,384]{1,0:T(8,128)(2,1)S(1)} %collective-permute-done.4.refs_2_.rest_1_), channel_id=1, source_target_pairs={{2,6},{4,0},{6,10},{8,4},{10,14},{12,8},{3,7},{5,1},{7,11},{9,5},{... | collective-permute-start | bytes 1179656 | tf_op jit(solution)/shard_map/ppermute | solution.py:427
  42.8 4.8 %collective-permute-start.13 = (bf16[512,384]{1,0:T(8,128)(2,1)S(1)}, bf16[512,384]{1,0:T(8,128)(2,1)S(1)}, u32[]{:S(2)}, u32[]{:S(2)}) collective-permute-start(bf16[512,384]{1,0:T(8,128)(2,1)S(1)} %collective-permute-done.2.refs_0_.rest_1_), channel_id=1, source_target_pairs={{0,4},{4,8},{6,2},{8,12},{10,6},{14,10},{1,5},{5,9},{7,3},{9,13},{... | collective-permute-start | bytes 1179656 | tf_op jit(solution)/shard_map/ppermute | solution.py:426
  47.6 1.9 %own_part.4 = (f32[256,384]{1,0:T(8,128)S(1)}, f32[256,128]{1,0:T(8,128)S(1)}) custom-call(s32[8,8]{1,0:T(8,128)S(1)} %copy-done.3, bf16[256,1536]{1,0:T(8,128)(2,1)S(1)} %copy-done.2, bf16[256,1536]{1,0:T(8,128)(2,1)S(1)} %copy-done, bf16[256,1536]{1,0:T(8,128)(2,1)S(1)} %copy-done.1, bf16[256,1536]{1,0:T(8,128)(2,1)S(1)} %collective-permute-done.5.sib_keys, ...), custom_call_target="tpu_custom_call" | custom-call | flops 301989888 | bytes 1048576 | tf_op jit(solution)/shard_map/own_part/pallas_call | solution.py:321
  49.5 1.9 %partner_part.4.rest_2_ = bf16[272,384]{1,0:T(8,128)(2,1)S(1)} custom-call(s32[8,8]{1,0:T(8,128)S(1)} %copy-done.3, bf16[256,1536]{1,0:T(8,128)(2,1)S(1)} %collective-permute-done.3.refs_1_.query, bf16[256,1536]{1,0:T(8,128)(2,1)S(1)} %copy-done, bf16[256,1536]{1,0:T(8,128)(2,1)S(1)} %copy-done.1, bf16[256,1536]{1,0:T(8,128)(2,1)S(1)} %collective-permute-done.5.sib_keys, ...), custom_call_target="tpu_custom_call" | custom-call | flops 301989888 | bytes 1048576 | tf_op jit(solution)/shard_map/partner_part/pallas_call | solution.py:321
  51.4 0.3 collective-permute-done.8.rest_0_
  51.6 2.4 %collective-permute-start.14 = (bf16[272,384]{1,0:T(8,128)(2,1)S(1)}, bf16[272,384]{1,0:T(8,128)(2,1)S(1)}, u32[]{:S(2)}, u32[]{:S(2)}) collective-permute-start(bf16[272,384]{1,0:T(8,128)(2,1)S(1)} %partner_part.4.rest_2_), channel_id=1, source_target_pairs={{0,2},{2,0},{4,6},{6,4},{8,10},{10,8},{12,14},{14,12},{1,3},{3,1},... | collective-permute-start | bytes 626696 | tf_op jit(solution)/shard_map/ppermute | solution.py:481
  54.1 1.9 %own_part.5 = (f32[256,384]{1,0:T(8,128)S(1)}, f32[256,128]{1,0:T(8,128)S(1)}) custom-call(s32[8,8]{1,0:T(8,128)S(1)} %copy-done.3, bf16[256,1536]{1,0:T(8,128)(2,1)S(1)} %copy-done.2, bf16[256,1536]{1,0:T(8,128)(2,1)S(1)} %copy-done, bf16[256,1536]{1,0:T(8,128)(2,1)S(1)} %copy-done.1, bf16[256,1536]{1,0:T(8,128)(2,1)S(1)} %collective-permute-done.5.sib_keys, ...), custom_call_target="tpu_custom_call" | custom-call | flops 301989888 | bytes 1048576 | tf_op jit(solution)/shard_map/own_part/pallas_call | solution.py:321
  56.0 0.1 collective-permute-done.10.rest_2_
  56.1 2.3 %partner_part.5.rest_4_ = bf16[272,384]{1,0:T(8,128)(2,1)S(1)} custom-call(s32[8,8]{1,0:T(8,128)S(1)} %copy-done.3, bf16[256,1536]{1,0:T(8,128)(2,1)S(1)} %collective-permute-done.3.refs_1_.query, bf16[256,1536]{1,0:T(8,128)(2,1)S(1)} %copy-done, bf16[256,1536]{1,0:T(8,128)(2,1)S(1)} %copy-done.1, bf16[256,1536]{1,0:T(8,128)(2,1)S(1)} %collective-permute-done.5.sib_keys, ...), custom_call_target="tpu_custom_call" | custom-call | flops 301989888 | bytes 1048576 | tf_op jit(solution)/shard_map/partner_part/pallas_call | solution.py:321
  58.4 2.3 %partner_part.6.rest_2_ = bf16[272,384]{1,0:T(8,128)(2,1)S(1)} custom-call(s32[8,8]{1,0:T(8,128)S(1)} %copy-done.3, bf16[256,1536]{1,0:T(8,128)(2,1)S(1)} %collective-permute-done.3.refs_1_.query, bf16[256,1536]{1,0:T(8,128)(2,1)S(1)} %copy-done, bf16[256,1536]{1,0:T(8,128)(2,1)S(1)} %copy-done.1, bf16[256,1536]{1,0:T(8,128)(2,1)S(1)} %collective-permute-done.5.sib_keys, ...), custom_call_target="tpu_custom_call" | custom-call | flops 301989888 | bytes 1048576 | tf_op jit(solution)/shard_map/partner_part/pallas_call | solution.py:321
  60.7 2.1 %collective-permute-start.17 = (bf16[272,384]{1,0:T(8,128)(2,1)S(1)}, bf16[272,384]{1,0:T(8,128)(2,1)S(1)}, u32[]{:S(2)}, u32[]{:S(2)}) collective-permute-start(bf16[272,384]{1,0:T(8,128)(2,1)S(1)} %partner_part.6.rest_2_), channel_id=1, source_target_pairs={{0,2},{2,0},{4,6},{6,4},{8,10},{10,8},{12,14},{14,12},{1,3},{3,1},... | collective-permute-start | bytes 626696 | tf_op jit(solution)/shard_map/ppermute | solution.py:484
  62.8 1.9 %own_part.6 = (f32[256,384]{1,0:T(8,128)S(1)}, f32[256,128]{1,0:T(8,128)S(1)}) custom-call(s32[8,8]{1,0:T(8,128)S(1)} %copy-done.3, bf16[256,1536]{1,0:T(8,128)(2,1)S(1)} %copy-done.2, bf16[256,1536]{1,0:T(8,128)(2,1)S(1)} %copy-done, bf16[256,1536]{1,0:T(8,128)(2,1)S(1)} %copy-done.1, bf16[256,1536]{1,0:T(8,128)(2,1)S(1)} %collective-permute-done.5.sib_keys, ...), custom_call_target="tpu_custom_call" | custom-call | flops 301989888 | bytes 1048576 | tf_op jit(solution)/shard_map/own_part/pallas_call | solution.py:321
  64.7 2.3 %partner_part.7 = bf16[272,384]{1,0:T(8,128)(2,1)S(1)} custom-call(s32[8,8]{1,0:T(8,128)S(1)} %copy-done.3, bf16[256,1536]{1,0:T(8,128)(2,1)S(1)} %collective-permute-done.3.refs_1_.query, bf16[256,1536]{1,0:T(8,128)(2,1)S(1)} %copy-done, bf16[256,1536]{1,0:T(8,128)(2,1)S(1)} %copy-done.1, bf16[256,1536]{1,0:T(8,128)(2,1)S(1)} %collective-permute-done.5.sib_keys, ...), custom_call_target="tpu_custom_call" | custom-call | flops 301989888 | bytes 1048576 | tf_op jit(solution)/shard_map/partner_part/pallas_call | solution.py:321
  67.1 2.2 %own_part.7 = (f32[256,384]{1,0:T(8,128)S(1)}, f32[256,128]{1,0:T(8,128)S(1)}) custom-call(s32[8,8]{1,0:T(8,128)S(1)} %copy-done.3, bf16[256,1536]{1,0:T(8,128)(2,1)S(1)} %copy-done.2, bf16[256,1536]{1,0:T(8,128)(2,1)S(1)} %copy-done, bf16[256,1536]{1,0:T(8,128)(2,1)S(1)} %copy-done.1, bf16[256,1536]{1,0:T(8,128)(2,1)S(1)} %collective-permute-done.5.sib_keys, ...), custom_call_target="tpu_custom_call" | custom-call | flops 301989888 | bytes 1048576 | tf_op jit(solution)/shard_map/own_part/pallas_call | solution.py:321
  69.4 1.3 %collective-permute-done.17.refs_10_ = bf16[272,384]{1,0:T(8,128)(2,1)S(1)} collective-permute-done((bf16[272,384]{1,0:T(8,128)(2,1)S(1)}, bf16[272,384]{1,0:T(8,128)(2,1)S(1)}, u32[]{:S(2)}, u32[]{:S(2)}) %collective-permute-start.17) | collective-permute-done | bytes 208928 | tf_op jit(solution)/shard_map/ppermute | solution.py:484
  70.6 3.7 %merge_and_project.2.refs_5_ = f32[256,3072]{1,0:T(8,128)S(1)} custom-call(bf16[768,3072]{1,0:T(8,128)(2,1)S(1)} %bitcast.1, bf16[768,3072]{1,0:T(8,128)(2,1)S(1)} %collective-permute-done.refs_0_.rest_7_.refs_1_, f32[256,384]{1,0:T(8,128)S(1)} %get-tuple-element.25.refs_2_, f32[256,128]{1,0:T(8,128)S(1)} %get-tuple-element.26.refs_3_, ...), custom_call_target="tpu_custom_call" | custom-call | flops 1811939328 | bytes 4194304 | tf_op jit(solution)/shard_map/merge_and_project/pallas_call | solution.py:369
  74.3 2.4 %merge_and_project.3 = bf16[256,3072]{1,0:T(8,128)(2,1)} custom-call(bf16[768,3072]{1,0:T(8,128)(2,1)S(1)} %bitcast.1, bf16[768,3072]{1,0:T(8,128)(2,1)S(1)} %collective-permute-done.refs_0_.rest_7_.refs_1_, f32[256,384]{1,0:T(8,128)S(1)} %get-tuple-element.23.refs_2_, f32[256,128]{1,0:T(8,128)S(1)} %get-tuple-element.24.rest_4_.refs_3_, ...), custom_call_target="tpu_custom_call" | custom-call | flops 603979776 | bytes 4194304 | tf_op jit(solution)/shard_map/merge_and_project/pallas_call | solution.py:369
  (43 shorter events, 0.8 us)
Async XLA Ops:
  0.0 21.2 %collective-permute-start = (bf16[768,3072]{1,0:T(8,128)(2,1)}, bf16[768,3072]{1,0:T(8,128)(2,1)S(1)}, u32[]{:S(2)}, u32[]{:S(2)}) collective-permute-start(bf16[768,3072]{1,0:T(8,128)(2,1)} %refs_0_.3), channel_id=1, source_target_pairs={{0,1},{1,0},{2,3},{3,2},{4,5},{5,4},{6,7},{7,6},{8,9},{9,8},{10,11... | collective-permute-start | bytes 14155784 | tf_op jit(solution)/shard_map/ppermute | solution.py:417
  2.2 6.3 %copy-start = (bf16[256,1536]{1,0:T(8,128)(2,1)S(1)}, bf16[256,1536]{1,0:T(8,128)(2,1)}, u32[]{:S(2)}) copy-start(bf16[256,1536]{1,0:T(8,128)(2,1)} %keys.15) | copy-start | bytes 2359300
  2.2 6.3 %copy-start.1 = (bf16[256,1536]{1,0:T(8,128)(2,1)S(1)}, bf16[256,1536]{1,0:T(8,128)(2,1)}, u32[]{:S(2)}) copy-start(bf16[256,1536]{1,0:T(8,128)(2,1)} %values.15) | copy-start | bytes 2359300
  2.3 24.4 %collective-permute-start.7 = (bf16[512,768]{1,0:T(8,128)(2,1)S(1)}, bf16[512,768]{1,0:T(8,128)(2,1)S(1)}, u32[]{:S(2)}, u32[]{:S(2)}) collective-permute-start(bf16[512,768]{1,0:T(8,128)(2,1)S(1)} %pad_maximum_fusion), channel_id=1, source_target_pairs={{0,4},{4,8},{6,2},{8,12},{10,6},{14,10},{1,5},{5,9},{7,3},{9,13},{... | collective-permute-start | bytes 2359304 | tf_op jit(solution)/shard_map/ppermute | solution.py:414
  7.0 4.3 %copy-start.2 = (bf16[256,1536]{1,0:T(8,128)(2,1)S(1)}, bf16[256,1536]{1,0:T(8,128)(2,1)}, u32[]{:S(2)}) copy-start(bf16[256,1536]{1,0:T(8,128)(2,1)} %query.7) | copy-start | bytes 2359300
  7.0 24.3 %collective-permute-start.9 = (bf16[512,768]{1,0:T(8,128)(2,1)S(1)}, bf16[512,768]{1,0:T(8,128)(2,1)S(1)}, u32[]{:S(2)}, u32[]{:S(2)}) collective-permute-start(bf16[512,768]{1,0:T(8,128)(2,1)S(1)} %pad_maximum_fusion.2), channel_id=1, source_target_pairs={{2,6},{4,0},{6,10},{8,4},{10,14},{12,8},{3,7},{5,1},{7,11},{9,5},{... | collective-permute-start | bytes 2359304 | tf_op jit(solution)/shard_map/ppermute | solution.py:415
  8.6 12.6 %collective-permute-start.1 = (bf16[512,384]{1,0:T(8,128)(2,1)S(1)}, bf16[512,384]{1,0:T(8,128)(2,1)S(1)}, u32[]{:S(2)}, u32[]{:S(2)}) collective-permute-start(bf16[512,384]{1,0:T(8,128)(2,1)S(1)} %pad_maximum_fusion.3), channel_id=1, source_target_pairs={{0,2},{2,0},{4,6},{6,4},{8,10},{10,8},{12,14},{14,12},{1,3},{3,1},... | collective-permute-start | bytes 1179656 | tf_op jit(solution)/shard_map/ppermute | solution.py:418
  11.3 26.1 %collective-permute-start.3 = (bf16[256,1536]{1,0:T(8,128)(2,1)S(1)}, bf16[256,1536]{1,0:T(8,128)(2,1)S(1)}, u32[]{:S(2)}, u32[]{:S(2)}) collective-permute-start(bf16[256,1536]{1,0:T(8,128)(2,1)S(1)} %copy-done.2), channel_id=1, source_target_pairs={{0,2},{2,0},{4,6},{6,4},{8,10},{10,8},{12,14},{14,12},{1,3},{3,1},... | collective-permute-start | bytes 2359304 | tf_op jit(solution)/shard_map/ppermute | solution.py:421
  21.2 16.1 %collective-permute-start.2 = (bf16[512,384]{1,0:T(8,128)(2,1)S(1)}, bf16[512,384]{1,0:T(8,128)(2,1)S(1)}, u32[]{:S(2)}, u32[]{:S(2)}) collective-permute-start(bf16[512,384]{1,0:T(8,128)(2,1)S(1)} %get-tuple-element.17), channel_id=1, source_target_pairs={{0,4},{4,8},{6,2},{8,12},{10,6},{14,10},{1,5},{5,9},{7,3},{9,13},{... | collective-permute-start | bytes 1179656 | tf_op jit(solution)/shard_map/ppermute | solution.py:422
  25.3 13.9 %collective-permute-start.4 = (bf16[512,384]{1,0:T(8,128)(2,1)S(1)}, bf16[512,384]{1,0:T(8,128)(2,1)S(1)}, u32[]{:S(2)}, u32[]{:S(2)}) collective-permute-start(bf16[512,384]{1,0:T(8,128)(2,1)S(1)} %get-tuple-element.18), channel_id=1, source_target_pairs={{2,6},{4,0},{6,10},{8,4},{10,14},{12,8},{3,7},{5,1},{7,11},{9,5},{... | collective-permute-start | bytes 1179656 | tf_op jit(solution)/shard_map/ppermute | solution.py:420
  26.8 24.9 %collective-permute-start.8 = (bf16[512,768]{1,0:T(8,128)(2,1)S(1)}, bf16[512,768]{1,0:T(8,128)(2,1)S(1)}, u32[]{:S(2)}, u32[]{:S(2)}) collective-permute-start(bf16[512,768]{1,0:T(8,128)(2,1)S(1)} %tie.5), channel_id=1, source_target_pairs={{0,4},{4,8},{6,2},{8,12},{10,6},{14,10},{1,5},{5,9},{7,3},{9,13},{... | collective-permute-start | bytes 2359304 | tf_op jit(solution)/shard_map/ppermute | solution.py:425
  31.4 24.7 %collective-permute-start.10 = (bf16[512,768]{1,0:T(8,128)(2,1)S(1)}, bf16[512,768]{1,0:T(8,128)(2,1)S(1)}, u32[]{:S(2)}, u32[]{:S(2)}) collective-permute-start(bf16[512,768]{1,0:T(8,128)(2,1)S(1)} %collective-permute-done.9.rest_1_), channel_id=1, source_target_pairs={{2,6},{4,0},{6,10},{8,4},{10,14},{12,8},{3,7},{5,1},{7,11},{9,5},{... | collective-permute-start | bytes 2359304 | tf_op jit(solution)/shard_map/ppermute | solution.py:423
  39.2 8.3 %copy-start.3 = (s32[8,8]{1,0:T(8,128)S(1)}, s32[8,8]{1,0:T(8,128)}, u32[]{:S(2)}) copy-start(s32[8,8]{1,0:T(8,128)} %table_ref.15) | copy-start | bytes 772
  39.2 2.3 %collective-permute-start.5 = (bf16[256,1536]{1,0:T(8,128)(2,1)S(1)}, bf16[256,1536]{1,0:T(8,128)(2,1)S(1)}, u32[]{:S(2)}, u32[]{:S(2)}) collective-permute-start(bf16[256,1536]{1,0:T(8,128)(2,1)S(1)} %get-tuple-element.19), channel_id=1, source_target_pairs={{0,1},{1,0},{2,3},{3,2},{4,5},{5,4},{6,7},{7,6},{8,9},{9,8},{10,11... | collective-permute-start | bytes 2359304 | tf_op jit(solution)/shard_map/ppermute | solution.py:429
  39.2 3.6 %collective-permute-start.6 = (bf16[256,1536]{1,0:T(8,128)(2,1)S(1)}, bf16[256,1536]{1,0:T(8,128)(2,1)S(1)}, u32[]{:S(2)}, u32[]{:S(2)}) collective-permute-start(bf16[256,1536]{1,0:T(8,128)(2,1)S(1)} %get-tuple-element.20), channel_id=1, source_target_pairs={{0,1},{1,0},{2,3},{3,2},{4,5},{5,4},{6,7},{7,6},{8,9},{9,8},{10,11... | collective-permute-start | bytes 2359304 | tf_op jit(solution)/shard_map/ppermute | solution.py:430
  39.8 16.2 %collective-permute-start.11 = (bf16[256,1536]{1,0:T(8,128)(2,1)S(1)}, bf16[256,1536]{1,0:T(8,128)(2,1)S(1)}, u32[]{:S(2)}, u32[]{:S(2)}) collective-permute-start(bf16[256,1536]{1,0:T(8,128)(2,1)S(1)} %maximum_maximum_fusion), channel_id=1, source_target_pairs={{0,1},{1,0},{2,3},{3,2},{4,5},{5,4},{6,7},{7,6},{8,9},{9,8},{10,11... | collective-permute-start | bytes 2359304 | tf_op jit(solution)/shard_map/ppermute | solution.py:431
  41.5 23.2 %collective-permute-start.12 = (bf16[512,384]{1,0:T(8,128)(2,1)S(1)}, bf16[512,384]{1,0:T(8,128)(2,1)S(1)}, u32[]{:S(2)}, u32[]{:S(2)}) collective-permute-start(bf16[512,384]{1,0:T(8,128)(2,1)S(1)} %collective-permute-done.4.refs_2_.rest_1_), channel_id=1, source_target_pairs={{2,6},{4,0},{6,10},{8,4},{10,14},{12,8},{3,7},{5,1},{7,11},{9,5},{... | collective-permute-start | bytes 1179656 | tf_op jit(solution)/shard_map/ppermute | solution.py:427
  42.8 21.9 %collective-permute-start.13 = (bf16[512,384]{1,0:T(8,128)(2,1)S(1)}, bf16[512,384]{1,0:T(8,128)(2,1)S(1)}, u32[]{:S(2)}, u32[]{:S(2)}) collective-permute-start(bf16[512,384]{1,0:T(8,128)(2,1)S(1)} %collective-permute-done.2.refs_0_.rest_1_), channel_id=1, source_target_pairs={{0,4},{4,8},{6,2},{8,12},{10,6},{14,10},{1,5},{5,9},{7,3},{9,13},{... | collective-permute-start | bytes 1179656 | tf_op jit(solution)/shard_map/ppermute | solution.py:426
  51.6 13.1 %collective-permute-start.14 = (bf16[272,384]{1,0:T(8,128)(2,1)S(1)}, bf16[272,384]{1,0:T(8,128)(2,1)S(1)}, u32[]{:S(2)}, u32[]{:S(2)}) collective-permute-start(bf16[272,384]{1,0:T(8,128)(2,1)S(1)} %partner_part.4.rest_2_), channel_id=1, source_target_pairs={{0,2},{2,0},{4,6},{6,4},{8,10},{10,8},{12,14},{14,12},{1,3},{3,1},... | collective-permute-start | bytes 626696 | tf_op jit(solution)/shard_map/ppermute | solution.py:481
  58.4 11.0 %collective-permute-start.16 = (bf16[272,384]{1,0:T(8,128)(2,1)S(1)}, bf16[272,384]{1,0:T(8,128)(2,1)S(1)}, u32[]{:S(2)}, u32[]{:S(2)}) collective-permute-start(bf16[272,384]{1,0:T(8,128)(2,1)S(1)} %partner_part.5.rest_4_), channel_id=1, source_target_pairs={{0,2},{2,0},{4,6},{6,4},{8,10},{10,8},{12,14},{14,12},{1,3},{3,1},... | collective-permute-start | bytes 626696 | tf_op jit(solution)/shard_map/ppermute | solution.py:482
  60.7 9.9 %collective-permute-start.17 = (bf16[272,384]{1,0:T(8,128)(2,1)S(1)}, bf16[272,384]{1,0:T(8,128)(2,1)S(1)}, u32[]{:S(2)}, u32[]{:S(2)}) collective-permute-start(bf16[272,384]{1,0:T(8,128)(2,1)S(1)} %partner_part.6.rest_2_), channel_id=1, source_target_pairs={{0,2},{2,0},{4,6},{6,4},{8,10},{10,8},{12,14},{14,12},{1,3},{3,1},... | collective-permute-start | bytes 626696 | tf_op jit(solution)/shard_map/ppermute | solution.py:484
  64.7 5.9 %slice-start = ((s8[4718592]{0:T(1024)(128)(4,1)}), s8[4194304]{0:T(1024)(128)(4,1)S(1)}, s32[]{:S(2)}) async-start(s8[4718592]{0:T(1024)(128)(4,1)} %bitcast), calls=%async_computation | async-start | bytes 8388608
  64.7 5.9 %slice-start.1 = ((s8[4718592]{0:T(1024)(128)(4,1)}), s8[524288]{0:T(1024)(128)(4,1)S(1)}, s32[]{:S(2)}) async-start(s8[4718592]{0:T(1024)(128)(4,1)} %bitcast), calls=%async_computation.1 | async-start | bytes 1048576
  67.0 7.2 %collective-permute-start.15 = (bf16[272,384]{1,0:T(8,128)(2,1)S(1)}, bf16[272,384]{1,0:T(8,128)(2,1)S(1)}, u32[]{:S(2)}, u32[]{:S(2)}) collective-permute-start(bf16[272,384]{1,0:T(8,128)(2,1)S(1)} %partner_part.7), channel_id=1, source_target_pairs={{0,2},{2,0},{4,6},{6,4},{8,10},{10,8},{12,14},{14,12},{1,3},{3,1},... | collective-permute-start | bytes 626696 | tf_op jit(solution)/shard_map/ppermute | solution.py:490
